TPU v7x, 32 devices: a whole 2x2x4 slice. The times are simulated.
32 devices in a mesh: sec: 2 (over x), dev: 16 (over z, y, core).
Axes of the slice: x: 2, y: 2, z: 4, core: 2. Of those that a mesh axis runs over, the one named last changes fastest.
Arguments:
- hidden_in: bfloat16 [128, 7168], P(('sec', 'dev')), may hold values from -6 to 6
- expert_ids: int32 [128, 2], P(('sec', 'dev')), may hold values from 0 to 3, all different within a row; in each aligned block of 4 rows (0 to 3, 4 to 7, ...) at most 4 rows name the same one
- gate_scores: bfloat16 [128, 2], P(('sec', 'dev')), may hold values from 0.099609375 to 1
- w_gate: bfloat16 [7168, 8192], P(None, ('sec', 'dev')), may hold values from -0.0625 to 0.0625
- w_up: bfloat16 [7168, 8192], P(None, ('sec', 'dev')), may hold values from -0.0625 to 0.0625
- w_down: bfloat16 [8192, 7168], P(('sec', 'dev')), may hold values from -0.125 to 0.125
- norm_gain: float32 [7168], replicated, may hold values from 0.1 to 1.9
- w_kv: bfloat16 [7168, 576], P('dev'), may hold values from -0.0625 to 0.0625
- queries: bfloat16 [128, 64, 576], P(('sec', 'dev')), may hold values from -40 to 40
- kv_cache: bfloat16 [128, 256, 576], P(('sec', 'dev')), may hold values from -6 to 6
- lengths: int32 [128], P(('sec', 'dev')), may hold values from 2 to 256, as said below
Outputs:
- moe_out: bfloat16 [128, 7168], P(('sec', 'dev'))
- new_latent: bfloat16 [128, 576], P(('sec', 'dev'))
- attended: bfloat16 [128, 64, 512], P(('sec', 'dev'))
Inputs may be any that keep to these rules, and one draw needn't show every extreme that they name: `expert_ids`: each row names 2 different experts; among the 4 rows of one device no expert is named by more than 4 rows, and some device's rows name some expert exactly 4 times in every draw. `lengths`: some rows have all 256 positions filled in every draw.
All inputs are finite; a program needn't handle non-finite values.
Results may differ from a plain program's by a relative error of at most 0.009.
Values may be sent and summed in bfloat16 or wider, within the bound.
No kernel may reach another device: no remote copies, remote signals or barrier semaphores. Data moves between devices by JAX's collectives and lax.ppermute only.
A program may use at most 128 MiB of HBM per device.

v0:
```python
import jax
import jax.numpy as jnp
from jax import lax
from jax.sharding import PartitionSpec as P

FF = 2048
KV = 512


score_scale = 192.0 ** (-0.5)
norm_eps = 1e-06


def shifted(x, axis, by):
    length = lax.axis_size(axis)
    return lax.ppermute(x, axis, [(i, (i + by) % length) for i in range(length)])


def attend(queries, kv_cache, lengths, latent_new, value_width):
    length_max = kv_cache.shape[1]
    scores = (
        jnp.einsum("bhl,bpl->bhp", queries, kv_cache, preferred_element_type=jnp.float32)
        * score_scale
    )
    visible = jnp.arange(length_max, dtype=jnp.int32)[None, None, :] < lengths[:, None, None]
    scores = jnp.where(visible, scores, -1e30)
    own_score = (
        jnp.einsum("bhl,bl->bh", queries, latent_new, preferred_element_type=jnp.float32)
        * score_scale
    )
    peak = jnp.maximum(jnp.max(scores, axis=2), own_score)
    spread = jnp.exp(scores - peak[:, :, None])
    own_weight = jnp.exp(own_score - peak)
    denominator = jnp.sum(spread, axis=2) + own_weight
    cache_weights = (spread / denominator[:, :, None]).astype(jnp.bfloat16)
    own_prob = (own_weight / denominator).astype(jnp.bfloat16)
    values = kv_cache[:, :, :value_width]
    combined = jnp.einsum("bhp,bpv->bhv", cache_weights, values, preferred_element_type=jnp.float32)
    combined = combined + own_prob.astype(jnp.float32)[:, :, None] * latent_new[
        :, None, :value_width
    ].astype(jnp.float32)
    return combined.astype(jnp.bfloat16)


def route_tables(expert_ids, gate_scores, section, per_section, total_experts, capacity):
    row_count, pick_count = expert_ids.shape
    weights = gate_scores.astype(jnp.float32)
    weights = weights / jnp.sum(weights, axis=1, keepdims=True)
    flat_ids = expert_ids.reshape(-1)
    onehot = (flat_ids[:, None] == jnp.arange(total_experts, dtype=jnp.int32)[None, :]).astype(
        jnp.int32
    )
    before = jnp.cumsum(onehot, axis=0) - onehot
    position = jnp.sum(before * onehot, axis=1)
    local_ids = flat_ids - section * per_section
    matches = (
        local_ids[None, None, :] == jnp.arange(per_section, dtype=jnp.int32)[:, None, None]
    ) & (position[None, None, :] == jnp.arange(capacity, dtype=jnp.int32)[None, :, None])
    matches = matches.reshape(per_section, capacity, row_count, pick_count)
    members = jnp.sum(matches.astype(jnp.float32), axis=3).astype(jnp.bfloat16)
    shares = jnp.sum(jnp.where(matches, weights[None, None], 0.0), axis=3)
    return (members, shares)


def pack_rows(members, rows_in, shard_count):
    per_section, capacity = (members.shape[0], members.shape[1])
    packed = jnp.einsum("ecb,bd->ecd", members, rows_in, preferred_element_type=jnp.float32).astype(
        jnp.bfloat16
    )
    widened = jnp.broadcast_to(
        packed[:, None], (per_section, shard_count, capacity, rows_in.shape[1])
    )
    return widened.reshape(per_section * shard_count, capacity, rows_in.shape[1])


def unpack(returned, shares, shard_count):
    per_section, capacity = (shares.shape[0], shares.shape[1])
    summed = jnp.sum(
        returned.astype(jnp.float32).reshape(per_section, shard_count, capacity, returned.shape[2]),
        axis=1,
    )
    return jnp.einsum("ecb,ecd->bd", shares, summed, precision=lax.Precision.HIGHEST)


def run_expert(slots, w_gate, w_up, w_down):
    flat_rows = slots.reshape(-1, slots.shape[-1])
    gate_act = jnp.dot(flat_rows, w_gate, preferred_element_type=jnp.float32)
    up_act = jnp.dot(flat_rows, w_up, preferred_element_type=jnp.float32)
    hidden = (jax.nn.silu(gate_act) * up_act).astype(jnp.bfloat16)
    partial_value = jnp.dot(hidden, w_down, preferred_element_type=jnp.float32).astype(jnp.bfloat16)
    return partial_value.reshape(slots.shape)


def per_device(
    hidden_in,
    expert_ids,
    gate_scores,
    w_gate,
    w_up,
    w_down,
    norm_gain,
    w_kv,
    queries,
    kv_cache,
    lengths,
):
    sections = lax.axis_size("sec")
    devices = lax.axis_size("dev")
    section = lax.axis_index("sec")
    shard_count = FF // w_gate.shape[1]
    per_section = devices // shard_count
    total_experts = sections * per_section
    row_count, pick_count = expert_ids.shape
    capacity = max(2, (2 * row_count * pick_count + total_experts - 1) // total_experts)
    tables = [
        route_tables(
            expert_ids,
            gate_scores,
            (section + offset) % sections,
            per_section,
            total_experts,
            capacity,
        )
        for offset in range(2)
    ]
    outgoing = jnp.stack(
        [pack_rows(tables[offset][0], hidden_in, shard_count) for offset in range(2)]
    )
    incoming = lax.all_to_all(outgoing, "dev", split_axis=1, concat_axis=1, tiled=True)
    crossed = shifted(incoming[1], "sec", 1)
    local_slots = jnp.stack([incoming[0], crossed])
    results = run_expert(local_slots, w_gate, w_up, w_down)
    returned = shifted(results[1], "sec", 1)
    sending = jnp.stack([results[0], returned])
    back = lax.all_to_all(sending, "dev", split_axis=1, concat_axis=1, tiled=True)
    mixture = unpack(back[0], tables[0][1], shard_count) + unpack(
        back[1], tables[1][1], shard_count
    )
    moe_out = (hidden_in.astype(jnp.float32) + mixture).astype(jnp.bfloat16)
    widened = moe_out.astype(jnp.float32)
    normed = (
        widened
        * lax.rsqrt(jnp.mean(widened * widened, axis=1, keepdims=True) + norm_eps)
        * norm_gain
    ).astype(jnp.bfloat16)
    pieces = lax.all_to_all(normed, "dev", split_axis=1, concat_axis=0, tiled=True)
    latent_sum = lax.psum_scatter(
        jnp.dot(pieces, w_kv, preferred_element_type=jnp.float32),
        "dev",
        scatter_dimension=0,
        tiled=True,
    )
    new_latent = latent_sum.astype(jnp.bfloat16)
    attended = attend(queries, kv_cache, lengths, new_latent, KV)
    return (moe_out, new_latent, attended)


def solution(mesh):
    in_specs = (
        P(("sec", "dev"), None),
        P(("sec", "dev"), None),
        P(("sec", "dev"), None),
        P(None, ("sec", "dev")),
        P(None, ("sec", "dev")),
        P(("sec", "dev"), None),
        P(),
        P("dev", None),
        P(("sec", "dev"), None, None),
        P(("sec", "dev"), None, None),
        P(("sec", "dev")),
    )
    out_specs = (P(("sec", "dev"), None), P(("sec", "dev"), None), P(("sec", "dev"), None, None))
    return jax.shard_map(
        per_device, mesh=mesh, in_specs=in_specs, out_specs=out_specs, check_vma=False
    )
```

profile of v0, /device:TPU:0, one launch (start us, length us, event | category | flops | bytes accessed | tf_op | source)
XLA Modules:
  0.0 246.1 jit_solution(13929084105707279377)
XLA Ops:
  0.6 0.0 copy-start
  0.7 0.8 copy.33
  1.5 0.1 reshape.159
  1.6 0.2 reduce_window_sum.12
  1.8 0.1 eq.92
  1.9 0.1 copy.34
  2.0 0.7 convert_reduce_fusion.2
  2.7 0.7 convert_divide_fusion
  3.3 0.7 broadcast_subtract_fusion
  4.0 1.0 convolution_convert_fusion.2
  5.0 1.0 convolution_convert_fusion.1
  6.0 0.2 broadcast_in_dim.30
  6.3 0.2 broadcast_in_dim.31
  6.5 1.2 pad_maximum_fusion
  7.7 49.9 %all_to_all.29 = bf16[2,16,4,7168]{3,2,0,1:T(4,128)(2,1)S(1)} all-to-all(bf16[2,16,4,7168]{3,2,0,1:T(4,128)(2,1)S(1)} %pad_maximum_fusion), channel_id=1, replica_groups=mesh['sec'=2,'dev'=16] {'dev'}, dimensions={1} | all-to-all | bytes 3670016 | tf_op jit(solution)/shard_map/all_to_all | solution.py:129
  57.6 0.6 slice_bitcast_fusion.1
  58.3 1.6 collective-permute-start
  59.8 21.5 %collective-permute-done = bf16[16,4,7168]{2,1,0:T(4,128)(2,1)S(1)} collective-permute-done((bf16[16,4,7168]{2,1,0:T(4,128)(2,1)S(1)}, bf16[16,4,7168]{2,1,0:T(4,128)(2,1)S(1)}, u32[]{:S(2)}, u32[]{:S(2)}) %collective-permute-start) | collective-permute-done | bytes 917536 | tf_op jit(solution)/shard_map/ppermute | solution.py:16
  81.4 2.6 %pad_maximum_fusion.1 = bf16[2,16,4,7168]{3,2,1,0:T(4,128)(2,1)} fusion(bf16[1,16,4,7168]{3,2,1,0:T(4,128)(2,1)S(1)} %bitcast.56, bf16[1,16,4,7168]{3,2,1,0:T(4,128)(2,1)S(1)} %get-tuple-element.11), kind=kLoop, calls=%fused_computation.9 | loop fusion | flops 917504 | bytes 3670016 | tf_op jit(solution)/shard_map/stack | solution.py:131
  83.9 2.9 %reshape.160 = bf16[128,7168]{1,0:T(8,128)(2,1)S(1)} reshape(bf16[2,16,4,7168]{3,2,1,0:T(4,128)(2,1)} %pad_maximum_fusion.1) | data formatting | bytes 3670016 | tf_op jit(solution)/shard_map/reshape | solution.py:86
  86.9 2.7 %fusion.32 = f32[128,256]{1,0:T(8,128)S(1)} fusion(bf16[128,7168]{1,0:T(8,128)(2,1)S(1)} %reshape.160, bf16[7168,256]{1,0:T(8,128)(2,1)} %param.14), kind=kOutput, calls=%fused_computation.70 | convolution fusion | flops 469762048 | bytes 5636096 | tf_op jit(solution)/shard_map/dot_general | solution.py:87
  89.6 6.5 %convolution_convert_fusion = bf16[128,7168]{1,0:T(8,128)(2,1)} fusion(bf16[256,7168]{1,0:T(8,128)(2,1)} %param.16, f32[128,256]{1,0:T(8,128)S(1)} %fusion.32, bf16[128,7168]{1,0:T(8,128)(2,1)S(1)} %reshape.160, bf16[7168,256]{1,0:T(8,128)(2,1)} %param.15), kind=kOutput, calls=%fused_computation | convolution fusion | flops 940638208 | bytes 11141120 | tf_op jit(solution)/shard_map/dot_general | solution.py:90
  96.1 1.6 fusion.30
  97.7 1.3 squeeze.9
  99.0 1.5 collective-permute-start.1
  100.5 0.3 slice.31
  100.8 20.6 %collective-permute-done.1 = bf16[16,4,7168]{2,1,0:T(4,128)(2,1)S(1)} collective-permute-done((bf16[16,4,7168]{2,1,0:T(4,128)(2,1)}, bf16[16,4,7168]{2,1,0:T(4,128)(2,1)S(1)}, u32[]{:S(2)}, u32[]{:S(2)}) %collective-permute-start.1) | collective-permute-done | bytes 917536 | tf_op jit(solution)/shard_map/ppermute | solution.py:16
  121.3 2.4 pad_maximum_fusion.2
  123.8 0.0 copy-start.7
  123.8 4.0 %all-to-all-start.1 = ((bf16[2,16,4,7168]{3,2,0,1:T(4,128)(2,1)}), bf16[2,16,4,7168]{3,2,0,1:T(4,128)(2,1)S(1)}, u32[]{:S(2)}, u32[]{:S(2)}) async-start(bf16[2,16,4,7168]{3,2,0,1:T(4,128)(2,1)} %pad_maximum_fusion.2), calls=%async_computation.1 | async-start | bytes 3670016 | tf_op jit(solution)/shard_map/all_to_all | solution.py:135
  127.8 0.0 copy-done.7
  127.8 0.1 iota_compare_fusion
  127.9 36.2 %all-to-all-done.1 = bf16[2,16,4,7168]{3,2,0,1:T(4,128)(2,1)S(1)} async-done(((bf16[2,16,4,7168]{3,2,0,1:T(4,128)(2,1)}), bf16[2,16,4,7168]{3,2,0,1:T(4,128)(2,1)S(1)}, u32[]{:S(2)}, u32[]{:S(2)}) %all-to-all-start.1) | async-done | bytes 1835040 | tf_op jit(solution)/shard_map/all_to_all | solution.py:135
  164.1 0.6 fusion.29
  164.7 0.0 copy-start.2
  164.8 0.0 copy-start.5
  164.8 0.0 copy-start.1
  164.8 0.0 copy-start.3
  164.8 0.4 convert_reduce_fusion
  165.2 0.4 convert_reduce_fusion.1
  165.6 0.0 copy-start.8
  165.6 0.4 convolution_bitcast_fusion
  166.1 0.0 copy-done.2
  166.1 0.6 fusion.9
  166.7 0.0 copy-done.5
  166.7 0.1 fusion.11
  166.8 0.1 all_to_all.22
  166.9 0.7 copy.39
  167.6 10.1 %all-to-all-start.2 = ((bf16[4,16,448]{2,0,1:T(4,128)(2,1)}), bf16[4,16,448]{2,0,1:T(4,128)(2,1)S(1)}, u32[]{:S(2)}, u32[]{:S(2)}) async-start(bf16[4,16,448]{2,0,1:T(4,128)(2,1)} %copy.39), calls=%async_computation.2 | async-start | bytes 131072 | tf_op jit(solution)/shard_map/all_to_all | solution.py:146
  177.8 0.0 copy-done.1
  177.8 0.0 copy-done.3
  177.8 0.4 fusion.31
  178.2 0.0 copy-done.8
  178.2 0.6 dynamic-slice
  179.5 5.2 %all-to-all-done.2 = bf16[4,16,448]{2,0,1:T(4,128)(2,1)S(1)} async-done(((bf16[4,16,448]{2,0,1:T(4,128)(2,1)}), bf16[4,16,448]{2,0,1:T(4,128)(2,1)S(1)}, u32[]{:S(2)}, u32[]{:S(2)}) %all-to-all-start.2) | async-done | bytes 57376 | tf_op jit(solution)/shard_map/all_to_all | solution.py:146
  184.7 0.0 copy-done
  184.7 0.2 fusion.33
  184.9 59.5 %all-reduce.2 = bf16[64,576]{1,0:T(8,128)(2,1)S(1)} all-reduce(f32[64,576]{1,0:T(8,128)S(1)} %fusion.33), channel_id=2, replica_groups=mesh['sec'=2,'dev'=16] {'dev'}, use_global_device_ids=true, to_apply=%region_10.11.clone | all-reduce | flops 36864 | bytes 221184
  244.5 0.0 copy-start.6
  244.5 0.2 fusion.17
  244.7 0.0 copy-done.4
  244.7 0.2 fusion.6
  245.0 1.2 fusion.3
  246.1 0.0 copy-done.6
  (13 shorter events, 0.2 us)
Async XLA Ops:
  0.6 184.1 %copy-start = (bf16[448,576]{1,0:T(8,128)(2,1)S(1)}, bf16[448,576]{1,0:T(8,128)(2,1)}, u32[]{:S(2)}) copy-start(bf16[448,576]{1,0:T(8,128)(2,1)} %param.18) | copy-start | bytes 1548292
  58.3 23.1 %collective-permute-start = (bf16[16,4,7168]{2,1,0:T(4,128)(2,1)S(1)}, bf16[16,4,7168]{2,1,0:T(4,128)(2,1)S(1)}, u32[]{:S(2)}, u32[]{:S(2)}) collective-permute-start(bf16[16,4,7168]{2,1,0:T(4,128)(2,1)S(1)} %get-tuple-element.12), channel_id=1, source_target_pairs={{0,16},{16,0},{1,17},{17,1},{2,18},{18,2},{3,19},{19,3},{4,20},{20... | collective-permute-start | bytes 2752520 | tf_op jit(solution)/shard_map/ppermute | solution.py:16
  99.0 22.4 %collective-permute-start.1 = (bf16[16,4,7168]{2,1,0:T(4,128)(2,1)}, bf16[16,4,7168]{2,1,0:T(4,128)(2,1)S(1)}, u32[]{:S(2)}, u32[]{:S(2)}) collective-permute-start(bf16[16,4,7168]{2,1,0:T(4,128)(2,1)} %squeeze.9), channel_id=1, source_target_pairs={{0,16},{16,0},{1,17},{17,1},{2,18},{18,2},{3,19},{19,3},{4,20},{20... | collective-permute-start | bytes 2752520 | tf_op jit(solution)/shard_map/ppermute | solution.py:16
  123.8 4.0 %copy-start.7 = (s32[4]{0:T(128)S(1)}, s32[4]{0:T(128)}, u32[]{:S(2)}) copy-start(s32[4]{0:T(128)} %param.21) | copy-start | bytes 52
  123.8 40.3 %all-to-all-start.1 = ((bf16[2,16,4,7168]{3,2,0,1:T(4,128)(2,1)}), bf16[2,16,4,7168]{3,2,0,1:T(4,128)(2,1)S(1)}, u32[]{:S(2)}, u32[]{:S(2)}) async-start(bf16[2,16,4,7168]{3,2,0,1:T(4,128)(2,1)} %pad_maximum_fusion.2), calls=%async_computation.1 | async-start | bytes 3670016 | tf_op jit(solution)/shard_map/all_to_all | solution.py:135
  164.7 1.3 copy-start.2
  164.8 1.9 copy-start.5
  164.8 13.0 %copy-start.1 = (bf16[4,256,576]{1,2,0:T(8,128)(2,1)S(1)}, bf16[4,256,576]{1,2,0:T(8,128)(2,1)}, u32[]{:S(2)}) copy-start(bf16[4,256,576]{1,2,0:T(8,128)(2,1)} %param.20) | copy-start | bytes 3538948
  164.8 13.0 %copy-start.3 = (bf16[4,64,576]{2,1,0:T(8,128)(2,1)S(1)}, bf16[4,64,576]{2,1,0:T(8,128)(2,1)}, u32[]{:S(2)}) copy-start(bf16[4,64,576]{2,1,0:T(8,128)(2,1)} %param.19) | copy-start | bytes 884740
  165.6 12.6 %copy-start.8 = (u32[32]{0:T(128)S(1)}, u32[32]{0:T(128)}, u32[]{:S(2)}) copy-start(u32[32]{0:T(128)} %constant.55) | copy-start | bytes 388
  166.7 78.1 %copy-start.4 = (bf16[4,7168]{1,0:T(4,128)(2,1)}, bf16[4,7168]{1,0:T(4,128)(2,1)S(1)}, u32[]{:S(2)}) copy-start(bf16[4,7168]{1,0:T(4,128)(2,1)S(1)} %get-tuple-element.18) | copy-start | bytes 172036
  167.6 17.0 %all-to-all-start.2 = ((bf16[4,16,448]{2,0,1:T(4,128)(2,1)}), bf16[4,16,448]{2,0,1:T(4,128)(2,1)S(1)}, u32[]{:S(2)}, u32[]{:S(2)}) async-start(bf16[4,16,448]{2,0,1:T(4,128)(2,1)} %copy.39), calls=%async_computation.2 | async-start | bytes 131072 | tf_op jit(solution)/shard_map/all_to_all | solution.py:146
  244.5 1.6 copy-start.6
where the time goes:
time: 247 us; the launch traced here: 246 us
  blocking collectives  109 us (44%)
  waiting for transfers between devices  83.5 us (34%)
  starting transfers between devices  17.2 us (7%)
  matrix products  14.2 us (6%)
  local copies, waits for them, and re-layouts  10.4 us (4%)
  other arithmetic  9.7 us (4%)
    unnamed x1, blocking collectives  59.5 us
    all_to_all x1, blocking collectives, per_device(): lax.all_to_all(outgoing, 'dev', split_axis=1, concat_axis=1, tiled=True)  49.9 us
    ppermute x2, waiting for transfers between devices, shifted(): lax.ppermute(x, axis, [(i, (i + by) % length) for i in range(length)])  42.1 us
    all_to_all x1, waiting for transfers between devices, per_device(): lax.all_to_all(sending, 'dev', split_axis=1, concat_axis=1, tiled=True)  36.2 us
    all_to_all x1, starting transfers between devices, per_device(): lax.all_to_all(normed, 'dev', split_axis=1, concat_axis=0, tiled=True)  10.1 us
    dot_general x1, matrix products, run_expert(): jnp.dot(hidden, w_down, preferred_element_type=jnp.float32)  6.55 us
    all_to_all x1, waiting for transfers between devices, per_device(): lax.all_to_all(normed, 'dev', split_axis=1, concat_axis=0, tiled=True)  5.19 us
  transfers between devices with their start and end apart: 4, of which 4 were waited for; matrix products, arithmetic and copies ran while one was open for 1% of the time, Pallas kernels for 0%

commit v1 on v0

v1 whole, which is shorter than its diff:
```python
import jax
import jax.numpy as jnp
from jax import lax
from jax.experimental import pallas as pl
from jax.experimental.pallas import tpu as pltpu
from jax.sharding import PartitionSpec as P

FF = 2048
KV = 512
LANES = 128

score_scale = 192.0 ** (-0.5)
norm_eps = 1e-06


def swap(x, bit):
    if bit == "sec":
        return lax.ppermute(x, "sec", [(i, i ^ 1) for i in range(lax.axis_size("sec"))])
    return lax.ppermute(x, "dev", [(i, i ^ (1 << bit)) for i in range(lax.axis_size("dev"))])


def total(kept, received):
    return (kept.astype(jnp.float32) + received.astype(jnp.float32)).astype(jnp.bfloat16)


def flipped(x, rows):
    blocks = x.reshape(-1, 2, rows, x.shape[1])
    return jnp.concatenate([blocks[:, 1:], blocks[:, :1]], axis=1).reshape(x.shape)


def cache_part(queries, kv_cache, lengths):
    scores = (
        jnp.einsum("bhl,bpl->bhp", queries, kv_cache, preferred_element_type=jnp.float32)
        * score_scale
    )
    visible = jnp.arange(kv_cache.shape[1], dtype=jnp.int32)[None, None, :] < lengths[:, None, None]
    scores = jnp.where(visible, scores, -1e30)
    peak = jnp.max(scores, axis=2)
    spread = jnp.exp(scores - peak[:, :, None])
    combined = jnp.einsum(
        "bhp,bpv->bhv",
        spread.astype(jnp.bfloat16),
        kv_cache[:, :, :KV],
        preferred_element_type=jnp.float32,
    )
    return peak, jnp.sum(spread, axis=2), combined


def own_part(queries, latent, peak, denominator, combined):
    own_score = (
        jnp.einsum("bhl,bl->bh", queries, latent, preferred_element_type=jnp.float32) * score_scale
    )
    top = jnp.maximum(peak, own_score)
    shrink = jnp.exp(peak - top)
    own_weight = jnp.exp(own_score - top)
    scale = 1.0 / (denominator * shrink + own_weight)
    own_prob = (own_weight * scale).astype(jnp.bfloat16).astype(jnp.float32)
    value = latent[:, None, :KV].astype(jnp.float32)
    return (combined * (shrink * scale)[:, :, None] + own_prob[:, :, None] * value).astype(
        jnp.bfloat16
    )


def gather_rows(hidden_in, expert_ids, gate_scores, high, w_kv):
    width = hidden_in.shape[1]
    picks = expert_ids.shape[1]
    half = width // 2
    x = hidden_in
    info = jnp.concatenate([expert_ids.astype(jnp.bfloat16), gate_scores], axis=1)
    info = jnp.pad(info, ((0, 0), (0, LANES - 2 * picks)))
    w_low = swap(w_kv, 1)
    for bit in reversed(high):
        x, info = (jnp.concatenate([v, swap(v, bit)], axis=0) for v in (x, info))
    a, b = x[:, :half], x[:, half:]
    group = (a, b)
    b = jnp.concatenate([b, info], axis=1)
    a, b = (jnp.concatenate([v, swap(v, 2)], axis=0) for v in (a, b))
    a, b, w_low = lax.optimization_barrier((a, b, w_low))
    w_mid = swap(w_kv, 2)
    a_low, b_sec = swap(a, 1), swap(b, "sec")
    a_sec = swap(jnp.concatenate([a, a_low], axis=0), "sec")
    b_low = swap(jnp.concatenate([b, b_sec], axis=0), 1)
    w_both = swap(w_low, 2)
    a_all = (a, a_low, a_sec)
    b_all = (b, b_sec, b_low)
    a_all += tuple(swap(v, 0) for v in a_all)
    b_all += tuple(swap(v, 0) for v in b_all)
    return group, a_all, b_all, (w_kv, w_low, w_mid, w_both)


def experts_kernel(picks, expert_ref, *refs):
    a_refs, b_refs = refs[:6], refs[6:12]
    gate_ref, up_ref, down_ref, keep_a, keep_b, send_a, send_b, x_ref, info_ref = refs[12:]
    half = a_refs[0].shape[1]
    size = a_refs[0].shape[0]
    rows = 8 * size
    for side in range(2):
        first = side * 4 * size
        own, low, sec = a_refs[3 * side : 3 * side + 3]
        x_ref[first : first + size, :half] = own[...]
        x_ref[first + size : first + 2 * size, :half] = low[...]
        x_ref[first + 2 * size : first + 4 * size, :half] = sec[...]
        own, sec, low = b_refs[3 * side : 3 * side + 3]
        places = ((own, 0, 0), (low, 0, 1), (sec, 0, 2), (low, size, 3))
        for ref, start, slot in places:
            to = pl.ds(first + slot * size, size)
            x_ref[to, half:] = ref[start : start + size, :half]
            info_ref[to, :] = ref[start : start + size, half:].astype(jnp.float32)
    info = info_ref[...]
    lane = lax.broadcasted_iota(jnp.int32, info.shape, 1)
    scores = jnp.where(lane < picks, pltpu.roll(info, LANES - picks, 1), 0.0)
    named = jnp.where(info == expert_ref[0].astype(jnp.float32), scores, 0.0)
    share = jnp.sum(named, axis=1, keepdims=True) / jnp.sum(scores, axis=1, keepdims=True)
    depth = 1024
    gate_act = jnp.zeros((rows, gate_ref.shape[1]), jnp.float32)
    up_act = jnp.zeros((rows, gate_ref.shape[1]), jnp.float32)
    for k in range(0, 2 * half, depth):
        x = x_ref[:, k : k + depth]
        gate_act += jnp.dot(x, gate_ref[k : k + depth, :], preferred_element_type=jnp.float32)
        up_act += jnp.dot(x, up_ref[k : k + depth, :], preferred_element_type=jnp.float32)
    hidden = (gate_act / (1.0 + jnp.exp(-gate_act)) * up_act).astype(jnp.bfloat16)
    cols = 512
    for first, kept, sent in ((0, keep_a, send_a), (half, keep_b, send_b)):
        for c in range(0, half, cols):
            partial = jnp.dot(
                hidden,
                down_ref[:, first + c : first + c + cols],
                preferred_element_type=jnp.float32,
            )
            partial = (partial * share).astype(jnp.bfloat16)
            kept[:, c : c + cols] = partial[: rows // 2]
            sent[:, c : c + cols] = partial[rows // 2 :]


def experts(a_all, b_all, picks, expert, w_gate, w_up, w_down):
    size, half = a_all[0].shape
    out = jax.ShapeDtypeStruct((4 * size, half), jnp.bfloat16)
    vmem = pl.BlockSpec(memory_space=pltpu.VMEM)
    return pl.pallas_call(
        lambda *refs: experts_kernel(picks, *refs),
        out_shape=(out,) * 4,
        in_specs=[pl.BlockSpec(memory_space=pltpu.SMEM)] + [vmem] * 15,
        out_specs=[vmem] * 4,
        scratch_shapes=[
            pltpu.VMEM((8 * size, 2 * half), jnp.bfloat16),
            pltpu.VMEM((8 * size, LANES), jnp.float32),
        ],
        compiler_params=pltpu.CompilerParams(vmem_limit_bytes=48 << 20),
        name="experts",
    )(expert.reshape(1), *a_all, *b_all, w_gate, w_up, w_down)


def experts_wide(a_all, b_all, picks, expert, w_gate, w_up, w_down):
    size, half = a_all[0].shape
    b_all = [
        v
        for own, sec, low in (b_all[:3], b_all[3:])
        for v in (own, low[:size], sec, low[size:])
    ]
    a, b = jnp.concatenate(a_all, axis=0), jnp.concatenate(b_all, axis=0)
    info = b[:, half:].astype(jnp.float32)
    scores = info[:, picks : 2 * picks]
    named = jnp.where(info[:, :picks] == expert.astype(jnp.float32), scores, 0.0)
    share = jnp.sum(named, axis=1, keepdims=True) / jnp.sum(scores, axis=1, keepdims=True)
    x = jnp.concatenate([a, b[:, :half]], axis=1)
    gate_act = jnp.dot(x, w_gate, preferred_element_type=jnp.float32)
    up_act = jnp.dot(x, w_up, preferred_element_type=jnp.float32)
    hidden = (jax.nn.silu(gate_act) * up_act).astype(jnp.bfloat16)
    partial = jnp.dot(hidden, w_down, preferred_element_type=jnp.float32)
    partial = (share * partial).astype(jnp.bfloat16)
    rows = 4 * size
    return partial[:rows, :half], partial[:rows, half:], partial[rows:, :half], partial[rows:, half:]


def scatter_rows(keep_a, keep_b, send_a, send_b):
    rows = keep_a.shape[0] // 2
    quarter = rows // 2
    a, b = total(keep_a, swap(send_a, 0)), total(keep_b, swap(send_b, 0))
    a_in = swap(a[rows:], "sec")
    b_in = swap(jnp.concatenate([b[quarter:rows], b[rows + quarter :]], axis=0), 1)
    a = total(a[:rows], a_in)
    b = total(jnp.concatenate([b[:quarter], b[rows : rows + quarter]], axis=0), b_in)
    a_in, b_in = swap(a[quarter:], 1), swap(b[quarter:], "sec")
    a, b = total(a[:quarter], a_in), total(b[:quarter], b_in)
    rows = quarter // 2
    return tuple(total(v[:rows], swap(v[rows:], 2)) for v in (a, b))


def latent_parts_kernel(
    place_ref, a_ref, b_ref, in_ref, res_a, res_b, gain_ref, *refs
):
    slices = refs[:8]
    sums_ref, sums_out, moe_ref, moe_out, piece_ref = refs[8:]
    rows, half = a_ref.shape
    own = rows // 2
    piece, lat = slices[0].shape
    upper = place_ref[0] == 1
    kept = jnp.where(upper, b_ref[...], a_ref[...]).astype(jnp.float32)
    residual = jnp.where(upper, res_b[...], res_a[...]).astype(jnp.float32)
    moe = (residual + (kept + in_ref[...].astype(jnp.float32))).astype(jnp.bfloat16)
    moe_ref[...] = moe[:own]
    moe_out[...] = moe[own:]
    widened = moe.astype(jnp.float32)
    scaled = widened * gain_ref[pl.ds(place_ref[0], 1), :]
    for p in range(8):
        piece_ref[p] = scaled[:, p * piece : (p + 1) * piece]
    sums = jnp.zeros((rows, lat), jnp.float32)
    for slot, w_ref in enumerate(slices):
        flips = ((slot & 1) << 1) | ((slot & 2) << 1) | (slot >> 2)
        x = piece_ref[place_ref[1] ^ flips].astype(jnp.bfloat16)
        sums += jnp.dot(x, w_ref[...], preferred_element_type=jnp.float32)
    squares = jnp.sum(widened * widened, axis=1, keepdims=True)
    tail = jnp.broadcast_to(squares, (rows, LANES))
    for ref, first in ((sums_ref, 0), (sums_out, own)):
        ref[:, :lat] = sums[first : first + own]
        ref[:, lat:] = tail[first : first + own, : ref.shape[1] - lat]


def latent_parts(place, a, b, received, res_a, res_b, gain, slices):
    rows, half = a.shape
    piece, lat = slices[0].shape
    own = rows // 2
    vmem = pl.BlockSpec(memory_space=pltpu.VMEM)
    padded = -(-(lat + 1) // LANES) * LANES
    sums = jax.ShapeDtypeStruct((own, padded), jnp.float32)
    moe = jax.ShapeDtypeStruct((own, half), jnp.bfloat16)
    return pl.pallas_call(
        latent_parts_kernel,
        out_shape=(sums, sums, moe, moe),
        in_specs=[pl.BlockSpec(memory_space=pltpu.SMEM)] + [vmem] * 14,
        out_specs=[vmem] * 4,
        scratch_shapes=[pltpu.VMEM((8, rows, piece), jnp.float32)],
        compiler_params=pltpu.CompilerParams(vmem_limit_bytes=32 << 20),
        name="latent_parts",
    )(place, a, b, received, res_a, res_b, gain.reshape(2, half), *slices)


def latent_parts_wide(device, high, mixture, residual, own_rows, norm_gain, slices):
    for bit in reversed(high[:-1]):
        part = mixture.shape[1] // 2
        upper = ((device >> bit) & 1) == 1
        lo, hi = mixture[:, :part], mixture[:, part:]
        sent = flipped(jnp.where(upper, lo, hi), own_rows << (high[-1] - bit))
        mixture = total(jnp.where(upper, hi, lo), swap(sent, bit))
        residual = jnp.where(upper, residual[:, part:], residual[:, :part])
    part = mixture.shape[1]
    moe = (residual.astype(jnp.float32) + mixture.astype(jnp.float32)).astype(jnp.bfloat16)
    widened = moe.astype(jnp.float32)
    gain = lax.dynamic_slice_in_dim(norm_gain, (device >> 3) * part, part, axis=0)
    squares = jnp.sum(widened * widened, axis=1, keepdims=True)
    scaled = (widened * gain).astype(jnp.bfloat16)
    slices = jnp.stack(slices)
    piece = slices.shape[1]
    latent = jnp.zeros((moe.shape[0], slices.shape[2]), jnp.float32)
    for p in range(8):
        flips = (device & 7) ^ p
        slot = ((flips >> 1) & 1) | ((flips >> 1) & 2) | ((flips & 1) << 2)
        weight = lax.dynamic_index_in_dim(slices, slot, axis=0, keepdims=False)
        latent += jnp.dot(
            scaled[:, p * piece : (p + 1) * piece], weight, preferred_element_type=jnp.float32
        )
    sums = jnp.concatenate([latent, squares], axis=1)
    for bit in high:
        rows = sums.shape[0] // 2
        sums = sums[:rows] + swap(sums[rows:], bit)
    for bit in high:
        rows = moe.shape[0] // 2
        upper = ((device >> bit) & 1) == 1
        kept, received = moe[:rows], swap(moe[rows:], bit)
        moe = jnp.where(
            upper,
            jnp.concatenate([received, kept], axis=1),
            jnp.concatenate([kept, received], axis=1),
        )
    return sums, moe


def per_device(
    hidden_in,
    expert_ids,
    gate_scores,
    w_gate,
    w_up,
    w_down,
    norm_gain,
    w_kv,
    queries,
    kv_cache,
    lengths,
):
    devices = lax.axis_size("dev")
    device = lax.axis_index("dev")
    shard_count = FF // w_gate.shape[1]
    expert = lax.axis_index("sec") * (devices // shard_count) + device // shard_count
    high = range(3, devices.bit_length() - 1)
    own_rows, width = hidden_in.shape

    picks = expert_ids.shape[1]
    half = width // 2

    group, a_all, b_all, slices = gather_rows(hidden_in, expert_ids, gate_scores, high, w_kv)
    peak, denominator, combined = cache_part(queries, kv_cache, lengths)
    run = experts if len(high) == 1 else experts_wide
    partial = run(a_all, b_all, picks, expert, w_gate, w_up, w_down)
    partial, slices = lax.optimization_barrier((partial, slices))
    a, b = scatter_rows(*partial)
    slices += tuple(swap(v, 0) for v in slices)

    upper = (device >> high[-1]) & 1
    sent = flipped(jnp.where(upper == 1, a, b), own_rows)
    received = swap(sent, high[-1])
    if len(high) == 1:
        place = jnp.stack([upper, device & 7])
        sums, sums_out, moe, moe_out = latent_parts(place, a, b, received, *group, norm_gain, slices)
        sums = sums + swap(sums_out, high[0])
        moe_in = swap(moe_out, high[0])
        moe = jnp.concatenate([moe, moe_in], axis=1)
        swapped = jnp.concatenate([moe_in, moe[:, :half]], axis=1)
        moe = jnp.where(upper == 1, swapped, moe)
    else:
        mixture = total(jnp.where(upper == 1, b, a), received)
        residual = jnp.where(upper == 1, group[1], group[0])
        sums, moe = latent_parts_wide(device, high, mixture, residual, own_rows, norm_gain, slices)
    lat = w_kv.shape[1]
    inverse = lax.rsqrt(sums[:, lat : lat + 1] / width + norm_eps)
    new_latent = (sums[:, :lat] * inverse).astype(jnp.bfloat16)
    attended = own_part(queries, new_latent, peak, denominator, combined)
    return (moe, new_latent, attended)


def solution(mesh):
    in_specs = (
        P(("sec", "dev"), None),
        P(("sec", "dev"), None),
        P(("sec", "dev"), None),
        P(None, ("sec", "dev")),
        P(None, ("sec", "dev")),
        P(("sec", "dev"), None),
        P(),
        P("dev", None),
        P(("sec", "dev"), None, None),
        P(("sec", "dev"), None, None),
        P(("sec", "dev")),
    )
    out_specs = (P(("sec", "dev"), None), P(("sec", "dev"), None), P(("sec", "dev"), None, None))
    return jax.shard_map(
        per_device, mesh=mesh, in_specs=in_specs, out_specs=out_specs, check_vma=False
    )
```

time: 247 us -> 88.9 us (0.36)
  blocking collectives: 109 us -> 0 us
  waiting for transfers between devices: 83.5 us -> 31.9 us
  starting transfers between devices: 17.2 us -> 31.9 us
  matrix products: 14.2 us -> 2.42 us
  Pallas kernels: 0 us -> 8.47 us
  other arithmetic: 9.7 us -> 4.4 us
    unnamed x1 -> x0, blocking collectives: 59.5 us -> none
    all_to_all x1 -> x0, blocking collectives: 49.9 us -> none  [per_device(): lax.all_to_all(outgoing, 'dev', split_axis=1, concat_axis=1, tiled=True)]
    all_to_all x2 -> x0, waiting for transfers between devices: 41.4 us -> none  [the longest x1 36.2 us: per_device(): lax.all_to_all(sending, 'dev', split_axis=1, concat_axis=1, tiled=True)]
    ppermute x2 -> x32, starting transfers between devices: 3.05 us -> 31.9 us  [the longest x28 28.3 us: swap(): lax.ppermute(x, 'dev', [(i, i ^ 1 << bit) for i in range(lax.axis_size('d...]
    all_to_all x2 -> x0, starting transfers between devices: 14.2 us -> none  [the longest x1 10.1 us: per_device(): lax.all_to_all(normed, 'dev', split_axis=1, concat_axis=0, tiled=True)]
    dot_general x10 -> x3, matrix products: 14.2 us -> 2.42 us  [the longest x1 1.16 us: cache_part(): jnp.einsum('bhp,bpv->bhv', spread.astype(jnp.bfloat16), kv_cache[:, :, :K...]
    ppermute x2 -> x32, waiting for transfers between devices: 42.1 us -> 31.9 us  [the longest x28 26.5 us: swap(): lax.ppermute(x, 'dev', [(i, i ^ 1 << bit) for i in range(lax.axis_size('d...]
    pallas_call x0 -> x2, Pallas kernels: none -> 8.47 us  [the longest x1 6.09 us: experts(): pl.pallas_call(lambda *refs: experts_kernel(picks, *refs), out_shape=(out...]
  transfers between devices with their start and end apart: 4 -> 32, of which waited for: 4 -> 16; matrix products, arithmetic and copies ran while one was open for 1% -> 10% of each run, Pallas kernels for 0% -> 7%
where the time goes in v1:
time: 88.9 us; the launch traced here: 88.5 us
  starting transfers between devices  31.9 us (36%)
  waiting for transfers between devices  31.9 us (36%)
  local copies, waits for them, and re-layouts  8.53 us (10%)
  Pallas kernels  8.47 us (10%)
  other arithmetic  4.4 us (5%)
  matrix products  2.42 us (3%)
  between operations  0.91 us (1%)
    ppermute x28, starting transfers between devices, swap(): lax.ppermute(x, 'dev', [(i, i ^ 1 << bit) for i in range(lax.axis_size('d...  28.3 us
    ppermute x28, waiting for transfers between devices, swap(): lax.ppermute(x, 'dev', [(i, i ^ 1 << bit) for i in range(lax.axis_size('d...  26.5 us
    unnamed x35, local copies, waits for them, and re-layouts  6.26 us
    pallas_call x1, Pallas kernels, experts(): pl.pallas_call(lambda *refs: experts_kernel(picks, *refs), out_shape=(out...  6.09 us
    ppermute x4, waiting for transfers between devices, swap(): lax.ppermute(x, 'sec', [(i, i ^ 1) for i in range(lax.axis_size('sec'))])  5.35 us
    ppermute x4, starting transfers between devices, swap(): lax.ppermute(x, 'sec', [(i, i ^ 1) for i in range(lax.axis_size('sec'))])  3.56 us
    pallas_call x1, Pallas kernels, latent_parts(): pl.pallas_call(latent_parts_kernel, out_shape=(sums, sums, moe, moe), in_...  2.37 us
  transfers between devices with their start and end apart: 32, of which 16 were waited for; matrix products, arithmetic and copies ran while one was open for 10% of the time, Pallas kernels for 7%

profile of v1, /device:TPU:0, one launch (start us, length us, event | category | flops | bytes accessed | tf_op | source)
XLA Modules:
  0.0 88.5 jit_solution(16878566280779551297)
XLA Ops:
  0.6 4.1 %collective-permute-start = (bf16[4,7168]{1,0:T(4,128)(2,1)}, bf16[4,7168]{1,0:T(4,128)(2,1)S(1)}, u32[]{:S(2)}, u32[]{:S(2)}) collective-permute-start(bf16[4,7168]{1,0:T(4,128)(2,1)} %param.11), channel_id=1, source_target_pairs={{0,8},{1,9},{2,10},{3,11},{4,12},{5,13},{6,14},{7,15},{8,0},{9,1},... | collective-permute-start | bytes 172040 | tf_op jit(solution)/shard_map/ppermute | solution.py:19
  4.7 0.7 convert_element_type.96
  5.4 0.1 copy.20
  5.5 0.8 copy.21
  6.4 1.8 %collective-permute-start.4 = (bf16[448,576]{1,0:T(8,128)(2,1)}, bf16[448,576]{1,0:T(8,128)(2,1)S(1)}, u32[]{:S(2)}, u32[]{:S(2)}) collective-permute-start(bf16[448,576]{1,0:T(8,128)(2,1)} %refs_0_), channel_id=1, source_target_pairs={{0,2},{1,3},{2,0},{3,1},{4,6},{5,7},{6,4},{7,5},{8,10},{9,11},{10,... | collective-permute-start | bytes 1548296 | tf_op jit(solution)/shard_map/ppermute | solution.py:19
  8.2 0.8 pad_maximum_fusion.5
  9.1 1.6 %collective-permute-start.1 = (bf16[8,3584]{1,0:T(8,128)(2,1)S(1)}, bf16[8,3584]{1,0:T(8,128)(2,1)S(1)}, u32[]{:S(2)}, u32[]{:S(2)}) collective-permute-start(bf16[8,3584]{1,0:T(8,128)(2,1)S(1)} %get-tuple-element.49.res_a), channel_id=1, source_target_pairs={{0,4},{1,5},{2,6},{3,7},{4,0},{5,1},{6,2},{7,3},{8,12},{9,13},{10,... | collective-permute-start | bytes 172040 | tf_op jit(solution)/shard_map/ppermute | solution.py:19
  10.7 0.1 collective-permute-done.2
  10.9 1.6 %collective-permute-start.3 = (bf16[8,3712]{1,0:T(8,128)(2,1)S(1)}, bf16[8,3712]{1,0:T(8,128)(2,1)S(1)}, u32[]{:S(2)}, u32[]{:S(2)}) collective-permute-start(bf16[8,3712]{1,0:T(8,128)(2,1)S(1)} %maximum_maximum_fusion), channel_id=1, source_target_pairs={{0,4},{1,5},{2,6},{3,7},{4,0},{5,1},{6,2},{7,3},{8,12},{9,13},{10,... | collective-permute-start | bytes 178184 | tf_op jit(solution)/shard_map/ppermute | solution.py:19
  12.5 0.9 collective-permute-done.1
  13.4 1.7 %collective-permute-done.3 = bf16[8,3712]{1,0:T(8,128)(2,1)S(1)} collective-permute-done((bf16[8,3712]{1,0:T(8,128)(2,1)S(1)}, bf16[8,3712]{1,0:T(8,128)(2,1)S(1)}, u32[]{:S(2)}, u32[]{:S(2)}) %collective-permute-start.3) | collective-permute-done | bytes 59424 | tf_op jit(solution)/shard_map/ppermute | solution.py:19
  15.1 6.0 %collective-permute-done.4.refs_1_ = bf16[448,576]{1,0:T(8,128)(2,1)S(1)} collective-permute-done((bf16[448,576]{1,0:T(8,128)(2,1)}, bf16[448,576]{1,0:T(8,128)(2,1)S(1)}, u32[]{:S(2)}, u32[]{:S(2)}) %collective-permute-start.4) | collective-permute-done | bytes 516128 | tf_op jit(solution)/shard_map/ppermute | solution.py:19
  21.1 1.5 %collective-permute-start.10 = (bf16[16,3712]{1,0:T(8,128)(2,1)S(1)}, bf16[16,3712]{1,0:T(8,128)(2,1)S(1)}, u32[]{:S(2)}, u32[]{:S(2)}) collective-permute-start(bf16[16,3712]{1,0:T(8,128)(2,1)S(1)} %pad_maximum_fusion.3.refs_7_), channel_id=1, source_target_pairs={{0,16},{16,0},{1,17},{17,1},{2,18},{18,2},{3,19},{19,3},{4,20},{20... | collective-permute-start | bytes 356360 | tf_op jit(solution)/shard_map/ppermute | solution.py:18
  22.6 1.6 %collective-permute-start.15 = (bf16[448,576]{1,0:T(8,128)(2,1)}, bf16[448,576]{1,0:T(8,128)(2,1)S(1)}, u32[]{:S(2)}, u32[]{:S(2)}) collective-permute-start(bf16[448,576]{1,0:T(8,128)(2,1)} %refs_0_), channel_id=1, source_target_pairs={{0,4},{1,5},{2,6},{3,7},{4,0},{5,1},{6,2},{7,3},{8,12},{9,13},{10,... | collective-permute-start | bytes 1548296 | tf_op jit(solution)/shard_map/ppermute | solution.py:19
  24.2 1.5 %collective-permute-start.5 = (bf16[16,3584]{1,0:T(8,128)(2,1)S(1)}, bf16[16,3584]{1,0:T(8,128)(2,1)S(1)}, u32[]{:S(2)}, u32[]{:S(2)}) collective-permute-start(bf16[16,3584]{1,0:T(8,128)(2,1)S(1)} %pad_maximum_fusion.4.refs_1_), channel_id=1, source_target_pairs={{0,2},{1,3},{2,0},{3,1},{4,6},{5,7},{6,4},{7,5},{8,10},{9,11},{10,... | collective-permute-start | bytes 344072 | tf_op jit(solution)/shard_map/ppermute | solution.py:19
  25.7 0.4 collective-permute-start.16
  26.2 1.4 %collective-permute-start.11 = (bf16[32,3712]{1,0:T(8,128)(2,1)S(1)}, bf16[32,3712]{1,0:T(8,128)(2,1)S(1)}, u32[]{:S(2)}, u32[]{:S(2)}) collective-permute-start(bf16[32,3712]{1,0:T(8,128)(2,1)S(1)} %pad_maximum_fusion), channel_id=1, source_target_pairs={{0,2},{1,3},{2,0},{3,1},{4,6},{5,7},{6,4},{7,5},{8,10},{9,11},{10,... | collective-permute-start | bytes 712712 | tf_op jit(solution)/shard_map/ppermute | solution.py:19
  27.5 1.4 %collective-permute-done.5.refs_2_ = bf16[16,3584]{1,0:T(8,128)(2,1)S(1)} collective-permute-done((bf16[16,3584]{1,0:T(8,128)(2,1)S(1)}, bf16[16,3584]{1,0:T(8,128)(2,1)S(1)}, u32[]{:S(2)}, u32[]{:S(2)}) %collective-permute-start.5) | collective-permute-done | bytes 114720 | tf_op jit(solution)/shard_map/ppermute | solution.py:19
  29.0 0.6 collective-permute-start.6
  29.6 0.6 copy-done.4
  30.2 3.9 %collective-permute-done.11.refs_9_ = bf16[32,3712]{1,0:T(8,128)(2,1)S(1)} collective-permute-done((bf16[32,3712]{1,0:T(8,128)(2,1)S(1)}, bf16[32,3712]{1,0:T(8,128)(2,1)S(1)}, u32[]{:S(2)}, u32[]{:S(2)}) %collective-permute-start.11) | collective-permute-done | bytes 237600 | tf_op jit(solution)/shard_map/ppermute | solution.py:19
  34.2 0.6 copy-done.2
  34.8 0.5 collective-permute-start.8
  35.3 1.0 %collective-permute-done.8.refs_5_ = bf16[16,3584]{1,0:T(8,128)(2,1)S(1)} collective-permute-done((bf16[16,3584]{1,0:T(8,128)(2,1)S(1)}, bf16[16,3584]{1,0:T(8,128)(2,1)S(1)}, u32[]{:S(2)}, u32[]{:S(2)}) %collective-permute-start.8) | collective-permute-done | bytes 114720 | tf_op jit(solution)/shard_map/ppermute | solution.py:19
  36.3 0.6 copy-done.6
  37.0 0.4 collective-permute-start.13
  37.4 1.1 %collective-permute-done.13.refs_11_ = bf16[16,3712]{1,0:T(8,128)(2,1)} collective-permute-done((bf16[16,3712]{1,0:T(8,128)(2,1)S(1)}, bf16[16,3712]{1,0:T(8,128)(2,1)}, u32[]{:S(2)}, u32[]{:S(2)}) %collective-permute-start.13) | collective-permute-done | bytes 118816 | tf_op jit(solution)/shard_map/ppermute | solution.py:19
  38.5 0.9 %copy-done.3 = bf16[16,3712]{1,0:T(8,128)(2,1)S(1)} copy-done((bf16[16,3712]{1,0:T(8,128)(2,1)S(1)}, bf16[16,3712]{1,0:T(8,128)(2,1)}, u32[]{:S(2)}) %copy-start.3) | copy-done | bytes 118808
  39.4 0.9 %copy-done.5 = bf16[16,3584]{1,0:T(8,128)(2,1)S(1)} copy-done((bf16[16,3584]{1,0:T(8,128)(2,1)S(1)}, bf16[16,3584]{1,0:T(8,128)(2,1)}, u32[]{:S(2)}) %copy-start.5) | copy-done | bytes 114712
  40.3 0.9 %copy-done.7 = bf16[16,3584]{1,0:T(8,128)(2,1)S(1)} copy-done((bf16[16,3584]{1,0:T(8,128)(2,1)S(1)}, bf16[16,3584]{1,0:T(8,128)(2,1)}, u32[]{:S(2)}) %copy-start.7) | copy-done | bytes 114712
  41.2 6.1 %experts.1 = (bf16[64,3584]{1,0:T(8,128)(2,1)S(1)}, bf16[64,3584]{1,0:T(8,128)(2,1)S(1)}, bf16[64,3584]{1,0:T(8,128)(2,1)S(1)}, bf16[64,3584]{1,0:T(8,128)(2,1)S(1)}) custom-call(s32[1]{0:T(128)} %bitcast.2.refs_0_, bf16[16,3584]{1,0:T(8,128)(2,1)S(1)} %pad_maximum_fusion.4.refs_1_, bf16[16,3584]{1,0:T(8,128)(2,1)S(1)} %collective-permute-done.5.refs_2_, ...), custom_call_target="tpu_custom_call" | custom-call | tf_op jit(solution)/shard_map/experts/pallas_call | solution.py:139
  47.3 0.8 collective-permute-done.16.refs_3_
  48.1 0.5 collective-permute-start.21
  48.6 1.2 %collective-permute-done.17 = bf16[64,3584]{1,0:T(8,128)(2,1)S(1)} collective-permute-done((bf16[64,3584]{1,0:T(8,128)(2,1)S(1)}, bf16[64,3584]{1,0:T(8,128)(2,1)S(1)}, u32[]{:S(2)}, u32[]{:S(2)}) %collective-permute-start.17) | collective-permute-done | bytes 458784 | tf_op jit(solution)/shard_map/ppermute | solution.py:19
  50.0 0.9 collective-permute-start.18
  51.1 1.3 %collective-permute-start.22 = (bf16[32,3584]{1,0:T(8,128)(2,1)S(1)}, bf16[32,3584]{1,0:T(8,128)(2,1)S(1)}, u32[]{:S(2)}, u32[]{:S(2)}) collective-permute-start(bf16[32,3584]{1,0:T(8,128)(2,1)S(1)} %pad_maximum_fusion.2), channel_id=1, source_target_pairs={{0,2},{1,3},{2,0},{3,1},{4,6},{5,7},{6,4},{7,5},{8,10},{9,11},{10,... | collective-permute-start | bytes 688136 | tf_op jit(solution)/shard_map/ppermute | solution.py:19
  52.4 5.3 %collective-permute-done.18 = bf16[32,3584]{1,0:T(8,128)(2,1)S(1)} collective-permute-done((bf16[32,3584]{1,0:T(8,128)(2,1)S(1)}, bf16[32,3584]{1,0:T(8,128)(2,1)S(1)}, u32[]{:S(2)}, u32[]{:S(2)}) %collective-permute-start.18) | collective-permute-done | bytes 229408 | tf_op jit(solution)/shard_map/ppermute | solution.py:18
  57.8 1.6 %collective-permute-start.19 = (bf16[16,3584]{1,0:T(8,128)(2,1)S(1)}, bf16[16,3584]{1,0:T(8,128)(2,1)S(1)}, u32[]{:S(2)}, u32[]{:S(2)}) collective-permute-start(bf16[16,3584]{1,0:T(8,128)(2,1)S(1)} %slice.93), channel_id=1, source_target_pairs={{0,2},{1,3},{2,0},{3,1},{4,6},{5,7},{6,4},{7,5},{8,10},{9,11},{10,... | collective-permute-start | bytes 344072 | tf_op jit(solution)/shard_map/ppermute | solution.py:19
  59.5 0.6 collective-permute-start.23
  60.1 2.6 %collective-permute-done.19 = bf16[16,3584]{1,0:T(8,128)(2,1)S(1)} collective-permute-done((bf16[16,3584]{1,0:T(8,128)(2,1)S(1)}, bf16[16,3584]{1,0:T(8,128)(2,1)S(1)}, u32[]{:S(2)}, u32[]{:S(2)}) %collective-permute-start.19) | collective-permute-done | bytes 114720 | tf_op jit(solution)/shard_map/ppermute | solution.py:19
  62.8 1.6 %collective-permute-start.20 = (bf16[8,3584]{1,0:T(8,128)(2,1)S(1)}, bf16[8,3584]{1,0:T(8,128)(2,1)S(1)}, u32[]{:S(2)}, u32[]{:S(2)}) collective-permute-start(bf16[8,3584]{1,0:T(8,128)(2,1)S(1)} %slice.95), channel_id=1, source_target_pairs={{0,4},{1,5},{2,6},{3,7},{4,0},{5,1},{6,2},{7,3},{8,12},{9,13},{10,... | collective-permute-start | bytes 172040 | tf_op jit(solution)/shard_map/ppermute | solution.py:19
  64.5 0.6 copy-done.12
  65.1 1.5 %collective-permute-start.24 = (bf16[8,3584]{1,0:T(8,128)(2,1)S(1)}, bf16[8,3584]{1,0:T(8,128)(2,1)}, u32[]{:S(2)}, u32[]{:S(2)}) collective-permute-start(bf16[8,3584]{1,0:T(8,128)(2,1)S(1)} %slice.103), channel_id=1, source_target_pairs={{0,4},{1,5},{2,6},{3,7},{4,0},{5,1},{6,2},{7,3},{8,12},{9,13},{10,... | collective-permute-start | bytes 172040 | tf_op jit(solution)/shard_map/ppermute | solution.py:19
  66.6 1.1 %fusion.24 = (f32[4,64]{1,0:T(4,128)S(1)}, f32[4,64,256]{2,1,0:T(8,128)}) fusion(bf16[4,64,576]{2,1,0:T(8,128)(2,1)S(1)} %copy-done, bf16[4,256,576]{1,2,0:T(8,128)(2,1)S(1)} %copy-done.8, pred[4,256]{1,0:T(4,128)(4,1)S(1)} %iota_compare_fusion), kind=kOutput, calls=%fused_computation.56 | convolution fusion | flops 75693824 | bytes 1738752 | tf_op jit(solution)/shard_map/bhl,bpl->bhp/dot_general | solution.py:33
  67.8 0.5 collective-permute-start.27
  68.4 0.4 collective-permute-start.29
  68.8 0.2 copy-done.13
  69.0 0.4 collective-permute-done.24
  69.4 0.9 %broadcast_select_fusion = (bf16[8,3584]{1,0:T(8,128)(2,1)S(1)}, bf16[8,3584]{1,0:T(8,128)(2,1)S(1)}, bf16[8,3584]{1,0:T(8,128)(2,1)S(1)}) fusion(pred[]{:T(512)S(6)} %eq.4, bf16[8,3584]{1,0:T(8,128)(2,1)} %collective-permute-done.24, bf16[16,3584]{1,0:T(8,128)(2,1)} %copy-done.12, bf16[8,3584]{1,0:T(8,128)(2,1)} %copy-done.13, bf16[16,3584]{1,0:T(8,128)(2,1)} %copy-done.11), kind=kLoop, calls=%fused_computation.30 | loop fusion | flops 258048 | bytes 401409 | tf_op jit(solution)/shard_map/jit(_where)/select_n | solution.py:310
  70.3 0.6 reshape.45
  71.0 0.8 fusion.23
  71.8 0.6 reshape.46
  72.5 2.5 %collective-permute-start.25 = (bf16[8,3584]{1,0:T(8,128)(2,1)}, bf16[8,3584]{1,0:T(8,128)(2,1)S(1)}, u32[]{:S(2)}, u32[]{:S(2)}) collective-permute-start(bf16[8,3584]{1,0:T(8,128)(2,1)} %reshape.46), channel_id=1, source_target_pairs={{0,8},{1,9},{2,10},{3,11},{4,12},{5,13},{6,14},{7,15},{8,0},{9,1},... | collective-permute-start | bytes 172040 | tf_op jit(solution)/shard_map/ppermute | solution.py:19
  75.1 2.9 %collective-permute-done.25.in_ref = bf16[8,3584]{1,0:T(8,128)(2,1)S(1)} collective-permute-done((bf16[8,3584]{1,0:T(8,128)(2,1)}, bf16[8,3584]{1,0:T(8,128)(2,1)S(1)}, u32[]{:S(2)}, u32[]{:S(2)}) %collective-permute-start.25) | collective-permute-done | bytes 57376 | tf_op jit(solution)/shard_map/ppermute | solution.py:19
  78.0 2.4 %latent_parts.1 = (f32[4,640]{1,0:T(4,128)S(1)}, f32[4,640]{1,0:T(4,128)S(1)}, bf16[4,3584]{1,0:T(4,128)(2,1)S(1)}, bf16[4,3584]{1,0:T(4,128)(2,1)S(1)}) custom-call(s32[2]{0:T(128)S(1)} %pad_add_fusion.place_ref, bf16[8,3584]{1,0:T(8,128)(2,1)S(1)} %get-tuple-element.43.a_ref, bf16[8,3584]{1,0:T(8,128)(2,1)S(1)} %get-tuple-element.42.b_ref, ...), custom_call_target="tpu_custom_call" | custom-call | tf_op jit(solution)/shard_map/latent_parts/pallas_call | solution.py:227
  80.4 2.4 %collective-permute-start.31 = (f32[4,640]{1,0:T(4,128)S(1)}, f32[4,640]{1,0:T(4,128)S(1)}, u32[]{:S(2)}, u32[]{:S(2)}) collective-permute-start(f32[4,640]{1,0:T(4,128)S(1)} %get-tuple-element.40), channel_id=1, source_target_pairs={{0,8},{1,9},{2,10},{3,11},{4,12},{5,13},{6,14},{7,15},{8,0},{9,1},... | collective-permute-start | bytes 30728 | tf_op jit(solution)/shard_map/ppermute | solution.py:19
  82.8 0.2 fusion.4
  83.0 0.6 collective-permute-start.30
  83.6 1.4 %collective-permute-done.31 = f32[4,640]{1,0:T(4,128)S(1)} collective-permute-done((f32[4,640]{1,0:T(4,128)S(1)}, f32[4,640]{1,0:T(4,128)S(1)}, u32[]{:S(2)}, u32[]{:S(2)}) %collective-permute-start.31) | collective-permute-done | bytes 10272 | tf_op jit(solution)/shard_map/ppermute | solution.py:19
  85.0 0.2 fusion.16
  85.3 0.2 fusion.10
  85.6 1.2 %fusion.1 = bf16[4,64,512]{2,1,0:T(8,128)(2,1)} fusion(bf16[4,256,576]{1,2,0:T(8,128)(2,1)S(1)} %copy-done.9, f32[4,512]{1,0:T(4,128)S(1)} %slice_convert_fusion, f32[4,64]{1,0:T(4,128)S(1)} %get-tuple-element.53, f32[4,64]{1,0:T(4,128)S(1)} %get-tuple-element.52, f32[4,64,256]{2,1,0:T(8,128)S(1)} %copy-done.10, f32[4,64]{1,0:T(4,128)S(1)} %get-tuple-element.54), kind=kOutput, calls=%fused_computation.2 | convolution fusion | flops 67764224 | bytes 1587200 | tf_op jit(solution)/shard_map/bhp,bpv->bhv/dot_general | solution.py:40
  86.8 1.1 %collective-permute-done.30 = bf16[4,3584]{1,0:T(4,128)(2,1)S(1)} collective-permute-done((bf16[4,3584]{1,0:T(4,128)(2,1)S(1)}, bf16[4,3584]{1,0:T(4,128)(2,1)S(1)}, u32[]{:S(2)}, u32[]{:S(2)}) %collective-permute-start.30) | collective-permute-done | bytes 28704 | tf_op jit(solution)/shard_map/ppermute | solution.py:19
  87.8 0.7 maximum_select_fusion
  (78 shorter events, 1.3 us)
Async XLA Ops:
  0.6 66.0 %copy-start = (bf16[4,64,576]{2,1,0:T(8,128)(2,1)S(1)}, bf16[4,64,576]{2,1,0:T(8,128)(2,1)}, u32[]{:S(2)}) copy-start(bf16[4,64,576]{2,1,0:T(8,128)(2,1)} %param.19) | copy-start | bytes 884740
  0.6 7.6 %collective-permute-start = (bf16[4,7168]{1,0:T(4,128)(2,1)}, bf16[4,7168]{1,0:T(4,128)(2,1)S(1)}, u32[]{:S(2)}, u32[]{:S(2)}) collective-permute-start(bf16[4,7168]{1,0:T(4,128)(2,1)} %param.11), channel_id=1, source_target_pairs={{0,8},{1,9},{2,10},{3,11},{4,12},{5,13},{6,14},{7,15},{8,0},{9,1},... | collective-permute-start | bytes 172040 | tf_op jit(solution)/shard_map/ppermute | solution.py:19
  6.4 4.5 %collective-permute-start.2 = (bf16[4,128]{1,0:T(4,128)(2,1)S(1)}, bf16[4,128]{1,0:T(4,128)(2,1)S(1)}, u32[]{:S(2)}, u32[]{:S(2)}) collective-permute-start(bf16[4,128]{1,0:T(4,128)(2,1)S(1)} %fusion.20), channel_id=1, source_target_pairs={{0,8},{1,9},{2,10},{3,11},{4,12},{5,13},{6,14},{7,15},{8,0},{9,1},... | collective-permute-start | bytes 3080 | tf_op jit(solution)/shard_map/ppermute | solution.py:19
  6.4 14.7 %collective-permute-start.4 = (bf16[448,576]{1,0:T(8,128)(2,1)}, bf16[448,576]{1,0:T(8,128)(2,1)S(1)}, u32[]{:S(2)}, u32[]{:S(2)}) collective-permute-start(bf16[448,576]{1,0:T(8,128)(2,1)} %refs_0_), channel_id=1, source_target_pairs={{0,2},{1,3},{2,0},{3,1},{4,6},{5,7},{6,4},{7,5},{8,10},{9,11},{10,... | collective-permute-start | bytes 1548296 | tf_op jit(solution)/shard_map/ppermute | solution.py:19
  9.1 4.3 %collective-permute-start.1 = (bf16[8,3584]{1,0:T(8,128)(2,1)S(1)}, bf16[8,3584]{1,0:T(8,128)(2,1)S(1)}, u32[]{:S(2)}, u32[]{:S(2)}) collective-permute-start(bf16[8,3584]{1,0:T(8,128)(2,1)S(1)} %get-tuple-element.49.res_a), channel_id=1, source_target_pairs={{0,4},{1,5},{2,6},{3,7},{4,0},{5,1},{6,2},{7,3},{8,12},{9,13},{10,... | collective-permute-start | bytes 172040 | tf_op jit(solution)/shard_map/ppermute | solution.py:19
  10.9 4.3 %collective-permute-start.3 = (bf16[8,3712]{1,0:T(8,128)(2,1)S(1)}, bf16[8,3712]{1,0:T(8,128)(2,1)S(1)}, u32[]{:S(2)}, u32[]{:S(2)}) collective-permute-start(bf16[8,3712]{1,0:T(8,128)(2,1)S(1)} %maximum_maximum_fusion), channel_id=1, source_target_pairs={{0,4},{1,5},{2,6},{3,7},{4,0},{5,1},{6,2},{7,3},{8,12},{9,13},{10,... | collective-permute-start | bytes 178184 | tf_op jit(solution)/shard_map/ppermute | solution.py:19
  21.1 5.0 %collective-permute-start.10 = (bf16[16,3712]{1,0:T(8,128)(2,1)S(1)}, bf16[16,3712]{1,0:T(8,128)(2,1)S(1)}, u32[]{:S(2)}, u32[]{:S(2)}) collective-permute-start(bf16[16,3712]{1,0:T(8,128)(2,1)S(1)} %pad_maximum_fusion.3.refs_7_), channel_id=1, source_target_pairs={{0,16},{16,0},{1,17},{17,1},{2,18},{18,2},{3,19},{19,3},{4,20},{20... | collective-permute-start | bytes 356360 | tf_op jit(solution)/shard_map/ppermute | solution.py:18
  22.6 24.7 %collective-permute-start.15 = (bf16[448,576]{1,0:T(8,128)(2,1)}, bf16[448,576]{1,0:T(8,128)(2,1)S(1)}, u32[]{:S(2)}, u32[]{:S(2)}) collective-permute-start(bf16[448,576]{1,0:T(8,128)(2,1)} %refs_0_), channel_id=1, source_target_pairs={{0,4},{1,5},{2,6},{3,7},{4,0},{5,1},{6,2},{7,3},{8,12},{9,13},{10,... | collective-permute-start | bytes 1548296 | tf_op jit(solution)/shard_map/ppermute | solution.py:19
  24.2 4.8 %collective-permute-start.5 = (bf16[16,3584]{1,0:T(8,128)(2,1)S(1)}, bf16[16,3584]{1,0:T(8,128)(2,1)S(1)}, u32[]{:S(2)}, u32[]{:S(2)}) collective-permute-start(bf16[16,3584]{1,0:T(8,128)(2,1)S(1)} %pad_maximum_fusion.4.refs_1_), channel_id=1, source_target_pairs={{0,2},{1,3},{2,0},{3,1},{4,6},{5,7},{6,4},{7,5},{8,10},{9,11},{10,... | collective-permute-start | bytes 344072 | tf_op jit(solution)/shard_map/ppermute | solution.py:19
  25.7 3.9 %collective-permute-start.7 = (bf16[16,3584]{1,0:T(8,128)(2,1)S(1)}, bf16[16,3584]{1,0:T(8,128)(2,1)S(1)}, u32[]{:S(2)}, u32[]{:S(2)}) collective-permute-start(bf16[16,3584]{1,0:T(8,128)(2,1)S(1)} %pad_maximum_fusion.4.refs_1_), channel_id=1, source_target_pairs={{0,1},{1,0},{2,3},{3,2},{4,5},{5,4},{6,7},{7,6},{8,9},{9,8},{10,11... | collective-permute-start | bytes 344072 | tf_op jit(solution)/shard_map/ppermute | solution.py:19
  25.7 22.4 %collective-permute-start.16 = (bf16[448,576]{1,0:T(8,128)(2,1)S(1)}, bf16[448,576]{1,0:T(8,128)(2,1)S(1)}, u32[]{:S(2)}, u32[]{:S(2)}) collective-permute-start(bf16[448,576]{1,0:T(8,128)(2,1)S(1)} %collective-permute-done.4.refs_1_), channel_id=1, source_target_pairs={{0,4},{1,5},{2,6},{3,7},{4,0},{5,1},{6,2},{7,3},{8,12},{9,13},{10,... | collective-permute-start | bytes 1548296 | tf_op jit(solution)/shard_map/ppermute | solution.py:19
  26.2 8.0 %collective-permute-start.11 = (bf16[32,3712]{1,0:T(8,128)(2,1)S(1)}, bf16[32,3712]{1,0:T(8,128)(2,1)S(1)}, u32[]{:S(2)}, u32[]{:S(2)}) collective-permute-start(bf16[32,3712]{1,0:T(8,128)(2,1)S(1)} %pad_maximum_fusion), channel_id=1, source_target_pairs={{0,2},{1,3},{2,0},{3,1},{4,6},{5,7},{6,4},{7,5},{8,10},{9,11},{10,... | collective-permute-start | bytes 712712 | tf_op jit(solution)/shard_map/ppermute | solution.py:19
  29.0 6.3 %collective-permute-start.6 = (bf16[32,3584]{1,0:T(8,128)(2,1)S(1)}, bf16[32,3584]{1,0:T(8,128)(2,1)S(1)}, u32[]{:S(2)}, u32[]{:S(2)}) collective-permute-start(bf16[32,3584]{1,0:T(8,128)(2,1)S(1)} %pad_maximum_fusion.1), channel_id=1, source_target_pairs={{0,16},{16,0},{1,17},{17,1},{2,18},{18,2},{3,19},{19,3},{4,20},{20... | collective-permute-start | bytes 688136 | tf_op jit(solution)/shard_map/ppermute | solution.py:18
  29.6 0.6 copy-start.4
  30.2 3.9 %collective-permute-start.12 = (bf16[16,3712]{1,0:T(8,128)(2,1)S(1)}, bf16[16,3712]{1,0:T(8,128)(2,1)S(1)}, u32[]{:S(2)}, u32[]{:S(2)}) collective-permute-start(bf16[16,3712]{1,0:T(8,128)(2,1)S(1)} %pad_maximum_fusion.3.refs_7_), channel_id=1, source_target_pairs={{0,1},{1,0},{2,3},{3,2},{4,5},{5,4},{6,7},{7,6},{8,9},{9,8},{10,11... | collective-permute-start | bytes 356360 | tf_op jit(solution)/shard_map/ppermute | solution.py:19
  34.1 4.3 %collective-permute-start.14 = (bf16[32,3712]{1,0:T(8,128)(2,1)S(1)}, bf16[32,3712]{1,0:T(8,128)(2,1)S(1)}, u32[]{:S(2)}, u32[]{:S(2)}) collective-permute-start(bf16[32,3712]{1,0:T(8,128)(2,1)S(1)} %collective-permute-done.11.refs_9_), channel_id=1, source_target_pairs={{0,1},{1,0},{2,3},{3,2},{4,5},{5,4},{6,7},{7,6},{8,9},{9,8},{10,11... | collective-permute-start | bytes 712712 | tf_op jit(solution)/shard_map/ppermute | solution.py:19
  34.1 0.6 copy-start.2
  34.8 1.5 %collective-permute-start.8 = (bf16[16,3584]{1,0:T(8,128)(2,1)S(1)}, bf16[16,3584]{1,0:T(8,128)(2,1)S(1)}, u32[]{:S(2)}, u32[]{:S(2)}) collective-permute-start(bf16[16,3584]{1,0:T(8,128)(2,1)S(1)} %collective-permute-done.5.refs_2_), channel_id=1, source_target_pairs={{0,1},{1,0},{2,3},{3,2},{4,5},{5,4},{6,7},{7,6},{8,9},{9,8},{10,11... | collective-permute-start | bytes 344072 | tf_op jit(solution)/shard_map/ppermute | solution.py:19
  35.3 3.2 %collective-permute-start.9 = (bf16[32,3584]{1,0:T(8,128)(2,1)S(1)}, bf16[32,3584]{1,0:T(8,128)(2,1)}, u32[]{:S(2)}, u32[]{:S(2)}) collective-permute-start(bf16[32,3584]{1,0:T(8,128)(2,1)S(1)} %collective-permute-done.6.refs_3_), channel_id=1, source_target_pairs={{0,1},{1,0},{2,3},{3,2},{4,5},{5,4},{6,7},{7,6},{8,9},{9,8},{10,11... | collective-permute-start | bytes 688136 | tf_op jit(solution)/shard_map/ppermute | solution.py:19
  36.3 0.6 copy-start.6
  37.0 1.5 %collective-permute-start.13 = (bf16[16,3712]{1,0:T(8,128)(2,1)S(1)}, bf16[16,3712]{1,0:T(8,128)(2,1)}, u32[]{:S(2)}, u32[]{:S(2)}) collective-permute-start(bf16[16,3712]{1,0:T(8,128)(2,1)S(1)} %collective-permute-done.10.refs_8_), channel_id=1, source_target_pairs={{0,1},{1,0},{2,3},{3,2},{4,5},{5,4},{6,7},{7,6},{8,9},{9,8},{10,11... | collective-permute-start | bytes 356360 | tf_op jit(solution)/shard_map/ppermute | solution.py:19
  38.5 0.9 %copy-start.3 = (bf16[16,3712]{1,0:T(8,128)(2,1)S(1)}, bf16[16,3712]{1,0:T(8,128)(2,1)}, u32[]{:S(2)}) copy-start(bf16[16,3712]{1,0:T(8,128)(2,1)} %copy-done.2) | copy-start | bytes 356356
  39.4 0.9 %copy-start.5 = (bf16[16,3584]{1,0:T(8,128)(2,1)S(1)}, bf16[16,3584]{1,0:T(8,128)(2,1)}, u32[]{:S(2)}) copy-start(bf16[16,3584]{1,0:T(8,128)(2,1)} %copy-done.4) | copy-start | bytes 344068
  40.3 0.9 %copy-start.7 = (bf16[16,3584]{1,0:T(8,128)(2,1)S(1)}, bf16[16,3584]{1,0:T(8,128)(2,1)}, u32[]{:S(2)}) copy-start(bf16[16,3584]{1,0:T(8,128)(2,1)} %copy-done.6) | copy-start | bytes 344068
  41.2 6.9 %copy-start.16 = (s32[4]{0:T(128)S(1)}, s32[4]{0:T(128)}, u32[]{:S(2)}) copy-start(s32[4]{0:T(128)} %param.21) | copy-start | bytes 52
  48.1 1.8 %collective-permute-start.17 = (bf16[64,3584]{1,0:T(8,128)(2,1)S(1)}, bf16[64,3584]{1,0:T(8,128)(2,1)S(1)}, u32[]{:S(2)}, u32[]{:S(2)}) collective-permute-start(bf16[64,3584]{1,0:T(8,128)(2,1)S(1)} %get-tuple-element.30), channel_id=1, source_target_pairs={{0,1},{1,0},{2,3},{3,2},{4,5},{5,4},{6,7},{7,6},{8,9},{9,8},{10,11... | collective-permute-start | bytes 1376264 | tf_op jit(solution)/shard_map/ppermute | solution.py:19
  48.1 2.8 %collective-permute-start.21 = (bf16[64,3584]{1,0:T(8,128)(2,1)S(1)}, bf16[64,3584]{1,0:T(8,128)(2,1)S(1)}, u32[]{:S(2)}, u32[]{:S(2)}) collective-permute-start(bf16[64,3584]{1,0:T(8,128)(2,1)S(1)} %get-tuple-element.32), channel_id=1, source_target_pairs={{0,1},{1,0},{2,3},{3,2},{4,5},{5,4},{6,7},{7,6},{8,9},{9,8},{10,11... | collective-permute-start | bytes 1376264 | tf_op jit(solution)/shard_map/ppermute | solution.py:19
  50.0 7.7 %collective-permute-start.18 = (bf16[32,3584]{1,0:T(8,128)(2,1)S(1)}, bf16[32,3584]{1,0:T(8,128)(2,1)S(1)}, u32[]{:S(2)}, u32[]{:S(2)}) collective-permute-start(bf16[32,3584]{1,0:T(8,128)(2,1)S(1)} %slice.91), channel_id=1, source_target_pairs={{0,16},{16,0},{1,17},{17,1},{2,18},{18,2},{3,19},{19,3},{4,20},{20... | collective-permute-start | bytes 688136 | tf_op jit(solution)/shard_map/ppermute | solution.py:18
  51.1 8.3 %collective-permute-start.22 = (bf16[32,3584]{1,0:T(8,128)(2,1)S(1)}, bf16[32,3584]{1,0:T(8,128)(2,1)S(1)}, u32[]{:S(2)}, u32[]{:S(2)}) collective-permute-start(bf16[32,3584]{1,0:T(8,128)(2,1)S(1)} %pad_maximum_fusion.2), channel_id=1, source_target_pairs={{0,2},{1,3},{2,0},{3,1},{4,6},{5,7},{6,4},{7,5},{8,10},{9,11},{10,... | collective-permute-start | bytes 688136 | tf_op jit(solution)/shard_map/ppermute | solution.py:19
  57.8 8.8 %copy-start.8 = (bf16[4,256,576]{1,2,0:T(8,128)(2,1)S(1)}, bf16[4,256,576]{1,2,0:T(8,128)(2,1)}, u32[]{:S(2)}) copy-start(bf16[4,256,576]{1,2,0:T(8,128)(2,1)} %param.20) | copy-start | bytes 3538948
  57.8 4.9 %collective-permute-start.19 = (bf16[16,3584]{1,0:T(8,128)(2,1)S(1)}, bf16[16,3584]{1,0:T(8,128)(2,1)S(1)}, u32[]{:S(2)}, u32[]{:S(2)}) collective-permute-start(bf16[16,3584]{1,0:T(8,128)(2,1)S(1)} %slice.93), channel_id=1, source_target_pairs={{0,2},{1,3},{2,0},{3,1},{4,6},{5,7},{6,4},{7,5},{8,10},{9,11},{10,... | collective-permute-start | bytes 344072 | tf_op jit(solution)/shard_map/ppermute | solution.py:19
  59.5 4.9 %collective-permute-start.23 = (bf16[16,3584]{1,0:T(8,128)(2,1)S(1)}, bf16[16,3584]{1,0:T(8,128)(2,1)S(1)}, u32[]{:S(2)}, u32[]{:S(2)}) collective-permute-start(bf16[16,3584]{1,0:T(8,128)(2,1)S(1)} %slice.101), channel_id=1, source_target_pairs={{0,16},{16,0},{1,17},{17,1},{2,18},{18,2},{3,19},{19,3},{4,20},{20... | collective-permute-start | bytes 344072 | tf_op jit(solution)/shard_map/ppermute | solution.py:18
  62.7 1.7 %copy-start.11 = (bf16[16,3584]{1,0:T(8,128)(2,1)}, bf16[16,3584]{1,0:T(8,128)(2,1)S(1)}, u32[]{:S(2)}) copy-start(bf16[16,3584]{1,0:T(8,128)(2,1)S(1)} %add_convert_fusion.5) | copy-start | bytes 344068
  62.7 5.0 %copy-start.14 = (f32[7168]{0:T(1024)S(1)}, f32[7168]{0:T(1024)}, u32[]{:S(2)}) copy-start(f32[7168]{0:T(1024)} %param.17) | copy-start | bytes 86020
  62.7 5.0 %copy-start.1 = (bf16[448,576]{1,0:T(8,128)(2,1)S(1)}, bf16[448,576]{1,0:T(8,128)(2,1)}, u32[]{:S(2)}) copy-start(bf16[448,576]{1,0:T(8,128)(2,1)} %refs_0_) | copy-start | bytes 1548292
  62.8 5.6 %collective-permute-start.20 = (bf16[8,3584]{1,0:T(8,128)(2,1)S(1)}, bf16[8,3584]{1,0:T(8,128)(2,1)S(1)}, u32[]{:S(2)}, u32[]{:S(2)}) collective-permute-start(bf16[8,3584]{1,0:T(8,128)(2,1)S(1)} %slice.95), channel_id=1, source_target_pairs={{0,4},{1,5},{2,6},{3,7},{4,0},{5,1},{6,2},{7,3},{8,12},{9,13},{10,... | collective-permute-start | bytes 172040 | tf_op jit(solution)/shard_map/ppermute | solution.py:19
  64.4 0.7 copy-start.12
  65.1 4.3 %collective-permute-start.24 = (bf16[8,3584]{1,0:T(8,128)(2,1)S(1)}, bf16[8,3584]{1,0:T(8,128)(2,1)}, u32[]{:S(2)}, u32[]{:S(2)}) collective-permute-start(bf16[8,3584]{1,0:T(8,128)(2,1)S(1)} %slice.103), channel_id=1, source_target_pairs={{0,4},{1,5},{2,6},{3,7},{4,0},{5,1},{6,2},{7,3},{8,12},{9,13},{10,... | collective-permute-start | bytes 172040 | tf_op jit(solution)/shard_map/ppermute | solution.py:19
  67.7 7.4 %collective-permute-start.26 = (bf16[448,576]{1,0:T(8,128)(2,1)S(1)}, bf16[448,576]{1,0:T(8,128)(2,1)S(1)}, u32[]{:S(2)}, u32[]{:S(2)}) collective-permute-start(bf16[448,576]{1,0:T(8,128)(2,1)S(1)} %copy-done.1), channel_id=1, source_target_pairs={{0,1},{1,0},{2,3},{3,2},{4,5},{5,4},{6,7},{7,6},{8,9},{9,8},{10,11... | collective-permute-start | bytes 1548296 | tf_op jit(solution)/shard_map/ppermute | solution.py:19
  67.8 7.3 %collective-permute-start.27 = (bf16[448,576]{1,0:T(8,128)(2,1)S(1)}, bf16[448,576]{1,0:T(8,128)(2,1)}, u32[]{:S(2)}, u32[]{:S(2)}) collective-permute-start(bf16[448,576]{1,0:T(8,128)(2,1)S(1)} %collective-permute-done.4.refs_1_), channel_id=1, source_target_pairs={{0,1},{1,0},{2,3},{3,2},{4,5},{5,4},{6,7},{7,6},{8,9},{9,8},{10,11... | collective-permute-start | bytes 1548296 | tf_op jit(solution)/shard_map/ppermute | solution.py:19
  68.3 6.8 %collective-permute-start.28 = (bf16[448,576]{1,0:T(8,128)(2,1)S(1)}, bf16[448,576]{1,0:T(8,128)(2,1)}, u32[]{:S(2)}, u32[]{:S(2)}) collective-permute-start(bf16[448,576]{1,0:T(8,128)(2,1)S(1)} %collective-permute-done.15.refs_2_), channel_id=1, source_target_pairs={{0,1},{1,0},{2,3},{3,2},{4,5},{5,4},{6,7},{7,6},{8,9},{9,8},{10,11... | collective-permute-start | bytes 1548296 | tf_op jit(solution)/shard_map/ppermute | solution.py:19
  68.4 0.6 copy-start.13
  68.4 6.7 %collective-permute-start.29 = (bf16[448,576]{1,0:T(8,128)(2,1)S(1)}, bf16[448,576]{1,0:T(8,128)(2,1)}, u32[]{:S(2)}, u32[]{:S(2)}) collective-permute-start(bf16[448,576]{1,0:T(8,128)(2,1)S(1)} %collective-permute-done.16.refs_3_), channel_id=1, source_target_pairs={{0,1},{1,0},{2,3},{3,2},{4,5},{5,4},{6,7},{7,6},{8,9},{9,8},{10,11... | collective-permute-start | bytes 1548296 | tf_op jit(solution)/shard_map/ppermute | solution.py:19
  72.5 5.5 %collective-permute-start.25 = (bf16[8,3584]{1,0:T(8,128)(2,1)}, bf16[8,3584]{1,0:T(8,128)(2,1)S(1)}, u32[]{:S(2)}, u32[]{:S(2)}) collective-permute-start(bf16[8,3584]{1,0:T(8,128)(2,1)} %reshape.46), channel_id=1, source_target_pairs={{0,8},{1,9},{2,10},{3,11},{4,12},{5,13},{6,14},{7,15},{8,0},{9,1},... | collective-permute-start | bytes 172040 | tf_op jit(solution)/shard_map/ppermute | solution.py:19
  78.0 4.8 %copy-start.10 = (f32[4,64,256]{2,1,0:T(8,128)S(1)}, f32[4,64,256]{2,1,0:T(8,128)}, u32[]{:S(2)}) copy-start(f32[4,64,256]{2,1,0:T(8,128)} %get-tuple-element.55) | copy-start | bytes 786436
  78.0 7.6 %copy-start.9 = (bf16[4,256,576]{1,2,0:T(8,128)(2,1)S(1)}, bf16[4,256,576]{1,2,0:T(8,128)(2,1)}, u32[]{:S(2)}) copy-start(bf16[4,256,576]{1,2,0:T(8,128)(2,1)} %param.20) | copy-start | bytes 3538948
  80.4 4.6 %collective-permute-start.31 = (f32[4,640]{1,0:T(4,128)S(1)}, f32[4,640]{1,0:T(4,128)S(1)}, u32[]{:S(2)}, u32[]{:S(2)}) collective-permute-start(f32[4,640]{1,0:T(4,128)S(1)} %get-tuple-element.40), channel_id=1, source_target_pairs={{0,8},{1,9},{2,10},{3,11},{4,12},{5,13},{6,14},{7,15},{8,0},{9,1},... | collective-permute-start | bytes 30728 | tf_op jit(solution)/shard_map/ppermute | solution.py:19
  83.0 4.8 %collective-permute-start.30 = (bf16[4,3584]{1,0:T(4,128)(2,1)S(1)}, bf16[4,3584]{1,0:T(4,128)(2,1)S(1)}, u32[]{:S(2)}, u32[]{:S(2)}) collective-permute-start(bf16[4,3584]{1,0:T(4,128)(2,1)S(1)} %get-tuple-element.37), channel_id=1, source_target_pairs={{0,8},{1,9},{2,10},{3,11},{4,12},{5,13},{6,14},{7,15},{8,0},{9,1},... | collective-permute-start | bytes 86024 | tf_op jit(solution)/shard_map/ppermute | solution.py:19
  85.3 3.1 %copy-start.15 = (bf16[4,576]{1,0:T(4,128)(2,1)}, bf16[4,576]{1,0:T(4,128)(2,1)S(1)}, u32[]{:S(2)}) copy-start(bf16[4,576]{1,0:T(4,128)(2,1)S(1)} %fusion.9) | copy-start | bytes 13828

commit v2 on v1

v2 whole, which is shorter than its diff:
```python
import jax
import jax.numpy as jnp
from jax import lax
from jax.experimental import pallas as pl
from jax.experimental.pallas import tpu as pltpu
from jax.sharding import PartitionSpec as P

FF = 2048
KV = 512
LANES = 128

score_scale = 192.0 ** (-0.5)
norm_eps = 1e-06


def swap(x, bit):
    if bit == "sec":
        return lax.ppermute(x, "sec", [(i, i ^ 1) for i in range(lax.axis_size("sec"))])
    return lax.ppermute(x, "dev", [(i, i ^ (1 << bit)) for i in range(lax.axis_size("dev"))])


def wide_total(kept, received):
    return kept.astype(jnp.float32) + received.astype(jnp.float32)


def total(kept, received):
    return wide_total(kept, received).astype(jnp.bfloat16)


def flipped(x, rows):
    blocks = x.reshape(-1, 2, rows, x.shape[1])
    return jnp.concatenate([blocks[:, 1:], blocks[:, :1]], axis=1).reshape(x.shape)


def cache_kernel(lengths_ref, q_ref, kv_ref, stats_ref, out_ref):
    heads, count = q_ref.shape[1], kv_ref.shape[2]
    lane = lax.broadcasted_iota(jnp.int32, (heads, LANES), 1)
    position = lax.broadcasted_iota(jnp.int32, (heads, count), 1)
    for row in range(q_ref.shape[0]):
        scores = jnp.dot(q_ref[row], kv_ref[row], preferred_element_type=jnp.float32) * score_scale
        scores = jnp.where(position < lengths_ref[row], scores, -1e30)
        peak = jnp.max(scores, axis=1, keepdims=True)
        spread = jnp.exp(scores - peak)
        denominator = jnp.sum(spread, axis=1, keepdims=True)
        out_ref[row] = lax.dot_general(
            spread.astype(jnp.bfloat16),
            kv_ref[row, :KV, :],
            (((1,), (1,)), ((), ())),
            preferred_element_type=jnp.float32,
        )
        stats_ref[row] = jnp.where(lane == 0, peak, denominator)


def cache_part(queries, kv_cache, lengths):
    rows, heads = queries.shape[:2]
    vmem = pl.BlockSpec(memory_space=pltpu.VMEM)
    return pl.pallas_call(
        cache_kernel,
        out_shape=(
            jax.ShapeDtypeStruct((rows, heads, LANES), jnp.float32),
            jax.ShapeDtypeStruct((rows, heads, KV), jnp.float32),
        ),
        in_specs=[pl.BlockSpec(memory_space=pltpu.SMEM), vmem, vmem],
        out_specs=[vmem] * 2,
        compiler_params=pltpu.CompilerParams(vmem_limit_bytes=8 << 20),
        cost_estimate=pl.CostEstimate(
            flops=4 * queries.size * kv_cache.shape[1],
            bytes_accessed=2 * kv_cache.size,
            transcendentals=0,
        ),
        name="cache_part",
    )(lengths, queries, jnp.swapaxes(kv_cache, 1, 2))


def finish_kernel(width, sums_ref, in_ref, q_ref, stats_ref, part_ref, latent_ref, out_ref):
    lat = q_ref.shape[2]
    sums = sums_ref[...] + in_ref[...]
    inverse = lax.rsqrt(sums[:, lat : lat + 1] / width + norm_eps)
    rounded = (sums[:, :lat] * inverse).astype(jnp.bfloat16)
    latent_ref[...] = rounded
    latent = rounded.astype(jnp.float32)
    for row in range(q_ref.shape[0]):
        own = latent[row : row + 1]
        own_score = jnp.sum(q_ref[row].astype(jnp.float32) * own, axis=1, keepdims=True) * score_scale
        peak, denominator = stats_ref[row, :, 0:1], stats_ref[row, :, 1:2]
        top = jnp.maximum(peak, own_score)
        shrink = jnp.exp(peak - top)
        own_weight = jnp.exp(own_score - top)
        scale = 1.0 / (denominator * shrink + own_weight)
        own_prob = (own_weight * scale).astype(jnp.bfloat16).astype(jnp.float32)
        value = part_ref[row] * (shrink * scale) + own_prob * own[:, :KV]
        out_ref[row] = value.astype(jnp.bfloat16)


def finish(width, sums, sums_in, queries, stats, combined):
    rows, heads, lat = queries.shape
    vmem = pl.BlockSpec(memory_space=pltpu.VMEM)
    return pl.pallas_call(
        lambda *refs: finish_kernel(width, *refs),
        out_shape=(
            jax.ShapeDtypeStruct((rows, lat), jnp.bfloat16),
            jax.ShapeDtypeStruct((rows, heads, KV), jnp.bfloat16),
        ),
        in_specs=[vmem] * 5,
        out_specs=[vmem] * 2,
        compiler_params=pltpu.CompilerParams(vmem_limit_bytes=8 << 20),
        name="finish",
    )(sums, sums_in, queries, stats, combined)


def gather_rows(hidden_in, expert_ids, gate_scores, high, w_kv):
    width = hidden_in.shape[1]
    picks = expert_ids.shape[1]
    half = width // 2
    x = hidden_in
    info = jnp.concatenate([expert_ids.astype(jnp.bfloat16), gate_scores], axis=1)
    info = jnp.pad(info, ((0, 0), (0, LANES - 2 * picks)))
    w_low = swap(w_kv, 1)
    for bit in reversed(high):
        x, info = (jnp.concatenate([v, swap(v, bit)], axis=0) for v in (x, info))
    a, b = x[:, :half], x[:, half:]
    group = (a, b)
    b = jnp.concatenate([b, info], axis=1)
    a, b = (jnp.concatenate([v, swap(v, 2)], axis=0) for v in (a, b))
    a, b, w_own = lax.optimization_barrier((a, b, w_kv))
    w_mid = swap(w_own, 2)
    a_low, b_sec = swap(a, 1), swap(b, "sec")
    a, b = jnp.concatenate([a, a_low], axis=0), jnp.concatenate([b, b_sec], axis=0)
    a_sec, b_low = swap(a, "sec"), swap(b, 1)
    *a_all, w_low = lax.optimization_barrier((a, a_sec, w_low))
    w_both = swap(w_low, 2)
    a_all, b_all = tuple(a_all), (b, b_low)
    a_all += tuple(swap(v, 0) for v in a_all)
    b_all += tuple(swap(v, 0) for v in b_all)
    return group, a_all, b_all, (w_own, w_low, w_mid, w_both)


CHUNK = 512


def experts_kernel(picks, expert_ref, *refs):
    a_refs, b_refs, w_refs, outs = refs[:4], refs[4:8], refs[8:11], refs[11:15]
    gate_ref, up_ref, down_ref, sems = refs[15:]
    keep_a, keep_b, send_a, send_b = outs
    size, half = a_refs[0].shape
    size //= 2
    moves = []
    for part in (pl.ds(0, half), pl.ds(half, half)):
        moves.append((w_refs[0].at[part], gate_ref.at[part]))
        moves.append((w_refs[1].at[part], up_ref.at[part]))
    for part in (pl.ds(0, half), pl.ds(half, half)):
        moves.append((w_refs[2].at[:, part], down_ref.at[:, part]))
    copies = [pltpu.make_async_copy(*move, sems.at[i]) for i, move in enumerate(moves)]
    for copy in copies:
        copy.start()

    def rows_of(part, cols):
        if part == 0:
            return jnp.concatenate([ref[:, cols] for ref in a_refs], axis=0)
        blocks = []
        for side in range(2):
            early, late = b_refs[2 * side][:, cols], b_refs[2 * side + 1][:, cols]
            blocks += [early[:size], late[:size], early[size:], late[size:]]
        return jnp.concatenate(blocks, axis=0)

    info = rows_of(1, slice(half, half + LANES)).astype(jnp.float32)
    rows, hid = info.shape[0], gate_ref.shape[1]
    lane = lax.broadcasted_iota(jnp.int32, info.shape, 1)
    scores = jnp.where(lane < picks, pltpu.roll(info, LANES - picks, 1), 0.0)
    named = jnp.where(info == expert_ref[0].astype(jnp.float32), scores, 0.0)
    share = jnp.sum(named, axis=1, keepdims=True) / jnp.sum(scores, axis=1, keepdims=True)
    gate_act = jnp.zeros((rows, hid), jnp.float32)
    up_act = jnp.zeros((rows, hid), jnp.float32)
    for part in range(2):
        copies[2 * part].wait()
        copies[2 * part + 1].wait()
        for k in range(0, half, CHUNK):
            x = rows_of(part, slice(k, k + CHUNK))
            depth = slice(part * half + k, part * half + k + CHUNK)
            gate_act += jnp.dot(x, gate_ref[depth, :], preferred_element_type=jnp.float32)
            up_act += jnp.dot(x, up_ref[depth, :], preferred_element_type=jnp.float32)
    hidden = (gate_act / (1.0 + jnp.exp(-gate_act)) * up_act).astype(jnp.bfloat16)
    for part, kept, sent in ((0, keep_a, send_a), (1, keep_b, send_b)):
        copies[4 + part].wait()
        for c in range(0, half, CHUNK):
            cols = slice(part * half + c, part * half + c + CHUNK)
            partial = jnp.dot(hidden, down_ref[:, cols], preferred_element_type=jnp.float32)
            partial = (partial * share).astype(jnp.bfloat16)
            kept[:, c : c + CHUNK] = partial[: rows // 2]
            sent[:, c : c + CHUNK] = partial[rows // 2 :]


def experts(a_all, b_all, picks, expert, w_gate, w_up, w_down):
    rows, half = a_all[0].shape
    out = jax.ShapeDtypeStruct((2 * rows, half), jnp.bfloat16)
    vmem = pl.BlockSpec(memory_space=pltpu.VMEM)
    anywhere = pl.BlockSpec(memory_space=pl.ANY)
    return pl.pallas_call(
        lambda *refs: experts_kernel(picks, *refs),
        out_shape=(out,) * 4,
        in_specs=[pl.BlockSpec(memory_space=pltpu.SMEM)] + [vmem] * 8 + [anywhere] * 3,
        out_specs=[vmem] * 4,
        scratch_shapes=[
            pltpu.VMEM(w_gate.shape, w_gate.dtype),
            pltpu.VMEM(w_up.shape, w_up.dtype),
            pltpu.VMEM(w_down.shape, w_down.dtype),
            pltpu.SemaphoreType.DMA((6,)),
        ],
        compiler_params=pltpu.CompilerParams(vmem_limit_bytes=48 << 20),
        name="experts",
    )(expert.reshape(1), *a_all, *b_all, w_gate, w_up, w_down)


def experts_wide(a_all, b_all, picks, expert, w_gate, w_up, w_down):
    size, half = a_all[0].shape
    size //= 2
    b_all = [
        v
        for early, late in (b_all[:2], b_all[2:])
        for v in (early[:size], late[:size], early[size:], late[size:])
    ]
    a, b = jnp.concatenate(a_all, axis=0), jnp.concatenate(b_all, axis=0)
    info = b[:, half:].astype(jnp.float32)
    scores = info[:, picks : 2 * picks]
    named = jnp.where(info[:, :picks] == expert.astype(jnp.float32), scores, 0.0)
    share = jnp.sum(named, axis=1, keepdims=True) / jnp.sum(scores, axis=1, keepdims=True)
    x = jnp.concatenate([a, b[:, :half]], axis=1)
    gate_act = jnp.dot(x, w_gate, preferred_element_type=jnp.float32)
    up_act = jnp.dot(x, w_up, preferred_element_type=jnp.float32)
    hidden = (jax.nn.silu(gate_act) * up_act).astype(jnp.bfloat16)
    partial = jnp.dot(hidden, w_down, preferred_element_type=jnp.float32)
    partial = (share * partial).astype(jnp.bfloat16)
    rows = 4 * size
    return partial[:rows, :half], partial[:rows, half:], partial[rows:, :half], partial[rows:, half:]


def scatter_rows(keep_a, keep_b, send_a, send_b, slices, cache):
    rows = keep_a.shape[0] // 2
    quarter = rows // 2
    a, b = total(keep_a, swap(send_a, 0)), total(keep_b, swap(send_b, 0))
    a_in = swap(a[rows:], "sec")
    b_in = swap(jnp.concatenate([b[quarter:rows], b[rows + quarter :]], axis=0), 1)
    a_in, b_in, slices, cache = lax.optimization_barrier((a_in, b_in, slices, cache))
    a = total(a[:rows], a_in)
    b = total(jnp.concatenate([b[:quarter], b[rows : rows + quarter]], axis=0), b_in)
    a_in, b_in = swap(a[quarter:], 1), swap(b[quarter:], "sec")
    a, b = total(a[:quarter], a_in), total(b[:quarter], b_in)
    rows = quarter // 2
    a, b = (total(v[:rows], swap(v[rows:], 2)) for v in (a, b))
    return a, b, slices, cache


def latent_kernel(place_ref, kept_ref, in_ref, group_ref, gain_ref, *refs):
    w_refs = refs[:8]
    sums_ref, sums_out, moe_ref, piece_ref = refs[8:]
    rows, half = in_ref.shape
    own = rows // 2
    piece, lat = w_refs[0].shape
    upper = place_ref[0] == 1
    group = jnp.where(upper, group_ref[:, half:], group_ref[:, :half]).astype(jnp.float32)
    received = pltpu.roll(in_ref[...].astype(jnp.float32), own, 0)
    moe = (group + (kept_ref[...] + received)).astype(jnp.bfloat16)
    moe_ref[...] = moe[:own]
    widened = moe.astype(jnp.float32)
    scaled = widened * gain_ref[pl.ds(place_ref[0], 1), :]
    for p in range(8):
        piece_ref[p] = scaled[:, p * piece : (p + 1) * piece]
    sums = jnp.zeros((rows, lat), jnp.float32)
    for slot, w_ref in enumerate(w_refs):
        flips = ((slot & 1) << 1) | ((slot & 2) << 1) | (slot >> 2)
        x = piece_ref[place_ref[1] ^ flips].astype(jnp.bfloat16)
        sums += jnp.dot(x, w_ref[...], preferred_element_type=jnp.float32)
    squares = jnp.sum(widened * widened, axis=1, keepdims=True)
    tail = jnp.broadcast_to(squares, (rows, LANES))
    for ref, first in ((sums_ref, 0), (sums_out, own)):
        ref[:, :lat] = sums[first : first + own]
        ref[:, lat:] = tail[first : first + own, : ref.shape[1] - lat]


def latent_parts(place, kept, received, group, gain, slices):
    rows, half = received.shape
    piece, lat = slices[0].shape
    own = rows // 2
    vmem = pl.BlockSpec(memory_space=pltpu.VMEM)
    padded = -(-(lat + 1) // LANES) * LANES
    sums = jax.ShapeDtypeStruct((own, padded), jnp.float32)
    moe = jax.ShapeDtypeStruct((own, half), jnp.bfloat16)
    return pl.pallas_call(
        latent_kernel,
        out_shape=(sums, sums, moe),
        in_specs=[pl.BlockSpec(memory_space=pltpu.SMEM)] + [vmem] * 12,
        out_specs=[vmem] * 3,
        scratch_shapes=[pltpu.VMEM((8, rows, piece), jnp.float32)],
        compiler_params=pltpu.CompilerParams(vmem_limit_bytes=12 << 20),
        name="latent_parts",
    )(place, kept, received, group, gain.reshape(2, half), *slices)


def moe_kernel(place_ref, mine_ref, extra_ref, sum_ref, group_ref, moe_ref):
    own, half = mine_ref.shape
    upper = place_ref[0] == 1
    group = jnp.where(upper, group_ref[:, :half], group_ref[:, half:])
    other = (sum_ref[...].astype(jnp.float32) + group.astype(jnp.float32))[:own]
    other = (other + extra_ref[...].astype(jnp.float32)).astype(jnp.bfloat16)
    mine = mine_ref[...]
    moe_ref[:, :half] = jnp.where(upper, other, mine)
    moe_ref[:, half:] = jnp.where(upper, mine, other)


def moe_rows(place, mine, extra, other, group):
    own, half = mine.shape
    vmem = pl.BlockSpec(memory_space=pltpu.VMEM)
    return pl.pallas_call(
        moe_kernel,
        out_shape=jax.ShapeDtypeStruct((own, 2 * half), jnp.bfloat16),
        in_specs=[pl.BlockSpec(memory_space=pltpu.SMEM)] + [vmem] * 4,
        out_specs=vmem,
        compiler_params=pltpu.CompilerParams(vmem_limit_bytes=4 << 20),
        name="moe_rows",
    )(place, mine, extra, other, group)


def latent_parts_wide(device, high, mixture, residual, own_rows, norm_gain, slices):
    for bit in reversed(high[:-1]):
        part = mixture.shape[1] // 2
        upper = ((device >> bit) & 1) == 1
        lo, hi = mixture[:, :part], mixture[:, part:]
        sent = flipped(jnp.where(upper, lo, hi), own_rows << (high[-1] - bit))
        mixture = total(jnp.where(upper, hi, lo), swap(sent, bit))
        residual = jnp.where(upper, residual[:, part:], residual[:, :part])
    part = mixture.shape[1]
    moe = (residual.astype(jnp.float32) + mixture.astype(jnp.float32)).astype(jnp.bfloat16)
    widened = moe.astype(jnp.float32)
    gain = lax.dynamic_slice_in_dim(norm_gain, (device >> 3) * part, part, axis=0)
    squares = jnp.sum(widened * widened, axis=1, keepdims=True)
    scaled = (widened * gain).astype(jnp.bfloat16)
    slices = jnp.stack(slices)
    piece = slices.shape[1]
    latent = jnp.zeros((moe.shape[0], slices.shape[2]), jnp.float32)
    for p in range(8):
        flips = (device & 7) ^ p
        slot = ((flips >> 1) & 1) | ((flips >> 1) & 2) | ((flips & 1) << 2)
        weight = lax.dynamic_index_in_dim(slices, slot, axis=0, keepdims=False)
        latent += jnp.dot(
            scaled[:, p * piece : (p + 1) * piece], weight, preferred_element_type=jnp.float32
        )
    sums = jnp.concatenate([latent, squares], axis=1)
    for bit in high:
        rows = sums.shape[0] // 2
        sums = sums[:rows] + swap(sums[rows:], bit)
    for bit in high:
        rows = moe.shape[0] // 2
        upper = ((device >> bit) & 1) == 1
        kept, received = moe[:rows], swap(moe[rows:], bit)
        moe = jnp.where(
            upper,
            jnp.concatenate([received, kept], axis=1),
            jnp.concatenate([kept, received], axis=1),
        )
    return sums, moe


def per_device(
    hidden_in,
    expert_ids,
    gate_scores,
    w_gate,
    w_up,
    w_down,
    norm_gain,
    w_kv,
    queries,
    kv_cache,
    lengths,
):
    devices = lax.axis_size("dev")
    device = lax.axis_index("dev")
    shard_count = FF // w_gate.shape[1]
    expert = lax.axis_index("sec") * (devices // shard_count) + device // shard_count
    high = range(3, devices.bit_length() - 1)
    own_rows, width = hidden_in.shape

    picks = expert_ids.shape[1]
    half = width // 2

    cache = cache_part(queries, kv_cache, lengths)
    group, a_all, b_all, slices = gather_rows(hidden_in, expert_ids, gate_scores, high, w_kv)
    run = experts if len(high) == 1 else experts_wide
    partial = run(a_all, b_all, picks, expert, w_gate, w_up, w_down)
    partial, early = lax.optimization_barrier((partial, slices[:3]))
    a, b, late, (stats, combined) = scatter_rows(*partial, slices[3], cache)
    slices = (*early, late)
    slices += tuple(swap(v, 0) for v in slices)

    upper = (device >> high[-1]) & 1
    if len(high) == 1:
        place = jnp.stack([upper, device & 7])
        kept, other = jnp.where(upper == 1, b, a), jnp.where(upper == 1, a, b)
        received, extra = swap(other, high[0]), swap(kept[own_rows:], high[0])
        pair = jnp.concatenate(group, axis=1)
        sums, sums_out, mine = latent_parts(
            place, kept.astype(jnp.float32), received, pair, norm_gain, slices
        )
        sums_in = swap(sums_out, high[0])
        moe = moe_rows(place, mine, extra, other, pair)
    else:
        mixture = total(jnp.where(upper == 1, b, a), swap(flipped(jnp.where(upper == 1, a, b), own_rows), high[-1]))
        residual = jnp.where(upper == 1, group[1], group[0])
        sums, moe = latent_parts_wide(device, high, mixture, residual, own_rows, norm_gain, slices)
        sums = jnp.pad(sums, ((0, 0), (0, -sums.shape[1] % LANES)))
        sums_in = jnp.zeros_like(sums)
    new_latent, attended = finish(width, sums, sums_in, queries, stats, combined)
    return (moe, new_latent, attended)


def solution(mesh):
    in_specs = (
        P(("sec", "dev"), None),
        P(("sec", "dev"), None),
        P(("sec", "dev"), None),
        P(None, ("sec", "dev")),
        P(None, ("sec", "dev")),
        P(("sec", "dev"), None),
        P(),
        P("dev", None),
        P(("sec", "dev"), None, None),
        P(("sec", "dev"), None, None),
        P(("sec", "dev")),
    )
    out_specs = (P(("sec", "dev"), None), P(("sec", "dev"), None), P(("sec", "dev"), None, None))
    return jax.shard_map(
        per_device, mesh=mesh, in_specs=in_specs, out_specs=out_specs, check_vma=False
    )
```

time: 88.9 us -> 81 us (0.911)
  waiting for transfers between devices: 31.9 us -> 26.4 us
  local copies, waits for them, and re-layouts: 8.53 us -> 3.28 us
  matrix products: 2.42 us -> 0 us
  starting transfers between devices: 31.9 us -> 34.3 us
  Pallas kernels: 8.47 us -> 10.8 us
    ppermute x28 -> x26, waiting for transfers between devices: 26.5 us -> 21.8 us  [swap(): lax.ppermute(x, 'dev', [(i, i ^ 1 << bit) for i in range(lax.axis_size('d...]
    unnamed x35 -> x19, local copies, waits for them, and re-layouts: 6.26 us -> 1.6 us
    pallas_call x1 -> x4, Pallas kernels: 2.37 us -> 6.05 us  [the longest x1 1.91 us: latent_parts(): pl.pallas_call(latent_kernel, out_shape=(sums, sums, moe), in_specs=[pl.B...]
    ppermute x4, starting transfers between devices: 3.56 us -> 6.54 us  [swap(): lax.ppermute(x, 'sec', [(i, i ^ 1) for i in range(lax.axis_size('sec'))])]
    dot_general x3 -> x0, matrix products: 2.42 us -> none  [the longest x1 1.16 us: cache_part(): jnp.einsum('bhp,bpv->bhv', spread.astype(jnp.bfloat16), kv_cache[:, :, :K...]
    convert_element_type x9 -> x7, other arithmetic: 0.54 us -> 2.41 us  [the longest x6 2.38 us: total(): return wide_total(kept, received).astype(jnp.bfloat16)]
    select_n x2 -> x0, other arithmetic: 1.6 us -> none  [the longest x1 0.94 us: per_device(): sent = flipped(jnp.where(upper == 1, a, b), own_rows)]
    pallas_call x1, Pallas kernels: 6.09 us -> 4.75 us  [experts(): pl.pallas_call(lambda *refs: experts_kernel(picks, *refs), out_shape=(out...]
  transfers between devices with their start and end apart: 32 -> 30, of which waited for: 16 -> 15; matrix products, arithmetic and copies ran while one was open for 10% -> 8% of each run, Pallas kernels for 7% -> 12%
where the time goes in v2:
time: 81 us; the launch traced here: 80.6 us
  starting transfers between devices  34.3 us (42%)
  waiting for transfers between devices  26.4 us (33%)
  Pallas kernels  10.8 us (13%)
  other arithmetic  4.89 us (6%)
  local copies, waits for them, and re-layouts  3.28 us (4%)
  between operations  0.89 us (1%)
    ppermute x26, starting transfers between devices, swap(): lax.ppermute(x, 'dev', [(i, i ^ 1 << bit) for i in range(lax.axis_size('d...  27.8 us
    ppermute x26, waiting for transfers between devices, swap(): lax.ppermute(x, 'dev', [(i, i ^ 1 << bit) for i in range(lax.axis_size('d...  21.8 us
    ppermute x4, starting transfers between devices, swap(): lax.ppermute(x, 'sec', [(i, i ^ 1) for i in range(lax.axis_size('sec'))])  6.54 us
    pallas_call x1, Pallas kernels, experts(): pl.pallas_call(lambda *refs: experts_kernel(picks, *refs), out_shape=(out...  4.75 us
    ppermute x4, waiting for transfers between devices, swap(): lax.ppermute(x, 'sec', [(i, i ^ 1) for i in range(lax.axis_size('sec'))])  4.58 us
    convert_element_type x6, other arithmetic, total(): return wide_total(kept, received).astype(jnp.bfloat16)  2.38 us
    pallas_call x1, Pallas kernels, latent_parts(): pl.pallas_call(latent_kernel, out_shape=(sums, sums, moe), in_specs=[pl.B...  1.91 us
    pallas_call x1, Pallas kernels, cache_part(): pl.pallas_call(cache_kernel, out_shape=(jax.ShapeDtypeStruct((rows, heads...  1.71 us
  transfers between devices with their start and end apart: 30, of which 15 were waited for; matrix products, arithmetic and copies ran while one was open for 8% of the time, Pallas kernels for 12%

profile of v2, /device:TPU:0, one launch (start us, length us, event | category | flops | bytes accessed | tf_op | source)
XLA Modules:
  0.0 80.6 jit_solution(4116577562527972580)
XLA Ops:
  0.6 4.1 %collective-permute-start = (bf16[4,7168]{1,0:T(4,128)(2,1)}, bf16[4,7168]{1,0:T(4,128)(2,1)S(1)}, u32[]{:S(2)}, u32[]{:S(2)}) collective-permute-start(bf16[4,7168]{1,0:T(4,128)(2,1)} %param.11), channel_id=1, source_target_pairs={{0,8},{1,9},{2,10},{3,11},{4,12},{5,13},{6,14},{7,15},{8,0},{9,1},... | collective-permute-start | bytes 172040 | tf_op jit(solution)/shard_map/ppermute | solution.py:19
  4.7 0.7 convert_element_type.80
  5.4 0.1 copy.16
  5.5 0.8 copy.17
  6.3 0.1 fusion.4
  6.4 0.0 collective-permute-start.2
  6.4 1.8 %collective-permute-start.6 = (bf16[448,576]{1,0:T(8,128)(2,1)}, bf16[448,576]{1,0:T(8,128)(2,1)S(1)}, u32[]{:S(2)}, u32[]{:S(2)}) collective-permute-start(bf16[448,576]{1,0:T(8,128)(2,1)} %refs_0_), channel_id=1, source_target_pairs={{0,2},{1,3},{2,0},{3,1},{4,6},{5,7},{6,4},{7,5},{8,10},{9,11},{10,... | collective-permute-start | bytes 1548296 | tf_op jit(solution)/shard_map/ppermute | solution.py:19
  8.2 0.8 %fusion.1 = (bf16[8,3584]{1,0:T(8,128)(2,1)S(1)}, bf16[8,3584]{1,0:T(8,128)(2,1)S(1)}) fusion(bf16[4,7168]{1,0:T(4,128)(2,1)} %param.11, bf16[4,7168]{1,0:T(4,128)(2,1)S(1)} %collective-permute-done), kind=kLoop, calls=%fused_computation.18 | loop fusion | flops 229376 | bytes 229376 | tf_op jit(solution)/shard_map/concatenate | solution.py:120
  9.1 1.6 %collective-permute-start.1 = (bf16[8,3584]{1,0:T(8,128)(2,1)S(1)}, bf16[8,3584]{1,0:T(8,128)(2,1)S(1)}, u32[]{:S(2)}, u32[]{:S(2)}) collective-permute-start(bf16[8,3584]{1,0:T(8,128)(2,1)S(1)} %get-tuple-element.69), channel_id=1, source_target_pairs={{0,4},{1,5},{2,6},{3,7},{4,0},{5,1},{6,2},{7,3},{8,12},{9,13},{10,... | collective-permute-start | bytes 172040 | tf_op jit(solution)/shard_map/ppermute | solution.py:19
  10.7 0.1 collective-permute-done.2
  10.8 1.6 %collective-permute-start.3 = (bf16[8,3712]{1,0:T(8,128)(2,1)S(1)}, bf16[8,3712]{1,0:T(8,128)(2,1)S(1)}, u32[]{:S(2)}, u32[]{:S(2)}) collective-permute-start(bf16[8,3712]{1,0:T(8,128)(2,1)S(1)} %maximum_maximum_fusion), channel_id=1, source_target_pairs={{0,4},{1,5},{2,6},{3,7},{4,0},{5,1},{6,2},{7,3},{8,12},{9,13},{10,... | collective-permute-start | bytes 178184 | tf_op jit(solution)/shard_map/ppermute | solution.py:19
  12.5 0.9 %collective-permute-done.1 = bf16[8,3584]{1,0:T(8,128)(2,1)S(1)} collective-permute-done((bf16[8,3584]{1,0:T(8,128)(2,1)S(1)}, bf16[8,3584]{1,0:T(8,128)(2,1)S(1)}, u32[]{:S(2)}, u32[]{:S(2)}) %collective-permute-start.1) | collective-permute-done | bytes 57376 | tf_op jit(solution)/shard_map/ppermute | solution.py:19
  13.4 1.7 %collective-permute-done.3 = bf16[8,3712]{1,0:T(8,128)(2,1)S(1)} collective-permute-done((bf16[8,3712]{1,0:T(8,128)(2,1)S(1)}, bf16[8,3712]{1,0:T(8,128)(2,1)S(1)}, u32[]{:S(2)}, u32[]{:S(2)}) %collective-permute-start.3) | collective-permute-done | bytes 59424 | tf_op jit(solution)/shard_map/ppermute | solution.py:19
  15.1 1.6 %collective-permute-start.4 = (bf16[16,3584]{1,0:T(8,128)(2,1)S(1)}, bf16[16,3584]{1,0:T(8,128)(2,1)S(1)}, u32[]{:S(2)}, u32[]{:S(2)}) collective-permute-start(bf16[16,3584]{1,0:T(8,128)(2,1)S(1)} %pad_maximum_fusion.3), channel_id=1, source_target_pairs={{0,2},{1,3},{2,0},{3,1},{4,6},{5,7},{6,4},{7,5},{8,10},{9,11},{10,... | collective-permute-start | bytes 344072 | tf_op jit(solution)/shard_map/ppermute | solution.py:19
  16.7 1.5 %collective-permute-start.9 = (bf16[16,3712]{1,0:T(8,128)(2,1)S(1)}, bf16[16,3712]{1,0:T(8,128)(2,1)S(1)}, u32[]{:S(2)}, u32[]{:S(2)}) collective-permute-start(bf16[16,3712]{1,0:T(8,128)(2,1)S(1)} %pad_maximum_fusion.2), channel_id=1, source_target_pairs={{0,16},{16,0},{1,17},{17,1},{2,18},{18,2},{3,19},{19,3},{4,20},{20... | collective-permute-start | bytes 356360 | tf_op jit(solution)/shard_map/ppermute | solution.py:18
  18.2 1.6 %collective-permute-start.13 = (bf16[448,576]{1,0:T(8,128)(2,1)}, bf16[448,576]{1,0:T(8,128)(2,1)S(1)}, u32[]{:S(2)}, u32[]{:S(2)}) collective-permute-start(bf16[448,576]{1,0:T(8,128)(2,1)} %refs_0_), channel_id=1, source_target_pairs={{0,4},{1,5},{2,6},{3,7},{4,0},{5,1},{6,2},{7,3},{8,12},{9,13},{10,... | collective-permute-start | bytes 1548296 | tf_op jit(solution)/shard_map/ppermute | solution.py:19
  19.9 1.7 %collective-permute-done.9 = bf16[16,3712]{1,0:T(8,128)(2,1)S(1)} collective-permute-done((bf16[16,3712]{1,0:T(8,128)(2,1)S(1)}, bf16[16,3712]{1,0:T(8,128)(2,1)S(1)}, u32[]{:S(2)}, u32[]{:S(2)}) %collective-permute-start.9) | collective-permute-done | bytes 118816 | tf_op jit(solution)/shard_map/ppermute | solution.py:18
  21.6 0.6 collective-permute-start.10
  22.1 2.9 %collective-permute-done.4 = bf16[16,3584]{1,0:T(8,128)(2,1)S(1)} collective-permute-done((bf16[16,3584]{1,0:T(8,128)(2,1)S(1)}, bf16[16,3584]{1,0:T(8,128)(2,1)S(1)}, u32[]{:S(2)}, u32[]{:S(2)}) %collective-permute-start.4) | collective-permute-done | bytes 114720 | tf_op jit(solution)/shard_map/ppermute | solution.py:19
  25.0 1.8 %collective-permute-start.5 = (bf16[32,3584]{1,0:T(8,128)(2,1)S(1)}, bf16[32,3584]{1,0:T(8,128)(2,1)S(1)}, u32[]{:S(2)}, u32[]{:S(2)}) collective-permute-start(bf16[32,3584]{1,0:T(8,128)(2,1)S(1)} %constant_dynamic-update-slice_fusion.refs_1_), channel_id=1, source_target_pairs={{0,16},{16,0},{1,17},{17,1},{2,18},{18,2},{3,19},{19,3},{4,20},{20... | collective-permute-start | bytes 688136 | tf_op jit(solution)/shard_map/ppermute | solution.py:18
  26.9 1.8 %collective-permute-done.10.refs_6_ = bf16[32,3712]{1,0:T(8,128)(2,1)S(1)} collective-permute-done((bf16[32,3712]{1,0:T(8,128)(2,1)S(1)}, bf16[32,3712]{1,0:T(8,128)(2,1)S(1)}, u32[]{:S(2)}, u32[]{:S(2)}) %collective-permute-start.10) | collective-permute-done | bytes 237600 | tf_op jit(solution)/shard_map/ppermute | solution.py:19
  28.6 2.5 %collective-permute-done.5.refs_2_ = bf16[32,3584]{1,0:T(8,128)(2,1)S(1)} collective-permute-done((bf16[32,3584]{1,0:T(8,128)(2,1)S(1)}, bf16[32,3584]{1,0:T(8,128)(2,1)S(1)}, u32[]{:S(2)}, u32[]{:S(2)}) %collective-permute-start.5) | collective-permute-done | bytes 229408 | tf_op jit(solution)/shard_map/ppermute | solution.py:18
  31.1 0.5 collective-permute-start.8
  31.6 1.0 %collective-permute-done.7.refs_3_ = bf16[32,3584]{1,0:T(8,128)(2,1)S(1)} collective-permute-done((bf16[32,3584]{1,0:T(8,128)(2,1)S(1)}, bf16[32,3584]{1,0:T(8,128)(2,1)S(1)}, u32[]{:S(2)}, u32[]{:S(2)}) %collective-permute-start.7) | collective-permute-done | bytes 229408 | tf_op jit(solution)/shard_map/ppermute | solution.py:19
  32.6 0.3 collective-permute-done.8.refs_4_
  32.9 4.7 %experts.1 = (bf16[64,3584]{1,0:T(8,128)(2,1)S(1)}, bf16[64,3584]{1,0:T(8,128)(2,1)S(1)}, bf16[64,3584]{1,0:T(8,128)(2,1)S(1)}, bf16[64,3584]{1,0:T(8,128)(2,1)S(1)}) custom-call(s32[1]{0:T(128)} %bitcast.2.refs_0_, bf16[32,3584]{1,0:T(8,128)(2,1)S(1)} %constant_dynamic-update-slice_fusion.refs_1_, bf16[32,3584]{1,0:T(8,128)(2,1)S(1)} %collective-permute-done.5.refs_2_, ...), custom_call_target="tpu_custom_call" | custom-call | tf_op jit(solution)/shard_map/experts/pallas_call | solution.py:198
  37.7 0.0 copy-start.1
  37.7 0.0 copy-start.3
  37.7 0.2 collective-permute-start.14
  38.0 1.9 %collective-permute-start.18 = (bf16[448,576]{1,0:T(8,128)(2,1)S(1)}, bf16[448,576]{1,0:T(8,128)(2,1)}, u32[]{:S(2)}, u32[]{:S(2)}) collective-permute-start(bf16[448,576]{1,0:T(8,128)(2,1)S(1)} %collective-permute-done.6.refs_1_), channel_id=1, source_target_pairs={{0,4},{1,5},{2,6},{3,7},{4,0},{5,1},{6,2},{7,3},{8,12},{9,13},{10,... | collective-permute-start | bytes 1548296 | tf_op jit(solution)/shard_map/ppermute | solution.py:19
  39.8 0.0 collective-permute-start.15
  39.9 0.1 add_convert_fusion.1
  40.1 0.7 pad_maximum_fusion
  40.8 1.5 %collective-permute-start.17 = (bf16[32,3584]{1,0:T(8,128)(2,1)}, bf16[32,3584]{1,0:T(8,128)(2,1)}, u32[]{:S(2)}, u32[]{:S(2)}) collective-permute-start(bf16[32,3584]{1,0:T(8,128)(2,1)} %pad_maximum_fusion), channel_id=1, source_target_pairs={{0,2},{1,3},{2,0},{3,1},{4,6},{5,7},{6,4},{7,5},{8,10},{9,11},{10,... | collective-permute-start | bytes 688136 | tf_op jit(solution)/shard_map/ppermute | solution.py:19
  42.3 0.1 add_convert_fusion
  42.4 0.8 copy-done.4
  43.2 0.7 slice.75
  43.9 1.5 %collective-permute-start.16 = (bf16[32,3584]{1,0:T(8,128)(2,1)}, bf16[32,3584]{1,0:T(8,128)(2,1)}, u32[]{:S(2)}, u32[]{:S(2)}) collective-permute-start(bf16[32,3584]{1,0:T(8,128)(2,1)} %slice.75), channel_id=1, source_target_pairs={{0,16},{16,0},{1,17},{17,1},{2,18},{18,2},{3,19},{19,3},{4,20},{20... | collective-permute-start | bytes 688136 | tf_op jit(solution)/shard_map/ppermute | solution.py:18
  45.4 0.8 reshape.13.gain_ref
  46.2 1.7 %cache_part.1 = (f32[4,64,128]{2,1,0:T(8,128)S(1)}, f32[4,64,512]{2,1,0:T(8,128)S(1)}) custom-call(s32[4]{0:T(128)S(1)} %copy-done.3, bf16[4,64,576]{2,1,0:T(8,128)(2,1)S(1)} %copy-done, bf16[4,576,256]{2,1,0:T(8,128)(2,1)S(1)} %bitcast.4), custom_call_target="tpu_custom_call" | custom-call | flops 150994944 | bytes 1179648 | tf_op jit(solution)/shard_map/cache_part/pallas_call | solution.py:57
  47.9 5.5 %collective-permute-done.18.refs_3_ = bf16[448,576]{1,0:T(8,128)(2,1)} collective-permute-done((bf16[448,576]{1,0:T(8,128)(2,1)S(1)}, bf16[448,576]{1,0:T(8,128)(2,1)}, u32[]{:S(2)}, u32[]{:S(2)}) %collective-permute-start.18) | collective-permute-done | bytes 516128 | tf_op jit(solution)/shard_map/ppermute | solution.py:19
  53.4 1.0 %add_convert_fusion.3 = bf16[32,3584]{1,0:T(8,128)(2,1)S(1)} fusion(bf16[32,3584]{1,0:T(8,128)(2,1)} %collective-permute-done.17, bf16[16,3584]{1,0:T(8,128)(2,1)S(1)} %get-tuple-element.66, bf16[16,3584]{1,0:T(8,128)(2,1)S(1)} %get-tuple-element.63), kind=kLoop, calls=%fused_computation.3 | loop fusion | flops 802816 | bytes 688128 | tf_op jit(solution)/shard_map/convert_element_type | solution.py:27
  54.4 1.7 %collective-permute-start.19 = (bf16[16,3584]{1,0:T(8,128)(2,1)S(1)}, bf16[16,3584]{1,0:T(8,128)(2,1)S(1)}, u32[]{:S(2)}, u32[]{:S(2)}) collective-permute-start(bf16[16,3584]{1,0:T(8,128)(2,1)S(1)} %slice.79), channel_id=1, source_target_pairs={{0,16},{16,0},{1,17},{17,1},{2,18},{18,2},{3,19},{19,3},{4,20},{20... | collective-permute-start | bytes 344072 | tf_op jit(solution)/shard_map/ppermute | solution.py:18
  56.2 1.1 %add_convert_fusion.2 = bf16[32,3584]{1,0:T(8,128)(2,1)S(1)} fusion(bf16[32,3584]{1,0:T(8,128)(2,1)} %collective-permute-done.16, bf16[64,3584]{1,0:T(8,128)(2,1)} %copy-done.4), kind=kLoop, calls=%fused_computation.2 | loop fusion | flops 458752 | bytes 688128 | tf_op jit(solution)/shard_map/convert_element_type | solution.py:27
  57.3 1.6 %collective-permute-start.21 = (bf16[16,3584]{1,0:T(8,128)(2,1)S(1)}, bf16[16,3584]{1,0:T(8,128)(2,1)S(1)}, u32[]{:S(2)}, u32[]{:S(2)}) collective-permute-start(bf16[16,3584]{1,0:T(8,128)(2,1)S(1)} %slice.84), channel_id=1, source_target_pairs={{0,2},{1,3},{2,0},{3,1},{4,6},{5,7},{6,4},{7,5},{8,10},{9,11},{10,... | collective-permute-start | bytes 344072 | tf_op jit(solution)/shard_map/ppermute | solution.py:19
  58.9 0.4 collective-permute-done.19
  59.3 1.8 %collective-permute-start.20 = (bf16[8,3584]{1,0:T(8,128)(2,1)S(1)}, bf16[8,3584]{1,0:T(8,128)(2,1)S(1)}, u32[]{:S(2)}, u32[]{:S(2)}) collective-permute-start(bf16[8,3584]{1,0:T(8,128)(2,1)S(1)} %slice.81), channel_id=1, source_target_pairs={{0,4},{1,5},{2,6},{3,7},{4,0},{5,1},{6,2},{7,3},{8,12},{9,13},{10,... | collective-permute-start | bytes 172040 | tf_op jit(solution)/shard_map/ppermute | solution.py:19
  61.1 1.0 %collective-permute-done.21 = bf16[16,3584]{1,0:T(8,128)(2,1)S(1)} collective-permute-done((bf16[16,3584]{1,0:T(8,128)(2,1)S(1)}, bf16[16,3584]{1,0:T(8,128)(2,1)S(1)}, u32[]{:S(2)}, u32[]{:S(2)}) %collective-permute-start.21) | collective-permute-done | bytes 114720 | tf_op jit(solution)/shard_map/ppermute | solution.py:19
  62.2 1.6 %collective-permute-start.22 = (bf16[8,3584]{1,0:T(8,128)(2,1)S(1)}, bf16[8,3584]{1,0:T(8,128)(2,1)S(1)}, u32[]{:S(2)}, u32[]{:S(2)}) collective-permute-start(bf16[8,3584]{1,0:T(8,128)(2,1)S(1)} %slice.86), channel_id=1, source_target_pairs={{0,4},{1,5},{2,6},{3,7},{4,0},{5,1},{6,2},{7,3},{8,12},{9,13},{10,... | collective-permute-start | bytes 172040 | tf_op jit(solution)/shard_map/ppermute | solution.py:19
  63.8 0.1 pad_add_fusion.place_ref
  63.9 0.0 collective-permute-start.24
  63.9 0.5 collective-permute-start.25
  64.4 0.1 collective-permute-start.26
  64.5 0.4 collective-permute-start.27
  64.9 1.5 %collective-permute-done.22 = bf16[8,3584]{1,0:T(8,128)(2,1)S(1)} collective-permute-done((bf16[8,3584]{1,0:T(8,128)(2,1)S(1)}, bf16[8,3584]{1,0:T(8,128)(2,1)S(1)}, u32[]{:S(2)}, u32[]{:S(2)}) %collective-permute-start.22) | collective-permute-done | bytes 57376 | tf_op jit(solution)/shard_map/ppermute | solution.py:19
  66.5 2.7 %collective-permute-start.23 = (bf16[8,3584]{1,0:T(8,128)(2,1)S(1)}, bf16[8,3584]{1,0:T(8,128)(2,1)S(1)}, u32[]{:S(2)}, u32[]{:S(2)}) collective-permute-start(bf16[8,3584]{1,0:T(8,128)(2,1)S(1)} %get-tuple-element.67.sum_ref), channel_id=1, source_target_pairs={{0,8},{1,9},{2,10},{3,11},{4,12},{5,13},{6,14},{7,15},{8,0},{9,1},... | collective-permute-start | bytes 172040 | tf_op jit(solution)/shard_map/ppermute | solution.py:19
  69.2 0.4 collective-permute-start.28
  69.6 0.1 pad_maximum_fusion.1.group_ref
  69.6 3.2 %collective-permute-done.23.in_ref = bf16[8,3584]{1,0:T(8,128)(2,1)S(1)} collective-permute-done((bf16[8,3584]{1,0:T(8,128)(2,1)S(1)}, bf16[8,3584]{1,0:T(8,128)(2,1)S(1)}, u32[]{:S(2)}, u32[]{:S(2)}) %collective-permute-start.23) | collective-permute-done | bytes 57376 | tf_op jit(solution)/shard_map/ppermute | solution.py:19
  72.8 1.9 %latent_parts.1 = (f32[4,640]{1,0:T(4,128)S(1)}, f32[4,640]{1,0:T(4,128)S(1)}, bf16[4,3584]{1,0:T(4,128)(2,1)S(1)}) custom-call(s32[2]{0:T(128)S(1)} %pad_add_fusion.place_ref, f32[8,3584]{1,0:T(8,128)S(1)} %get-tuple-element.61.kept_ref, bf16[8,3584]{1,0:T(8,128)(2,1)S(1)} %collective-permute-done.23.in_ref, ...), custom_call_target="tpu_custom_call" | custom-call | tf_op jit(solution)/shard_map/latent_parts/pallas_call | solution.py:288
  74.8 1.5 %collective-permute-start.29 = (f32[4,640]{1,0:T(4,128)S(1)}, f32[4,640]{1,0:T(4,128)S(1)}, u32[]{:S(2)}, u32[]{:S(2)}) collective-permute-start(f32[4,640]{1,0:T(4,128)S(1)} %get-tuple-element.56), channel_id=1, source_target_pairs={{0,8},{1,9},{2,10},{3,11},{4,12},{5,13},{6,14},{7,15},{8,0},{9,1},... | collective-permute-start | bytes 30728 | tf_op jit(solution)/shard_map/ppermute | solution.py:19
  76.2 1.2 %moe_rows.1 = bf16[4,7168]{1,0:T(4,128)(2,1)} custom-call(s32[2]{0:T(128)S(1)} %pad_add_fusion.place_ref, bf16[4,3584]{1,0:T(4,128)(2,1)S(1)} %get-tuple-element.54.mine_ref, bf16[4,3584]{1,0:T(4,128)(2,1)S(1)} %collective-permute-done.28.extra_ref, bf16[8,3584]{1,0:T(8,128)(2,1)S(1)} %get-tuple-element.67.sum_ref, ...), custom_call_target="tpu_custom_call" | custom-call | tf_op jit(solution)/shard_map/moe_rows/pallas_call | solution.py:313
  77.4 1.9 %collective-permute-done.29.refs_1_ = f32[4,640]{1,0:T(4,128)S(1)} collective-permute-done((f32[4,640]{1,0:T(4,128)S(1)}, f32[4,640]{1,0:T(4,128)S(1)}, u32[]{:S(2)}, u32[]{:S(2)}) %collective-permute-start.29) | collective-permute-done | bytes 10272 | tf_op jit(solution)/shard_map/ppermute | solution.py:19
  79.4 1.2 %finish.1 = (bf16[4,576]{1,0:T(4,128)(2,1)}, bf16[4,64,512]{2,1,0:T(8,128)(2,1)}) custom-call(f32[4,640]{1,0:T(4,128)S(1)} %get-tuple-element.55.refs_0_, f32[4,640]{1,0:T(4,128)S(1)} %collective-permute-done.29.refs_1_, bf16[4,64,576]{2,1,0:T(8,128)(2,1)S(1)} %copy-done, f32[4,64,128]{2,1,0:T(8,128)S(1)} %get-tuple-element.57.refs_3_, ...), custom_call_target="tpu_custom_call" | custom-call | tf_op jit(solution)/shard_map/finish/pallas_call | solution.py:98
  (47 shorter events, 0.3 us)
Async XLA Ops:
  0.6 7.6 %collective-permute-start = (bf16[4,7168]{1,0:T(4,128)(2,1)}, bf16[4,7168]{1,0:T(4,128)(2,1)S(1)}, u32[]{:S(2)}, u32[]{:S(2)}) collective-permute-start(bf16[4,7168]{1,0:T(4,128)(2,1)} %param.11), channel_id=1, source_target_pairs={{0,8},{1,9},{2,10},{3,11},{4,12},{5,13},{6,14},{7,15},{8,0},{9,1},... | collective-permute-start | bytes 172040 | tf_op jit(solution)/shard_map/ppermute | solution.py:19
  6.4 4.5 %collective-permute-start.2 = (bf16[4,128]{1,0:T(4,128)(2,1)S(1)}, bf16[4,128]{1,0:T(4,128)(2,1)S(1)}, u32[]{:S(2)}, u32[]{:S(2)}) collective-permute-start(bf16[4,128]{1,0:T(4,128)(2,1)S(1)} %fusion.4), channel_id=1, source_target_pairs={{0,8},{1,9},{2,10},{3,11},{4,12},{5,13},{6,14},{7,15},{8,0},{9,1},... | collective-permute-start | bytes 3080 | tf_op jit(solution)/shard_map/ppermute | solution.py:19
  6.4 24.7 %collective-permute-start.6 = (bf16[448,576]{1,0:T(8,128)(2,1)}, bf16[448,576]{1,0:T(8,128)(2,1)S(1)}, u32[]{:S(2)}, u32[]{:S(2)}) collective-permute-start(bf16[448,576]{1,0:T(8,128)(2,1)} %refs_0_), channel_id=1, source_target_pairs={{0,2},{1,3},{2,0},{3,1},{4,6},{5,7},{6,4},{7,5},{8,10},{9,11},{10,... | collective-permute-start | bytes 1548296 | tf_op jit(solution)/shard_map/ppermute | solution.py:19
  8.2 10.0 %copy-start.6 = (bf16[4,7168]{1,0:T(4,128)(2,1)}, bf16[4,7168]{1,0:T(4,128)(2,1)S(1)}, u32[]{:S(2)}) copy-start(bf16[4,7168]{1,0:T(4,128)(2,1)S(1)} %collective-permute-done) | copy-start | bytes 172036
  9.1 4.3 %collective-permute-start.1 = (bf16[8,3584]{1,0:T(8,128)(2,1)S(1)}, bf16[8,3584]{1,0:T(8,128)(2,1)S(1)}, u32[]{:S(2)}, u32[]{:S(2)}) collective-permute-start(bf16[8,3584]{1,0:T(8,128)(2,1)S(1)} %get-tuple-element.69), channel_id=1, source_target_pairs={{0,4},{1,5},{2,6},{3,7},{4,0},{5,1},{6,2},{7,3},{8,12},{9,13},{10,... | collective-permute-start | bytes 172040 | tf_op jit(solution)/shard_map/ppermute | solution.py:19
  10.8 4.3 %collective-permute-start.3 = (bf16[8,3712]{1,0:T(8,128)(2,1)S(1)}, bf16[8,3712]{1,0:T(8,128)(2,1)S(1)}, u32[]{:S(2)}, u32[]{:S(2)}) collective-permute-start(bf16[8,3712]{1,0:T(8,128)(2,1)S(1)} %maximum_maximum_fusion), channel_id=1, source_target_pairs={{0,4},{1,5},{2,6},{3,7},{4,0},{5,1},{6,2},{7,3},{8,12},{9,13},{10,... | collective-permute-start | bytes 178184 | tf_op jit(solution)/shard_map/ppermute | solution.py:19
  15.1 9.9 %collective-permute-start.4 = (bf16[16,3584]{1,0:T(8,128)(2,1)S(1)}, bf16[16,3584]{1,0:T(8,128)(2,1)S(1)}, u32[]{:S(2)}, u32[]{:S(2)}) collective-permute-start(bf16[16,3584]{1,0:T(8,128)(2,1)S(1)} %pad_maximum_fusion.3), channel_id=1, source_target_pairs={{0,2},{1,3},{2,0},{3,1},{4,6},{5,7},{6,4},{7,5},{8,10},{9,11},{10,... | collective-permute-start | bytes 344072 | tf_op jit(solution)/shard_map/ppermute | solution.py:19
  16.7 4.8 %collective-permute-start.9 = (bf16[16,3712]{1,0:T(8,128)(2,1)S(1)}, bf16[16,3712]{1,0:T(8,128)(2,1)S(1)}, u32[]{:S(2)}, u32[]{:S(2)}) collective-permute-start(bf16[16,3712]{1,0:T(8,128)(2,1)S(1)} %pad_maximum_fusion.2), channel_id=1, source_target_pairs={{0,16},{16,0},{1,17},{17,1},{2,18},{18,2},{3,19},{19,3},{4,20},{20... | collective-permute-start | bytes 356360 | tf_op jit(solution)/shard_map/ppermute | solution.py:18
  18.2 19.5 %collective-permute-start.13 = (bf16[448,576]{1,0:T(8,128)(2,1)}, bf16[448,576]{1,0:T(8,128)(2,1)S(1)}, u32[]{:S(2)}, u32[]{:S(2)}) collective-permute-start(bf16[448,576]{1,0:T(8,128)(2,1)} %refs_0_), channel_id=1, source_target_pairs={{0,4},{1,5},{2,6},{3,7},{4,0},{5,1},{6,2},{7,3},{8,12},{9,13},{10,... | collective-permute-start | bytes 1548296 | tf_op jit(solution)/shard_map/ppermute | solution.py:19
  21.6 7.1 %collective-permute-start.10 = (bf16[32,3712]{1,0:T(8,128)(2,1)S(1)}, bf16[32,3712]{1,0:T(8,128)(2,1)S(1)}, u32[]{:S(2)}, u32[]{:S(2)}) collective-permute-start(bf16[32,3712]{1,0:T(8,128)(2,1)S(1)} %constant_dynamic-update-slice_fusion.2.refs_5_), channel_id=1, source_target_pairs={{0,2},{1,3},{2,0},{3,1},{4,6},{5,7},{6,4},{7,5},{8,10},{9,11},{10,... | collective-permute-start | bytes 712712 | tf_op jit(solution)/shard_map/ppermute | solution.py:19
  25.0 6.1 %collective-permute-start.5 = (bf16[32,3584]{1,0:T(8,128)(2,1)S(1)}, bf16[32,3584]{1,0:T(8,128)(2,1)S(1)}, u32[]{:S(2)}, u32[]{:S(2)}) collective-permute-start(bf16[32,3584]{1,0:T(8,128)(2,1)S(1)} %constant_dynamic-update-slice_fusion.refs_1_), channel_id=1, source_target_pairs={{0,16},{16,0},{1,17},{17,1},{2,18},{18,2},{3,19},{19,3},{4,20},{20... | collective-permute-start | bytes 688136 | tf_op jit(solution)/shard_map/ppermute | solution.py:18
  26.8 4.8 %collective-permute-start.11 = (bf16[32,3712]{1,0:T(8,128)(2,1)S(1)}, bf16[32,3712]{1,0:T(8,128)(2,1)S(1)}, u32[]{:S(2)}, u32[]{:S(2)}) collective-permute-start(bf16[32,3712]{1,0:T(8,128)(2,1)S(1)} %constant_dynamic-update-slice_fusion.2.refs_5_), channel_id=1, source_target_pairs={{0,1},{1,0},{2,3},{3,2},{4,5},{5,4},{6,7},{7,6},{8,9},{9,8},{10,11... | collective-permute-start | bytes 712712 | tf_op jit(solution)/shard_map/ppermute | solution.py:19
  28.6 3.0 %collective-permute-start.12 = (bf16[32,3712]{1,0:T(8,128)(2,1)S(1)}, bf16[32,3712]{1,0:T(8,128)(2,1)S(1)}, u32[]{:S(2)}, u32[]{:S(2)}) collective-permute-start(bf16[32,3712]{1,0:T(8,128)(2,1)S(1)} %collective-permute-done.10.refs_6_), channel_id=1, source_target_pairs={{0,1},{1,0},{2,3},{3,2},{4,5},{5,4},{6,7},{7,6},{8,9},{9,8},{10,11... | collective-permute-start | bytes 712712 | tf_op jit(solution)/shard_map/ppermute | solution.py:19
  31.1 1.5 %collective-permute-start.7 = (bf16[32,3584]{1,0:T(8,128)(2,1)S(1)}, bf16[32,3584]{1,0:T(8,128)(2,1)S(1)}, u32[]{:S(2)}, u32[]{:S(2)}) collective-permute-start(bf16[32,3584]{1,0:T(8,128)(2,1)S(1)} %constant_dynamic-update-slice_fusion.refs_1_), channel_id=1, source_target_pairs={{0,1},{1,0},{2,3},{3,2},{4,5},{5,4},{6,7},{7,6},{8,9},{9,8},{10,11... | collective-permute-start | bytes 688136 | tf_op jit(solution)/shard_map/ppermute | solution.py:19
  31.1 1.8 %collective-permute-start.8 = (bf16[32,3584]{1,0:T(8,128)(2,1)S(1)}, bf16[32,3584]{1,0:T(8,128)(2,1)S(1)}, u32[]{:S(2)}, u32[]{:S(2)}) collective-permute-start(bf16[32,3584]{1,0:T(8,128)(2,1)S(1)} %collective-permute-done.5.refs_2_), channel_id=1, source_target_pairs={{0,1},{1,0},{2,3},{3,2},{4,5},{5,4},{6,7},{7,6},{8,9},{9,8},{10,11... | collective-permute-start | bytes 688136 | tf_op jit(solution)/shard_map/ppermute | solution.py:19
  37.7 8.5 %copy-start = (bf16[4,64,576]{2,1,0:T(8,128)(2,1)S(1)}, bf16[4,64,576]{2,1,0:T(8,128)(2,1)}, u32[]{:S(2)}) copy-start(bf16[4,64,576]{2,1,0:T(8,128)(2,1)} %refs_2_.1) | copy-start | bytes 884740
  37.7 8.5 %copy-start.1 = (bf16[4,256,576]{1,2,0:T(8,128)(2,1)S(1)}, bf16[4,256,576]{1,2,0:T(8,128)(2,1)}, u32[]{:S(2)}) copy-start(bf16[4,256,576]{1,2,0:T(8,128)(2,1)} %param.20) | copy-start | bytes 3538948
  37.7 8.5 %copy-start.3 = (s32[4]{0:T(128)S(1)}, s32[4]{0:T(128)}, u32[]{:S(2)}) copy-start(s32[4]{0:T(128)} %lengths_ref.1) | copy-start | bytes 52
  37.7 2.1 %collective-permute-start.14 = (bf16[64,3584]{1,0:T(8,128)(2,1)S(1)}, bf16[64,3584]{1,0:T(8,128)(2,1)S(1)}, u32[]{:S(2)}, u32[]{:S(2)}) collective-permute-start(bf16[64,3584]{1,0:T(8,128)(2,1)S(1)} %get-tuple-element.43), channel_id=1, source_target_pairs={{0,1},{1,0},{2,3},{3,2},{4,5},{5,4},{6,7},{7,6},{8,9},{9,8},{10,11... | collective-permute-start | bytes 1376264 | tf_op jit(solution)/shard_map/ppermute | solution.py:19
  38.0 15.4 %collective-permute-start.18 = (bf16[448,576]{1,0:T(8,128)(2,1)S(1)}, bf16[448,576]{1,0:T(8,128)(2,1)}, u32[]{:S(2)}, u32[]{:S(2)}) collective-permute-start(bf16[448,576]{1,0:T(8,128)(2,1)S(1)} %collective-permute-done.6.refs_1_), channel_id=1, source_target_pairs={{0,4},{1,5},{2,6},{3,7},{4,0},{5,1},{6,2},{7,3},{8,12},{9,13},{10,... | collective-permute-start | bytes 1548296 | tf_op jit(solution)/shard_map/ppermute | solution.py:19
  39.8 2.5 %collective-permute-start.15 = (bf16[64,3584]{1,0:T(8,128)(2,1)S(1)}, bf16[64,3584]{1,0:T(8,128)(2,1)S(1)}, u32[]{:S(2)}, u32[]{:S(2)}) collective-permute-start(bf16[64,3584]{1,0:T(8,128)(2,1)S(1)} %get-tuple-element.45), channel_id=1, source_target_pairs={{0,1},{1,0},{2,3},{3,2},{4,5},{5,4},{6,7},{7,6},{8,9},{9,8},{10,11... | collective-permute-start | bytes 1376264 | tf_op jit(solution)/shard_map/ppermute | solution.py:19
  40.0 23.9 %copy-start.2 = (bf16[448,576]{1,0:T(8,128)(2,1)S(1)}, bf16[448,576]{1,0:T(8,128)(2,1)}, u32[]{:S(2)}) copy-start(bf16[448,576]{1,0:T(8,128)(2,1)} %refs_0_) | copy-start | bytes 1548292
  40.0 29.5 %copy-start.5 = (bf16[4,7168]{1,0:T(4,128)(2,1)S(1)}, bf16[4,7168]{1,0:T(4,128)(2,1)}, u32[]{:S(2)}) copy-start(bf16[4,7168]{1,0:T(4,128)(2,1)} %param.11) | copy-start | bytes 172036
  40.8 12.6 %collective-permute-start.17 = (bf16[32,3584]{1,0:T(8,128)(2,1)}, bf16[32,3584]{1,0:T(8,128)(2,1)}, u32[]{:S(2)}, u32[]{:S(2)}) collective-permute-start(bf16[32,3584]{1,0:T(8,128)(2,1)} %pad_maximum_fusion), channel_id=1, source_target_pairs={{0,2},{1,3},{2,0},{3,1},{4,6},{5,7},{6,4},{7,5},{8,10},{9,11},{10,... | collective-permute-start | bytes 688136 | tf_op jit(solution)/shard_map/ppermute | solution.py:19
  42.4 0.8 copy-start.4
  43.9 9.5 %collective-permute-start.16 = (bf16[32,3584]{1,0:T(8,128)(2,1)}, bf16[32,3584]{1,0:T(8,128)(2,1)}, u32[]{:S(2)}, u32[]{:S(2)}) collective-permute-start(bf16[32,3584]{1,0:T(8,128)(2,1)} %slice.75), channel_id=1, source_target_pairs={{0,16},{16,0},{1,17},{17,1},{2,18},{18,2},{3,19},{19,3},{4,20},{20... | collective-permute-start | bytes 688136 | tf_op jit(solution)/shard_map/ppermute | solution.py:18
  46.2 23.4 %copy-start.7 = (bf16[4,7168]{1,0:T(4,128)(2,1)S(1)}, bf16[4,7168]{1,0:T(4,128)(2,1)}, u32[]{:S(2)}) copy-start(bf16[4,7168]{1,0:T(4,128)(2,1)} %copy-done.6) | copy-start | bytes 172036
  54.4 4.9 %collective-permute-start.19 = (bf16[16,3584]{1,0:T(8,128)(2,1)S(1)}, bf16[16,3584]{1,0:T(8,128)(2,1)S(1)}, u32[]{:S(2)}, u32[]{:S(2)}) collective-permute-start(bf16[16,3584]{1,0:T(8,128)(2,1)S(1)} %slice.79), channel_id=1, source_target_pairs={{0,16},{16,0},{1,17},{17,1},{2,18},{18,2},{3,19},{19,3},{4,20},{20... | collective-permute-start | bytes 344072 | tf_op jit(solution)/shard_map/ppermute | solution.py:18
  57.3 4.9 %collective-permute-start.21 = (bf16[16,3584]{1,0:T(8,128)(2,1)S(1)}, bf16[16,3584]{1,0:T(8,128)(2,1)S(1)}, u32[]{:S(2)}, u32[]{:S(2)}) collective-permute-start(bf16[16,3584]{1,0:T(8,128)(2,1)S(1)} %slice.84), channel_id=1, source_target_pairs={{0,2},{1,3},{2,0},{3,1},{4,6},{5,7},{6,4},{7,5},{8,10},{9,11},{10,... | collective-permute-start | bytes 344072 | tf_op jit(solution)/shard_map/ppermute | solution.py:19
  59.3 5.2 %collective-permute-start.20 = (bf16[8,3584]{1,0:T(8,128)(2,1)S(1)}, bf16[8,3584]{1,0:T(8,128)(2,1)S(1)}, u32[]{:S(2)}, u32[]{:S(2)}) collective-permute-start(bf16[8,3584]{1,0:T(8,128)(2,1)S(1)} %slice.81), channel_id=1, source_target_pairs={{0,4},{1,5},{2,6},{3,7},{4,0},{5,1},{6,2},{7,3},{8,12},{9,13},{10,... | collective-permute-start | bytes 172040 | tf_op jit(solution)/shard_map/ppermute | solution.py:19
  62.2 4.2 %collective-permute-start.22 = (bf16[8,3584]{1,0:T(8,128)(2,1)S(1)}, bf16[8,3584]{1,0:T(8,128)(2,1)S(1)}, u32[]{:S(2)}, u32[]{:S(2)}) collective-permute-start(bf16[8,3584]{1,0:T(8,128)(2,1)S(1)} %slice.86), channel_id=1, source_target_pairs={{0,4},{1,5},{2,6},{3,7},{4,0},{5,1},{6,2},{7,3},{8,12},{9,13},{10,... | collective-permute-start | bytes 172040 | tf_op jit(solution)/shard_map/ppermute | solution.py:19
  63.9 5.2 %collective-permute-start.24 = (bf16[448,576]{1,0:T(8,128)(2,1)S(1)}, bf16[448,576]{1,0:T(8,128)(2,1)S(1)}, u32[]{:S(2)}, u32[]{:S(2)}) collective-permute-start(bf16[448,576]{1,0:T(8,128)(2,1)S(1)} %copy-done.2), channel_id=1, source_target_pairs={{0,1},{1,0},{2,3},{3,2},{4,5},{5,4},{6,7},{7,6},{8,9},{9,8},{10,11... | collective-permute-start | bytes 1548296 | tf_op jit(solution)/shard_map/ppermute | solution.py:19
  63.9 5.7 %collective-permute-start.25 = (bf16[448,576]{1,0:T(8,128)(2,1)S(1)}, bf16[448,576]{1,0:T(8,128)(2,1)S(1)}, u32[]{:S(2)}, u32[]{:S(2)}) collective-permute-start(bf16[448,576]{1,0:T(8,128)(2,1)S(1)} %collective-permute-done.6.refs_1_), channel_id=1, source_target_pairs={{0,1},{1,0},{2,3},{3,2},{4,5},{5,4},{6,7},{7,6},{8,9},{9,8},{10,11... | collective-permute-start | bytes 1548296 | tf_op jit(solution)/shard_map/ppermute | solution.py:19
  64.4 5.2 %collective-permute-start.26 = (bf16[448,576]{1,0:T(8,128)(2,1)S(1)}, bf16[448,576]{1,0:T(8,128)(2,1)S(1)}, u32[]{:S(2)}, u32[]{:S(2)}) collective-permute-start(bf16[448,576]{1,0:T(8,128)(2,1)S(1)} %collective-permute-done.13.refs_2_), channel_id=1, source_target_pairs={{0,1},{1,0},{2,3},{3,2},{4,5},{5,4},{6,7},{7,6},{8,9},{9,8},{10,11... | collective-permute-start | bytes 1548296 | tf_op jit(solution)/shard_map/ppermute | solution.py:19
  64.5 8.3 %collective-permute-start.27 = (bf16[448,576]{1,0:T(8,128)(2,1)}, bf16[448,576]{1,0:T(8,128)(2,1)S(1)}, u32[]{:S(2)}, u32[]{:S(2)}) collective-permute-start(bf16[448,576]{1,0:T(8,128)(2,1)} %collective-permute-done.18.refs_3_), channel_id=1, source_target_pairs={{0,1},{1,0},{2,3},{3,2},{4,5},{5,4},{6,7},{7,6},{8,9},{9,8},{10,11... | collective-permute-start | bytes 1548296 | tf_op jit(solution)/shard_map/ppermute | solution.py:19
  66.5 6.4 %collective-permute-start.23 = (bf16[8,3584]{1,0:T(8,128)(2,1)S(1)}, bf16[8,3584]{1,0:T(8,128)(2,1)S(1)}, u32[]{:S(2)}, u32[]{:S(2)}) collective-permute-start(bf16[8,3584]{1,0:T(8,128)(2,1)S(1)} %get-tuple-element.67.sum_ref), channel_id=1, source_target_pairs={{0,8},{1,9},{2,10},{3,11},{4,12},{5,13},{6,14},{7,15},{8,0},{9,1},... | collective-permute-start | bytes 172040 | tf_op jit(solution)/shard_map/ppermute | solution.py:19
  69.2 7.1 %collective-permute-start.28 = (bf16[4,3584]{1,0:T(4,128)(2,1)S(1)}, bf16[4,3584]{1,0:T(4,128)(2,1)S(1)}, u32[]{:S(2)}, u32[]{:S(2)}) collective-permute-start(bf16[4,3584]{1,0:T(4,128)(2,1)S(1)} %slice.87), channel_id=1, source_target_pairs={{0,8},{1,9},{2,10},{3,11},{4,12},{5,13},{6,14},{7,15},{8,0},{9,1},... | collective-permute-start | bytes 86024 | tf_op jit(solution)/shard_map/ppermute | solution.py:19
  74.8 4.6 %collective-permute-start.29 = (f32[4,640]{1,0:T(4,128)S(1)}, f32[4,640]{1,0:T(4,128)S(1)}, u32[]{:S(2)}, u32[]{:S(2)}) collective-permute-start(f32[4,640]{1,0:T(4,128)S(1)} %get-tuple-element.56), channel_id=1, source_target_pairs={{0,8},{1,9},{2,10},{3,11},{4,12},{5,13},{6,14},{7,15},{8,0},{9,1},... | collective-permute-start | bytes 30728 | tf_op jit(solution)/shard_map/ppermute | solution.py:19

commit v3 on v0

--- a/solution.py
+++ b/solution.py
@@ -1,14 +1,474 @@
 import jax
 import jax.numpy as jnp
 from jax import lax
+from jax.experimental import pallas as pl
+from jax.experimental.pallas import tpu as pltpu
 from jax.sharding import PartitionSpec as P
 
 FF = 2048
 KV = 512
+LANES = 128
+CHUNK = 512
+CORE, LOW, MID, HIGH = 0, 1, 2, 3
 
 
 score_scale = 192.0 ** (-0.5)
 norm_eps = 1e-06
+
+
+def swap(x, *bits):
+    if bits == ("sec",):
+        return lax.ppermute(x, "sec", [(i, i ^ 1) for i in range(lax.axis_size("sec"))])
+    flips = sum(1 << bit for bit in bits)
+    return lax.ppermute(x, "dev", [(i, i ^ flips) for i in range(lax.axis_size("dev"))])
+
+
+def wide_total(*parts):
+    return sum(part.astype(jnp.float32) for part in parts)
+
+
+def total(*parts):
+    return wide_total(*parts).astype(jnp.bfloat16)
+
+
+def cache_kernel(lengths_ref, q_ref, kv_ref, stats_ref, out_ref):
+    heads, count = q_ref.shape[1], kv_ref.shape[2]
+    lane = lax.broadcasted_iota(jnp.int32, (heads, LANES), 1)
+    position = lax.broadcasted_iota(jnp.int32, (heads, count), 1)
+    for row in range(q_ref.shape[0]):
+        scores = jnp.dot(q_ref[row], kv_ref[row], preferred_element_type=jnp.float32) * score_scale
+        scores = jnp.where(position < lengths_ref[row], scores, -1e30)
+        peak = jnp.max(scores, axis=1, keepdims=True)
+        spread = jnp.exp(scores - peak)
+        denominator = jnp.sum(spread, axis=1, keepdims=True)
+        out_ref[row] = lax.dot_general(
+            spread.astype(jnp.bfloat16),
+            kv_ref[row, :KV, :],
+            (((1,), (1,)), ((), ())),
+            preferred_element_type=jnp.float32,
+        )
+        stats_ref[row] = jnp.where(lane == 0, peak, denominator)
+
+
+def cache_part(queries, kv_cache, lengths):
+    rows, heads = queries.shape[:2]
+    vmem = pl.BlockSpec(memory_space=pltpu.VMEM)
+    return pl.pallas_call(
+        cache_kernel,
+        out_shape=(
+            jax.ShapeDtypeStruct((rows, heads, LANES), jnp.float32),
+            jax.ShapeDtypeStruct((rows, heads, KV), jnp.float32),
+        ),
+        in_specs=[pl.BlockSpec(memory_space=pltpu.SMEM), vmem, vmem],
+        out_specs=[vmem] * 2,
+        compiler_params=pltpu.CompilerParams(vmem_limit_bytes=8 << 20),
+        cost_estimate=pl.CostEstimate(
+            flops=4 * queries.size * kv_cache.shape[1],
+            bytes_accessed=2 * kv_cache.size,
+            transcendentals=0,
+        ),
+        name="cache_part",
+    )(lengths, queries, jnp.swapaxes(kv_cache, 1, 2))
+
+
+def kernel_call(body, out_shape, scalars, *arrays, name, mib, anywhere=0, scratch=()):
+    vmem = pl.BlockSpec(memory_space=pltpu.VMEM)
+    specs = [pl.BlockSpec(memory_space=pltpu.SMEM)] + [vmem] * (len(arrays) - anywhere)
+    specs += [pl.BlockSpec(memory_space=pl.ANY)] * anywhere
+    return pl.pallas_call(
+        body,
+        out_shape=out_shape,
+        in_specs=specs,
+        out_specs=jax.tree.map(lambda _: vmem, out_shape),
+        scratch_shapes=scratch,
+        compiler_params=pltpu.CompilerParams(vmem_limit_bytes=mib << 20),
+        name=name,
+    )(scalars, *arrays)
+
+
+def info_kernel(_, x_ref, ids_ref, scores_ref, out_ref):
+    (rows, width), picks = x_ref.shape, ids_ref.shape[0]
+    out_ref[:, :width] = x_ref[...]
+    lane = lax.broadcasted_iota(jnp.int32, (rows, LANES), 1)
+    row = lax.broadcasted_iota(jnp.int32, (rows, rows), 0)
+    here = row == lax.broadcasted_iota(jnp.int32, (rows, rows), 1)
+    info = jnp.zeros((rows, LANES), jnp.float32)
+    for i, values in enumerate((ids_ref[...], scores_ref[...])):
+        values = values.astype(jnp.float32)
+        for k in range(picks):
+            column = jnp.sum(jnp.where(here, values[k : k + 1], 0.0), axis=1, keepdims=True)
+            info = jnp.where(lane == i * picks + k, column, info)
+    out_ref[:, width:] = info.astype(out_ref.dtype)
+
+
+def with_info(hidden_in, expert_ids, gate_scores):
+    rows, width = hidden_in.shape
+    return kernel_call(
+        info_kernel,
+        jax.ShapeDtypeStruct((rows, width + LANES), hidden_in.dtype),
+        jnp.zeros((1,), jnp.int32),
+        hidden_in,
+        expert_ids.T,
+        gate_scores.T,
+        name="with_info",
+        mib=2,
+    )
+
+
+def pack_kernel(_, *refs):
+    blocks, (a_ref, b_ref) = refs[:4], refs[4:]
+    half = a_ref.shape[1]
+    for ref, cols in ((a_ref, slice(0, half)), (b_ref, slice(half, None))):
+        x = jnp.concatenate([block[:, cols].astype(jnp.float32) for block in blocks], axis=0)
+        ref[...] = x.astype(ref.dtype)
+
+
+def pack_rows_of(*blocks):
+    rows, width = blocks[0].shape
+    half = (width - LANES) // 2
+    outs = [jax.ShapeDtypeStruct((4 * rows, cols), jnp.bfloat16) for cols in (half, half + LANES)]
+    return kernel_call(
+        pack_kernel, tuple(outs), jnp.zeros((1,), jnp.int32), *blocks, name="pack_rows", mib=4
+    )
+
+
+def gather_rows(hidden_in, expert_ids, gate_scores, w_kv):
+    x = with_info(hidden_in, expert_ids, gate_scores)
+    a, b = pack_rows_of(x, swap(x, HIGH), swap(x, MID), swap(x, MID, HIGH))
+    a, b, w_own = lax.optimization_barrier((a, b, w_kv))
+    w_mid = swap(w_own, MID)
+    a_low, b_sec = swap(a, LOW), swap(b, "sec")
+    a, b = jnp.concatenate([a, a_low], axis=0), jnp.concatenate([b, b_sec], axis=0)
+    a_all, b_all = (a, swap(a, "sec")), (b, swap(b, LOW))
+    a_all += tuple(swap(v, CORE) for v in a_all)
+    b_all += tuple(swap(v, CORE) for v in b_all)
+    return a_all, b_all, w_mid
+
+
+def experts_kernel(picks, place_ref, *refs):
+    a_refs, b_refs, w_refs, outs = refs[:4], refs[4:8], refs[8:11], refs[11:15]
+    gate_ref, up_ref, down_ref, sems = refs[15:]
+    size, half = a_refs[0].shape
+    size //= 2
+    moves = []
+    for part in (pl.ds(0, half), pl.ds(half, half)):
+        moves.append((w_refs[0].at[part], gate_ref.at[part]))
+        moves.append((w_refs[1].at[part], up_ref.at[part]))
+    for part in (pl.ds(0, half), pl.ds(half, half)):
+        moves.append((w_refs[2].at[:, part], down_ref.at[:, part]))
+    copies = [pltpu.make_async_copy(*move, sems.at[i]) for i, move in enumerate(moves)]
+    for copy in copies:
+        copy.start()
+
+    def rows_of(part, cols):
+        if part == 0:
+            return jnp.concatenate([ref[:, cols] for ref in a_refs], axis=0)
+        blocks = []
+        for side in range(2):
+            early, late = b_refs[2 * side][:, cols], b_refs[2 * side + 1][:, cols]
+            blocks += [early[:size], late[:size], early[size:], late[size:]]
+        return jnp.concatenate(blocks, axis=0)
+
+    def ordered(x):
+        n = size // 2
+        parts = [x[i * n : (i + 1) * n] for i in range(x.shape[0] // n)]
+        parts = [jnp.where(place_ref[2] == 1, pltpu.roll(v, n // 2, 0), v) for v in parts]
+        done = []
+        for i in range(0, len(parts), 4):
+            for mid in range(2):
+                pair = parts[i + mid], parts[i + 2 + mid]
+                done.append(jnp.where(place_ref[1] == 1, pair[1], pair[0]))
+                done.append(jnp.where(place_ref[1] == 1, pair[0], pair[1]))
+        return jnp.concatenate(done, axis=0)
+
+    info = rows_of(1, slice(half, half + LANES)).astype(jnp.float32)
+    rows, hid = info.shape[0], gate_ref.shape[1]
+    lane = lax.broadcasted_iota(jnp.int32, info.shape, 1)
+    scores = jnp.where(lane < picks, pltpu.roll(info, LANES - picks, 1), 0.0)
+    named = jnp.where(info == place_ref[0].astype(jnp.float32), scores, 0.0)
+    share = jnp.sum(named, axis=1, keepdims=True) / jnp.sum(scores, axis=1, keepdims=True)
+    gate_act = jnp.zeros((rows, hid), jnp.float32)
+    up_act = jnp.zeros((rows, hid), jnp.float32)
+    for part in range(2):
+        copies[2 * part].wait()
+        copies[2 * part + 1].wait()
+        for k in range(0, half, CHUNK):
+            x = rows_of(part, slice(k, k + CHUNK))
+            depth = slice(part * half + k, part * half + k + CHUNK)
+            gate_act += jnp.dot(x, gate_ref[depth, :], preferred_element_type=jnp.float32)
+            up_act += jnp.dot(x, up_ref[depth, :], preferred_element_type=jnp.float32)
+    hidden = ordered(gate_act / (1.0 + jnp.exp(-gate_act)) * up_act).astype(jnp.bfloat16)
+    share = ordered(jnp.broadcast_to(share, (rows, LANES)))[:, :1]
+    copies[4].wait()
+    copies[5].wait()
+    block = half // 4
+    for part in range(2):
+        kept, sent = outs[2 * part : 2 * part + 2]
+        for i in range(4):
+            flip, mid = i // 2, i % 2
+            first = (place_ref[2] ^ part) * half + mid * 2 * block + (place_ref[1] ^ flip) * block
+            for c in range(0, block, CHUNK):
+                wide = min(CHUNK, block - c)
+                cols = pl.ds(pl.multiple_of(first + c, LANES), wide)
+                partial = jnp.dot(hidden, down_ref[:, cols], preferred_element_type=jnp.float32)
+                partial = (partial * share).astype(jnp.bfloat16)
+                to = slice(i * block + c, i * block + c + wide)
+                kept[:, to] = partial[: rows // 2]
+                sent[:, to] = partial[rows // 2 :]
+
+
+def experts(place, a_all, b_all, picks, w_gate, w_up, w_down):
+    rows, half = a_all[0].shape
+    out = jax.ShapeDtypeStruct((2 * rows, half), jnp.bfloat16)
+    weights = (w_gate, w_up, w_down)
+    return kernel_call(
+        lambda *refs: experts_kernel(picks, *refs),
+        (out,) * 4,
+        place,
+        *a_all,
+        *b_all,
+        *weights,
+        name="experts",
+        mib=48,
+        anywhere=3,
+        scratch=[pltpu.VMEM(w.shape, w.dtype) for w in weights] + [pltpu.SemaphoreType.DMA((6,))],
+    )
+
+
+def scatter_rows(keep_a, send_a, keep_b, send_b, late):
+    rows, cols = keep_a.shape[0] // 2, keep_a.shape[1] // 2
+    left, right = slice(0, cols), slice(cols, None)
+    a, b = [keep_a, swap(send_a, CORE)], [keep_b, swap(send_b, CORE)]
+    a.append(swap(total(*(v[rows:] for v in a)), "sec"))
+    b.append(swap(total(*(v[:, right] for v in b)), LOW))
+    a, b, late = lax.optimization_barrier((a, b, late))
+    a.append(swap(total(*(v[:rows, right] for v in a)), LOW))
+    b.append(swap(total(*(v[rows:, left] for v in b)), "sec"))
+    a, b = lax.optimization_barrier((a, b))
+    rows //= 2
+    here, there = slice(0, rows), slice(rows, 2 * rows)
+    ins = (
+        swap(total(*(v[there, left] for v in a)), MID),
+        swap(total(*(v[here, left] for v in b)), HIGH),
+        swap(total(*(v[there, left] for v in b)), MID, HIGH),
+    )
+    a, ins = lax.optimization_barrier((a, ins))
+    return wide_total(*(v[here, left] for v in a)), ins, late
+
+
+def residual_kernel(place_ref, a_ref, b_ref, low_ref, out_ref):
+    rows, half = a_ref.shape
+    n, block = rows // 4, half // 4
+    upper, odd = place_ref[2] == 1, place_ref[1] == 1
+    pair = []
+    for a, b in ((a_ref[:n], b_ref[:n]), (a_ref[2 * n : 3 * n], low_ref[:n])):
+        x = jnp.where(upper, b[:, :half].astype(jnp.float32), a.astype(jnp.float32))
+        pair.append(jnp.where(upper, pltpu.roll(x, n // 2, 0), x))
+    pair = [jnp.where(odd, pair[1], pair[0]), jnp.where(odd, pair[0], pair[1])]
+    x = jnp.concatenate(pair, axis=0)
+    for mid in range(2):
+        first = 2 * mid * block
+        even = x[:, first : first + block]
+        out_ref[:, mid * block : (mid + 1) * block] = jnp.where(
+            odd, x[:, first + block : first + 2 * block], even
+        )
+
+
+def residual_rows(place, a, b, b_low):
+    rows, half = a.shape
+    return kernel_call(
+        residual_kernel,
+        jax.ShapeDtypeStruct((rows // 2, half // 2), jnp.float32),
+        place,
+        a,
+        b,
+        b_low,
+        name="residual_rows",
+        mib=4,
+    )
+
+
+def put_split(ref, first, apart, x):
+    cols = x.shape[1]
+    upper = x.astype(jnp.bfloat16)
+    ref[:, first : first + cols] = upper
+    rest = (x - upper.astype(jnp.float32)).astype(jnp.bfloat16)
+    ref[:, first + apart : first + apart + cols] = rest
+
+
+def get_split(ref, first, cols):
+    upper = ref[:, first : first + cols].astype(jnp.float32)
+    return upper + ref[:, first + cols : first + 2 * cols].astype(jnp.float32)
+
+
+def latent_kernel(place_ref, sum_ref, residual_ref, gain_ref, *refs):
+    in_refs, w_refs = refs[:3], refs[3:7]
+    sums_ref, moe_ref, out_ref, piece_ref = refs[7:]
+    rows, cols = sum_ref.shape
+    block, n = cols // 2, rows // 2
+    piece, lat = w_refs[0].shape
+    odd = place_ref[1] == 1
+    mixture = sum_ref[...] + wide_total(*(ref[...] for ref in in_refs))
+    moe = (residual_ref[...] + mixture).astype(jnp.bfloat16)
+    widened = moe.astype(jnp.float32)
+    moe_ref[...] = jnp.where(odd, widened[n:], widened[:n]).astype(jnp.bfloat16)
+    out_ref[:, :cols] = jnp.where(odd, widened[:n], widened[n:]).astype(jnp.bfloat16)
+    for mid in range(2):
+        gain = gain_ref[pl.ds(4 * place_ref[2] + 2 * mid + place_ref[1], 1), :]
+        scaled = widened[:, mid * block : (mid + 1) * block] * gain
+        for core in range(2):
+            piece_ref[2 * mid + core] = scaled[:, core * piece : (core + 1) * piece]
+    sums = jnp.zeros((rows, lat), jnp.float32)
+    for flips, w_ref in enumerate(w_refs):
+        x = piece_ref[place_ref[3] ^ flips].astype(jnp.bfloat16)
+        sums += jnp.dot(x, w_ref[...], preferred_element_type=jnp.float32)
+    squares = jnp.sum(widened * widened, axis=1, keepdims=True)
+    tail = jnp.broadcast_to(squares, (rows, LANES))
+    wide = sums_ref.shape[1]
+    for to, x in ((slice(0, lat), sums), (slice(lat, wide), tail[:, : wide - lat])):
+        sums_ref[:, to] = jnp.where(odd, x[n:], x[:n])
+        put_split(out_ref, cols + to.start, wide, jnp.where(odd, x[:n], x[n:]))
+
+
+def latent_parts(place, kept, received, residual, gain, slices):
+    rows, cols = kept.shape
+    piece, lat = slices[0].shape
+    padded = -(-(lat + 1) // LANES) * LANES
+    sums = jax.ShapeDtypeStruct((rows // 2, padded), jnp.float32)
+    moe = jax.ShapeDtypeStruct((rows // 2, cols), jnp.bfloat16)
+    sent = jax.ShapeDtypeStruct((rows // 2, cols + 2 * padded), jnp.bfloat16)
+    return kernel_call(
+        latent_kernel,
+        (sums, moe, sent),
+        place,
+        kept,
+        residual,
+        gain.reshape(8, cols // 2),
+        *received,
+        *slices,
+        name="latent_parts",
+        mib=12,
+        scratch=[pltpu.VMEM((4, rows, piece), jnp.float32)],
+    )
+
+
+def turn_kernel(place_ref, sums_ref, moe_ref, in_ref, sums_out, moe_out, send_ref):
+    rows, cols = moe_ref.shape
+    n, wide = rows // 2, sums_ref.shape[1]
+    upper = place_ref[2] == 1
+    sums = sums_ref[...] + get_split(in_ref, cols, wide)
+    sums_out[...] = jnp.where(upper, sums[n:], sums[:n])
+    put_split(send_ref, 2 * cols, wide, jnp.where(upper, sums[:n], sums[n:]))
+    for first, x in ((0, moe_ref[...]), (cols, in_ref[:, :cols])):
+        x = x.astype(jnp.float32)
+        to = slice(first, first + cols)
+        moe_out[:, to] = jnp.where(upper, x[n:], x[:n]).astype(jnp.bfloat16)
+        send_ref[:, to] = jnp.where(upper, x[:n], x[n:]).astype(jnp.bfloat16)
+
+
+def turn(place, sums, moe, received):
+    (rows, cols), wide = moe.shape, sums.shape[1]
+    return kernel_call(
+        turn_kernel,
+        (
+            jax.ShapeDtypeStruct((rows // 2, wide), sums.dtype),
+            jax.ShapeDtypeStruct((rows // 2, 2 * cols), moe.dtype),
+            jax.ShapeDtypeStruct((rows // 2, 2 * cols + 2 * wide), moe.dtype),
+        ),
+        place,
+        sums,
+        moe,
+        received,
+        name="turn",
+        mib=2,
+    )
+
+
+def put_rows(place_ref, keep_ref, in_ref, out_ref):
+    half = keep_ref.shape[1]
+    block = half // 4
+    upper, odd = place_ref[2] == 1, place_ref[1] == 1
+    for part, ref, other in ((0, keep_ref, in_ref), (1, in_ref, keep_ref)):
+        x = jnp.where(upper, other[:, :half], ref[:, :half])
+        for mid in range(2):
+            even = x[:, mid * block : (mid + 1) * block]
+            uneven = x[:, (2 + mid) * block : (3 + mid) * block]
+            first = part * half + mid * 2 * block
+            out_ref[:, first : first + block] = jnp.where(odd, uneven, even)
+            out_ref[:, first + block : first + 2 * block] = jnp.where(odd, even, uneven)
+
+
+def finish_kernel(place_ref, sums_ref, moe_ref, in_ref, q_ref, stats_ref, part_ref, *outs):
+    moe_out, latent_ref, out_ref = outs
+    lat, half = q_ref.shape[2], moe_ref.shape[1]
+    sums = sums_ref[...] + get_split(in_ref, half, sums_ref.shape[1])
+    inverse = lax.rsqrt(sums[:, lat : lat + 1] / (2 * half) + norm_eps)
+    rounded = (sums[:, :lat] * inverse).astype(jnp.bfloat16)
+    latent_ref[...] = rounded
+    latent = rounded.astype(jnp.float32)
+    for row in range(q_ref.shape[0]):
+        own = latent[row : row + 1]
+        own_score = jnp.sum(q_ref[row].astype(jnp.float32) * own, axis=1, keepdims=True) * score_scale
+        peak, denominator = stats_ref[row, :, 0:1], stats_ref[row, :, 1:2]
+        top = jnp.maximum(peak, own_score)
+        shrink = jnp.exp(peak - top)
+        own_weight = jnp.exp(own_score - top)
+        scale = 1.0 / (denominator * shrink + own_weight)
+        own_prob = (own_weight * scale).astype(jnp.bfloat16).astype(jnp.float32)
+        value = part_ref[row] * (shrink * scale) + own_prob * own[:, :KV]
+        out_ref[row] = value.astype(jnp.bfloat16)
+    put_rows(place_ref, moe_ref, in_ref, moe_out)
+
+
+def finish(place, sums, moe, received, queries, stats, combined):
+    rows, heads, lat = queries.shape
+    outs = ((rows, 2 * moe.shape[1]), (rows, lat), (rows, heads, KV))
+    return kernel_call(
+        finish_kernel,
+        tuple(jax.ShapeDtypeStruct(shape, jnp.bfloat16) for shape in outs),
+        place,
+        sums,
+        moe,
+        received,
+        queries,
+        stats,
+        combined,
+        name="finish",
+        mib=8,
+    )
+
+
+def per_device(
+    hidden_in,
+    expert_ids,
+    gate_scores,
+    w_gate,
+    w_up,
+    w_down,
+    norm_gain,
+    w_kv,
+    queries,
+    kv_cache,
+    lengths,
+):
+    devices = lax.axis_size("dev")
+    device = lax.axis_index("dev")
+    shard_count = FF // w_gate.shape[1]
+    expert = lax.axis_index("sec") * (devices // shard_count) + device // shard_count
+    picks = expert_ids.shape[1]
+    core_mid = (((device >> MID) & 1) << 1) | (device & 1)
+    place = jnp.stack([expert, (device >> LOW) & 1, (device >> HIGH) & 1, core_mid])
+
+    cache = cache_part(queries, kv_cache, lengths)
+    a_all, b_all, w_mid = gather_rows(hidden_in, expert_ids, gate_scores, w_kv)
+    partial = experts(place, a_all, b_all, picks, w_gate, w_up, w_down)
+    partial, w_mid = lax.optimization_barrier((partial, w_mid))
+    kept, received, (stats, combined) = scatter_rows(*partial, cache)
+    slices = (w_kv, swap(w_kv, CORE), w_mid, swap(w_mid, CORE))
+    residual = residual_rows(place, a_all[0], b_all[0], b_all[1])
+    sums, moe, sent = latent_parts(place, kept, received, residual, norm_gain, slices)
+    sums, moe, sent = turn(place, sums, moe, swap(sent, LOW))
+    return finish(place, sums, moe, swap(sent, HIGH), queries, stats, combined)
 
 
 def shifted(x, axis, by):
@@ -91,7 +551,7 @@
     return partial_value.reshape(slots.shape)
 
 
-def per_device(
+def per_device_wide(
     hidden_in,
     expert_ids,
     gate_scores,
@@ -170,6 +630,7 @@
         P(("sec", "dev")),
     )
     out_specs = (P(("sec", "dev"), None), P(("sec", "dev"), None), P(("sec", "dev"), None, None))
+    pairwise = mesh.shape["sec"] == 2 and mesh.shape["dev"] == 2 << HIGH
     return jax.shard_map(
-        per_device, mesh=mesh, in_specs=in_specs, out_specs=out_specs, check_vma=False
-    )
+        per_device if pairwise else per_device_wide, mesh=mesh, in_specs=in_specs, out_specs=out_specs, check_vma=False
+    )

time: 247 us -> 73.9 us (0.30)
  blocking collectives: 109 us -> 0 us
  waiting for transfers between devices: 83.5 us -> 33.6 us
  matrix products: 14.2 us -> 0 us
  Pallas kernels: 0 us -> 11.7 us
  other arithmetic: 9.7 us -> 2.58 us
  local copies, waits for them, and re-layouts: 10.4 us -> 3.76 us
  starting transfers between devices: 17.2 us -> 21.1 us
    unnamed x1 -> x0, blocking collectives: 59.5 us -> none
    all_to_all x1 -> x0, blocking collectives: 49.9 us -> none  [per_device(): lax.all_to_all(outgoing, 'dev', split_axis=1, concat_axis=1, tiled=True)]
    all_to_all x2 -> x0, waiting for transfers between devices: 41.4 us -> none  [the longest x1 36.2 us: per_device(): lax.all_to_all(sending, 'dev', split_axis=1, concat_axis=1, tiled=True)]
    ppermute x2 -> x25, starting transfers between devices: 3.05 us -> 21.1 us  [the longest x21 18.4 us: swap(): lax.ppermute(x, 'dev', [(i, i ^ flips) for i in range(lax.axis_size('dev'...]
    dot_general x10 -> x0, matrix products: 14.2 us -> none  [the longest x1 6.55 us: run_expert(): jnp.dot(hidden, w_down, preferred_element_type=jnp.float32)]
    all_to_all x2 -> x0, starting transfers between devices: 14.2 us -> none  [the longest x1 10.1 us: per_device(): lax.all_to_all(normed, 'dev', split_axis=1, concat_axis=0, tiled=True)]
    pallas_call x0 -> x8, Pallas kernels: none -> 11.7 us  [the longest x7 9.98 us: kernel_call(): pl.pallas_call(body, out_shape=out_shape, in_specs=specs, out_specs=jax.t...]
    ppermute x2 -> x25, waiting for transfers between devices: 42.1 us -> 33.6 us  [the longest x21 25.3 us: swap(): lax.ppermute(x, 'dev', [(i, i ^ flips) for i in range(lax.axis_size('dev'...]
  transfers between devices with their start and end apart: 4 -> 25, of which waited for: 4 -> 17; matrix products, arithmetic and copies ran while one was open for 1% -> 5% of each run, Pallas kernels for 0% -> 11%
where the time goes in v3:
time: 73.9 us; the launch traced here: 73.5 us
  waiting for transfers between devices  33.6 us (45%)
  starting transfers between devices  21.1 us (29%)
  Pallas kernels  11.7 us (16%)
  local copies, waits for them, and re-layouts  3.76 us (5%)
  other arithmetic  2.58 us (3%)
  between operations  0.8 us (1%)
    ppermute x21, waiting for transfers between devices, swap(): lax.ppermute(x, 'dev', [(i, i ^ flips) for i in range(lax.axis_size('dev'...  25.3 us
    ppermute x21, starting transfers between devices, swap(): lax.ppermute(x, 'dev', [(i, i ^ flips) for i in range(lax.axis_size('dev'...  18.4 us
    pallas_call x7, Pallas kernels, kernel_call(): pl.pallas_call(body, out_shape=out_shape, in_specs=specs, out_specs=jax.t...  9.98 us
    ppermute x4, waiting for transfers between devices, swap(): lax.ppermute(x, 'sec', [(i, i ^ 1) for i in range(lax.axis_size('sec'))])  8.27 us
    unnamed x28, local copies, waits for them, and re-layouts  2.98 us
    ppermute x4, starting transfers between devices, swap(): lax.ppermute(x, 'sec', [(i, i ^ 1) for i in range(lax.axis_size('sec'))])  2.73 us
    pallas_call x1, Pallas kernels, cache_part(): pl.pallas_call(cache_kernel, out_shape=(jax.ShapeDtypeStruct((rows, heads...  1.7 us
    convert_element_type x6, other arithmetic, total(): return wide_total(*parts).astype(jnp.bfloat16)  1.57 us
  transfers between devices with their start and end apart: 25, of which 17 were waited for; matrix products, arithmetic and copies ran while one was open for 5% of the time, Pallas kernels for 11%

profile of v3, /device:TPU:0, one launch (start us, length us, event | category | flops | bytes accessed | tf_op | source)
XLA Modules:
  0.0 73.5 jit_solution(15847138207127752764)
XLA Ops:
  0.6 0.8 %copy-done.6 = bf16[4,7168]{1,0:T(4,128)(2,1)S(1)} copy-done((bf16[4,7168]{1,0:T(4,128)(2,1)S(1)}, bf16[4,7168]{1,0:T(4,128)(2,1)}, u32[]{:S(2)}) %copy-start.6) | copy-done | bytes 57368
  1.5 0.7 copy-done.7
  2.1 0.7 copy-done.8
  2.8 0.1 with_info.1.refs_0_
  2.9 4.0 %collective-permute-start = (bf16[4,7296]{1,0:T(4,128)(2,1)S(1)}, bf16[4,7296]{1,0:T(4,128)(2,1)S(1)}, u32[]{:S(2)}, u32[]{:S(2)}) collective-permute-start(bf16[4,7296]{1,0:T(4,128)(2,1)S(1)} %with_info.1.refs_0_), channel_id=1, source_target_pairs={{0,8},{1,9},{2,10},{3,11},{4,12},{5,13},{6,14},{7,15},{8,0},{9,1},... | collective-permute-start | bytes 175112 | tf_op jit(solution)/shard_map/ppermute | solution.py:23
  6.9 1.6 %collective-permute-start.1 = (bf16[4,7296]{1,0:T(4,128)(2,1)S(1)}, bf16[4,7296]{1,0:T(4,128)(2,1)S(1)}, u32[]{:S(2)}, u32[]{:S(2)}) collective-permute-start(bf16[4,7296]{1,0:T(4,128)(2,1)S(1)} %with_info.1.refs_0_), channel_id=1, source_target_pairs={{0,4},{1,5},{2,6},{3,7},{4,0},{5,1},{6,2},{7,3},{8,12},{9,13},{10,... | collective-permute-start | bytes 175112 | tf_op jit(solution)/shard_map/ppermute | solution.py:23
  8.5 0.0 collective-permute-start.2
  8.5 1.3 %collective-permute-done.refs_1_ = bf16[4,7296]{1,0:T(4,128)(2,1)S(1)} collective-permute-done((bf16[4,7296]{1,0:T(4,128)(2,1)S(1)}, bf16[4,7296]{1,0:T(4,128)(2,1)S(1)}, u32[]{:S(2)}, u32[]{:S(2)}) %collective-permute-start) | collective-permute-done | bytes 58400 | tf_op jit(solution)/shard_map/ppermute | solution.py:23
  9.8 1.3 %collective-permute-done.1.refs_2_ = bf16[4,7296]{1,0:T(4,128)(2,1)S(1)} collective-permute-done((bf16[4,7296]{1,0:T(4,128)(2,1)S(1)}, bf16[4,7296]{1,0:T(4,128)(2,1)S(1)}, u32[]{:S(2)}, u32[]{:S(2)}) %collective-permute-start.1) | collective-permute-done | bytes 58400 | tf_op jit(solution)/shard_map/ppermute | solution.py:23
  11.1 3.4 %collective-permute-done.2.refs_3_ = bf16[4,7296]{1,0:T(4,128)(2,1)S(1)} collective-permute-done((bf16[4,7296]{1,0:T(4,128)(2,1)S(1)}, bf16[4,7296]{1,0:T(4,128)(2,1)S(1)}, u32[]{:S(2)}, u32[]{:S(2)}) %collective-permute-start.2) | collective-permute-done | bytes 58400 | tf_op jit(solution)/shard_map/ppermute | solution.py:23
  14.5 0.1 pack_rows.1
  14.6 1.6 %collective-permute-start.7 = (bf16[16,3712]{1,0:T(8,128)(2,1)S(1)}, bf16[16,3712]{1,0:T(8,128)(2,1)S(1)}, u32[]{:S(2)}, u32[]{:S(2)}) collective-permute-start(bf16[16,3712]{1,0:T(8,128)(2,1)S(1)} %get-tuple-element.51), channel_id=1, source_target_pairs={{0,16},{16,0},{1,17},{17,1},{2,18},{18,2},{3,19},{19,3},{4,20},{20... | collective-permute-start | bytes 356360 | tf_op jit(solution)/shard_map/ppermute | solution.py:21
  16.1 1.6 %collective-permute-start.3 = (bf16[16,3584]{1,0:T(8,128)(2,1)S(1)}, bf16[16,3584]{1,0:T(8,128)(2,1)S(1)}, u32[]{:S(2)}, u32[]{:S(2)}) collective-permute-start(bf16[16,3584]{1,0:T(8,128)(2,1)S(1)} %get-tuple-element.50), channel_id=1, source_target_pairs={{0,2},{1,3},{2,0},{3,1},{4,6},{5,7},{6,4},{7,5},{8,10},{9,11},{10,... | collective-permute-start | bytes 344072 | tf_op jit(solution)/shard_map/ppermute | solution.py:23
  17.7 1.7 %collective-permute-done.7 = bf16[16,3712]{1,0:T(8,128)(2,1)S(1)} collective-permute-done((bf16[16,3712]{1,0:T(8,128)(2,1)S(1)}, bf16[16,3712]{1,0:T(8,128)(2,1)S(1)}, u32[]{:S(2)}, u32[]{:S(2)}) %collective-permute-start.7) | collective-permute-done | bytes 118816 | tf_op jit(solution)/shard_map/ppermute | solution.py:21
  19.5 1.6 %collective-permute-start.8 = (bf16[32,3712]{1,0:T(8,128)(2,1)S(1)}, bf16[32,3712]{1,0:T(8,128)(2,1)S(1)}, u32[]{:S(2)}, u32[]{:S(2)}) collective-permute-start(bf16[32,3712]{1,0:T(8,128)(2,1)S(1)} %constant_dynamic-update-slice_fusion.2.refs_5_.b_ref), channel_id=1, source_target_pairs={{0,2},{1,3},{2,0},{3,1},{4,6},{5,7},{6,4},{7,5},{8,10},{9,11},{10,... | collective-permute-start | bytes 712712 | tf_op jit(solution)/shard_map/ppermute | solution.py:23
  21.1 1.1 %collective-permute-done.3 = bf16[16,3584]{1,0:T(8,128)(2,1)S(1)} collective-permute-done((bf16[16,3584]{1,0:T(8,128)(2,1)S(1)}, bf16[16,3584]{1,0:T(8,128)(2,1)S(1)}, u32[]{:S(2)}, u32[]{:S(2)}) %collective-permute-start.3) | collective-permute-done | bytes 114720 | tf_op jit(solution)/shard_map/ppermute | solution.py:23
  22.1 0.5 collective-permute-start.4
  22.6 3.0 %collective-permute-done.8.refs_6_.low_ref = bf16[32,3712]{1,0:T(8,128)(2,1)S(1)} collective-permute-done((bf16[32,3712]{1,0:T(8,128)(2,1)S(1)}, bf16[32,3712]{1,0:T(8,128)(2,1)S(1)}, u32[]{:S(2)}, u32[]{:S(2)}) %collective-permute-start.8) | collective-permute-done | bytes 237600 | tf_op jit(solution)/shard_map/ppermute | solution.py:23
  25.6 0.5 collective-permute-start.5
  26.2 2.1 %collective-permute-done.4.refs_2_ = bf16[32,3584]{1,0:T(8,128)(2,1)S(1)} collective-permute-done((bf16[32,3584]{1,0:T(8,128)(2,1)S(1)}, bf16[32,3584]{1,0:T(8,128)(2,1)S(1)}, u32[]{:S(2)}, u32[]{:S(2)}) %collective-permute-start.4) | collective-permute-done | bytes 229408 | tf_op jit(solution)/shard_map/ppermute | solution.py:21
  28.2 0.0 collective-permute-start.6
  28.2 0.1 pad_add_fusion.refs_0_.place_ref
  28.3 0.0 collective-permute-done.5.refs_3_
  28.3 0.0 collective-permute-done.9.refs_7_
  28.3 1.4 %collective-permute-done.6.refs_4_ = bf16[32,3584]{1,0:T(8,128)(2,1)S(1)} collective-permute-done((bf16[32,3584]{1,0:T(8,128)(2,1)S(1)}, bf16[32,3584]{1,0:T(8,128)(2,1)S(1)}, u32[]{:S(2)}, u32[]{:S(2)}) %collective-permute-start.6) | collective-permute-done | bytes 229408 | tf_op jit(solution)/shard_map/ppermute | solution.py:23
  29.7 0.0 collective-permute-done.10.refs_8_
  29.7 5.5 %experts.1 = (bf16[64,3584]{1,0:T(8,128)(2,1)S(1)}, bf16[64,3584]{1,0:T(8,128)(2,1)S(1)}, bf16[64,3584]{1,0:T(8,128)(2,1)S(1)}, bf16[64,3584]{1,0:T(8,128)(2,1)S(1)}) custom-call(s32[4]{0:T(128)S(1)} %pad_add_fusion.refs_0_.place_ref, bf16[32,3584]{1,0:T(8,128)(2,1)S(1)} %constant_dynamic-update-slice_fusion.refs_1_.a_ref, ...), custom_call_target="tpu_custom_call" | custom-call | tf_op jit(solution)/shard_map/experts/pallas_call | solution.py:78
  35.3 0.0 copy-start.2
  35.3 0.2 collective-permute-start.14
  35.5 0.4 collective-permute-start.12
  35.9 1.3 %collective-permute-done.14 = bf16[64,3584]{1,0:T(8,128)(2,1)S(1)} collective-permute-done((bf16[64,3584]{1,0:T(8,128)(2,1)S(1)}, bf16[64,3584]{1,0:T(8,128)(2,1)S(1)}, u32[]{:S(2)}, u32[]{:S(2)}) %collective-permute-start.14) | collective-permute-done | bytes 458784 | tf_op jit(solution)/shard_map/ppermute | solution.py:23
  37.2 0.1 add_convert_fusion
  37.2 1.6 %collective-permute-start.15 = (bf16[64,1792]{1,0:T(8,128)(2,1)S(1)}, bf16[64,1792]{1,0:T(8,128)(2,1)S(1)}, u32[]{:S(2)}, u32[]{:S(2)}) collective-permute-start(bf16[64,1792]{1,0:T(8,128)(2,1)S(1)} %add_convert_fusion), channel_id=1, source_target_pairs={{0,2},{1,3},{2,0},{3,1},{4,6},{5,7},{6,4},{7,5},{8,10},{9,11},{10,... | collective-permute-start | bytes 688136 | tf_op jit(solution)/shard_map/ppermute | solution.py:23
  38.8 0.1 add_convert_fusion.1
  38.9 0.3 collective-permute-start.13
  39.2 1.7 %cache_part.1 = (f32[4,64,128]{2,1,0:T(8,128)S(1)}, f32[4,64,512]{2,1,0:T(8,128)S(1)}) custom-call(s32[4]{0:T(128)S(1)} %copy-done.9, bf16[4,64,576]{2,1,0:T(8,128)(2,1)S(1)} %copy-done, bf16[4,576,256]{2,1,0:T(8,128)(2,1)S(1)} %bitcast.7), custom_call_target="tpu_custom_call" | custom-call | flops 150994944 | bytes 1179648 | tf_op jit(solution)/shard_map/cache_part/pallas_call | solution.py:56
  40.9 0.8 %copy-done.3 = f32[4,64,512]{2,1,0:T(8,128)} copy-done((f32[4,64,512]{2,1,0:T(8,128)}, f32[4,64,512]{2,1,0:T(8,128)S(1)}, u32[]{:S(2)}) %copy-start.3) | copy-done | bytes 524312
  41.7 3.2 %collective-permute-done.15 = bf16[64,1792]{1,0:T(8,128)(2,1)S(1)} collective-permute-done((bf16[64,1792]{1,0:T(8,128)(2,1)S(1)}, bf16[64,1792]{1,0:T(8,128)(2,1)S(1)}, u32[]{:S(2)}, u32[]{:S(2)}) %collective-permute-start.15) | collective-permute-done | bytes 229408 | tf_op jit(solution)/shard_map/ppermute | solution.py:23
  44.9 1.4 %collective-permute-done.13 = bf16[32,3584]{1,0:T(8,128)(2,1)S(1)} collective-permute-done((bf16[32,3584]{1,0:T(8,128)(2,1)S(1)}, bf16[32,3584]{1,0:T(8,128)(2,1)S(1)}, u32[]{:S(2)}, u32[]{:S(2)}) %collective-permute-start.13) | collective-permute-done | bytes 229408 | tf_op jit(solution)/shard_map/ppermute | solution.py:21
  46.3 0.1 add_convert_fusion.2
  46.4 0.4 collective-permute-start.17
  46.8 0.9 %collective-permute-start.16 = (bf16[32,1792]{1,0:T(8,128)(2,1)S(1)}, bf16[32,1792]{1,0:T(8,128)(2,1)S(1)}, u32[]{:S(2)}, u32[]{:S(2)}) collective-permute-start(bf16[32,1792]{1,0:T(8,128)(2,1)S(1)} %add_convert_fusion.3), channel_id=1, source_target_pairs={{0,2},{1,3},{2,0},{3,1},{4,6},{5,7},{6,4},{7,5},{8,10},{9,11},{10,... | collective-permute-start | bytes 344072 | tf_op jit(solution)/shard_map/ppermute | solution.py:23
  47.6 0.5 collective-permute-start.22
  48.1 3.1 %collective-permute-done.17 = bf16[32,1792]{1,0:T(8,128)(2,1)S(1)} collective-permute-done((bf16[32,1792]{1,0:T(8,128)(2,1)S(1)}, bf16[32,1792]{1,0:T(8,128)(2,1)S(1)}, u32[]{:S(2)}, u32[]{:S(2)}) %collective-permute-start.17) | collective-permute-done | bytes 114720 | tf_op jit(solution)/shard_map/ppermute | solution.py:21
  51.2 0.4 collective-permute-done.16
  51.6 0.7 add_convert_fusion.4
  52.3 0.5 collective-permute-start.19
  52.8 1.2 %collective-permute-start.20 = (bf16[16,1792]{1,0:T(8,128)(2,1)}, bf16[16,1792]{1,0:T(8,128)(2,1)}, u32[]{:S(2)}, u32[]{:S(2)}) collective-permute-start(bf16[16,1792]{1,0:T(8,128)(2,1)} %get-tuple-element.93), channel_id=1, source_target_pairs={{0,12},{1,13},{2,14},{3,15},{4,8},{5,9},{6,10},{7,11},{8,4},{9,5},... | collective-permute-start | bytes 172040 | tf_op jit(solution)/shard_map/ppermute | solution.py:23
  54.0 0.7 add_convert_fusion.6
  54.7 1.8 %collective-permute-start.18 = (bf16[16,1792]{1,0:T(8,128)(2,1)}, bf16[16,1792]{1,0:T(8,128)(2,1)}, u32[]{:S(2)}, u32[]{:S(2)}) collective-permute-start(bf16[16,1792]{1,0:T(8,128)(2,1)} %add_convert_fusion.6), channel_id=1, source_target_pairs={{0,4},{1,5},{2,6},{3,7},{4,0},{5,1},{6,2},{7,3},{8,12},{9,13},{10,... | collective-permute-start | bytes 172040 | tf_op jit(solution)/shard_map/ppermute | solution.py:23
  56.5 0.8 %reshape.9.gain_ref = f32[8,896]{1,0:T(8,128)S(1)} reshape(f32[7168]{0:T(1024)} %param.17) | data formatting | bytes 57344 | tf_op jit(solution)/shard_map/reshape | solution.py:346
  57.3 0.6 residual_rows.1.residual_ref
  57.9 1.3 %collective-permute-done.20.refs_2_ = bf16[16,1792]{1,0:T(8,128)(2,1)} collective-permute-done((bf16[16,1792]{1,0:T(8,128)(2,1)}, bf16[16,1792]{1,0:T(8,128)(2,1)}, u32[]{:S(2)}, u32[]{:S(2)}) %collective-permute-start.20) | collective-permute-done | bytes 57376 | tf_op jit(solution)/shard_map/ppermute | solution.py:23
  59.2 0.6 collective-permute-done.18.refs_0_
  59.7 0.9 %convert_add_fusion.sum_ref = f32[16,1792]{1,0:T(8,128)S(1)} fusion(bf16[32,1792]{1,0:T(8,128)(2,1)} %copy-done.12, bf16[32,3584]{1,0:T(8,128)(2,1)} %copy-done.11, bf16[64,3584]{1,0:T(8,128)(2,1)} %copy-done.10, bf16[64,3584]{1,0:T(8,128)(2,1)} %copy-done.5), kind=kLoop, calls=%fused_computation.4 | loop fusion | flops 200704 | bytes 344064 | tf_op jit(solution)/shard_map/add | solution.py:27
  60.7 0.0 collective-permute-done.21.refs_4_
  60.7 0.0 collective-permute-done.22.refs_6_
  60.7 1.4 %latent_parts.1 = (f32[8,640]{1,0:T(8,128)S(1)}, bf16[8,1792]{1,0:T(8,128)(2,1)S(1)}, bf16[8,3072]{1,0:T(8,128)(2,1)S(1)}) custom-call(s32[4]{0:T(128)S(1)} %pad_add_fusion.refs_0_.place_ref, f32[16,1792]{1,0:T(8,128)S(1)} %convert_add_fusion.sum_ref, f32[16,1792]{1,0:T(8,128)S(1)} %residual_rows.1.residual_ref, f32[8,896]{1,0:T(8,128)S(1)} %reshape.9.gain_ref, ...), custom_call_target="tpu_custom_call" | custom-call | tf_op jit(solution)/shard_map/latent_parts/pallas_call | solution.py:78
  62.1 1.0 %collective-permute-start.23 = (bf16[8,3072]{1,0:T(8,128)(2,1)S(1)}, bf16[8,3072]{1,0:T(8,128)(2,1)S(1)}, u32[]{:S(2)}, u32[]{:S(2)}) collective-permute-start(bf16[8,3072]{1,0:T(8,128)(2,1)S(1)} %get-tuple-element.87), channel_id=1, source_target_pairs={{0,2},{1,3},{2,0},{3,1},{4,6},{5,7},{6,4},{7,5},{8,10},{9,11},{10,... | collective-permute-start | bytes 147464 | tf_op jit(solution)/shard_map/ppermute | solution.py:23
  63.1 3.2 %collective-permute-done.23.in_ref = bf16[8,3072]{1,0:T(8,128)(2,1)S(1)} collective-permute-done((bf16[8,3072]{1,0:T(8,128)(2,1)S(1)}, bf16[8,3072]{1,0:T(8,128)(2,1)S(1)}, u32[]{:S(2)}, u32[]{:S(2)}) %collective-permute-start.23) | collective-permute-done | bytes 49184 | tf_op jit(solution)/shard_map/ppermute | solution.py:23
  66.2 0.6 turn.1
  66.8 1.0 %collective-permute-start.24 = (bf16[4,4864]{1,0:T(4,128)(2,1)S(1)}, bf16[4,4864]{1,0:T(4,128)(2,1)S(1)}, u32[]{:S(2)}, u32[]{:S(2)}) collective-permute-start(bf16[4,4864]{1,0:T(4,128)(2,1)S(1)} %get-tuple-element.90), channel_id=1, source_target_pairs={{0,8},{1,9},{2,10},{3,11},{4,12},{5,13},{6,14},{7,15},{8,0},{9,1},... | collective-permute-start | bytes 116744 | tf_op jit(solution)/shard_map/ppermute | solution.py:23
  67.8 3.9 %collective-permute-done.24.in_ref = bf16[4,4864]{1,0:T(4,128)(2,1)S(1)} collective-permute-done((bf16[4,4864]{1,0:T(4,128)(2,1)S(1)}, bf16[4,4864]{1,0:T(4,128)(2,1)S(1)}, u32[]{:S(2)}, u32[]{:S(2)}) %collective-permute-start.24) | collective-permute-done | bytes 38944 | tf_op jit(solution)/shard_map/ppermute | solution.py:23
  71.8 1.8 %finish.1 = (bf16[4,7168]{1,0:T(4,128)(2,1)}, bf16[4,576]{1,0:T(4,128)(2,1)}, bf16[4,64,512]{2,1,0:T(8,128)(2,1)}) custom-call(s32[4]{0:T(128)S(1)} %pad_add_fusion.refs_0_.place_ref, f32[4,640]{1,0:T(4,128)S(1)} %get-tuple-element.88.sums_ref, bf16[4,3584]{1,0:T(4,128)(2,1)S(1)} %get-tuple-element.89.moe_ref, ...), custom_call_target="tpu_custom_call" | custom-call | tf_op jit(solution)/shard_map/finish/pallas_call | solution.py:78
  (33 shorter events, 0.1 us)
Async XLA Ops:
  0.6 0.8 %copy-start.6 = (bf16[4,7168]{1,0:T(4,128)(2,1)S(1)}, bf16[4,7168]{1,0:T(4,128)(2,1)}, u32[]{:S(2)}) copy-start(bf16[4,7168]{1,0:T(4,128)(2,1)} %x_ref.1) | copy-start | bytes 172036
  1.5 0.7 copy-start.7
  2.1 0.7 copy-start.8
  2.9 6.9 %collective-permute-start = (bf16[4,7296]{1,0:T(4,128)(2,1)S(1)}, bf16[4,7296]{1,0:T(4,128)(2,1)S(1)}, u32[]{:S(2)}, u32[]{:S(2)}) collective-permute-start(bf16[4,7296]{1,0:T(4,128)(2,1)S(1)} %with_info.1.refs_0_), channel_id=1, source_target_pairs={{0,8},{1,9},{2,10},{3,11},{4,12},{5,13},{6,14},{7,15},{8,0},{9,1},... | collective-permute-start | bytes 175112 | tf_op jit(solution)/shard_map/ppermute | solution.py:23
  6.9 4.2 %collective-permute-start.1 = (bf16[4,7296]{1,0:T(4,128)(2,1)S(1)}, bf16[4,7296]{1,0:T(4,128)(2,1)S(1)}, u32[]{:S(2)}, u32[]{:S(2)}) collective-permute-start(bf16[4,7296]{1,0:T(4,128)(2,1)S(1)} %with_info.1.refs_0_), channel_id=1, source_target_pairs={{0,4},{1,5},{2,6},{3,7},{4,0},{5,1},{6,2},{7,3},{8,12},{9,13},{10,... | collective-permute-start | bytes 175112 | tf_op jit(solution)/shard_map/ppermute | solution.py:23
  8.5 6.0 %collective-permute-start.2 = (bf16[4,7296]{1,0:T(4,128)(2,1)S(1)}, bf16[4,7296]{1,0:T(4,128)(2,1)S(1)}, u32[]{:S(2)}, u32[]{:S(2)}) collective-permute-start(bf16[4,7296]{1,0:T(4,128)(2,1)S(1)} %with_info.1.refs_0_), channel_id=1, source_target_pairs={{0,12},{1,13},{2,14},{3,15},{4,8},{5,9},{6,10},{7,11},{8,4},{9,5},... | collective-permute-start | bytes 175112 | tf_op jit(solution)/shard_map/ppermute | solution.py:23
  14.6 4.9 %collective-permute-start.7 = (bf16[16,3712]{1,0:T(8,128)(2,1)S(1)}, bf16[16,3712]{1,0:T(8,128)(2,1)S(1)}, u32[]{:S(2)}, u32[]{:S(2)}) collective-permute-start(bf16[16,3712]{1,0:T(8,128)(2,1)S(1)} %get-tuple-element.51), channel_id=1, source_target_pairs={{0,16},{16,0},{1,17},{17,1},{2,18},{18,2},{3,19},{19,3},{4,20},{20... | collective-permute-start | bytes 356360 | tf_op jit(solution)/shard_map/ppermute | solution.py:21
  16.1 6.0 %collective-permute-start.3 = (bf16[16,3584]{1,0:T(8,128)(2,1)S(1)}, bf16[16,3584]{1,0:T(8,128)(2,1)S(1)}, u32[]{:S(2)}, u32[]{:S(2)}) collective-permute-start(bf16[16,3584]{1,0:T(8,128)(2,1)S(1)} %get-tuple-element.50), channel_id=1, source_target_pairs={{0,2},{1,3},{2,0},{3,1},{4,6},{5,7},{6,4},{7,5},{8,10},{9,11},{10,... | collective-permute-start | bytes 344072 | tf_op jit(solution)/shard_map/ppermute | solution.py:23
  17.7 17.6 %collective-permute-start.11 = (bf16[448,576]{1,0:T(8,128)(2,1)}, bf16[448,576]{1,0:T(8,128)(2,1)S(1)}, u32[]{:S(2)}, u32[]{:S(2)}) collective-permute-start(bf16[448,576]{1,0:T(8,128)(2,1)} %refs_3_.1), channel_id=1, source_target_pairs={{0,4},{1,5},{2,6},{3,7},{4,0},{5,1},{6,2},{7,3},{8,12},{9,13},{10,... | collective-permute-start | bytes 1548296 | tf_op jit(solution)/shard_map/ppermute | solution.py:23
  19.5 6.2 %collective-permute-start.8 = (bf16[32,3712]{1,0:T(8,128)(2,1)S(1)}, bf16[32,3712]{1,0:T(8,128)(2,1)S(1)}, u32[]{:S(2)}, u32[]{:S(2)}) collective-permute-start(bf16[32,3712]{1,0:T(8,128)(2,1)S(1)} %constant_dynamic-update-slice_fusion.2.refs_5_.b_ref), channel_id=1, source_target_pairs={{0,2},{1,3},{2,0},{3,1},{4,6},{5,7},{6,4},{7,5},{8,10},{9,11},{10,... | collective-permute-start | bytes 712712 | tf_op jit(solution)/shard_map/ppermute | solution.py:23
  22.1 6.1 %collective-permute-start.4 = (bf16[32,3584]{1,0:T(8,128)(2,1)S(1)}, bf16[32,3584]{1,0:T(8,128)(2,1)S(1)}, u32[]{:S(2)}, u32[]{:S(2)}) collective-permute-start(bf16[32,3584]{1,0:T(8,128)(2,1)S(1)} %constant_dynamic-update-slice_fusion.refs_1_.a_ref), channel_id=1, source_target_pairs={{0,16},{16,0},{1,17},{17,1},{2,18},{18,2},{3,19},{19,3},{4,20},{20... | collective-permute-start | bytes 688136 | tf_op jit(solution)/shard_map/ppermute | solution.py:21
  22.6 5.7 %collective-permute-start.9 = (bf16[32,3712]{1,0:T(8,128)(2,1)S(1)}, bf16[32,3712]{1,0:T(8,128)(2,1)S(1)}, u32[]{:S(2)}, u32[]{:S(2)}) collective-permute-start(bf16[32,3712]{1,0:T(8,128)(2,1)S(1)} %constant_dynamic-update-slice_fusion.2.refs_5_.b_ref), channel_id=1, source_target_pairs={{0,1},{1,0},{2,3},{3,2},{4,5},{5,4},{6,7},{7,6},{8,9},{9,8},{10,11... | collective-permute-start | bytes 712712 | tf_op jit(solution)/shard_map/ppermute | solution.py:23
  25.6 4.1 %collective-permute-start.10 = (bf16[32,3712]{1,0:T(8,128)(2,1)S(1)}, bf16[32,3712]{1,0:T(8,128)(2,1)S(1)}, u32[]{:S(2)}, u32[]{:S(2)}) collective-permute-start(bf16[32,3712]{1,0:T(8,128)(2,1)S(1)} %collective-permute-done.8.refs_6_.low_ref), channel_id=1, source_target_pairs={{0,1},{1,0},{2,3},{3,2},{4,5},{5,4},{6,7},{7,6},{8,9},{9,8},{10,11... | collective-permute-start | bytes 712712 | tf_op jit(solution)/shard_map/ppermute | solution.py:23
  25.6 2.7 %collective-permute-start.5 = (bf16[32,3584]{1,0:T(8,128)(2,1)S(1)}, bf16[32,3584]{1,0:T(8,128)(2,1)S(1)}, u32[]{:S(2)}, u32[]{:S(2)}) collective-permute-start(bf16[32,3584]{1,0:T(8,128)(2,1)S(1)} %constant_dynamic-update-slice_fusion.refs_1_.a_ref), channel_id=1, source_target_pairs={{0,1},{1,0},{2,3},{3,2},{4,5},{5,4},{6,7},{7,6},{8,9},{9,8},{10,11... | collective-permute-start | bytes 688136 | tf_op jit(solution)/shard_map/ppermute | solution.py:23
  28.2 1.5 %collective-permute-start.6 = (bf16[32,3584]{1,0:T(8,128)(2,1)S(1)}, bf16[32,3584]{1,0:T(8,128)(2,1)S(1)}, u32[]{:S(2)}, u32[]{:S(2)}) collective-permute-start(bf16[32,3584]{1,0:T(8,128)(2,1)S(1)} %collective-permute-done.4.refs_2_), channel_id=1, source_target_pairs={{0,1},{1,0},{2,3},{3,2},{4,5},{5,4},{6,7},{7,6},{8,9},{9,8},{10,11... | collective-permute-start | bytes 688136 | tf_op jit(solution)/shard_map/ppermute | solution.py:23
  28.3 10.9 %copy-start = (bf16[4,64,576]{2,1,0:T(8,128)(2,1)S(1)}, bf16[4,64,576]{2,1,0:T(8,128)(2,1)}, u32[]{:S(2)}) copy-start(bf16[4,64,576]{2,1,0:T(8,128)(2,1)} %q_ref.3) | copy-start | bytes 884740
  28.3 10.9 %copy-start.1 = (bf16[4,256,576]{1,2,0:T(8,128)(2,1)S(1)}, bf16[4,256,576]{1,2,0:T(8,128)(2,1)}, u32[]{:S(2)}) copy-start(bf16[4,256,576]{1,2,0:T(8,128)(2,1)} %param.20) | copy-start | bytes 3538948
  28.3 10.9 %copy-start.9 = (s32[4]{0:T(128)S(1)}, s32[4]{0:T(128)}, u32[]{:S(2)}) copy-start(s32[4]{0:T(128)} %lengths_ref.1) | copy-start | bytes 52
  35.2 18.8 %copy-start.5 = (bf16[64,3584]{1,0:T(8,128)(2,1)}, bf16[64,3584]{1,0:T(8,128)(2,1)S(1)}, u32[]{:S(2)}) copy-start(bf16[64,3584]{1,0:T(8,128)(2,1)S(1)} %get-tuple-element.77) | copy-start | bytes 1376260
  35.3 12.4 %copy-start.2 = (bf16[448,576]{1,0:T(8,128)(2,1)S(1)}, bf16[448,576]{1,0:T(8,128)(2,1)}, u32[]{:S(2)}) copy-start(bf16[448,576]{1,0:T(8,128)(2,1)} %refs_3_.1) | copy-start | bytes 1548292
  35.3 1.9 %collective-permute-start.14 = (bf16[64,3584]{1,0:T(8,128)(2,1)S(1)}, bf16[64,3584]{1,0:T(8,128)(2,1)S(1)}, u32[]{:S(2)}, u32[]{:S(2)}) collective-permute-start(bf16[64,3584]{1,0:T(8,128)(2,1)S(1)} %get-tuple-element.60), channel_id=1, source_target_pairs={{0,1},{1,0},{2,3},{3,2},{4,5},{5,4},{6,7},{7,6},{8,9},{9,8},{10,11... | collective-permute-start | bytes 1376264 | tf_op jit(solution)/shard_map/ppermute | solution.py:23
  35.5 3.3 %collective-permute-start.12 = (bf16[64,3584]{1,0:T(8,128)(2,1)S(1)}, bf16[64,3584]{1,0:T(8,128)(2,1)S(1)}, u32[]{:S(2)}, u32[]{:S(2)}) collective-permute-start(bf16[64,3584]{1,0:T(8,128)(2,1)S(1)} %get-tuple-element.58), channel_id=1, source_target_pairs={{0,1},{1,0},{2,3},{3,2},{4,5},{5,4},{6,7},{7,6},{8,9},{9,8},{10,11... | collective-permute-start | bytes 1376264 | tf_op jit(solution)/shard_map/ppermute | solution.py:23
  37.2 7.7 %collective-permute-start.15 = (bf16[64,1792]{1,0:T(8,128)(2,1)S(1)}, bf16[64,1792]{1,0:T(8,128)(2,1)S(1)}, u32[]{:S(2)}, u32[]{:S(2)}) collective-permute-start(bf16[64,1792]{1,0:T(8,128)(2,1)S(1)} %add_convert_fusion), channel_id=1, source_target_pairs={{0,2},{1,3},{2,0},{3,1},{4,6},{5,7},{6,4},{7,5},{8,10},{9,11},{10,... | collective-permute-start | bytes 688136 | tf_op jit(solution)/shard_map/ppermute | solution.py:23
  38.8 15.9 %copy-start.10 = (bf16[64,3584]{1,0:T(8,128)(2,1)}, bf16[64,3584]{1,0:T(8,128)(2,1)S(1)}, u32[]{:S(2)}) copy-start(bf16[64,3584]{1,0:T(8,128)(2,1)S(1)} %collective-permute-done.12) | copy-start | bytes 1376260
  38.9 7.4 %collective-permute-start.13 = (bf16[32,3584]{1,0:T(8,128)(2,1)S(1)}, bf16[32,3584]{1,0:T(8,128)(2,1)S(1)}, u32[]{:S(2)}, u32[]{:S(2)}) collective-permute-start(bf16[32,3584]{1,0:T(8,128)(2,1)S(1)} %add_convert_fusion.1), channel_id=1, source_target_pairs={{0,16},{16,0},{1,17},{17,1},{2,18},{18,2},{3,19},{19,3},{4,20},{20... | collective-permute-start | bytes 688136 | tf_op jit(solution)/shard_map/ppermute | solution.py:21
  40.9 0.8 %copy-start.3 = (f32[4,64,512]{2,1,0:T(8,128)}, f32[4,64,512]{2,1,0:T(8,128)S(1)}, u32[]{:S(2)}) copy-start(f32[4,64,512]{2,1,0:T(8,128)S(1)} %get-tuple-element.92.part_ref) | copy-start | bytes 1572868
  46.3 8.4 %copy-start.11 = (bf16[32,3584]{1,0:T(8,128)(2,1)}, bf16[32,3584]{1,0:T(8,128)(2,1)S(1)}, u32[]{:S(2)}) copy-start(bf16[32,3584]{1,0:T(8,128)(2,1)S(1)} %collective-permute-done.13) | copy-start | bytes 688132
  46.4 4.9 %collective-permute-start.17 = (bf16[32,1792]{1,0:T(8,128)(2,1)S(1)}, bf16[32,1792]{1,0:T(8,128)(2,1)S(1)}, u32[]{:S(2)}, u32[]{:S(2)}) collective-permute-start(bf16[32,1792]{1,0:T(8,128)(2,1)S(1)} %add_convert_fusion.2), channel_id=1, source_target_pairs={{0,16},{16,0},{1,17},{17,1},{2,18},{18,2},{3,19},{19,3},{4,20},{20... | collective-permute-start | bytes 344072 | tf_op jit(solution)/shard_map/ppermute | solution.py:21
  46.8 4.9 %collective-permute-start.16 = (bf16[32,1792]{1,0:T(8,128)(2,1)S(1)}, bf16[32,1792]{1,0:T(8,128)(2,1)S(1)}, u32[]{:S(2)}, u32[]{:S(2)}) collective-permute-start(bf16[32,1792]{1,0:T(8,128)(2,1)S(1)} %add_convert_fusion.3), channel_id=1, source_target_pairs={{0,2},{1,3},{2,0},{3,1},{4,6},{5,7},{6,4},{7,5},{8,10},{9,11},{10,... | collective-permute-start | bytes 344072 | tf_op jit(solution)/shard_map/ppermute | solution.py:23
  47.6 13.0 %collective-permute-start.21 = (bf16[448,576]{1,0:T(8,128)(2,1)S(1)}, bf16[448,576]{1,0:T(8,128)(2,1)S(1)}, u32[]{:S(2)}, u32[]{:S(2)}) collective-permute-start(bf16[448,576]{1,0:T(8,128)(2,1)S(1)} %copy-done.2), channel_id=1, source_target_pairs={{0,1},{1,0},{2,3},{3,2},{4,5},{5,4},{6,7},{7,6},{8,9},{9,8},{10,11... | collective-permute-start | bytes 1548296 | tf_op jit(solution)/shard_map/ppermute | solution.py:23
  47.6 13.0 %collective-permute-start.22 = (bf16[448,576]{1,0:T(8,128)(2,1)S(1)}, bf16[448,576]{1,0:T(8,128)(2,1)S(1)}, u32[]{:S(2)}, u32[]{:S(2)}) collective-permute-start(bf16[448,576]{1,0:T(8,128)(2,1)S(1)} %collective-permute-done.11.refs_5_), channel_id=1, source_target_pairs={{0,1},{1,0},{2,3},{3,2},{4,5},{5,4},{6,7},{7,6},{8,9},{9,8},{10,11... | collective-permute-start | bytes 1548296 | tf_op jit(solution)/shard_map/ppermute | solution.py:23
  51.6 3.1 %copy-start.12 = (bf16[32,1792]{1,0:T(8,128)(2,1)}, bf16[32,1792]{1,0:T(8,128)(2,1)S(1)}, u32[]{:S(2)}) copy-start(bf16[32,1792]{1,0:T(8,128)(2,1)S(1)} %collective-permute-done.16) | copy-start | bytes 344068
  52.3 5.6 %collective-permute-start.19 = (bf16[16,1792]{1,0:T(8,128)(2,1)}, bf16[16,1792]{1,0:T(8,128)(2,1)S(1)}, u32[]{:S(2)}, u32[]{:S(2)}) collective-permute-start(bf16[16,1792]{1,0:T(8,128)(2,1)} %get-tuple-element.94), channel_id=1, source_target_pairs={{0,8},{1,9},{2,10},{3,11},{4,12},{5,13},{6,14},{7,15},{8,0},{9,1},... | collective-permute-start | bytes 172040 | tf_op jit(solution)/shard_map/ppermute | solution.py:23
  52.8 6.3 %collective-permute-start.20 = (bf16[16,1792]{1,0:T(8,128)(2,1)}, bf16[16,1792]{1,0:T(8,128)(2,1)}, u32[]{:S(2)}, u32[]{:S(2)}) collective-permute-start(bf16[16,1792]{1,0:T(8,128)(2,1)} %get-tuple-element.93), channel_id=1, source_target_pairs={{0,12},{1,13},{2,14},{3,15},{4,8},{5,9},{6,10},{7,11},{8,4},{9,5},... | collective-permute-start | bytes 172040 | tf_op jit(solution)/shard_map/ppermute | solution.py:23
  54.7 5.0 %collective-permute-start.18 = (bf16[16,1792]{1,0:T(8,128)(2,1)}, bf16[16,1792]{1,0:T(8,128)(2,1)}, u32[]{:S(2)}, u32[]{:S(2)}) collective-permute-start(bf16[16,1792]{1,0:T(8,128)(2,1)} %add_convert_fusion.6), channel_id=1, source_target_pairs={{0,4},{1,5},{2,6},{3,7},{4,0},{5,1},{6,2},{7,3},{8,12},{9,13},{10,... | collective-permute-start | bytes 172040 | tf_op jit(solution)/shard_map/ppermute | solution.py:23
  57.3 14.5 %copy-start.4 = (f32[4,64,512]{2,1,0:T(8,128)S(1)}, f32[4,64,512]{2,1,0:T(8,128)}, u32[]{:S(2)}) copy-start(f32[4,64,512]{2,1,0:T(8,128)} %copy-done.3) | copy-start | bytes 1572868
  62.1 4.2 %collective-permute-start.23 = (bf16[8,3072]{1,0:T(8,128)(2,1)S(1)}, bf16[8,3072]{1,0:T(8,128)(2,1)S(1)}, u32[]{:S(2)}, u32[]{:S(2)}) collective-permute-start(bf16[8,3072]{1,0:T(8,128)(2,1)S(1)} %get-tuple-element.87), channel_id=1, source_target_pairs={{0,2},{1,3},{2,0},{3,1},{4,6},{5,7},{6,4},{7,5},{8,10},{9,11},{10,... | collective-permute-start | bytes 147464 | tf_op jit(solution)/shard_map/ppermute | solution.py:23
  66.8 4.9 %collective-permute-start.24 = (bf16[4,4864]{1,0:T(4,128)(2,1)S(1)}, bf16[4,4864]{1,0:T(4,128)(2,1)S(1)}, u32[]{:S(2)}, u32[]{:S(2)}) collective-permute-start(bf16[4,4864]{1,0:T(4,128)(2,1)S(1)} %get-tuple-element.90), channel_id=1, source_target_pairs={{0,8},{1,9},{2,10},{3,11},{4,12},{5,13},{6,14},{7,15},{8,0},{9,1},... | collective-permute-start | bytes 116744 | tf_op jit(solution)/shard_map/ppermute | solution.py:23

commit v4 on v3

--- a/solution.py
+++ b/solution.py
@@ -9,6 +9,7 @@
 KV = 512
 LANES = 128
 CHUNK = 512
+COLS = 896
 CORE, LOW, MID, HIGH = 0, 1, 2, 3
 
 
@@ -21,6 +22,12 @@
         return lax.ppermute(x, "sec", [(i, i ^ 1) for i in range(lax.axis_size("sec"))])
     flips = sum(1 << bit for bit in bits)
     return lax.ppermute(x, "dev", [(i, i ^ flips) for i in range(lax.axis_size("dev"))])
+
+
+def swap_both(x, bit):
+    size = lax.axis_size("dev")
+    pairs = [(i, i ^ (1 << bit) ^ size) for i in range(2 * size)]
+    return lax.ppermute(x, ("sec", "dev"), pairs)
 
 
 def wide_total(*parts):
@@ -86,33 +93,14 @@
     )(scalars, *arrays)
 
 
-def info_kernel(_, x_ref, ids_ref, scores_ref, out_ref):
-    (rows, width), picks = x_ref.shape, ids_ref.shape[0]
-    out_ref[:, :width] = x_ref[...]
-    lane = lax.broadcasted_iota(jnp.int32, (rows, LANES), 1)
-    row = lax.broadcasted_iota(jnp.int32, (rows, rows), 0)
-    here = row == lax.broadcasted_iota(jnp.int32, (rows, rows), 1)
-    info = jnp.zeros((rows, LANES), jnp.float32)
-    for i, values in enumerate((ids_ref[...], scores_ref[...])):
-        values = values.astype(jnp.float32)
+def with_info(hidden_in, expert_ids, gate_scores):
+    width, picks = hidden_in.shape[1], expert_ids.shape[1]
+    x = jnp.pad(hidden_in, ((0, 0), (0, LANES)))
+    column = lax.broadcasted_iota(jnp.int32, x.shape, 1) - width
+    for i, values in enumerate((expert_ids.astype(x.dtype), gate_scores)):
         for k in range(picks):
-            column = jnp.sum(jnp.where(here, values[k : k + 1], 0.0), axis=1, keepdims=True)
-            info = jnp.where(lane == i * picks + k, column, info)
-    out_ref[:, width:] = info.astype(out_ref.dtype)
-
-
-def with_info(hidden_in, expert_ids, gate_scores):
-    rows, width = hidden_in.shape
-    return kernel_call(
-        info_kernel,
-        jax.ShapeDtypeStruct((rows, width + LANES), hidden_in.dtype),
-        jnp.zeros((1,), jnp.int32),
-        hidden_in,
-        expert_ids.T,
-        gate_scores.T,
-        name="with_info",
-        mib=2,
-    )
+            x = jnp.where(column == i * picks + k, values[:, k : k + 1], x)
+    return x
 
 
 def pack_kernel(_, *refs):
@@ -154,7 +142,8 @@
     for part in (pl.ds(0, half), pl.ds(half, half)):
         moves.append((w_refs[0].at[part], gate_ref.at[part]))
         moves.append((w_refs[1].at[part], up_ref.at[part]))
-    for part in (pl.ds(0, half), pl.ds(half, half)):
+    for flip in range(2):
+        part = pl.ds(pl.multiple_of((place_ref[2] ^ flip) * half, LANES), half)
         moves.append((w_refs[2].at[:, part], down_ref.at[:, part]))
     copies = [pltpu.make_async_copy(*move, sems.at[i]) for i, move in enumerate(moves)]
     for copy in copies:
@@ -199,16 +188,16 @@
             up_act += jnp.dot(x, up_ref[depth, :], preferred_element_type=jnp.float32)
     hidden = ordered(gate_act / (1.0 + jnp.exp(-gate_act)) * up_act).astype(jnp.bfloat16)
     share = ordered(jnp.broadcast_to(share, (rows, LANES)))[:, :1]
-    copies[4].wait()
-    copies[5].wait()
     block = half // 4
-    for part in range(2):
-        kept, sent = outs[2 * part : 2 * part + 2]
-        for i in range(4):
-            flip, mid = i // 2, i % 2
-            first = (place_ref[2] ^ part) * half + mid * 2 * block + (place_ref[1] ^ flip) * block
-            for c in range(0, block, CHUNK):
-                wide = min(CHUNK, block - c)
+    for flip in range(2):
+        copies[4 + flip].wait()
+        for j in range(4):
+            part, mid = j // 2, j % 2
+            i = 2 * flip + mid
+            kept, sent = outs[2 * part : 2 * part + 2]
+            first = (place_ref[2] ^ flip) * half + mid * 2 * block + (place_ref[1] ^ part) * block
+            for c in range(0, block, COLS):
+                wide = min(COLS, block - c)
                 cols = pl.ds(pl.multiple_of(first + c, LANES), wide)
                 partial = jnp.dot(hidden, down_ref[:, cols], preferred_element_type=jnp.float32)
                 partial = (partial * share).astype(jnp.bfloat16)
@@ -237,20 +226,22 @@
 
 def scatter_rows(keep_a, send_a, keep_b, send_b, late):
     rows, cols = keep_a.shape[0] // 2, keep_a.shape[1] // 2
-    left, right = slice(0, cols), slice(cols, None)
-    a, b = [keep_a, swap(send_a, CORE)], [keep_b, swap(send_b, CORE)]
-    a.append(swap(total(*(v[rows:] for v in a)), "sec"))
-    b.append(swap(total(*(v[:, right] for v in b)), LOW))
-    a, b, late = lax.optimization_barrier((a, b, late))
-    a.append(swap(total(*(v[:rows, right] for v in a)), LOW))
-    b.append(swap(total(*(v[rows:, left] for v in b)), "sec"))
-    a, b = lax.optimization_barrier((a, b))
+    here, there, left, right = slice(0, rows), slice(rows, None), slice(0, cols), slice(cols, None)
+    b = [keep_b, swap(send_b, CORE)]
+    a = [keep_a, swap(send_a, CORE)]
+    ins = [
+        swap(total(*(v[here] for v in b)), LOW),
+        swap(total(*(v[there] for v in a)), "sec"),
+        swap_both(total(*(v[there] for v in b)), LOW),
+    ]
+    a, ins, late = lax.optimization_barrier((a, ins, late))
+    a += ins
     rows //= 2
     here, there = slice(0, rows), slice(rows, 2 * rows)
     ins = (
+        swap(total(*(v[here, right] for v in a)), HIGH),
+        swap(total(*(v[there, right] for v in a)), MID, HIGH),
         swap(total(*(v[there, left] for v in a)), MID),
-        swap(total(*(v[here, left] for v in b)), HIGH),
-        swap(total(*(v[there, left] for v in b)), MID, HIGH),
     )
     a, ins = lax.optimization_barrier((a, ins))
     return wide_total(*(v[here, left] for v in a)), ins, late
@@ -288,6 +279,9 @@
     )
 
 
+OTHERS = ((1, 0), (0, 1), (1, 1))
+
+
 def put_split(ref, first, apart, x):
     cols = x.shape[1]
     upper = x.astype(jnp.bfloat16)
@@ -303,16 +297,19 @@
 
 def latent_kernel(place_ref, sum_ref, residual_ref, gain_ref, *refs):
     in_refs, w_refs = refs[:3], refs[3:7]
-    sums_ref, moe_ref, out_ref, piece_ref = refs[7:]
+    sums_ref, moe_ref, piece_ref = refs[7], refs[8], refs[12]
     rows, cols = sum_ref.shape
-    block, n = cols // 2, rows // 2
+    block, n = cols // 2, rows // 4
     piece, lat = w_refs[0].shape
-    odd = place_ref[1] == 1
+
+
+    def rows_for(x, low, high):
+        x = jnp.where(place_ref[1] == 1 - low, x[2 * n :], x[: 2 * n])
+        return jnp.where(place_ref[2] == 1 - high, x[n:], x[:n])
+
     mixture = sum_ref[...] + wide_total(*(ref[...] for ref in in_refs))
     moe = (residual_ref[...] + mixture).astype(jnp.bfloat16)
     widened = moe.astype(jnp.float32)
-    moe_ref[...] = jnp.where(odd, widened[n:], widened[:n]).astype(jnp.bfloat16)
-    out_ref[:, :cols] = jnp.where(odd, widened[:n], widened[n:]).astype(jnp.bfloat16)
     for mid in range(2):
         gain = gain_ref[pl.ds(4 * place_ref[2] + 2 * mid + place_ref[1], 1), :]
         scaled = widened[:, mid * block : (mid + 1) * block] * gain
@@ -325,84 +322,57 @@
     squares = jnp.sum(widened * widened, axis=1, keepdims=True)
     tail = jnp.broadcast_to(squares, (rows, LANES))
     wide = sums_ref.shape[1]
-    for to, x in ((slice(0, lat), sums), (slice(lat, wide), tail[:, : wide - lat])):
-        sums_ref[:, to] = jnp.where(odd, x[n:], x[:n])
-        put_split(out_ref, cols + to.start, wide, jnp.where(odd, x[:n], x[n:]))
+    tail = tail[:, : wide - lat]
+    moe_ref[...] = rows_for(widened, 0, 0).astype(jnp.bfloat16)
+    sums_ref[:, :lat] = rows_for(sums, 0, 0)
+    sums_ref[:, lat:] = rows_for(tail, 0, 0)
+    for (low, high), ref in zip(OTHERS, refs[9:12]):
+        ref[:, :cols] = rows_for(widened, low, high).astype(jnp.bfloat16)
+        put_split(ref, cols, wide, rows_for(sums, low, high))
+        put_split(ref, cols + lat, wide, rows_for(tail, low, high))
 
 
 def latent_parts(place, kept, received, residual, gain, slices):
     rows, cols = kept.shape
     piece, lat = slices[0].shape
     padded = -(-(lat + 1) // LANES) * LANES
-    sums = jax.ShapeDtypeStruct((rows // 2, padded), jnp.float32)
-    moe = jax.ShapeDtypeStruct((rows // 2, cols), jnp.bfloat16)
-    sent = jax.ShapeDtypeStruct((rows // 2, cols + 2 * padded), jnp.bfloat16)
+    sums = jax.ShapeDtypeStruct((rows // 4, padded), jnp.float32)
+    moe = jax.ShapeDtypeStruct((rows // 4, cols), jnp.bfloat16)
+    sent = jax.ShapeDtypeStruct((rows // 4, cols + 2 * padded), jnp.bfloat16)
     return kernel_call(
         latent_kernel,
-        (sums, moe, sent),
+        (sums, moe, sent, sent, sent),
         place,
         kept,
         residual,
-        gain.reshape(8, cols // 2),
+        gain,
         *received,
         *slices,
         name="latent_parts",
-        mib=12,
+        mib=32,
         scratch=[pltpu.VMEM((4, rows, piece), jnp.float32)],
     )
 
 
-def turn_kernel(place_ref, sums_ref, moe_ref, in_ref, sums_out, moe_out, send_ref):
-    rows, cols = moe_ref.shape
-    n, wide = rows // 2, sums_ref.shape[1]
-    upper = place_ref[2] == 1
-    sums = sums_ref[...] + get_split(in_ref, cols, wide)
-    sums_out[...] = jnp.where(upper, sums[n:], sums[:n])
-    put_split(send_ref, 2 * cols, wide, jnp.where(upper, sums[:n], sums[n:]))
-    for first, x in ((0, moe_ref[...]), (cols, in_ref[:, :cols])):
-        x = x.astype(jnp.float32)
-        to = slice(first, first + cols)
-        moe_out[:, to] = jnp.where(upper, x[n:], x[:n]).astype(jnp.bfloat16)
-        send_ref[:, to] = jnp.where(upper, x[:n], x[n:]).astype(jnp.bfloat16)
-
-
-def turn(place, sums, moe, received):
-    (rows, cols), wide = moe.shape, sums.shape[1]
-    return kernel_call(
-        turn_kernel,
-        (
-            jax.ShapeDtypeStruct((rows // 2, wide), sums.dtype),
-            jax.ShapeDtypeStruct((rows // 2, 2 * cols), moe.dtype),
-            jax.ShapeDtypeStruct((rows // 2, 2 * cols + 2 * wide), moe.dtype),
-        ),
-        place,
-        sums,
-        moe,
-        received,
-        name="turn",
-        mib=2,
-    )
-
-
-def put_rows(place_ref, keep_ref, in_ref, out_ref):
-    half = keep_ref.shape[1]
-    block = half // 4
-    upper, odd = place_ref[2] == 1, place_ref[1] == 1
-    for part, ref, other in ((0, keep_ref, in_ref), (1, in_ref, keep_ref)):
-        x = jnp.where(upper, other[:, :half], ref[:, :half])
-        for mid in range(2):
-            even = x[:, mid * block : (mid + 1) * block]
-            uneven = x[:, (2 + mid) * block : (3 + mid) * block]
-            first = part * half + mid * 2 * block
-            out_ref[:, first : first + block] = jnp.where(odd, uneven, even)
-            out_ref[:, first + block : first + 2 * block] = jnp.where(odd, even, uneven)
-
-
-def finish_kernel(place_ref, sums_ref, moe_ref, in_ref, q_ref, stats_ref, part_ref, *outs):
-    moe_out, latent_ref, out_ref = outs
-    lat, half = q_ref.shape[2], moe_ref.shape[1]
-    sums = sums_ref[...] + get_split(in_ref, half, sums_ref.shape[1])
-    inverse = lax.rsqrt(sums[:, lat : lat + 1] / (2 * half) + norm_eps)
+def put_rows(place_ref, blocks, out_ref):
+    cols = blocks[0][0].shape[1]
+    block = cols // 2
+    for high in range(2):
+        parts = [jnp.where(place_ref[2] == high, x[0], x[1]) for x in blocks]
+        for low in range(2):
+            x = jnp.where(place_ref[1] == low, parts[0], parts[1])
+            for mid in range(2):
+                first = 2 * high * cols + mid * cols + low * block
+                out_ref[:, first : first + block] = x[:, mid * block : (mid + 1) * block]
+
+
+def finish_kernel(place_ref, sums_ref, moe_ref, q_ref, stats_ref, part_ref, *refs):
+    in_refs, (moe_out, latent_ref, out_ref) = refs[:3], refs[3:]
+    lat, cols = q_ref.shape[2], moe_ref.shape[1]
+    sums = sums_ref[...]
+    for ref in in_refs:
+        sums += get_split(ref, cols, sums_ref.shape[1])
+    inverse = lax.rsqrt(sums[:, lat : lat + 1] / (4 * cols) + norm_eps)
     rounded = (sums[:, :lat] * inverse).astype(jnp.bfloat16)
     latent_ref[...] = rounded
     latent = rounded.astype(jnp.float32)
@@ -417,22 +387,23 @@
         own_prob = (own_weight * scale).astype(jnp.bfloat16).astype(jnp.float32)
         value = part_ref[row] * (shrink * scale) + own_prob * own[:, :KV]
         out_ref[row] = value.astype(jnp.bfloat16)
-    put_rows(place_ref, moe_ref, in_ref, moe_out)
+    other_low, other_high, other_both = (ref[:, :cols] for ref in in_refs)
+    put_rows(place_ref, ((moe_ref[...], other_high), (other_low, other_both)), moe_out)
 
 
 def finish(place, sums, moe, received, queries, stats, combined):
     rows, heads, lat = queries.shape
-    outs = ((rows, 2 * moe.shape[1]), (rows, lat), (rows, heads, KV))
+    outs = ((rows, 4 * moe.shape[1]), (rows, lat), (rows, heads, KV))
     return kernel_call(
         finish_kernel,
         tuple(jax.ShapeDtypeStruct(shape, jnp.bfloat16) for shape in outs),
         place,
         sums,
         moe,
-        received,
         queries,
         stats,
         combined,
+        *received,
         name="finish",
         mib=8,
     )
@@ -463,12 +434,17 @@
     a_all, b_all, w_mid = gather_rows(hidden_in, expert_ids, gate_scores, w_kv)
     partial = experts(place, a_all, b_all, picks, w_gate, w_up, w_down)
     partial, w_mid = lax.optimization_barrier((partial, w_mid))
-    kept, received, (stats, combined) = scatter_rows(*partial, cache)
+    kept, received, late = scatter_rows(*partial, (cache,))
+    (cache,) = late
+    stats, combined = cache
+    residual = residual_rows(place, a_all[0], b_all[0], b_all[1])
+    gain = norm_gain.reshape(8, -1)
     slices = (w_kv, swap(w_kv, CORE), w_mid, swap(w_mid, CORE))
-    residual = residual_rows(place, a_all[0], b_all[0], b_all[1])
-    sums, moe, sent = latent_parts(place, kept, received, residual, norm_gain, slices)
-    sums, moe, sent = turn(place, sums, moe, swap(sent, LOW))
-    return finish(place, sums, moe, swap(sent, HIGH), queries, stats, combined)
+    sums, moe, *sent = latent_parts(place, kept, received, residual, gain, slices)
+    bits = ((LOW,), (HIGH,), (LOW, HIGH))
+    received = {i: swap(sent[i], *bits[i]) for i in (1, 2, 0)}
+    received = [received[i] for i in range(3)]
+    return finish(place, sums, moe, received, queries, stats, combined)
 
 
 def shifted(x, axis, by):

time: 73.9 us -> 71.2 us (0.963)
  waiting for transfers between devices: 33.6 us -> 29.1 us
  starting transfers between devices: 21.1 us -> 24 us
  local copies, waits for them, and re-layouts: 3.76 us -> 2.37 us
  other arithmetic: 2.58 us -> 3.66 us
  Pallas kernels: 11.7 us -> 10.9 us
    ppermute x21, waiting for transfers between devices: 25.3 us -> 21.8 us  [swap(): lax.ppermute(x, 'dev', [(i, i ^ flips) for i in range(lax.axis_size('dev'...]
    ppermute x4 -> x3, waiting for transfers between devices: 8.27 us -> 6.09 us  [swap(): lax.ppermute(x, 'sec', [(i, i ^ 1) for i in range(lax.axis_size('sec'))])]
    unnamed x28 -> x24, local copies, waits for them, and re-layouts: 2.98 us -> 0.86 us
    ppermute x21, starting transfers between devices: 18.4 us -> 20 us  [swap(): lax.ppermute(x, 'dev', [(i, i ^ flips) for i in range(lax.axis_size('dev'...]
    ppermute x0 -> x1, starting transfers between devices: none -> 1.43 us  [swap_both(): return lax.ppermute(x, ('sec', 'dev'), pairs)]
    ppermute x0 -> x1, waiting for transfers between devices: none -> 1.21 us  [swap_both(): return lax.ppermute(x, ('sec', 'dev'), pairs)]
    select_n x0 -> x1, other arithmetic: none -> 0.98 us  [with_info(): x = jnp.where(column == i * picks + k, values[:, k:k + 1], x)]
    pallas_call x7 -> x5, Pallas kernels: 9.98 us -> 9.17 us  [kernel_call(): pl.pallas_call(body, out_shape=out_shape, in_specs=specs, out_specs=jax.t...]
  transfers between devices with their start and end apart: 25 -> 25, of which waited for: 17 -> 18; matrix products, arithmetic and copies ran while one was open for 5% -> 3% of each run, Pallas kernels for 11% -> 11%
where the time goes in v4:
time: 71.2 us; the launch traced here: 70.8 us
  waiting for transfers between devices  29.1 us (41%)
  starting transfers between devices  24 us (34%)
  Pallas kernels  10.9 us (15%)
  other arithmetic  3.66 us (5%)
  local copies, waits for them, and re-layouts  2.37 us (3%)
  between operations  0.82 us (1%)
    ppermute x21, waiting for transfers between devices, swap(): lax.ppermute(x, 'dev', [(i, i ^ flips) for i in range(lax.axis_size('dev'...  21.8 us
    ppermute x21, starting transfers between devices, swap(): lax.ppermute(x, 'dev', [(i, i ^ flips) for i in range(lax.axis_size('dev'...  20 us
    pallas_call x5, Pallas kernels, kernel_call(): pl.pallas_call(body, out_shape=out_shape, in_specs=specs, out_specs=jax.t...  9.17 us
    ppermute x3, waiting for transfers between devices, swap(): lax.ppermute(x, 'sec', [(i, i ^ 1) for i in range(lax.axis_size('sec'))])  6.09 us
    ppermute x3, starting transfers between devices, swap(): lax.ppermute(x, 'sec', [(i, i ^ 1) for i in range(lax.axis_size('sec'))])  2.52 us
    pallas_call x1, Pallas kernels, cache_part(): pl.pallas_call(cache_kernel, out_shape=(jax.ShapeDtypeStruct((rows, heads...  1.71 us
    ppermute x1, starting transfers between devices, swap_both(): return lax.ppermute(x, ('sec', 'dev'), pairs)  1.43 us
  transfers between devices with their start and end apart: 25, of which 18 were waited for; matrix products, arithmetic and copies ran while one was open for 3% of the time, Pallas kernels for 11%

profile of v4, /device:TPU:0, one launch (start us, length us, event | category | flops | bytes accessed | tf_op | source)
XLA Modules:
  0.0 70.8 jit_solution(12956510778863878114)
XLA Ops:
  0.7 0.7 convert_element_type.101
  1.3 0.7 %slice_bitcast_fusion.1 = (bf16[4]{0:T(256)(128)(2,1)S(1)}, bf16[4]{0:T(256)(128)(2,1)S(1)}, bf16[4]{0:T(256)(128)(2,1)S(1)}, bf16[4]{0:T(256)(128)(2,1)S(1)}) fusion(bf16[4,2]{0,1:T(2,128)(2,1)S(1)} %convert_element_type.101, bf16[4,2]{0,1:T(2,128)(2,1)} %param.13), kind=kLoop, calls=%fused_computation.19 | loop fusion | bytes 64 | tf_op jit(solution)/shard_map/jit(_where)/broadcast_in_dim | solution.py:102
  2.1 1.0 %select_select_fusion.refs_0_ = bf16[4,7296]{1,0:T(4,128)(2,1)S(1)} fusion(bf16[4,7168]{1,0:T(4,128)(2,1)} %param.11, pred[7296]{0:T(1024)(128)(4,1)S(1)} %get-tuple-element.84, pred[7296]{0:T(1024)(128)(4,1)S(1)} %get-tuple-element.85, pred[7296]{0:T(1024)(128)(4,1)S(1)} %get-tuple-element.86, pred[7296]{0:T(1024)(128)(4,1)S(1)} %get-tuple-element.87, ...), kind=kLoop, calls=%fused_computation.7 | loop fusion | flops 116736 | bytes 144928 | tf_op jit(solution)/shard_map/jit(_where)/select_n | solution.py:102
  3.1 4.1 %collective-permute-start = (bf16[4,7296]{1,0:T(4,128)(2,1)S(1)}, bf16[4,7296]{1,0:T(4,128)(2,1)S(1)}, u32[]{:S(2)}, u32[]{:S(2)}) collective-permute-start(bf16[4,7296]{1,0:T(4,128)(2,1)S(1)} %select_select_fusion.refs_0_), channel_id=1, source_target_pairs={{0,8},{1,9},{2,10},{3,11},{4,12},{5,13},{6,14},{7,15},{8,0},{9,1},... | collective-permute-start | bytes 175112 | tf_op jit(solution)/shard_map/ppermute | solution.py:24
  7.2 1.6 %collective-permute-start.1 = (bf16[4,7296]{1,0:T(4,128)(2,1)S(1)}, bf16[4,7296]{1,0:T(4,128)(2,1)S(1)}, u32[]{:S(2)}, u32[]{:S(2)}) collective-permute-start(bf16[4,7296]{1,0:T(4,128)(2,1)S(1)} %select_select_fusion.refs_0_), channel_id=1, source_target_pairs={{0,4},{1,5},{2,6},{3,7},{4,0},{5,1},{6,2},{7,3},{8,12},{9,13},{10,... | collective-permute-start | bytes 175112 | tf_op jit(solution)/shard_map/ppermute | solution.py:24
  8.7 0.0 collective-permute-start.2
  8.7 1.3 %collective-permute-done.refs_1_ = bf16[4,7296]{1,0:T(4,128)(2,1)S(1)} collective-permute-done((bf16[4,7296]{1,0:T(4,128)(2,1)S(1)}, bf16[4,7296]{1,0:T(4,128)(2,1)S(1)}, u32[]{:S(2)}, u32[]{:S(2)}) %collective-permute-start) | collective-permute-done | bytes 58400 | tf_op jit(solution)/shard_map/ppermute | solution.py:24
  10.1 1.3 %collective-permute-done.1.refs_2_ = bf16[4,7296]{1,0:T(4,128)(2,1)S(1)} collective-permute-done((bf16[4,7296]{1,0:T(4,128)(2,1)S(1)}, bf16[4,7296]{1,0:T(4,128)(2,1)S(1)}, u32[]{:S(2)}, u32[]{:S(2)}) %collective-permute-start.1) | collective-permute-done | bytes 58400 | tf_op jit(solution)/shard_map/ppermute | solution.py:24
  11.4 3.4 %collective-permute-done.2.refs_3_ = bf16[4,7296]{1,0:T(4,128)(2,1)S(1)} collective-permute-done((bf16[4,7296]{1,0:T(4,128)(2,1)S(1)}, bf16[4,7296]{1,0:T(4,128)(2,1)S(1)}, u32[]{:S(2)}, u32[]{:S(2)}) %collective-permute-start.2) | collective-permute-done | bytes 58400 | tf_op jit(solution)/shard_map/ppermute | solution.py:24
  14.7 0.1 pack_rows.1
  14.8 1.6 %collective-permute-start.7 = (bf16[16,3712]{1,0:T(8,128)(2,1)S(1)}, bf16[16,3712]{1,0:T(8,128)(2,1)S(1)}, u32[]{:S(2)}, u32[]{:S(2)}) collective-permute-start(bf16[16,3712]{1,0:T(8,128)(2,1)S(1)} %get-tuple-element.42), channel_id=1, source_target_pairs={{0,16},{16,0},{1,17},{17,1},{2,18},{18,2},{3,19},{19,3},{4,20},{20... | collective-permute-start | bytes 356360 | tf_op jit(solution)/shard_map/ppermute | solution.py:22
  16.4 1.6 %collective-permute-start.3 = (bf16[16,3584]{1,0:T(8,128)(2,1)S(1)}, bf16[16,3584]{1,0:T(8,128)(2,1)S(1)}, u32[]{:S(2)}, u32[]{:S(2)}) collective-permute-start(bf16[16,3584]{1,0:T(8,128)(2,1)S(1)} %get-tuple-element.41), channel_id=1, source_target_pairs={{0,2},{1,3},{2,0},{3,1},{4,6},{5,7},{6,4},{7,5},{8,10},{9,11},{10,... | collective-permute-start | bytes 344072 | tf_op jit(solution)/shard_map/ppermute | solution.py:24
  18.0 0.0 collective-permute-start.11
  18.0 1.7 %collective-permute-done.7 = bf16[16,3712]{1,0:T(8,128)(2,1)S(1)} collective-permute-done((bf16[16,3712]{1,0:T(8,128)(2,1)S(1)}, bf16[16,3712]{1,0:T(8,128)(2,1)S(1)}, u32[]{:S(2)}, u32[]{:S(2)}) %collective-permute-start.7) | collective-permute-done | bytes 118816 | tf_op jit(solution)/shard_map/ppermute | solution.py:22
  19.7 1.6 %collective-permute-start.8 = (bf16[32,3712]{1,0:T(8,128)(2,1)S(1)}, bf16[32,3712]{1,0:T(8,128)(2,1)S(1)}, u32[]{:S(2)}, u32[]{:S(2)}) collective-permute-start(bf16[32,3712]{1,0:T(8,128)(2,1)S(1)} %constant_dynamic-update-slice_fusion.2.refs_5_.b_ref), channel_id=1, source_target_pairs={{0,2},{1,3},{2,0},{3,1},{4,6},{5,7},{6,4},{7,5},{8,10},{9,11},{10,... | collective-permute-start | bytes 712712 | tf_op jit(solution)/shard_map/ppermute | solution.py:24
  21.3 1.1 %collective-permute-done.3 = bf16[16,3584]{1,0:T(8,128)(2,1)S(1)} collective-permute-done((bf16[16,3584]{1,0:T(8,128)(2,1)S(1)}, bf16[16,3584]{1,0:T(8,128)(2,1)S(1)}, u32[]{:S(2)}, u32[]{:S(2)}) %collective-permute-start.3) | collective-permute-done | bytes 114720 | tf_op jit(solution)/shard_map/ppermute | solution.py:24
  22.4 0.5 collective-permute-start.4
  22.9 0.0 collective-permute-start.9
  22.9 3.0 %collective-permute-done.8.refs_6_.low_ref = bf16[32,3712]{1,0:T(8,128)(2,1)S(1)} collective-permute-done((bf16[32,3712]{1,0:T(8,128)(2,1)S(1)}, bf16[32,3712]{1,0:T(8,128)(2,1)S(1)}, u32[]{:S(2)}, u32[]{:S(2)}) %collective-permute-start.8) | collective-permute-done | bytes 237600 | tf_op jit(solution)/shard_map/ppermute | solution.py:24
  25.9 0.0 collective-permute-start.10
  25.9 0.5 collective-permute-start.5
  26.4 2.1 %collective-permute-done.4.refs_2_ = bf16[32,3584]{1,0:T(8,128)(2,1)S(1)} collective-permute-done((bf16[32,3584]{1,0:T(8,128)(2,1)S(1)}, bf16[32,3584]{1,0:T(8,128)(2,1)S(1)}, u32[]{:S(2)}, u32[]{:S(2)}) %collective-permute-start.4) | collective-permute-done | bytes 229408 | tf_op jit(solution)/shard_map/ppermute | solution.py:22
  28.5 0.0 collective-permute-start.6
  28.5 0.1 pad_add_fusion.refs_0_.place_ref
  28.6 0.0 collective-permute-done.5.refs_3_
  28.6 1.4 %collective-permute-done.6.refs_4_ = bf16[32,3584]{1,0:T(8,128)(2,1)S(1)} collective-permute-done((bf16[32,3584]{1,0:T(8,128)(2,1)S(1)}, bf16[32,3584]{1,0:T(8,128)(2,1)S(1)}, u32[]{:S(2)}, u32[]{:S(2)}) %collective-permute-start.6) | collective-permute-done | bytes 229408 | tf_op jit(solution)/shard_map/ppermute | solution.py:24
  30.0 0.0 collective-permute-done.10.refs_8_
  30.0 5.3 %experts.1 = (bf16[64,3584]{1,0:T(8,128)(2,1)S(1)}, bf16[64,3584]{1,0:T(8,128)(2,1)S(1)}, bf16[64,3584]{1,0:T(8,128)(2,1)S(1)}, bf16[64,3584]{1,0:T(8,128)(2,1)S(1)}) custom-call(s32[4]{0:T(128)S(1)} %pad_add_fusion.refs_0_.place_ref, bf16[32,3584]{1,0:T(8,128)(2,1)S(1)} %constant_dynamic-update-slice_fusion.refs_1_.a_ref, ...), custom_call_target="tpu_custom_call" | custom-call | tf_op jit(solution)/shard_map/experts/pallas_call | solution.py:85
  35.3 0.0 copy-start.2
  35.4 0.2 collective-permute-start.12
  35.6 0.4 collective-permute-start.13
  35.9 1.3 %collective-permute-done.12 = bf16[64,3584]{1,0:T(8,128)(2,1)S(1)} collective-permute-done((bf16[64,3584]{1,0:T(8,128)(2,1)S(1)}, bf16[64,3584]{1,0:T(8,128)(2,1)S(1)}, u32[]{:S(2)}, u32[]{:S(2)}) %collective-permute-start.12) | collective-permute-done | bytes 458784 | tf_op jit(solution)/shard_map/ppermute | solution.py:24
  37.3 0.1 add_convert_fusion.1
  37.3 0.5 collective-permute-start.15
  37.8 0.1 collective-permute-done.13
  37.9 0.1 add_convert_fusion
  38.0 1.6 %collective-permute-start.14 = (bf16[32,3584]{1,0:T(8,128)(2,1)S(1)}, bf16[32,3584]{1,0:T(8,128)(2,1)S(1)}, u32[]{:S(2)}, u32[]{:S(2)}) collective-permute-start(bf16[32,3584]{1,0:T(8,128)(2,1)S(1)} %get-tuple-element.79), channel_id=1, source_target_pairs={{0,2},{1,3},{2,0},{3,1},{4,6},{5,7},{6,4},{7,5},{8,10},{9,11},{10,... | collective-permute-start | bytes 688136 | tf_op jit(solution)/shard_map/ppermute | solution.py:24
  39.6 1.4 %collective-permute-start.16 = (bf16[32,3584]{1,0:T(8,128)(2,1)S(1)}, bf16[32,3584]{1,0:T(8,128)(2,1)S(1)}, u32[]{:S(2)}, u32[]{:S(2)}) collective-permute-start(bf16[32,3584]{1,0:T(8,128)(2,1)S(1)} %get-tuple-element.78), channel_id=1, source_target_pairs={{0,18},{1,19},{2,16},{3,17},{4,22},{5,23},{6,20},{7,21},{8,26},{9,... | collective-permute-start | bytes 688136 | tf_op jit(solution)/shard_map/ppermute | solution.py:30
  41.1 1.7 %cache_part.1 = (f32[4,64,128]{2,1,0:T(8,128)S(1)}, f32[4,64,512]{2,1,0:T(8,128)S(1)}) custom-call(s32[4]{0:T(128)S(1)} %copy-done.6, bf16[4,64,576]{2,1,0:T(8,128)(2,1)S(1)} %copy-done, bf16[4,576,256]{2,1,0:T(8,128)(2,1)S(1)} %bitcast.13), custom_call_target="tpu_custom_call" | custom-call | flops 150994944 | bytes 1179648 | tf_op jit(solution)/shard_map/cache_part/pallas_call | solution.py:63
  42.8 0.8 %copy-done.3 = f32[4,64,512]{2,1,0:T(8,128)} copy-done((f32[4,64,512]{2,1,0:T(8,128)}, f32[4,64,512]{2,1,0:T(8,128)S(1)}, u32[]{:S(2)}) %copy-start.3) | copy-done | bytes 524312
  43.6 2.3 %collective-permute-done.15 = bf16[32,3584]{1,0:T(8,128)(2,1)S(1)} collective-permute-done((bf16[32,3584]{1,0:T(8,128)(2,1)S(1)}, bf16[32,3584]{1,0:T(8,128)(2,1)S(1)}, u32[]{:S(2)}, u32[]{:S(2)}) %collective-permute-start.15) | collective-permute-done | bytes 229408 | tf_op jit(solution)/shard_map/ppermute | solution.py:22
  45.8 3.9 %collective-permute-done.14 = bf16[32,3584]{1,0:T(8,128)(2,1)S(1)} collective-permute-done((bf16[32,3584]{1,0:T(8,128)(2,1)S(1)}, bf16[32,3584]{1,0:T(8,128)(2,1)S(1)}, u32[]{:S(2)}, u32[]{:S(2)}) %collective-permute-start.14) | collective-permute-done | bytes 229408 | tf_op jit(solution)/shard_map/ppermute | solution.py:24
  49.7 1.2 %collective-permute-done.16 = bf16[32,3584]{1,0:T(8,128)(2,1)S(1)} collective-permute-done((bf16[32,3584]{1,0:T(8,128)(2,1)S(1)}, bf16[32,3584]{1,0:T(8,128)(2,1)S(1)}, u32[]{:S(2)}, u32[]{:S(2)}) %collective-permute-start.16) | collective-permute-done | bytes 229408 | tf_op jit(solution)/shard_map/ppermute | solution.py:30
  50.9 0.8 %add_convert_fusion.3 = (bf16[16,1792]{1,0:T(8,128)(2,1)}, bf16[16,1792]{1,0:T(8,128)(2,1)}, bf16[16,1792]{1,0:T(8,128)(2,1)}) fusion(bf16[32,3584]{1,0:T(8,128)(2,1)S(1)} %collective-permute-done.16, bf16[32,3584]{1,0:T(8,128)(2,1)S(1)} %collective-permute-done.15, bf16[32,3584]{1,0:T(8,128)(2,1)S(1)} %collective-permute-done.14, ...), kind=kLoop, calls=%fused_computation.4 | loop fusion | flops 860160 | bytes 1032192 | tf_op jit(solution)/shard_map/convert_element_type | solution.py:38
  51.7 0.5 collective-permute-start.17
  52.2 1.2 %collective-permute-start.18 = (bf16[16,1792]{1,0:T(8,128)(2,1)}, bf16[16,1792]{1,0:T(8,128)(2,1)}, u32[]{:S(2)}, u32[]{:S(2)}) collective-permute-start(bf16[16,1792]{1,0:T(8,128)(2,1)} %get-tuple-element.76), channel_id=1, source_target_pairs={{0,12},{1,13},{2,14},{3,15},{4,8},{5,9},{6,10},{7,11},{8,4},{9,5},... | collective-permute-start | bytes 172040 | tf_op jit(solution)/shard_map/ppermute | solution.py:24
  53.4 1.8 %collective-permute-start.19 = (bf16[16,1792]{1,0:T(8,128)(2,1)}, bf16[16,1792]{1,0:T(8,128)(2,1)}, u32[]{:S(2)}, u32[]{:S(2)}) collective-permute-start(bf16[16,1792]{1,0:T(8,128)(2,1)} %get-tuple-element.75), channel_id=1, source_target_pairs={{0,4},{1,5},{2,6},{3,7},{4,0},{5,1},{6,2},{7,3},{8,12},{9,13},{10,... | collective-permute-start | bytes 172040 | tf_op jit(solution)/shard_map/ppermute | solution.py:24
  55.2 0.0 collective-permute-start.20
  55.2 0.5 collective-permute-start.21
  55.8 0.8 %reshape.9.gain_ref = f32[8,896]{1,0:T(8,128)S(1)} reshape(f32[7168]{0:T(1024)} %param.17) | data formatting | bytes 57344 | tf_op jit(solution)/shard_map/reshape | solution.py:441
  56.5 0.6 residual_rows.1.residual_ref
  57.1 0.7 %collective-permute-done.17.refs_0_ = bf16[16,1792]{1,0:T(8,128)(2,1)S(1)} collective-permute-done((bf16[16,1792]{1,0:T(8,128)(2,1)}, bf16[16,1792]{1,0:T(8,128)(2,1)S(1)}, u32[]{:S(2)}, u32[]{:S(2)}) %collective-permute-start.17) | collective-permute-done | bytes 57376 | tf_op jit(solution)/shard_map/ppermute | solution.py:24
  57.9 0.8 %collective-permute-done.18.refs_1_ = bf16[16,1792]{1,0:T(8,128)(2,1)} collective-permute-done((bf16[16,1792]{1,0:T(8,128)(2,1)}, bf16[16,1792]{1,0:T(8,128)(2,1)}, u32[]{:S(2)}, u32[]{:S(2)}) %collective-permute-start.18) | collective-permute-done | bytes 57376 | tf_op jit(solution)/shard_map/ppermute | solution.py:24
  58.6 0.2 collective-permute-done.19.refs_2_
  58.8 1.0 %convert_add_fusion.sum_ref = f32[16,1792]{1,0:T(8,128)S(1)} fusion(bf16[32,3584]{1,0:T(8,128)(2,1)} %copy-done.10, bf16[32,3584]{1,0:T(8,128)(2,1)} %copy-done.8, bf16[32,3584]{1,0:T(8,128)(2,1)} %copy-done.9, bf16[64,3584]{1,0:T(8,128)(2,1)} %copy-done.7, bf16[64,3584]{1,0:T(8,128)(2,1)} %copy-done.5), kind=kLoop, calls=%fused_computation.3 | loop fusion | flops 258048 | bytes 401408 | tf_op jit(solution)/shard_map/add | solution.py:34
  59.8 0.0 collective-permute-done.20.refs_4_
  59.8 0.0 collective-permute-done.21.refs_6_
  59.8 1.4 %latent_parts.1 = (f32[4,640]{1,0:T(4,128)S(1)}, bf16[4,1792]{1,0:T(4,128)(2,1)S(1)}, bf16[4,3072]{1,0:T(4,128)(2,1)S(1)}, bf16[4,3072]{1,0:T(4,128)(2,1)S(1)}, bf16[4,3072]{1,0:T(4,128)(2,1)S(1)}) custom-call(s32[4]{0:T(128)S(1)} %pad_add_fusion.refs_0_.place_ref, f32[16,1792]{1,0:T(8,128)S(1)} %convert_add_fusion.sum_ref, ...), custom_call_target="tpu_custom_call" | custom-call | tf_op jit(solution)/shard_map/latent_parts/pallas_call | solution.py:85
  61.2 1.1 %collective-permute-start.22 = (bf16[4,3072]{1,0:T(4,128)(2,1)S(1)}, bf16[4,3072]{1,0:T(4,128)(2,1)S(1)}, u32[]{:S(2)}, u32[]{:S(2)}) collective-permute-start(bf16[4,3072]{1,0:T(4,128)(2,1)S(1)} %get-tuple-element.72), channel_id=1, source_target_pairs={{0,2},{1,3},{2,0},{3,1},{4,6},{5,7},{6,4},{7,5},{8,10},{9,11},{10,... | collective-permute-start | bytes 73736 | tf_op jit(solution)/shard_map/ppermute | solution.py:24
  62.3 1.1 %collective-permute-start.23 = (bf16[4,3072]{1,0:T(4,128)(2,1)S(1)}, bf16[4,3072]{1,0:T(4,128)(2,1)S(1)}, u32[]{:S(2)}, u32[]{:S(2)}) collective-permute-start(bf16[4,3072]{1,0:T(4,128)(2,1)S(1)} %get-tuple-element.73), channel_id=1, source_target_pairs={{0,8},{1,9},{2,10},{3,11},{4,12},{5,13},{6,14},{7,15},{8,0},{9,1},... | collective-permute-start | bytes 73736 | tf_op jit(solution)/shard_map/ppermute | solution.py:24
  63.4 2.2 %collective-permute-start.24 = (bf16[4,3072]{1,0:T(4,128)(2,1)S(1)}, bf16[4,3072]{1,0:T(4,128)(2,1)S(1)}, u32[]{:S(2)}, u32[]{:S(2)}) collective-permute-start(bf16[4,3072]{1,0:T(4,128)(2,1)S(1)} %get-tuple-element.74), channel_id=1, source_target_pairs={{0,10},{1,11},{2,8},{3,9},{4,14},{5,15},{6,12},{7,13},{8,2},{9,3},... | collective-permute-start | bytes 73736 | tf_op jit(solution)/shard_map/ppermute | solution.py:24
  65.7 1.4 %collective-permute-done.23.refs_1_ = bf16[4,3072]{1,0:T(4,128)(2,1)S(1)} collective-permute-done((bf16[4,3072]{1,0:T(4,128)(2,1)S(1)}, bf16[4,3072]{1,0:T(4,128)(2,1)S(1)}, u32[]{:S(2)}, u32[]{:S(2)}) %collective-permute-start.23) | collective-permute-done | bytes 24608 | tf_op jit(solution)/shard_map/ppermute | solution.py:24
  67.0 2.0 %collective-permute-done.24.refs_2_ = bf16[4,3072]{1,0:T(4,128)(2,1)S(1)} collective-permute-done((bf16[4,3072]{1,0:T(4,128)(2,1)S(1)}, bf16[4,3072]{1,0:T(4,128)(2,1)S(1)}, u32[]{:S(2)}, u32[]{:S(2)}) %collective-permute-start.24) | collective-permute-done | bytes 24608 | tf_op jit(solution)/shard_map/ppermute | solution.py:24
  69.1 1.8 %finish.1 = (bf16[4,7168]{1,0:T(4,128)(2,1)}, bf16[4,576]{1,0:T(4,128)(2,1)}, bf16[4,64,512]{2,1,0:T(8,128)(2,1)}) custom-call(s32[4]{0:T(128)S(1)} %pad_add_fusion.refs_0_.place_ref, f32[4,640]{1,0:T(4,128)S(1)} %get-tuple-element.68.sums_ref, bf16[4,1792]{1,0:T(4,128)(2,1)S(1)} %get-tuple-element.69.moe_ref, bf16[4,64,576]{2,1,0:T(8,128)(2,1)S(1)} %copy-done, ...), custom_call_target="tpu_custom_call" | custom-call | tf_op jit(solution)/shard_map/finish/pallas_call | solution.py:85
  (29 shorter events, 0.1 us)
Async XLA Ops:
  3.1 7.0 %collective-permute-start = (bf16[4,7296]{1,0:T(4,128)(2,1)S(1)}, bf16[4,7296]{1,0:T(4,128)(2,1)S(1)}, u32[]{:S(2)}, u32[]{:S(2)}) collective-permute-start(bf16[4,7296]{1,0:T(4,128)(2,1)S(1)} %select_select_fusion.refs_0_), channel_id=1, source_target_pairs={{0,8},{1,9},{2,10},{3,11},{4,12},{5,13},{6,14},{7,15},{8,0},{9,1},... | collective-permute-start | bytes 175112 | tf_op jit(solution)/shard_map/ppermute | solution.py:24
  7.2 4.2 %collective-permute-start.1 = (bf16[4,7296]{1,0:T(4,128)(2,1)S(1)}, bf16[4,7296]{1,0:T(4,128)(2,1)S(1)}, u32[]{:S(2)}, u32[]{:S(2)}) collective-permute-start(bf16[4,7296]{1,0:T(4,128)(2,1)S(1)} %select_select_fusion.refs_0_), channel_id=1, source_target_pairs={{0,4},{1,5},{2,6},{3,7},{4,0},{5,1},{6,2},{7,3},{8,12},{9,13},{10,... | collective-permute-start | bytes 175112 | tf_op jit(solution)/shard_map/ppermute | solution.py:24
  8.7 6.0 %collective-permute-start.2 = (bf16[4,7296]{1,0:T(4,128)(2,1)S(1)}, bf16[4,7296]{1,0:T(4,128)(2,1)S(1)}, u32[]{:S(2)}, u32[]{:S(2)}) collective-permute-start(bf16[4,7296]{1,0:T(4,128)(2,1)S(1)} %select_select_fusion.refs_0_), channel_id=1, source_target_pairs={{0,12},{1,13},{2,14},{3,15},{4,8},{5,9},{6,10},{7,11},{8,4},{9,5},... | collective-permute-start | bytes 175112 | tf_op jit(solution)/shard_map/ppermute | solution.py:24
  14.8 4.9 %collective-permute-start.7 = (bf16[16,3712]{1,0:T(8,128)(2,1)S(1)}, bf16[16,3712]{1,0:T(8,128)(2,1)S(1)}, u32[]{:S(2)}, u32[]{:S(2)}) collective-permute-start(bf16[16,3712]{1,0:T(8,128)(2,1)S(1)} %get-tuple-element.42), channel_id=1, source_target_pairs={{0,16},{16,0},{1,17},{17,1},{2,18},{18,2},{3,19},{19,3},{4,20},{20... | collective-permute-start | bytes 356360 | tf_op jit(solution)/shard_map/ppermute | solution.py:22
  16.4 6.0 %collective-permute-start.3 = (bf16[16,3584]{1,0:T(8,128)(2,1)S(1)}, bf16[16,3584]{1,0:T(8,128)(2,1)S(1)}, u32[]{:S(2)}, u32[]{:S(2)}) collective-permute-start(bf16[16,3584]{1,0:T(8,128)(2,1)S(1)} %get-tuple-element.41), channel_id=1, source_target_pairs={{0,2},{1,3},{2,0},{3,1},{4,6},{5,7},{6,4},{7,5},{8,10},{9,11},{10,... | collective-permute-start | bytes 344072 | tf_op jit(solution)/shard_map/ppermute | solution.py:24
  18.0 17.4 %collective-permute-start.11 = (bf16[448,576]{1,0:T(8,128)(2,1)}, bf16[448,576]{1,0:T(8,128)(2,1)S(1)}, u32[]{:S(2)}, u32[]{:S(2)}) collective-permute-start(bf16[448,576]{1,0:T(8,128)(2,1)} %refs_3_.1), channel_id=1, source_target_pairs={{0,4},{1,5},{2,6},{3,7},{4,0},{5,1},{6,2},{7,3},{8,12},{9,13},{10,... | collective-permute-start | bytes 1548296 | tf_op jit(solution)/shard_map/ppermute | solution.py:24
  19.7 6.2 %collective-permute-start.8 = (bf16[32,3712]{1,0:T(8,128)(2,1)S(1)}, bf16[32,3712]{1,0:T(8,128)(2,1)S(1)}, u32[]{:S(2)}, u32[]{:S(2)}) collective-permute-start(bf16[32,3712]{1,0:T(8,128)(2,1)S(1)} %constant_dynamic-update-slice_fusion.2.refs_5_.b_ref), channel_id=1, source_target_pairs={{0,2},{1,3},{2,0},{3,1},{4,6},{5,7},{6,4},{7,5},{8,10},{9,11},{10,... | collective-permute-start | bytes 712712 | tf_op jit(solution)/shard_map/ppermute | solution.py:24
  22.4 6.1 %collective-permute-start.4 = (bf16[32,3584]{1,0:T(8,128)(2,1)S(1)}, bf16[32,3584]{1,0:T(8,128)(2,1)S(1)}, u32[]{:S(2)}, u32[]{:S(2)}) collective-permute-start(bf16[32,3584]{1,0:T(8,128)(2,1)S(1)} %constant_dynamic-update-slice_fusion.refs_1_.a_ref), channel_id=1, source_target_pairs={{0,16},{16,0},{1,17},{17,1},{2,18},{18,2},{3,19},{19,3},{4,20},{20... | collective-permute-start | bytes 688136 | tf_op jit(solution)/shard_map/ppermute | solution.py:22
  22.9 5.7 %collective-permute-start.9 = (bf16[32,3712]{1,0:T(8,128)(2,1)S(1)}, bf16[32,3712]{1,0:T(8,128)(2,1)S(1)}, u32[]{:S(2)}, u32[]{:S(2)}) collective-permute-start(bf16[32,3712]{1,0:T(8,128)(2,1)S(1)} %constant_dynamic-update-slice_fusion.2.refs_5_.b_ref), channel_id=1, source_target_pairs={{0,1},{1,0},{2,3},{3,2},{4,5},{5,4},{6,7},{7,6},{8,9},{9,8},{10,11... | collective-permute-start | bytes 712712 | tf_op jit(solution)/shard_map/ppermute | solution.py:24
  25.9 4.1 %collective-permute-start.10 = (bf16[32,3712]{1,0:T(8,128)(2,1)S(1)}, bf16[32,3712]{1,0:T(8,128)(2,1)S(1)}, u32[]{:S(2)}, u32[]{:S(2)}) collective-permute-start(bf16[32,3712]{1,0:T(8,128)(2,1)S(1)} %collective-permute-done.8.refs_6_.low_ref), channel_id=1, source_target_pairs={{0,1},{1,0},{2,3},{3,2},{4,5},{5,4},{6,7},{7,6},{8,9},{9,8},{10,11... | collective-permute-start | bytes 712712 | tf_op jit(solution)/shard_map/ppermute | solution.py:24
  25.9 2.7 %collective-permute-start.5 = (bf16[32,3584]{1,0:T(8,128)(2,1)S(1)}, bf16[32,3584]{1,0:T(8,128)(2,1)S(1)}, u32[]{:S(2)}, u32[]{:S(2)}) collective-permute-start(bf16[32,3584]{1,0:T(8,128)(2,1)S(1)} %constant_dynamic-update-slice_fusion.refs_1_.a_ref), channel_id=1, source_target_pairs={{0,1},{1,0},{2,3},{3,2},{4,5},{5,4},{6,7},{7,6},{8,9},{9,8},{10,11... | collective-permute-start | bytes 688136 | tf_op jit(solution)/shard_map/ppermute | solution.py:24
  28.5 1.5 %collective-permute-start.6 = (bf16[32,3584]{1,0:T(8,128)(2,1)S(1)}, bf16[32,3584]{1,0:T(8,128)(2,1)S(1)}, u32[]{:S(2)}, u32[]{:S(2)}) collective-permute-start(bf16[32,3584]{1,0:T(8,128)(2,1)S(1)} %collective-permute-done.4.refs_2_), channel_id=1, source_target_pairs={{0,1},{1,0},{2,3},{3,2},{4,5},{5,4},{6,7},{7,6},{8,9},{9,8},{10,11... | collective-permute-start | bytes 688136 | tf_op jit(solution)/shard_map/ppermute | solution.py:24
  28.6 12.5 %copy-start = (bf16[4,64,576]{2,1,0:T(8,128)(2,1)S(1)}, bf16[4,64,576]{2,1,0:T(8,128)(2,1)}, u32[]{:S(2)}) copy-start(bf16[4,64,576]{2,1,0:T(8,128)(2,1)} %q_ref.3) | copy-start | bytes 884740
  28.6 12.5 %copy-start.1 = (bf16[4,256,576]{1,2,0:T(8,128)(2,1)S(1)}, bf16[4,256,576]{1,2,0:T(8,128)(2,1)}, u32[]{:S(2)}) copy-start(bf16[4,256,576]{1,2,0:T(8,128)(2,1)} %param.20) | copy-start | bytes 3538948
  28.6 12.5 %copy-start.6 = (s32[4]{0:T(128)S(1)}, s32[4]{0:T(128)}, u32[]{:S(2)}) copy-start(s32[4]{0:T(128)} %lengths_ref.1) | copy-start | bytes 52
  35.3 19.8 %copy-start.5 = (bf16[64,3584]{1,0:T(8,128)(2,1)}, bf16[64,3584]{1,0:T(8,128)(2,1)S(1)}, u32[]{:S(2)}) copy-start(bf16[64,3584]{1,0:T(8,128)(2,1)S(1)} %get-tuple-element.59) | copy-start | bytes 1376260
  35.3 19.8 %copy-start.2 = (bf16[448,576]{1,0:T(8,128)(2,1)S(1)}, bf16[448,576]{1,0:T(8,128)(2,1)}, u32[]{:S(2)}) copy-start(bf16[448,576]{1,0:T(8,128)(2,1)} %refs_3_.1) | copy-start | bytes 1548292
  35.4 1.9 %collective-permute-start.12 = (bf16[64,3584]{1,0:T(8,128)(2,1)S(1)}, bf16[64,3584]{1,0:T(8,128)(2,1)S(1)}, u32[]{:S(2)}, u32[]{:S(2)}) collective-permute-start(bf16[64,3584]{1,0:T(8,128)(2,1)S(1)} %get-tuple-element.49), channel_id=1, source_target_pairs={{0,1},{1,0},{2,3},{3,2},{4,5},{5,4},{6,7},{7,6},{8,9},{9,8},{10,11... | collective-permute-start | bytes 1376264 | tf_op jit(solution)/shard_map/ppermute | solution.py:24
  35.6 2.3 %collective-permute-start.13 = (bf16[64,3584]{1,0:T(8,128)(2,1)S(1)}, bf16[64,3584]{1,0:T(8,128)(2,1)S(1)}, u32[]{:S(2)}, u32[]{:S(2)}) collective-permute-start(bf16[64,3584]{1,0:T(8,128)(2,1)S(1)} %get-tuple-element.51), channel_id=1, source_target_pairs={{0,1},{1,0},{2,3},{3,2},{4,5},{5,4},{6,7},{7,6},{8,9},{9,8},{10,11... | collective-permute-start | bytes 1376264 | tf_op jit(solution)/shard_map/ppermute | solution.py:24
  37.3 17.9 %copy-start.7 = (bf16[64,3584]{1,0:T(8,128)(2,1)}, bf16[64,3584]{1,0:T(8,128)(2,1)S(1)}, u32[]{:S(2)}) copy-start(bf16[64,3584]{1,0:T(8,128)(2,1)S(1)} %collective-permute-done.12) | copy-start | bytes 1376260
  37.3 8.5 %collective-permute-start.15 = (bf16[32,3584]{1,0:T(8,128)(2,1)S(1)}, bf16[32,3584]{1,0:T(8,128)(2,1)S(1)}, u32[]{:S(2)}, u32[]{:S(2)}) collective-permute-start(bf16[32,3584]{1,0:T(8,128)(2,1)S(1)} %add_convert_fusion.1), channel_id=1, source_target_pairs={{0,16},{16,0},{1,17},{17,1},{2,18},{18,2},{3,19},{19,3},{4,20},{20... | collective-permute-start | bytes 688136 | tf_op jit(solution)/shard_map/ppermute | solution.py:22
  38.0 11.7 %collective-permute-start.14 = (bf16[32,3584]{1,0:T(8,128)(2,1)S(1)}, bf16[32,3584]{1,0:T(8,128)(2,1)S(1)}, u32[]{:S(2)}, u32[]{:S(2)}) collective-permute-start(bf16[32,3584]{1,0:T(8,128)(2,1)S(1)} %get-tuple-element.79), channel_id=1, source_target_pairs={{0,2},{1,3},{2,0},{3,1},{4,6},{5,7},{6,4},{7,5},{8,10},{9,11},{10,... | collective-permute-start | bytes 688136 | tf_op jit(solution)/shard_map/ppermute | solution.py:24
  39.6 11.3 %collective-permute-start.16 = (bf16[32,3584]{1,0:T(8,128)(2,1)S(1)}, bf16[32,3584]{1,0:T(8,128)(2,1)S(1)}, u32[]{:S(2)}, u32[]{:S(2)}) collective-permute-start(bf16[32,3584]{1,0:T(8,128)(2,1)S(1)} %get-tuple-element.78), channel_id=1, source_target_pairs={{0,18},{1,19},{2,16},{3,17},{4,22},{5,23},{6,20},{7,21},{8,26},{9,... | collective-permute-start | bytes 688136 | tf_op jit(solution)/shard_map/ppermute | solution.py:30
  42.8 0.8 %copy-start.3 = (f32[4,64,512]{2,1,0:T(8,128)}, f32[4,64,512]{2,1,0:T(8,128)S(1)}, u32[]{:S(2)}) copy-start(f32[4,64,512]{2,1,0:T(8,128)S(1)} %get-tuple-element.71.part_ref) | copy-start | bytes 1572868
  45.8 9.4 %copy-start.8 = (bf16[32,3584]{1,0:T(8,128)(2,1)}, bf16[32,3584]{1,0:T(8,128)(2,1)S(1)}, u32[]{:S(2)}) copy-start(bf16[32,3584]{1,0:T(8,128)(2,1)S(1)} %collective-permute-done.15) | copy-start | bytes 688132
  49.7 5.5 %copy-start.9 = (bf16[32,3584]{1,0:T(8,128)(2,1)}, bf16[32,3584]{1,0:T(8,128)(2,1)S(1)}, u32[]{:S(2)}) copy-start(bf16[32,3584]{1,0:T(8,128)(2,1)S(1)} %collective-permute-done.14) | copy-start | bytes 688132
  50.9 4.3 %copy-start.10 = (bf16[32,3584]{1,0:T(8,128)(2,1)}, bf16[32,3584]{1,0:T(8,128)(2,1)S(1)}, u32[]{:S(2)}) copy-start(bf16[32,3584]{1,0:T(8,128)(2,1)S(1)} %collective-permute-done.16) | copy-start | bytes 688132
  51.7 6.2 %collective-permute-start.17 = (bf16[16,1792]{1,0:T(8,128)(2,1)}, bf16[16,1792]{1,0:T(8,128)(2,1)S(1)}, u32[]{:S(2)}, u32[]{:S(2)}) collective-permute-start(bf16[16,1792]{1,0:T(8,128)(2,1)} %get-tuple-element.77), channel_id=1, source_target_pairs={{0,8},{1,9},{2,10},{3,11},{4,12},{5,13},{6,14},{7,15},{8,0},{9,1},... | collective-permute-start | bytes 172040 | tf_op jit(solution)/shard_map/ppermute | solution.py:24
  52.2 6.4 %collective-permute-start.18 = (bf16[16,1792]{1,0:T(8,128)(2,1)}, bf16[16,1792]{1,0:T(8,128)(2,1)}, u32[]{:S(2)}, u32[]{:S(2)}) collective-permute-start(bf16[16,1792]{1,0:T(8,128)(2,1)} %get-tuple-element.76), channel_id=1, source_target_pairs={{0,12},{1,13},{2,14},{3,15},{4,8},{5,9},{6,10},{7,11},{8,4},{9,5},... | collective-permute-start | bytes 172040 | tf_op jit(solution)/shard_map/ppermute | solution.py:24
  53.4 5.4 %collective-permute-start.19 = (bf16[16,1792]{1,0:T(8,128)(2,1)}, bf16[16,1792]{1,0:T(8,128)(2,1)}, u32[]{:S(2)}, u32[]{:S(2)}) collective-permute-start(bf16[16,1792]{1,0:T(8,128)(2,1)} %get-tuple-element.75), channel_id=1, source_target_pairs={{0,4},{1,5},{2,6},{3,7},{4,0},{5,1},{6,2},{7,3},{8,12},{9,13},{10,... | collective-permute-start | bytes 172040 | tf_op jit(solution)/shard_map/ppermute | solution.py:24
  55.2 4.6 %collective-permute-start.20 = (bf16[448,576]{1,0:T(8,128)(2,1)S(1)}, bf16[448,576]{1,0:T(8,128)(2,1)S(1)}, u32[]{:S(2)}, u32[]{:S(2)}) collective-permute-start(bf16[448,576]{1,0:T(8,128)(2,1)S(1)} %copy-done.2), channel_id=1, source_target_pairs={{0,1},{1,0},{2,3},{3,2},{4,5},{5,4},{6,7},{7,6},{8,9},{9,8},{10,11... | collective-permute-start | bytes 1548296 | tf_op jit(solution)/shard_map/ppermute | solution.py:24
  55.2 4.6 %collective-permute-start.21 = (bf16[448,576]{1,0:T(8,128)(2,1)S(1)}, bf16[448,576]{1,0:T(8,128)(2,1)S(1)}, u32[]{:S(2)}, u32[]{:S(2)}) collective-permute-start(bf16[448,576]{1,0:T(8,128)(2,1)S(1)} %collective-permute-done.11.refs_5_), channel_id=1, source_target_pairs={{0,1},{1,0},{2,3},{3,2},{4,5},{5,4},{6,7},{7,6},{8,9},{9,8},{10,11... | collective-permute-start | bytes 1548296 | tf_op jit(solution)/shard_map/ppermute | solution.py:24
  56.5 12.5 %copy-start.4 = (f32[4,64,512]{2,1,0:T(8,128)S(1)}, f32[4,64,512]{2,1,0:T(8,128)}, u32[]{:S(2)}) copy-start(f32[4,64,512]{2,1,0:T(8,128)} %copy-done.3) | copy-start | bytes 1572868
  61.2 4.5 %collective-permute-start.22 = (bf16[4,3072]{1,0:T(4,128)(2,1)S(1)}, bf16[4,3072]{1,0:T(4,128)(2,1)S(1)}, u32[]{:S(2)}, u32[]{:S(2)}) collective-permute-start(bf16[4,3072]{1,0:T(4,128)(2,1)S(1)} %get-tuple-element.72), channel_id=1, source_target_pairs={{0,2},{1,3},{2,0},{3,1},{4,6},{5,7},{6,4},{7,5},{8,10},{9,11},{10,... | collective-permute-start | bytes 73736 | tf_op jit(solution)/shard_map/ppermute | solution.py:24
  62.3 4.7 %collective-permute-start.23 = (bf16[4,3072]{1,0:T(4,128)(2,1)S(1)}, bf16[4,3072]{1,0:T(4,128)(2,1)S(1)}, u32[]{:S(2)}, u32[]{:S(2)}) collective-permute-start(bf16[4,3072]{1,0:T(4,128)(2,1)S(1)} %get-tuple-element.73), channel_id=1, source_target_pairs={{0,8},{1,9},{2,10},{3,11},{4,12},{5,13},{6,14},{7,15},{8,0},{9,1},... | collective-permute-start | bytes 73736 | tf_op jit(solution)/shard_map/ppermute | solution.py:24
  63.4 5.6 %collective-permute-start.24 = (bf16[4,3072]{1,0:T(4,128)(2,1)S(1)}, bf16[4,3072]{1,0:T(4,128)(2,1)S(1)}, u32[]{:S(2)}, u32[]{:S(2)}) collective-permute-start(bf16[4,3072]{1,0:T(4,128)(2,1)S(1)} %get-tuple-element.74), channel_id=1, source_target_pairs={{0,10},{1,11},{2,8},{3,9},{4,14},{5,15},{6,12},{7,13},{8,2},{9,3},... | collective-permute-start | bytes 73736 | tf_op jit(solution)/shard_map/ppermute | solution.py:24

commit v5 on v4

--- a/solution.py
+++ b/solution.py
@@ -104,40 +104,34 @@
 
 
 def pack_kernel(_, *refs):
-    blocks, (a_ref, b_ref) = refs[:4], refs[4:]
-    half = a_ref.shape[1]
-    for ref, cols in ((a_ref, slice(0, half)), (b_ref, slice(half, None))):
-        x = jnp.concatenate([block[:, cols].astype(jnp.float32) for block in blocks], axis=0)
-        ref[...] = x.astype(ref.dtype)
+    *blocks, out_ref = refs
+    x = jnp.concatenate([block[...].astype(jnp.float32) for block in blocks], axis=0)
+    out_ref[...] = x.astype(out_ref.dtype)
 
 
 def pack_rows_of(*blocks):
     rows, width = blocks[0].shape
-    half = (width - LANES) // 2
-    outs = [jax.ShapeDtypeStruct((4 * rows, cols), jnp.bfloat16) for cols in (half, half + LANES)]
+    out = jax.ShapeDtypeStruct((len(blocks) * rows, width), blocks[0].dtype)
     return kernel_call(
-        pack_kernel, tuple(outs), jnp.zeros((1,), jnp.int32), *blocks, name="pack_rows", mib=4
+        pack_kernel, out, jnp.zeros((1,), jnp.int32), *blocks, name="pack_rows", mib=4
     )
 
 
 def gather_rows(hidden_in, expert_ids, gate_scores, w_kv):
     x = with_info(hidden_in, expert_ids, gate_scores)
-    a, b = pack_rows_of(x, swap(x, HIGH), swap(x, MID), swap(x, MID, HIGH))
-    a, b, w_own = lax.optimization_barrier((a, b, w_kv))
+    high, mid, both = swap(x, HIGH), swap(x, MID), swap(x, MID, HIGH)
+    mid, w_own = lax.optimization_barrier((mid, w_kv))
+    x = pack_rows_of(x, high, mid, both)
+    blocks = [x, swap(x, LOW), swap(x, "sec"), swap_both(x, LOW)]
     w_mid = swap(w_own, MID)
-    a_low, b_sec = swap(a, LOW), swap(b, "sec")
-    a, b = jnp.concatenate([a, a_low], axis=0), jnp.concatenate([b, b_sec], axis=0)
-    a_all, b_all = (a, swap(a, "sec")), (b, swap(b, LOW))
-    a_all += tuple(swap(v, CORE) for v in a_all)
-    b_all += tuple(swap(v, CORE) for v in b_all)
-    return a_all, b_all, w_mid
+    return blocks + [swap(v, CORE) for v in blocks], w_mid
 
 
 def experts_kernel(picks, place_ref, *refs):
-    a_refs, b_refs, w_refs, outs = refs[:4], refs[4:8], refs[8:11], refs[11:15]
+    x_refs, w_refs, outs = refs[:8], refs[8:11], refs[11:15]
     gate_ref, up_ref, down_ref, sems = refs[15:]
-    size, half = a_refs[0].shape
-    size //= 2
+    size, half = x_refs[0].shape
+    half = (half - LANES) // 2
     moves = []
     for part in (pl.ds(0, half), pl.ds(half, half)):
         moves.append((w_refs[0].at[part], gate_ref.at[part]))
@@ -149,14 +143,8 @@
     for copy in copies:
         copy.start()
 
-    def rows_of(part, cols):
-        if part == 0:
-            return jnp.concatenate([ref[:, cols] for ref in a_refs], axis=0)
-        blocks = []
-        for side in range(2):
-            early, late = b_refs[2 * side][:, cols], b_refs[2 * side + 1][:, cols]
-            blocks += [early[:size], late[:size], early[size:], late[size:]]
-        return jnp.concatenate(blocks, axis=0)
+    def columns(cols):
+        return jnp.concatenate([ref[:, cols] for ref in x_refs], axis=0)
 
     def ordered(x):
         n = size // 2
@@ -170,7 +158,7 @@
                 done.append(jnp.where(place_ref[1] == 1, pair[0], pair[1]))
         return jnp.concatenate(done, axis=0)
 
-    info = rows_of(1, slice(half, half + LANES)).astype(jnp.float32)
+    info = columns(slice(2 * half, None)).astype(jnp.float32)
     rows, hid = info.shape[0], gate_ref.shape[1]
     lane = lax.broadcasted_iota(jnp.int32, info.shape, 1)
     scores = jnp.where(lane < picks, pltpu.roll(info, LANES - picks, 1), 0.0)
@@ -182,8 +170,8 @@
         copies[2 * part].wait()
         copies[2 * part + 1].wait()
         for k in range(0, half, CHUNK):
-            x = rows_of(part, slice(k, k + CHUNK))
             depth = slice(part * half + k, part * half + k + CHUNK)
+            x = columns(depth)
             gate_act += jnp.dot(x, gate_ref[depth, :], preferred_element_type=jnp.float32)
             up_act += jnp.dot(x, up_ref[depth, :], preferred_element_type=jnp.float32)
     hidden = ordered(gate_act / (1.0 + jnp.exp(-gate_act)) * up_act).astype(jnp.bfloat16)
@@ -206,16 +194,14 @@
                 sent[:, to] = partial[rows // 2 :]
 
 
-def experts(place, a_all, b_all, picks, w_gate, w_up, w_down):
-    rows, half = a_all[0].shape
-    out = jax.ShapeDtypeStruct((2 * rows, half), jnp.bfloat16)
+def experts(place, blocks, picks, w_gate, w_up, w_down):
+    out = jax.ShapeDtypeStruct((4 * blocks[0].shape[0], w_gate.shape[0] // 2), jnp.bfloat16)
     weights = (w_gate, w_up, w_down)
     return kernel_call(
         lambda *refs: experts_kernel(picks, *refs),
         (out,) * 4,
         place,
-        *a_all,
-        *b_all,
+        *blocks,
         *weights,
         name="experts",
         mib=48,
@@ -243,17 +229,17 @@
         swap(total(*(v[there, right] for v in a)), MID, HIGH),
         swap(total(*(v[there, left] for v in a)), MID),
     )
-    a, ins = lax.optimization_barrier((a, ins))
     return wide_total(*(v[here, left] for v in a)), ins, late
 
 
-def residual_kernel(place_ref, a_ref, b_ref, low_ref, out_ref):
-    rows, half = a_ref.shape
-    n, block = rows // 4, half // 4
+def residual_kernel(place_ref, own_ref, low_ref, out_ref):
+    rows, cols = out_ref.shape
+    n, block = rows // 2, cols // 2
     upper, odd = place_ref[2] == 1, place_ref[1] == 1
     pair = []
-    for a, b in ((a_ref[:n], b_ref[:n]), (a_ref[2 * n : 3 * n], low_ref[:n])):
-        x = jnp.where(upper, b[:, :half].astype(jnp.float32), a.astype(jnp.float32))
+    for ref in (own_ref, low_ref):
+        x = ref[:n].astype(jnp.float32)
+        x = jnp.where(upper, x[:, 2 * cols : 4 * cols], x[:, : 2 * cols])
         pair.append(jnp.where(upper, pltpu.roll(x, n // 2, 0), x))
     pair = [jnp.where(odd, pair[1], pair[0]), jnp.where(odd, pair[0], pair[1])]
     x = jnp.concatenate(pair, axis=0)
@@ -265,22 +251,13 @@
         )
 
 
-def residual_rows(place, a, b, b_low):
-    rows, half = a.shape
-    return kernel_call(
-        residual_kernel,
-        jax.ShapeDtypeStruct((rows // 2, half // 2), jnp.float32),
-        place,
-        a,
-        b,
-        b_low,
-        name="residual_rows",
-        mib=4,
-    )
+def residual_rows(place, own, low):
+    rows, width = own.shape
+    out = jax.ShapeDtypeStruct((rows, (width - LANES) // 4), jnp.float32)
+    return kernel_call(residual_kernel, out, place, own, low, name="residual_rows", mib=4)
 
 
 OTHERS = ((1, 0), (0, 1), (1, 1))
-
 
 def put_split(ref, first, apart, x):
     cols = x.shape[1]
@@ -311,7 +288,8 @@
     moe = (residual_ref[...] + mixture).astype(jnp.bfloat16)
     widened = moe.astype(jnp.float32)
     for mid in range(2):
-        gain = gain_ref[pl.ds(4 * place_ref[2] + 2 * mid + place_ref[1], 1), :]
+        first = (4 * place_ref[2] + 2 * mid + place_ref[1]) * block
+        gain = gain_ref[:, pl.ds(pl.multiple_of(first, LANES), block)]
         scaled = widened[:, mid * block : (mid + 1) * block] * gain
         for core in range(2):
             piece_ref[2 * mid + core] = scaled[:, core * piece : (core + 1) * piece]
@@ -431,14 +409,14 @@
     place = jnp.stack([expert, (device >> LOW) & 1, (device >> HIGH) & 1, core_mid])
 
     cache = cache_part(queries, kv_cache, lengths)
-    a_all, b_all, w_mid = gather_rows(hidden_in, expert_ids, gate_scores, w_kv)
-    partial = experts(place, a_all, b_all, picks, w_gate, w_up, w_down)
+    blocks, w_mid = gather_rows(hidden_in, expert_ids, gate_scores, w_kv)
+    partial = experts(place, blocks, picks, w_gate, w_up, w_down)
     partial, w_mid = lax.optimization_barrier((partial, w_mid))
     kept, received, late = scatter_rows(*partial, (cache,))
     (cache,) = late
     stats, combined = cache
-    residual = residual_rows(place, a_all[0], b_all[0], b_all[1])
-    gain = norm_gain.reshape(8, -1)
+    residual = residual_rows(place, blocks[0], blocks[1])
+    gain = norm_gain.reshape(1, -1)
     slices = (w_kv, swap(w_kv, CORE), w_mid, swap(w_mid, CORE))
     sums, moe, *sent = latent_parts(place, kept, received, residual, gain, slices)
     bits = ((LOW,), (HIGH,), (LOW, HIGH))

time: 71.2 us -> 68.1 us (0.956)
  local copies, waits for them, and re-layouts: 2.37 us -> 0.76 us
  other arithmetic: 3.66 us -> 2.08 us
  waiting for transfers between devices: 29.1 us -> 30 us
    ppermute x3 -> x2, waiting for transfers between devices: 6.09 us -> 2.3 us  [swap(): lax.ppermute(x, 'sec', [(i, i ^ 1) for i in range(lax.axis_size('sec'))])]
    ppermute x21 -> x20, waiting for transfers between devices: 21.8 us -> 25.4 us  [swap(): lax.ppermute(x, 'dev', [(i, i ^ flips) for i in range(lax.axis_size('dev'...]
    ppermute x1 -> x2, waiting for transfers between devices: 1.21 us -> 2.34 us  [swap_both(): return lax.ppermute(x, ('sec', 'dev'), pairs)]
    add x1, other arithmetic: 0.97 us -> 0.04 us  [wide_total(): return sum((part.astype(jnp.float32) for part in parts))]
    unnamed x24 -> x10, local copies, waits for them, and re-layouts: 0.86 us -> 0.02 us
    reshape x1 -> x0, local copies, waits for them, and re-layouts: 0.75 us -> none  [per_device(): gain = norm_gain.reshape(8, -1)]
    ppermute x3 -> x2, starting transfers between devices: 2.52 us -> 3.05 us  [swap(): lax.ppermute(x, 'sec', [(i, i ^ 1) for i in range(lax.axis_size('sec'))])]
    ppermute x1 -> x2, starting transfers between devices: 1.43 us -> 0.94 us  [swap_both(): return lax.ppermute(x, ('sec', 'dev'), pairs)]
  transfers between devices with their start and end apart: 25 -> 24, of which waited for: 18 -> 13; matrix products, arithmetic and copies ran while one was open for 3% -> 1% of each run, Pallas kernels for 11% -> 11%
where the time goes in v5:
time: 68.1 us; the launch traced here: 67.9 us
  waiting for transfers between devices  30 us (44%)
  starting transfers between devices  23.7 us (35%)
  Pallas kernels  10.6 us (16%)
  other arithmetic  2.08 us (3%)
  between operations  0.79 us (1%)
  local copies, waits for them, and re-layouts  0.76 us (1%)
    ppermute x20, waiting for transfers between devices, swap(): lax.ppermute(x, 'dev', [(i, i ^ flips) for i in range(lax.axis_size('dev'...  25.4 us
    ppermute x20, starting transfers between devices, swap(): lax.ppermute(x, 'dev', [(i, i ^ flips) for i in range(lax.axis_size('dev'...  19.7 us
    pallas_call x5, Pallas kernels, kernel_call(): pl.pallas_call(body, out_shape=out_shape, in_specs=specs, out_specs=jax.t...  8.85 us
    ppermute x2, starting transfers between devices, swap(): lax.ppermute(x, 'sec', [(i, i ^ 1) for i in range(lax.axis_size('sec'))])  3.05 us
    ppermute x2, waiting for transfers between devices, swap_both(): return lax.ppermute(x, ('sec', 'dev'), pairs)  2.34 us
    ppermute x2, waiting for transfers between devices, swap(): lax.ppermute(x, 'sec', [(i, i ^ 1) for i in range(lax.axis_size('sec'))])  2.3 us
    pallas_call x1, Pallas kernels, cache_part(): pl.pallas_call(cache_kernel, out_shape=(jax.ShapeDtypeStruct((rows, heads...  1.7 us
  transfers between devices with their start and end apart: 24, of which 13 were waited for; matrix products, arithmetic and copies ran while one was open for 1% of the time, Pallas kernels for 11%

profile of v5, /device:TPU:0, one launch (start us, length us, event | category | flops | bytes accessed | tf_op | source)
XLA Modules:
  0.0 67.9 jit_solution(15159455647564831765)
XLA Ops:
  0.7 0.7 %convert_element_type.101 = bf16[4,2]{0,1:T(2,128)(2,1)S(1)} convert(s32[4,2]{0,1:T(2,128)} %param.12) | non-fusion elementwise | flops 8 | bytes 48 | tf_op jit(solution)/shard_map/convert_element_type | solution.py:100
  1.3 0.7 %slice_bitcast_fusion.1 = (bf16[4]{0:T(256)(128)(2,1)S(1)}, bf16[4]{0:T(256)(128)(2,1)S(1)}, bf16[4]{0:T(256)(128)(2,1)S(1)}, bf16[4]{0:T(256)(128)(2,1)S(1)}) fusion(bf16[4,2]{0,1:T(2,128)(2,1)S(1)} %convert_element_type.101, bf16[4,2]{0,1:T(2,128)(2,1)} %param.13), kind=kLoop, calls=%fused_computation.15 | loop fusion | bytes 64 | tf_op jit(solution)/shard_map/jit(_where)/broadcast_in_dim | solution.py:102
  2.1 1.0 %select_select_fusion.refs_0_ = bf16[4,7296]{1,0:T(4,128)(2,1)S(1)} fusion(bf16[4,7168]{1,0:T(4,128)(2,1)} %param.11, pred[7296]{0:T(1024)(128)(4,1)S(1)} %get-tuple-element.62, pred[7296]{0:T(1024)(128)(4,1)S(1)} %get-tuple-element.63, pred[7296]{0:T(1024)(128)(4,1)S(1)} %get-tuple-element.64, pred[7296]{0:T(1024)(128)(4,1)S(1)} %get-tuple-element.65, ...), kind=kLoop, calls=%fused_computation.7 | loop fusion | flops 116736 | bytes 144928 | tf_op jit(solution)/shard_map/jit(_where)/select_n | solution.py:102
  3.1 3.1 %collective-permute-start.1 = (bf16[4,7296]{1,0:T(4,128)(2,1)S(1)}, bf16[4,7296]{1,0:T(4,128)(2,1)S(1)}, u32[]{:S(2)}, u32[]{:S(2)}) collective-permute-start(bf16[4,7296]{1,0:T(4,128)(2,1)S(1)} %select_select_fusion.refs_0_), channel_id=1, source_target_pairs={{0,4},{1,5},{2,6},{3,7},{4,0},{5,1},{6,2},{7,3},{8,12},{9,13},{10,... | collective-permute-start | bytes 175112 | tf_op jit(solution)/shard_map/ppermute | solution.py:24
  6.2 2.6 %collective-permute-start = (bf16[4,7296]{1,0:T(4,128)(2,1)S(1)}, bf16[4,7296]{1,0:T(4,128)(2,1)S(1)}, u32[]{:S(2)}, u32[]{:S(2)}) collective-permute-start(bf16[4,7296]{1,0:T(4,128)(2,1)S(1)} %select_select_fusion.refs_0_), channel_id=1, source_target_pairs={{0,8},{1,9},{2,10},{3,11},{4,12},{5,13},{6,14},{7,15},{8,0},{9,1},... | collective-permute-start | bytes 175112 | tf_op jit(solution)/shard_map/ppermute | solution.py:24
  8.7 0.0 collective-permute-start.2
  8.7 0.0 collective-permute-done.1.refs_2_
  8.8 1.6 %collective-permute-start.10 = (bf16[448,576]{1,0:T(8,128)(2,1)}, bf16[448,576]{1,0:T(8,128)(2,1)S(1)}, u32[]{:S(2)}, u32[]{:S(2)}) collective-permute-start(bf16[448,576]{1,0:T(8,128)(2,1)} %refs_3_.1), channel_id=1, source_target_pairs={{0,4},{1,5},{2,6},{3,7},{4,0},{5,1},{6,2},{7,3},{8,12},{9,13},{10,... | collective-permute-start | bytes 1548296 | tf_op jit(solution)/shard_map/ppermute | solution.py:24
  10.3 2.1 %collective-permute-done.refs_1_ = bf16[4,7296]{1,0:T(4,128)(2,1)S(1)} collective-permute-done((bf16[4,7296]{1,0:T(4,128)(2,1)S(1)}, bf16[4,7296]{1,0:T(4,128)(2,1)S(1)}, u32[]{:S(2)}, u32[]{:S(2)}) %collective-permute-start) | collective-permute-done | bytes 58400 | tf_op jit(solution)/shard_map/ppermute | solution.py:24
  12.5 3.0 %collective-permute-done.2.refs_3_ = bf16[4,7296]{1,0:T(4,128)(2,1)S(1)} collective-permute-done((bf16[4,7296]{1,0:T(4,128)(2,1)S(1)}, bf16[4,7296]{1,0:T(4,128)(2,1)S(1)}, u32[]{:S(2)}, u32[]{:S(2)}) %collective-permute-start.2) | collective-permute-done | bytes 58400 | tf_op jit(solution)/shard_map/ppermute | solution.py:24
  15.4 0.1 pack_rows.1.refs_1_.own_ref
  15.5 1.6 %collective-permute-start.3 = (bf16[16,7296]{1,0:T(8,128)(2,1)S(1)}, bf16[16,7296]{1,0:T(8,128)(2,1)S(1)}, u32[]{:S(2)}, u32[]{:S(2)}) collective-permute-start(bf16[16,7296]{1,0:T(8,128)(2,1)S(1)} %pack_rows.1.refs_1_.own_ref), channel_id=1, source_target_pairs={{0,2},{1,3},{2,0},{3,1},{4,6},{5,7},{6,4},{7,5},{8,10},{9,11},{10,... | collective-permute-start | bytes 700424 | tf_op jit(solution)/shard_map/ppermute | solution.py:24
  17.1 1.5 %collective-permute-start.4 = (bf16[16,7296]{1,0:T(8,128)(2,1)S(1)}, bf16[16,7296]{1,0:T(8,128)(2,1)S(1)}, u32[]{:S(2)}, u32[]{:S(2)}) collective-permute-start(bf16[16,7296]{1,0:T(8,128)(2,1)S(1)} %pack_rows.1.refs_1_.own_ref), channel_id=1, source_target_pairs={{0,16},{16,0},{1,17},{17,1},{2,18},{18,2},{3,19},{19,3},{4,20},{20... | collective-permute-start | bytes 700424 | tf_op jit(solution)/shard_map/ppermute | solution.py:22
  18.6 0.5 collective-permute-start.5
  19.0 0.0 collective-permute-start.6
  19.0 5.1 %collective-permute-done.3.refs_2_.low_ref = bf16[16,7296]{1,0:T(8,128)(2,1)S(1)} collective-permute-done((bf16[16,7296]{1,0:T(8,128)(2,1)S(1)}, bf16[16,7296]{1,0:T(8,128)(2,1)S(1)}, u32[]{:S(2)}, u32[]{:S(2)}) %collective-permute-start.3) | collective-permute-done | bytes 233504 | tf_op jit(solution)/shard_map/ppermute | solution.py:24
  24.1 0.0 collective-permute-start.7
  24.1 0.4 collective-permute-done.4.refs_3_
  24.5 0.1 collective-permute-start.8
  24.6 2.3 %collective-permute-done.5.refs_4_ = bf16[16,7296]{1,0:T(8,128)(2,1)S(1)} collective-permute-done((bf16[16,7296]{1,0:T(8,128)(2,1)S(1)}, bf16[16,7296]{1,0:T(8,128)(2,1)S(1)}, u32[]{:S(2)}, u32[]{:S(2)}) %collective-permute-start.5) | collective-permute-done | bytes 233504 | tf_op jit(solution)/shard_map/ppermute | solution.py:30
  27.0 0.0 collective-permute-start.9
  27.0 0.1 pad_add_fusion.refs_0_.place_ref
  27.1 0.0 collective-permute-done.6.refs_5_
  27.1 0.0 collective-permute-done.7.refs_6_
  27.1 0.0 collective-permute-done.8.refs_7_
  27.1 1.4 %collective-permute-done.9.refs_8_ = bf16[16,7296]{1,0:T(8,128)(2,1)S(1)} collective-permute-done((bf16[16,7296]{1,0:T(8,128)(2,1)S(1)}, bf16[16,7296]{1,0:T(8,128)(2,1)S(1)}, u32[]{:S(2)}, u32[]{:S(2)}) %collective-permute-start.9) | collective-permute-done | bytes 233504 | tf_op jit(solution)/shard_map/ppermute | solution.py:24
  28.5 5.3 %experts.1 = (bf16[64,3584]{1,0:T(8,128)(2,1)S(1)}, bf16[64,3584]{1,0:T(8,128)(2,1)S(1)}, bf16[64,3584]{1,0:T(8,128)(2,1)S(1)}, bf16[64,3584]{1,0:T(8,128)(2,1)S(1)}) custom-call(s32[4]{0:T(128)S(1)} %pad_add_fusion.refs_0_.place_ref, bf16[16,7296]{1,0:T(8,128)(2,1)S(1)} %pack_rows.1.refs_1_.own_ref, ...), custom_call_target="tpu_custom_call" | custom-call | tf_op jit(solution)/shard_map/experts/pallas_call | solution.py:85
  33.8 0.0 copy-start.3
  33.8 0.0 collective-permute-done.10.refs_5_
  33.8 0.2 collective-permute-start.11
  34.0 0.4 collective-permute-start.12
  34.4 1.3 %collective-permute-done.11 = bf16[64,3584]{1,0:T(8,128)(2,1)S(1)} collective-permute-done((bf16[64,3584]{1,0:T(8,128)(2,1)S(1)}, bf16[64,3584]{1,0:T(8,128)(2,1)S(1)}, u32[]{:S(2)}, u32[]{:S(2)}) %collective-permute-start.11) | collective-permute-done | bytes 458784 | tf_op jit(solution)/shard_map/ppermute | solution.py:24
  35.7 0.1 add_convert_fusion.1
  35.8 1.6 %collective-permute-start.14 = (bf16[32,3584]{1,0:T(8,128)(2,1)S(1)}, bf16[32,3584]{1,0:T(8,128)(2,1)S(1)}, u32[]{:S(2)}, u32[]{:S(2)}) collective-permute-start(bf16[32,3584]{1,0:T(8,128)(2,1)S(1)} %add_convert_fusion.1), channel_id=1, source_target_pairs={{0,16},{16,0},{1,17},{17,1},{2,18},{18,2},{3,19},{19,3},{4,20},{20... | collective-permute-start | bytes 688136 | tf_op jit(solution)/shard_map/ppermute | solution.py:22
  37.3 0.0 collective-permute-done.12
  37.4 0.1 add_convert_fusion
  37.5 1.6 %collective-permute-start.13 = (bf16[32,3584]{1,0:T(8,128)(2,1)S(1)}, bf16[32,3584]{1,0:T(8,128)(2,1)S(1)}, u32[]{:S(2)}, u32[]{:S(2)}) collective-permute-start(bf16[32,3584]{1,0:T(8,128)(2,1)S(1)} %get-tuple-element.57), channel_id=1, source_target_pairs={{0,2},{1,3},{2,0},{3,1},{4,6},{5,7},{6,4},{7,5},{8,10},{9,11},{10,... | collective-permute-start | bytes 688136 | tf_op jit(solution)/shard_map/ppermute | solution.py:24
  39.1 0.5 collective-permute-start.15
  39.5 0.0 collective-permute-start.19
  39.5 0.0 copy-done.1
  39.5 0.0 copy-done.4
  39.5 1.7 %cache_part.1 = (f32[4,64,128]{2,1,0:T(8,128)S(1)}, f32[4,64,512]{2,1,0:T(8,128)S(1)}) custom-call(s32[4]{0:T(128)S(1)} %copy-done.4, bf16[4,64,576]{2,1,0:T(8,128)(2,1)S(1)} %copy-done, bf16[4,576,256]{2,1,0:T(8,128)(2,1)S(1)} %bitcast.14), custom_call_target="tpu_custom_call" | custom-call | flops 150994944 | bytes 1179648 | tf_op jit(solution)/shard_map/cache_part/pallas_call | solution.py:63
  41.3 0.6 residual_rows.1.residual_ref
  41.9 0.6 collective-permute-start.20
  42.4 1.9 %collective-permute-done.14 = bf16[32,3584]{1,0:T(8,128)(2,1)S(1)} collective-permute-done((bf16[32,3584]{1,0:T(8,128)(2,1)S(1)}, bf16[32,3584]{1,0:T(8,128)(2,1)S(1)}, u32[]{:S(2)}, u32[]{:S(2)}) %collective-permute-start.14) | collective-permute-done | bytes 229408 | tf_op jit(solution)/shard_map/ppermute | solution.py:22
  44.3 5.5 %collective-permute-done.13 = bf16[32,3584]{1,0:T(8,128)(2,1)S(1)} collective-permute-done((bf16[32,3584]{1,0:T(8,128)(2,1)S(1)}, bf16[32,3584]{1,0:T(8,128)(2,1)S(1)}, u32[]{:S(2)}, u32[]{:S(2)}) %collective-permute-start.13) | collective-permute-done | bytes 229408 | tf_op jit(solution)/shard_map/ppermute | solution.py:24
  49.8 0.0 collective-permute-done.15
  49.8 0.1 add_convert_fusion.3
  49.9 0.6 collective-permute-start.16
  50.6 1.4 %collective-permute-start.17 = (bf16[16,1792]{1,0:T(8,128)(2,1)S(1)}, bf16[16,1792]{1,0:T(8,128)(2,1)S(1)}, u32[]{:S(2)}, u32[]{:S(2)}) collective-permute-start(bf16[16,1792]{1,0:T(8,128)(2,1)S(1)} %get-tuple-element.54), channel_id=1, source_target_pairs={{0,12},{1,13},{2,14},{3,15},{4,8},{5,9},{6,10},{7,11},{8,4},{9,5},... | collective-permute-start | bytes 172040 | tf_op jit(solution)/shard_map/ppermute | solution.py:24
  51.9 1.6 %collective-permute-start.18 = (bf16[16,1792]{1,0:T(8,128)(2,1)S(1)}, bf16[16,1792]{1,0:T(8,128)(2,1)S(1)}, u32[]{:S(2)}, u32[]{:S(2)}) collective-permute-start(bf16[16,1792]{1,0:T(8,128)(2,1)S(1)} %get-tuple-element.53), channel_id=1, source_target_pairs={{0,4},{1,5},{2,6},{3,7},{4,0},{5,1},{6,2},{7,3},{8,12},{9,13},{10,... | collective-permute-start | bytes 172040 | tf_op jit(solution)/shard_map/ppermute | solution.py:24
  53.5 0.0 collective-permute-done.19.refs_4_
  53.5 0.0 collective-permute-done.20.refs_6_
  53.6 1.9 %collective-permute-done.16.refs_0_ = bf16[16,1792]{1,0:T(8,128)(2,1)S(1)} collective-permute-done((bf16[16,1792]{1,0:T(8,128)(2,1)S(1)}, bf16[16,1792]{1,0:T(8,128)(2,1)S(1)}, u32[]{:S(2)}, u32[]{:S(2)}) %collective-permute-start.16) | collective-permute-done | bytes 57376 | tf_op jit(solution)/shard_map/ppermute | solution.py:24
  55.5 1.2 %collective-permute-done.17.refs_1_ = bf16[16,1792]{1,0:T(8,128)(2,1)S(1)} collective-permute-done((bf16[16,1792]{1,0:T(8,128)(2,1)S(1)}, bf16[16,1792]{1,0:T(8,128)(2,1)S(1)}, u32[]{:S(2)}, u32[]{:S(2)}) %collective-permute-start.17) | collective-permute-done | bytes 57376 | tf_op jit(solution)/shard_map/ppermute | solution.py:24
  56.7 0.0 collective-permute-done.18.refs_2_
  56.7 1.1 %latent_parts.1 = (f32[4,640]{1,0:T(4,128)S(1)}, bf16[4,1792]{1,0:T(4,128)(2,1)S(1)}, bf16[4,3072]{1,0:T(4,128)(2,1)S(1)}, bf16[4,3072]{1,0:T(4,128)(2,1)S(1)}, bf16[4,3072]{1,0:T(4,128)(2,1)S(1)}) custom-call(s32[4]{0:T(128)S(1)} %pad_add_fusion.refs_0_.place_ref, f32[16,1792]{1,0:T(8,128)S(1)} %convert_add_fusion.sum_ref, ...), custom_call_target="tpu_custom_call" | custom-call | tf_op jit(solution)/shard_map/latent_parts/pallas_call | solution.py:85
  57.8 1.6 %collective-permute-start.21 = (bf16[4,3072]{1,0:T(4,128)(2,1)S(1)}, bf16[4,3072]{1,0:T(4,128)(2,1)S(1)}, u32[]{:S(2)}, u32[]{:S(2)}) collective-permute-start(bf16[4,3072]{1,0:T(4,128)(2,1)S(1)} %get-tuple-element.50), channel_id=1, source_target_pairs={{0,2},{1,3},{2,0},{3,1},{4,6},{5,7},{6,4},{7,5},{8,10},{9,11},{10,... | collective-permute-start | bytes 73736 | tf_op jit(solution)/shard_map/ppermute | solution.py:24
  59.5 1.0 %collective-permute-start.22 = (bf16[4,3072]{1,0:T(4,128)(2,1)S(1)}, bf16[4,3072]{1,0:T(4,128)(2,1)S(1)}, u32[]{:S(2)}, u32[]{:S(2)}) collective-permute-start(bf16[4,3072]{1,0:T(4,128)(2,1)S(1)} %get-tuple-element.51), channel_id=1, source_target_pairs={{0,8},{1,9},{2,10},{3,11},{4,12},{5,13},{6,14},{7,15},{8,0},{9,1},... | collective-permute-start | bytes 73736 | tf_op jit(solution)/shard_map/ppermute | solution.py:24
  60.5 1.8 %collective-permute-start.23 = (bf16[4,3072]{1,0:T(4,128)(2,1)S(1)}, bf16[4,3072]{1,0:T(4,128)(2,1)S(1)}, u32[]{:S(2)}, u32[]{:S(2)}) collective-permute-start(bf16[4,3072]{1,0:T(4,128)(2,1)S(1)} %get-tuple-element.52), channel_id=1, source_target_pairs={{0,10},{1,11},{2,8},{3,9},{4,14},{5,15},{6,12},{7,13},{8,2},{9,3},... | collective-permute-start | bytes 73736 | tf_op jit(solution)/shard_map/ppermute | solution.py:24
  62.3 0.0 collective-permute-done.21.refs_0_
  62.3 1.9 %collective-permute-done.22.refs_1_ = bf16[4,3072]{1,0:T(4,128)(2,1)S(1)} collective-permute-done((bf16[4,3072]{1,0:T(4,128)(2,1)S(1)}, bf16[4,3072]{1,0:T(4,128)(2,1)S(1)}, u32[]{:S(2)}, u32[]{:S(2)}) %collective-permute-start.22) | collective-permute-done | bytes 24608 | tf_op jit(solution)/shard_map/ppermute | solution.py:24
  64.2 1.9 %collective-permute-done.23.refs_2_ = bf16[4,3072]{1,0:T(4,128)(2,1)S(1)} collective-permute-done((bf16[4,3072]{1,0:T(4,128)(2,1)S(1)}, bf16[4,3072]{1,0:T(4,128)(2,1)S(1)}, u32[]{:S(2)}, u32[]{:S(2)}) %collective-permute-start.23) | collective-permute-done | bytes 24608 | tf_op jit(solution)/shard_map/ppermute | solution.py:24
  66.1 1.8 %finish.1 = (bf16[4,7168]{1,0:T(4,128)(2,1)}, bf16[4,576]{1,0:T(4,128)(2,1)}, bf16[4,64,512]{2,1,0:T(8,128)(2,1)}) custom-call(s32[4]{0:T(128)S(1)} %pad_add_fusion.refs_0_.place_ref, f32[4,640]{1,0:T(4,128)S(1)} %get-tuple-element.46.sums_ref, bf16[4,1792]{1,0:T(4,128)(2,1)S(1)} %get-tuple-element.47.moe_ref, bf16[4,64,576]{2,1,0:T(8,128)(2,1)S(1)} %copy-done, ...), custom_call_target="tpu_custom_call" | custom-call | tf_op jit(solution)/shard_map/finish/pallas_call | solution.py:85
  (10 shorter events, 0.1 us)
Async XLA Ops:
  3.1 5.7 %collective-permute-start.1 = (bf16[4,7296]{1,0:T(4,128)(2,1)S(1)}, bf16[4,7296]{1,0:T(4,128)(2,1)S(1)}, u32[]{:S(2)}, u32[]{:S(2)}) collective-permute-start(bf16[4,7296]{1,0:T(4,128)(2,1)S(1)} %select_select_fusion.refs_0_), channel_id=1, source_target_pairs={{0,4},{1,5},{2,6},{3,7},{4,0},{5,1},{6,2},{7,3},{8,12},{9,13},{10,... | collective-permute-start | bytes 175112 | tf_op jit(solution)/shard_map/ppermute | solution.py:24
  6.2 6.3 %collective-permute-start = (bf16[4,7296]{1,0:T(4,128)(2,1)S(1)}, bf16[4,7296]{1,0:T(4,128)(2,1)S(1)}, u32[]{:S(2)}, u32[]{:S(2)}) collective-permute-start(bf16[4,7296]{1,0:T(4,128)(2,1)S(1)} %select_select_fusion.refs_0_), channel_id=1, source_target_pairs={{0,8},{1,9},{2,10},{3,11},{4,12},{5,13},{6,14},{7,15},{8,0},{9,1},... | collective-permute-start | bytes 175112 | tf_op jit(solution)/shard_map/ppermute | solution.py:24
  8.7 6.7 %collective-permute-start.2 = (bf16[4,7296]{1,0:T(4,128)(2,1)S(1)}, bf16[4,7296]{1,0:T(4,128)(2,1)S(1)}, u32[]{:S(2)}, u32[]{:S(2)}) collective-permute-start(bf16[4,7296]{1,0:T(4,128)(2,1)S(1)} %select_select_fusion.refs_0_), channel_id=1, source_target_pairs={{0,12},{1,13},{2,14},{3,15},{4,8},{5,9},{6,10},{7,11},{8,4},{9,5},... | collective-permute-start | bytes 175112 | tf_op jit(solution)/shard_map/ppermute | solution.py:24
  8.8 25.1 %collective-permute-start.10 = (bf16[448,576]{1,0:T(8,128)(2,1)}, bf16[448,576]{1,0:T(8,128)(2,1)S(1)}, u32[]{:S(2)}, u32[]{:S(2)}) collective-permute-start(bf16[448,576]{1,0:T(8,128)(2,1)} %refs_3_.1), channel_id=1, source_target_pairs={{0,4},{1,5},{2,6},{3,7},{4,0},{5,1},{6,2},{7,3},{8,12},{9,13},{10,... | collective-permute-start | bytes 1548296 | tf_op jit(solution)/shard_map/ppermute | solution.py:24
  15.5 8.6 %collective-permute-start.3 = (bf16[16,7296]{1,0:T(8,128)(2,1)S(1)}, bf16[16,7296]{1,0:T(8,128)(2,1)S(1)}, u32[]{:S(2)}, u32[]{:S(2)}) collective-permute-start(bf16[16,7296]{1,0:T(8,128)(2,1)S(1)} %pack_rows.1.refs_1_.own_ref), channel_id=1, source_target_pairs={{0,2},{1,3},{2,0},{3,1},{4,6},{5,7},{6,4},{7,5},{8,10},{9,11},{10,... | collective-permute-start | bytes 700424 | tf_op jit(solution)/shard_map/ppermute | solution.py:24
  17.1 7.5 %collective-permute-start.4 = (bf16[16,7296]{1,0:T(8,128)(2,1)S(1)}, bf16[16,7296]{1,0:T(8,128)(2,1)S(1)}, u32[]{:S(2)}, u32[]{:S(2)}) collective-permute-start(bf16[16,7296]{1,0:T(8,128)(2,1)S(1)} %pack_rows.1.refs_1_.own_ref), channel_id=1, source_target_pairs={{0,16},{16,0},{1,17},{17,1},{2,18},{18,2},{3,19},{19,3},{4,20},{20... | collective-permute-start | bytes 700424 | tf_op jit(solution)/shard_map/ppermute | solution.py:22
  18.6 8.4 %collective-permute-start.5 = (bf16[16,7296]{1,0:T(8,128)(2,1)S(1)}, bf16[16,7296]{1,0:T(8,128)(2,1)S(1)}, u32[]{:S(2)}, u32[]{:S(2)}) collective-permute-start(bf16[16,7296]{1,0:T(8,128)(2,1)S(1)} %pack_rows.1.refs_1_.own_ref), channel_id=1, source_target_pairs={{0,18},{1,19},{2,16},{3,17},{4,22},{5,23},{6,20},{7,21},{8,26},{9,... | collective-permute-start | bytes 700424 | tf_op jit(solution)/shard_map/ppermute | solution.py:30
  19.0 8.0 %collective-permute-start.6 = (bf16[16,7296]{1,0:T(8,128)(2,1)S(1)}, bf16[16,7296]{1,0:T(8,128)(2,1)S(1)}, u32[]{:S(2)}, u32[]{:S(2)}) collective-permute-start(bf16[16,7296]{1,0:T(8,128)(2,1)S(1)} %pack_rows.1.refs_1_.own_ref), channel_id=1, source_target_pairs={{0,1},{1,0},{2,3},{3,2},{4,5},{5,4},{6,7},{7,6},{8,9},{9,8},{10,11... | collective-permute-start | bytes 700424 | tf_op jit(solution)/shard_map/ppermute | solution.py:24
  24.1 3.0 %collective-permute-start.7 = (bf16[16,7296]{1,0:T(8,128)(2,1)S(1)}, bf16[16,7296]{1,0:T(8,128)(2,1)S(1)}, u32[]{:S(2)}, u32[]{:S(2)}) collective-permute-start(bf16[16,7296]{1,0:T(8,128)(2,1)S(1)} %collective-permute-done.3.refs_2_.low_ref), channel_id=1, source_target_pairs={{0,1},{1,0},{2,3},{3,2},{4,5},{5,4},{6,7},{7,6},{8,9},{9,8},{10,11... | collective-permute-start | bytes 700424 | tf_op jit(solution)/shard_map/ppermute | solution.py:24
  24.5 2.6 %collective-permute-start.8 = (bf16[16,7296]{1,0:T(8,128)(2,1)S(1)}, bf16[16,7296]{1,0:T(8,128)(2,1)S(1)}, u32[]{:S(2)}, u32[]{:S(2)}) collective-permute-start(bf16[16,7296]{1,0:T(8,128)(2,1)S(1)} %collective-permute-done.4.refs_3_), channel_id=1, source_target_pairs={{0,1},{1,0},{2,3},{3,2},{4,5},{5,4},{6,7},{7,6},{8,9},{9,8},{10,11... | collective-permute-start | bytes 700424 | tf_op jit(solution)/shard_map/ppermute | solution.py:24
  27.0 1.5 %collective-permute-start.9 = (bf16[16,7296]{1,0:T(8,128)(2,1)S(1)}, bf16[16,7296]{1,0:T(8,128)(2,1)S(1)}, u32[]{:S(2)}, u32[]{:S(2)}) collective-permute-start(bf16[16,7296]{1,0:T(8,128)(2,1)S(1)} %collective-permute-done.5.refs_4_), channel_id=1, source_target_pairs={{0,1},{1,0},{2,3},{3,2},{4,5},{5,4},{6,7},{7,6},{8,9},{9,8},{10,11... | collective-permute-start | bytes 700424 | tf_op jit(solution)/shard_map/ppermute | solution.py:24
  27.1 12.5 %copy-start.2 = (bf16[448,576]{1,0:T(8,128)(2,1)S(1)}, bf16[448,576]{1,0:T(8,128)(2,1)}, u32[]{:S(2)}) copy-start(bf16[448,576]{1,0:T(8,128)(2,1)} %refs_3_.1) | copy-start | bytes 1548292
  27.1 12.5 %copy-start = (bf16[4,64,576]{2,1,0:T(8,128)(2,1)S(1)}, bf16[4,64,576]{2,1,0:T(8,128)(2,1)}, u32[]{:S(2)}) copy-start(bf16[4,64,576]{2,1,0:T(8,128)(2,1)} %q_ref.3) | copy-start | bytes 884740
  27.1 12.5 %copy-start.1 = (bf16[4,256,576]{1,2,0:T(8,128)(2,1)S(1)}, bf16[4,256,576]{1,2,0:T(8,128)(2,1)}, u32[]{:S(2)}) copy-start(bf16[4,256,576]{1,2,0:T(8,128)(2,1)} %param.20) | copy-start | bytes 3538948
  27.1 12.5 %copy-start.4 = (s32[4]{0:T(128)S(1)}, s32[4]{0:T(128)}, u32[]{:S(2)}) copy-start(s32[4]{0:T(128)} %lengths_ref.1) | copy-start | bytes 52
  33.8 22.9 %copy-start.3 = (f32[7168]{0:T(1024)S(1)}, f32[7168]{0:T(1024)}, u32[]{:S(2)}) copy-start(f32[7168]{0:T(1024)} %param.17) | copy-start | bytes 86020
  33.8 1.9 %collective-permute-start.11 = (bf16[64,3584]{1,0:T(8,128)(2,1)S(1)}, bf16[64,3584]{1,0:T(8,128)(2,1)S(1)}, u32[]{:S(2)}, u32[]{:S(2)}) collective-permute-start(bf16[64,3584]{1,0:T(8,128)(2,1)S(1)} %get-tuple-element.35), channel_id=1, source_target_pairs={{0,1},{1,0},{2,3},{3,2},{4,5},{5,4},{6,7},{7,6},{8,9},{9,8},{10,11... | collective-permute-start | bytes 1376264 | tf_op jit(solution)/shard_map/ppermute | solution.py:24
  34.0 3.3 %collective-permute-start.12 = (bf16[64,3584]{1,0:T(8,128)(2,1)S(1)}, bf16[64,3584]{1,0:T(8,128)(2,1)S(1)}, u32[]{:S(2)}, u32[]{:S(2)}) collective-permute-start(bf16[64,3584]{1,0:T(8,128)(2,1)S(1)} %get-tuple-element.37), channel_id=1, source_target_pairs={{0,1},{1,0},{2,3},{3,2},{4,5},{5,4},{6,7},{7,6},{8,9},{9,8},{10,11... | collective-permute-start | bytes 1376264 | tf_op jit(solution)/shard_map/ppermute | solution.py:24
  35.8 8.5 %collective-permute-start.14 = (bf16[32,3584]{1,0:T(8,128)(2,1)S(1)}, bf16[32,3584]{1,0:T(8,128)(2,1)S(1)}, u32[]{:S(2)}, u32[]{:S(2)}) collective-permute-start(bf16[32,3584]{1,0:T(8,128)(2,1)S(1)} %add_convert_fusion.1), channel_id=1, source_target_pairs={{0,16},{16,0},{1,17},{17,1},{2,18},{18,2},{3,19},{19,3},{4,20},{20... | collective-permute-start | bytes 688136 | tf_op jit(solution)/shard_map/ppermute | solution.py:22
  37.5 12.3 %collective-permute-start.13 = (bf16[32,3584]{1,0:T(8,128)(2,1)S(1)}, bf16[32,3584]{1,0:T(8,128)(2,1)S(1)}, u32[]{:S(2)}, u32[]{:S(2)}) collective-permute-start(bf16[32,3584]{1,0:T(8,128)(2,1)S(1)} %get-tuple-element.57), channel_id=1, source_target_pairs={{0,2},{1,3},{2,0},{3,1},{4,6},{5,7},{6,4},{7,5},{8,10},{9,11},{10,... | collective-permute-start | bytes 688136 | tf_op jit(solution)/shard_map/ppermute | solution.py:24
  39.1 10.8 %collective-permute-start.15 = (bf16[32,3584]{1,0:T(8,128)(2,1)S(1)}, bf16[32,3584]{1,0:T(8,128)(2,1)S(1)}, u32[]{:S(2)}, u32[]{:S(2)}) collective-permute-start(bf16[32,3584]{1,0:T(8,128)(2,1)S(1)} %get-tuple-element.56), channel_id=1, source_target_pairs={{0,18},{1,19},{2,16},{3,17},{4,22},{5,23},{6,20},{7,21},{8,26},{9,... | collective-permute-start | bytes 688136 | tf_op jit(solution)/shard_map/ppermute | solution.py:30
  39.5 14.0 %collective-permute-start.19 = (bf16[448,576]{1,0:T(8,128)(2,1)S(1)}, bf16[448,576]{1,0:T(8,128)(2,1)S(1)}, u32[]{:S(2)}, u32[]{:S(2)}) collective-permute-start(bf16[448,576]{1,0:T(8,128)(2,1)S(1)} %copy-done.2), channel_id=1, source_target_pairs={{0,1},{1,0},{2,3},{3,2},{4,5},{5,4},{6,7},{7,6},{8,9},{9,8},{10,11... | collective-permute-start | bytes 1548296 | tf_op jit(solution)/shard_map/ppermute | solution.py:24
  41.9 11.7 %collective-permute-start.20 = (bf16[448,576]{1,0:T(8,128)(2,1)S(1)}, bf16[448,576]{1,0:T(8,128)(2,1)S(1)}, u32[]{:S(2)}, u32[]{:S(2)}) collective-permute-start(bf16[448,576]{1,0:T(8,128)(2,1)S(1)} %collective-permute-done.10.refs_5_), channel_id=1, source_target_pairs={{0,1},{1,0},{2,3},{3,2},{4,5},{5,4},{6,7},{7,6},{8,9},{9,8},{10,11... | collective-permute-start | bytes 1548296 | tf_op jit(solution)/shard_map/ppermute | solution.py:24
  49.9 5.6 %collective-permute-start.16 = (bf16[16,1792]{1,0:T(8,128)(2,1)S(1)}, bf16[16,1792]{1,0:T(8,128)(2,1)S(1)}, u32[]{:S(2)}, u32[]{:S(2)}) collective-permute-start(bf16[16,1792]{1,0:T(8,128)(2,1)S(1)} %get-tuple-element.55), channel_id=1, source_target_pairs={{0,8},{1,9},{2,10},{3,11},{4,12},{5,13},{6,14},{7,15},{8,0},{9,1},... | collective-permute-start | bytes 172040 | tf_op jit(solution)/shard_map/ppermute | solution.py:24
  50.6 6.1 %collective-permute-start.17 = (bf16[16,1792]{1,0:T(8,128)(2,1)S(1)}, bf16[16,1792]{1,0:T(8,128)(2,1)S(1)}, u32[]{:S(2)}, u32[]{:S(2)}) collective-permute-start(bf16[16,1792]{1,0:T(8,128)(2,1)S(1)} %get-tuple-element.54), channel_id=1, source_target_pairs={{0,12},{1,13},{2,14},{3,15},{4,8},{5,9},{6,10},{7,11},{8,4},{9,5},... | collective-permute-start | bytes 172040 | tf_op jit(solution)/shard_map/ppermute | solution.py:24
  51.9 4.8 %collective-permute-start.18 = (bf16[16,1792]{1,0:T(8,128)(2,1)S(1)}, bf16[16,1792]{1,0:T(8,128)(2,1)S(1)}, u32[]{:S(2)}, u32[]{:S(2)}) collective-permute-start(bf16[16,1792]{1,0:T(8,128)(2,1)S(1)} %get-tuple-element.53), channel_id=1, source_target_pairs={{0,4},{1,5},{2,6},{3,7},{4,0},{5,1},{6,2},{7,3},{8,12},{9,13},{10,... | collective-permute-start | bytes 172040 | tf_op jit(solution)/shard_map/ppermute | solution.py:24
  57.8 4.5 %collective-permute-start.21 = (bf16[4,3072]{1,0:T(4,128)(2,1)S(1)}, bf16[4,3072]{1,0:T(4,128)(2,1)S(1)}, u32[]{:S(2)}, u32[]{:S(2)}) collective-permute-start(bf16[4,3072]{1,0:T(4,128)(2,1)S(1)} %get-tuple-element.50), channel_id=1, source_target_pairs={{0,2},{1,3},{2,0},{3,1},{4,6},{5,7},{6,4},{7,5},{8,10},{9,11},{10,... | collective-permute-start | bytes 73736 | tf_op jit(solution)/shard_map/ppermute | solution.py:24
  59.5 4.7 %collective-permute-start.22 = (bf16[4,3072]{1,0:T(4,128)(2,1)S(1)}, bf16[4,3072]{1,0:T(4,128)(2,1)S(1)}, u32[]{:S(2)}, u32[]{:S(2)}) collective-permute-start(bf16[4,3072]{1,0:T(4,128)(2,1)S(1)} %get-tuple-element.51), channel_id=1, source_target_pairs={{0,8},{1,9},{2,10},{3,11},{4,12},{5,13},{6,14},{7,15},{8,0},{9,1},... | collective-permute-start | bytes 73736 | tf_op jit(solution)/shard_map/ppermute | solution.py:24
  60.5 5.6 %collective-permute-start.23 = (bf16[4,3072]{1,0:T(4,128)(2,1)S(1)}, bf16[4,3072]{1,0:T(4,128)(2,1)S(1)}, u32[]{:S(2)}, u32[]{:S(2)}) collective-permute-start(bf16[4,3072]{1,0:T(4,128)(2,1)S(1)} %get-tuple-element.52), channel_id=1, source_target_pairs={{0,10},{1,11},{2,8},{3,9},{4,14},{5,15},{6,12},{7,13},{8,2},{9,3},... | collective-permute-start | bytes 73736 | tf_op jit(solution)/shard_map/ppermute | solution.py:24

commit v6 on v5

--- a/solution.py
+++ b/solution.py
@@ -94,13 +94,13 @@
 
 
 def with_info(hidden_in, expert_ids, gate_scores):
-    width, picks = hidden_in.shape[1], expert_ids.shape[1]
-    x = jnp.pad(hidden_in, ((0, 0), (0, LANES)))
-    column = lax.broadcasted_iota(jnp.int32, x.shape, 1) - width
-    for i, values in enumerate((expert_ids.astype(x.dtype), gate_scores)):
-        for k in range(picks):
-            x = jnp.where(column == i * picks + k, values[:, k : k + 1], x)
-    return x
+    picks = expert_ids.shape[1]
+    values = (expert_ids.astype(jnp.bfloat16), gate_scores)
+    info = sum(
+        jnp.dot(v, jnp.eye(picks, LANES, i * picks, jnp.bfloat16), preferred_element_type=jnp.float32)
+        for i, v in enumerate(values)
+    )
+    return jnp.concatenate([hidden_in, info.astype(hidden_in.dtype)], axis=1)
 
 
 def pack_kernel(_, *refs):

time: 68.1 us -> 67.6 us (level)
  matrix products: 0 us -> 1.05 us
  other arithmetic: 2.08 us -> 1.26 us
  local copies, waits for them, and re-layouts: 0.76 us -> 0.03 us
    dot_general x0 -> x2, matrix products: none -> 1.05 us  [with_info(): jnp.dot(v, jnp.eye(picks, LANES, i * picks, jnp.bfloat16), preferred_elem...]
    select_n x1 -> x0, other arithmetic: 0.98 us -> none  [with_info(): x = jnp.where(column == i * picks + k, values[:, k:k + 1], x)]
    concatenate x0 -> x1, other arithmetic: none -> 0.86 us  [with_info(): return jnp.concatenate([hidden_in, info.astype(hidden_in.dtype)], axis=1)]
    broadcast_in_dim x1 -> x0, local copies, waits for them, and re-layouts: 0.74 us -> none  [with_info(): x = jnp.where(column == i * picks + k, values[:, k:k + 1], x)]
    convert_element_type x1 -> x0, other arithmetic: 0.68 us -> none  [with_info(): expert_ids.astype(x.dtype)]
where the time goes in v6:
time: 67.6 us; the launch traced here: 67.4 us
  waiting for transfers between devices  30 us (44%)
  starting transfers between devices  23.7 us (35%)
  Pallas kernels  10.6 us (16%)
  other arithmetic  1.26 us (2%)
  matrix products  1.05 us (2%)
  between operations  0.8 us (1%)
    ppermute x20, waiting for transfers between devices, swap(): lax.ppermute(x, 'dev', [(i, i ^ flips) for i in range(lax.axis_size('dev'...  25.4 us
    ppermute x20, starting transfers between devices, swap(): lax.ppermute(x, 'dev', [(i, i ^ flips) for i in range(lax.axis_size('dev'...  19.7 us
    pallas_call x5, Pallas kernels, kernel_call(): pl.pallas_call(body, out_shape=out_shape, in_specs=specs, out_specs=jax.t...  8.87 us
    ppermute x2, starting transfers between devices, swap(): lax.ppermute(x, 'sec', [(i, i ^ 1) for i in range(lax.axis_size('sec'))])  3.04 us
    ppermute x2, waiting for transfers between devices, swap_both(): return lax.ppermute(x, ('sec', 'dev'), pairs)  2.34 us
    ppermute x2, waiting for transfers between devices, swap(): lax.ppermute(x, 'sec', [(i, i ^ 1) for i in range(lax.axis_size('sec'))])  2.29 us
    pallas_call x1, Pallas kernels, cache_part(): pl.pallas_call(cache_kernel, out_shape=(jax.ShapeDtypeStruct((rows, heads...  1.7 us
  transfers between devices with their start and end apart: 24, of which 13 were waited for; matrix products, arithmetic and copies ran while one was open for 1% of the time, Pallas kernels for 11%

profile of v6, /device:TPU:0, one launch (start us, length us, event | category | flops | bytes accessed | tf_op | source)
XLA Modules:
  0.0 67.4 jit_solution(2968904968075431845)
XLA Ops:
  0.6 0.0 copy-start
  0.7 0.9 %fusion.3 = f32[128,4]{0,1:T(4,128)S(1)} fusion(s32[4,2]{0,1:T(2,128)} %param.12), kind=kOutput, calls=%fused_computation.12 | convolution fusion | flops 2312 | bytes 2080 | tf_op jit(solution)/shard_map/dot_general | solution.py:100
  1.5 0.0 copy-done
  1.5 0.2 fusion.1
  1.7 0.9 %pad_maximum_fusion.refs_0_ = bf16[4,7296]{1,0:T(4,128)(2,1)S(1)} fusion(bf16[4,128]{1,0:T(4,128)(2,1)S(1)} %fusion.1, bf16[4,7168]{1,0:T(4,128)(2,1)} %param.11), kind=kLoop, calls=%fused_computation.10 | loop fusion | flops 116736 | bytes 116736 | tf_op jit(solution)/shard_map/concatenate | solution.py:103
  2.6 3.1 %collective-permute-start.1 = (bf16[4,7296]{1,0:T(4,128)(2,1)S(1)}, bf16[4,7296]{1,0:T(4,128)(2,1)S(1)}, u32[]{:S(2)}, u32[]{:S(2)}) collective-permute-start(bf16[4,7296]{1,0:T(4,128)(2,1)S(1)} %pad_maximum_fusion.refs_0_), channel_id=1, source_target_pairs={{0,4},{1,5},{2,6},{3,7},{4,0},{5,1},{6,2},{7,3},{8,12},{9,13},{10,... | collective-permute-start | bytes 175112 | tf_op jit(solution)/shard_map/ppermute | solution.py:24
  5.7 2.6 %collective-permute-start = (bf16[4,7296]{1,0:T(4,128)(2,1)S(1)}, bf16[4,7296]{1,0:T(4,128)(2,1)S(1)}, u32[]{:S(2)}, u32[]{:S(2)}) collective-permute-start(bf16[4,7296]{1,0:T(4,128)(2,1)S(1)} %pad_maximum_fusion.refs_0_), channel_id=1, source_target_pairs={{0,8},{1,9},{2,10},{3,11},{4,12},{5,13},{6,14},{7,15},{8,0},{9,1},... | collective-permute-start | bytes 175112 | tf_op jit(solution)/shard_map/ppermute | solution.py:24
  8.3 0.0 collective-permute-start.2
  8.3 0.0 collective-permute-done.1.refs_2_
  8.3 1.6 %collective-permute-start.10 = (bf16[448,576]{1,0:T(8,128)(2,1)}, bf16[448,576]{1,0:T(8,128)(2,1)S(1)}, u32[]{:S(2)}, u32[]{:S(2)}) collective-permute-start(bf16[448,576]{1,0:T(8,128)(2,1)} %refs_3_.1), channel_id=1, source_target_pairs={{0,4},{1,5},{2,6},{3,7},{4,0},{5,1},{6,2},{7,3},{8,12},{9,13},{10,... | collective-permute-start | bytes 1548296 | tf_op jit(solution)/shard_map/ppermute | solution.py:24
  9.9 2.1 %collective-permute-done.refs_1_ = bf16[4,7296]{1,0:T(4,128)(2,1)S(1)} collective-permute-done((bf16[4,7296]{1,0:T(4,128)(2,1)S(1)}, bf16[4,7296]{1,0:T(4,128)(2,1)S(1)}, u32[]{:S(2)}, u32[]{:S(2)}) %collective-permute-start) | collective-permute-done | bytes 58400 | tf_op jit(solution)/shard_map/ppermute | solution.py:24
  12.0 3.0 %collective-permute-done.2.refs_3_ = bf16[4,7296]{1,0:T(4,128)(2,1)S(1)} collective-permute-done((bf16[4,7296]{1,0:T(4,128)(2,1)S(1)}, bf16[4,7296]{1,0:T(4,128)(2,1)S(1)}, u32[]{:S(2)}, u32[]{:S(2)}) %collective-permute-start.2) | collective-permute-done | bytes 58400 | tf_op jit(solution)/shard_map/ppermute | solution.py:24
  14.9 0.1 pack_rows.1.refs_1_.own_ref
  15.0 1.6 %collective-permute-start.3 = (bf16[16,7296]{1,0:T(8,128)(2,1)S(1)}, bf16[16,7296]{1,0:T(8,128)(2,1)S(1)}, u32[]{:S(2)}, u32[]{:S(2)}) collective-permute-start(bf16[16,7296]{1,0:T(8,128)(2,1)S(1)} %pack_rows.1.refs_1_.own_ref), channel_id=1, source_target_pairs={{0,2},{1,3},{2,0},{3,1},{4,6},{5,7},{6,4},{7,5},{8,10},{9,11},{10,... | collective-permute-start | bytes 700424 | tf_op jit(solution)/shard_map/ppermute | solution.py:24
  16.6 1.5 %collective-permute-start.4 = (bf16[16,7296]{1,0:T(8,128)(2,1)S(1)}, bf16[16,7296]{1,0:T(8,128)(2,1)S(1)}, u32[]{:S(2)}, u32[]{:S(2)}) collective-permute-start(bf16[16,7296]{1,0:T(8,128)(2,1)S(1)} %pack_rows.1.refs_1_.own_ref), channel_id=1, source_target_pairs={{0,16},{16,0},{1,17},{17,1},{2,18},{18,2},{3,19},{19,3},{4,20},{20... | collective-permute-start | bytes 700424 | tf_op jit(solution)/shard_map/ppermute | solution.py:22
  18.1 0.5 collective-permute-start.5
  18.5 0.0 collective-permute-start.6
  18.6 5.1 %collective-permute-done.3.refs_2_.low_ref = bf16[16,7296]{1,0:T(8,128)(2,1)S(1)} collective-permute-done((bf16[16,7296]{1,0:T(8,128)(2,1)S(1)}, bf16[16,7296]{1,0:T(8,128)(2,1)S(1)}, u32[]{:S(2)}, u32[]{:S(2)}) %collective-permute-start.3) | collective-permute-done | bytes 233504 | tf_op jit(solution)/shard_map/ppermute | solution.py:24
  23.6 0.0 collective-permute-start.7
  23.6 0.4 collective-permute-done.4.refs_3_
  24.0 0.1 collective-permute-start.8
  24.1 2.3 %collective-permute-done.5.refs_4_ = bf16[16,7296]{1,0:T(8,128)(2,1)S(1)} collective-permute-done((bf16[16,7296]{1,0:T(8,128)(2,1)S(1)}, bf16[16,7296]{1,0:T(8,128)(2,1)S(1)}, u32[]{:S(2)}, u32[]{:S(2)}) %collective-permute-start.5) | collective-permute-done | bytes 233504 | tf_op jit(solution)/shard_map/ppermute | solution.py:30
  26.5 0.0 collective-permute-start.9
  26.5 0.1 pad_add_fusion.refs_0_.place_ref
  26.6 0.0 collective-permute-done.6.refs_5_
  26.6 0.0 collective-permute-done.7.refs_6_
  26.6 0.0 collective-permute-done.8.refs_7_
  26.6 1.4 %collective-permute-done.9.refs_8_ = bf16[16,7296]{1,0:T(8,128)(2,1)S(1)} collective-permute-done((bf16[16,7296]{1,0:T(8,128)(2,1)S(1)}, bf16[16,7296]{1,0:T(8,128)(2,1)S(1)}, u32[]{:S(2)}, u32[]{:S(2)}) %collective-permute-start.9) | collective-permute-done | bytes 233504 | tf_op jit(solution)/shard_map/ppermute | solution.py:24
  28.0 5.3 %experts.1 = (bf16[64,3584]{1,0:T(8,128)(2,1)S(1)}, bf16[64,3584]{1,0:T(8,128)(2,1)S(1)}, bf16[64,3584]{1,0:T(8,128)(2,1)S(1)}, bf16[64,3584]{1,0:T(8,128)(2,1)S(1)}) custom-call(s32[4]{0:T(128)S(1)} %pad_add_fusion.refs_0_.place_ref, bf16[16,7296]{1,0:T(8,128)(2,1)S(1)} %pack_rows.1.refs_1_.own_ref, ...), custom_call_target="tpu_custom_call" | custom-call | tf_op jit(solution)/shard_map/experts/pallas_call | solution.py:85
  33.3 0.0 copy-start.4
  33.3 0.0 collective-permute-done.10.refs_5_
  33.4 0.2 collective-permute-start.11
  33.5 0.4 collective-permute-start.12
  33.9 1.3 %collective-permute-done.11 = bf16[64,3584]{1,0:T(8,128)(2,1)S(1)} collective-permute-done((bf16[64,3584]{1,0:T(8,128)(2,1)S(1)}, bf16[64,3584]{1,0:T(8,128)(2,1)S(1)}, u32[]{:S(2)}, u32[]{:S(2)}) %collective-permute-start.11) | collective-permute-done | bytes 458784 | tf_op jit(solution)/shard_map/ppermute | solution.py:24
  35.2 0.1 add_convert_fusion.1
  35.3 1.5 %collective-permute-start.14 = (bf16[32,3584]{1,0:T(8,128)(2,1)S(1)}, bf16[32,3584]{1,0:T(8,128)(2,1)S(1)}, u32[]{:S(2)}, u32[]{:S(2)}) collective-permute-start(bf16[32,3584]{1,0:T(8,128)(2,1)S(1)} %add_convert_fusion.1), channel_id=1, source_target_pairs={{0,16},{16,0},{1,17},{17,1},{2,18},{18,2},{3,19},{19,3},{4,20},{20... | collective-permute-start | bytes 688136 | tf_op jit(solution)/shard_map/ppermute | solution.py:22
  36.8 0.0 collective-permute-done.12
  36.9 0.1 add_convert_fusion
  37.0 1.6 %collective-permute-start.13 = (bf16[32,3584]{1,0:T(8,128)(2,1)S(1)}, bf16[32,3584]{1,0:T(8,128)(2,1)S(1)}, u32[]{:S(2)}, u32[]{:S(2)}) collective-permute-start(bf16[32,3584]{1,0:T(8,128)(2,1)S(1)} %get-tuple-element.57), channel_id=1, source_target_pairs={{0,2},{1,3},{2,0},{3,1},{4,6},{5,7},{6,4},{7,5},{8,10},{9,11},{10,... | collective-permute-start | bytes 688136 | tf_op jit(solution)/shard_map/ppermute | solution.py:24
  38.6 0.5 collective-permute-start.15
  39.0 0.0 collective-permute-start.19
  39.1 1.7 %cache_part.1 = (f32[4,64,128]{2,1,0:T(8,128)S(1)}, f32[4,64,512]{2,1,0:T(8,128)S(1)}) custom-call(s32[4]{0:T(128)S(1)} %copy-done.5, bf16[4,64,576]{2,1,0:T(8,128)(2,1)S(1)} %copy-done.1, bf16[4,576,256]{2,1,0:T(8,128)(2,1)S(1)} %bitcast.9), custom_call_target="tpu_custom_call" | custom-call | flops 150994944 | bytes 1179648 | tf_op jit(solution)/shard_map/cache_part/pallas_call | solution.py:63
  40.8 0.6 residual_rows.1.residual_ref
  41.4 0.6 collective-permute-start.20
  41.9 1.9 %collective-permute-done.14 = bf16[32,3584]{1,0:T(8,128)(2,1)S(1)} collective-permute-done((bf16[32,3584]{1,0:T(8,128)(2,1)S(1)}, bf16[32,3584]{1,0:T(8,128)(2,1)S(1)}, u32[]{:S(2)}, u32[]{:S(2)}) %collective-permute-start.14) | collective-permute-done | bytes 229408 | tf_op jit(solution)/shard_map/ppermute | solution.py:22
  43.8 5.5 %collective-permute-done.13 = bf16[32,3584]{1,0:T(8,128)(2,1)S(1)} collective-permute-done((bf16[32,3584]{1,0:T(8,128)(2,1)S(1)}, bf16[32,3584]{1,0:T(8,128)(2,1)S(1)}, u32[]{:S(2)}, u32[]{:S(2)}) %collective-permute-start.13) | collective-permute-done | bytes 229408 | tf_op jit(solution)/shard_map/ppermute | solution.py:24
  49.3 0.0 collective-permute-done.15
  49.3 0.1 add_convert_fusion.3
  49.4 0.6 collective-permute-start.16
  50.1 1.4 %collective-permute-start.17 = (bf16[16,1792]{1,0:T(8,128)(2,1)S(1)}, bf16[16,1792]{1,0:T(8,128)(2,1)S(1)}, u32[]{:S(2)}, u32[]{:S(2)}) collective-permute-start(bf16[16,1792]{1,0:T(8,128)(2,1)S(1)} %get-tuple-element.54), channel_id=1, source_target_pairs={{0,12},{1,13},{2,14},{3,15},{4,8},{5,9},{6,10},{7,11},{8,4},{9,5},... | collective-permute-start | bytes 172040 | tf_op jit(solution)/shard_map/ppermute | solution.py:24
  51.4 1.6 %collective-permute-start.18 = (bf16[16,1792]{1,0:T(8,128)(2,1)S(1)}, bf16[16,1792]{1,0:T(8,128)(2,1)S(1)}, u32[]{:S(2)}, u32[]{:S(2)}) collective-permute-start(bf16[16,1792]{1,0:T(8,128)(2,1)S(1)} %get-tuple-element.53), channel_id=1, source_target_pairs={{0,4},{1,5},{2,6},{3,7},{4,0},{5,1},{6,2},{7,3},{8,12},{9,13},{10,... | collective-permute-start | bytes 172040 | tf_op jit(solution)/shard_map/ppermute | solution.py:24
  53.0 0.0 collective-permute-done.19.refs_4_
  53.1 0.0 collective-permute-done.20.refs_6_
  53.1 1.9 %collective-permute-done.16.refs_0_ = bf16[16,1792]{1,0:T(8,128)(2,1)S(1)} collective-permute-done((bf16[16,1792]{1,0:T(8,128)(2,1)S(1)}, bf16[16,1792]{1,0:T(8,128)(2,1)S(1)}, u32[]{:S(2)}, u32[]{:S(2)}) %collective-permute-start.16) | collective-permute-done | bytes 57376 | tf_op jit(solution)/shard_map/ppermute | solution.py:24
  55.0 1.2 %collective-permute-done.17.refs_1_ = bf16[16,1792]{1,0:T(8,128)(2,1)S(1)} collective-permute-done((bf16[16,1792]{1,0:T(8,128)(2,1)S(1)}, bf16[16,1792]{1,0:T(8,128)(2,1)S(1)}, u32[]{:S(2)}, u32[]{:S(2)}) %collective-permute-start.17) | collective-permute-done | bytes 57376 | tf_op jit(solution)/shard_map/ppermute | solution.py:24
  56.2 0.0 collective-permute-done.18.refs_2_
  56.2 1.1 %latent_parts.1 = (f32[4,640]{1,0:T(4,128)S(1)}, bf16[4,1792]{1,0:T(4,128)(2,1)S(1)}, bf16[4,3072]{1,0:T(4,128)(2,1)S(1)}, bf16[4,3072]{1,0:T(4,128)(2,1)S(1)}, bf16[4,3072]{1,0:T(4,128)(2,1)S(1)}) custom-call(s32[4]{0:T(128)S(1)} %pad_add_fusion.refs_0_.place_ref, f32[16,1792]{1,0:T(8,128)S(1)} %convert_add_fusion.sum_ref, ...), custom_call_target="tpu_custom_call" | custom-call | tf_op jit(solution)/shard_map/latent_parts/pallas_call | solution.py:85
  57.3 1.7 %collective-permute-start.21 = (bf16[4,3072]{1,0:T(4,128)(2,1)S(1)}, bf16[4,3072]{1,0:T(4,128)(2,1)S(1)}, u32[]{:S(2)}, u32[]{:S(2)}) collective-permute-start(bf16[4,3072]{1,0:T(4,128)(2,1)S(1)} %get-tuple-element.50), channel_id=1, source_target_pairs={{0,2},{1,3},{2,0},{3,1},{4,6},{5,7},{6,4},{7,5},{8,10},{9,11},{10,... | collective-permute-start | bytes 73736 | tf_op jit(solution)/shard_map/ppermute | solution.py:24
  59.0 1.0 %collective-permute-start.22 = (bf16[4,3072]{1,0:T(4,128)(2,1)S(1)}, bf16[4,3072]{1,0:T(4,128)(2,1)S(1)}, u32[]{:S(2)}, u32[]{:S(2)}) collective-permute-start(bf16[4,3072]{1,0:T(4,128)(2,1)S(1)} %get-tuple-element.51), channel_id=1, source_target_pairs={{0,8},{1,9},{2,10},{3,11},{4,12},{5,13},{6,14},{7,15},{8,0},{9,1},... | collective-permute-start | bytes 73736 | tf_op jit(solution)/shard_map/ppermute | solution.py:24
  60.0 1.7 %collective-permute-start.23 = (bf16[4,3072]{1,0:T(4,128)(2,1)S(1)}, bf16[4,3072]{1,0:T(4,128)(2,1)S(1)}, u32[]{:S(2)}, u32[]{:S(2)}) collective-permute-start(bf16[4,3072]{1,0:T(4,128)(2,1)S(1)} %get-tuple-element.52), channel_id=1, source_target_pairs={{0,10},{1,11},{2,8},{3,9},{4,14},{5,15},{6,12},{7,13},{8,2},{9,3},... | collective-permute-start | bytes 73736 | tf_op jit(solution)/shard_map/ppermute | solution.py:24
  61.8 0.0 collective-permute-done.21.refs_0_
  61.8 1.9 %collective-permute-done.22.refs_1_ = bf16[4,3072]{1,0:T(4,128)(2,1)S(1)} collective-permute-done((bf16[4,3072]{1,0:T(4,128)(2,1)S(1)}, bf16[4,3072]{1,0:T(4,128)(2,1)S(1)}, u32[]{:S(2)}, u32[]{:S(2)}) %collective-permute-start.22) | collective-permute-done | bytes 24608 | tf_op jit(solution)/shard_map/ppermute | solution.py:24
  63.7 1.9 %collective-permute-done.23.refs_2_ = bf16[4,3072]{1,0:T(4,128)(2,1)S(1)} collective-permute-done((bf16[4,3072]{1,0:T(4,128)(2,1)S(1)}, bf16[4,3072]{1,0:T(4,128)(2,1)S(1)}, u32[]{:S(2)}, u32[]{:S(2)}) %collective-permute-start.23) | collective-permute-done | bytes 24608 | tf_op jit(solution)/shard_map/ppermute | solution.py:24
  65.7 1.8 %finish.1 = (bf16[4,7168]{1,0:T(4,128)(2,1)}, bf16[4,576]{1,0:T(4,128)(2,1)}, bf16[4,64,512]{2,1,0:T(8,128)(2,1)}) custom-call(s32[4]{0:T(128)S(1)} %pad_add_fusion.refs_0_.place_ref, f32[4,640]{1,0:T(4,128)S(1)} %get-tuple-element.46.sums_ref, bf16[4,1792]{1,0:T(4,128)(2,1)S(1)} %get-tuple-element.47.moe_ref, bf16[4,64,576]{2,1,0:T(8,128)(2,1)S(1)} %copy-done.1, ...), custom_call_target="tpu_custom_call" | custom-call | tf_op jit(solution)/shard_map/finish/pallas_call | solution.py:85
  (11 shorter events, 0.1 us)
Async XLA Ops:
  0.6 0.9 %copy-start = (bf16[4,2]{0,1:T(2,128)(2,1)S(1)}, bf16[4,2]{0,1:T(2,128)(2,1)}, u32[]{:S(2)}) copy-start(bf16[4,2]{0,1:T(2,128)(2,1)} %param.13) | copy-start | bytes 52
  2.6 5.7 %collective-permute-start.1 = (bf16[4,7296]{1,0:T(4,128)(2,1)S(1)}, bf16[4,7296]{1,0:T(4,128)(2,1)S(1)}, u32[]{:S(2)}, u32[]{:S(2)}) collective-permute-start(bf16[4,7296]{1,0:T(4,128)(2,1)S(1)} %pad_maximum_fusion.refs_0_), channel_id=1, source_target_pairs={{0,4},{1,5},{2,6},{3,7},{4,0},{5,1},{6,2},{7,3},{8,12},{9,13},{10,... | collective-permute-start | bytes 175112 | tf_op jit(solution)/shard_map/ppermute | solution.py:24
  5.7 6.3 %collective-permute-start = (bf16[4,7296]{1,0:T(4,128)(2,1)S(1)}, bf16[4,7296]{1,0:T(4,128)(2,1)S(1)}, u32[]{:S(2)}, u32[]{:S(2)}) collective-permute-start(bf16[4,7296]{1,0:T(4,128)(2,1)S(1)} %pad_maximum_fusion.refs_0_), channel_id=1, source_target_pairs={{0,8},{1,9},{2,10},{3,11},{4,12},{5,13},{6,14},{7,15},{8,0},{9,1},... | collective-permute-start | bytes 175112 | tf_op jit(solution)/shard_map/ppermute | solution.py:24
  8.3 6.7 %collective-permute-start.2 = (bf16[4,7296]{1,0:T(4,128)(2,1)S(1)}, bf16[4,7296]{1,0:T(4,128)(2,1)S(1)}, u32[]{:S(2)}, u32[]{:S(2)}) collective-permute-start(bf16[4,7296]{1,0:T(4,128)(2,1)S(1)} %pad_maximum_fusion.refs_0_), channel_id=1, source_target_pairs={{0,12},{1,13},{2,14},{3,15},{4,8},{5,9},{6,10},{7,11},{8,4},{9,5},... | collective-permute-start | bytes 175112 | tf_op jit(solution)/shard_map/ppermute | solution.py:24
  8.3 25.1 %collective-permute-start.10 = (bf16[448,576]{1,0:T(8,128)(2,1)}, bf16[448,576]{1,0:T(8,128)(2,1)S(1)}, u32[]{:S(2)}, u32[]{:S(2)}) collective-permute-start(bf16[448,576]{1,0:T(8,128)(2,1)} %refs_3_.1), channel_id=1, source_target_pairs={{0,4},{1,5},{2,6},{3,7},{4,0},{5,1},{6,2},{7,3},{8,12},{9,13},{10,... | collective-permute-start | bytes 1548296 | tf_op jit(solution)/shard_map/ppermute | solution.py:24
  15.0 8.6 %collective-permute-start.3 = (bf16[16,7296]{1,0:T(8,128)(2,1)S(1)}, bf16[16,7296]{1,0:T(8,128)(2,1)S(1)}, u32[]{:S(2)}, u32[]{:S(2)}) collective-permute-start(bf16[16,7296]{1,0:T(8,128)(2,1)S(1)} %pack_rows.1.refs_1_.own_ref), channel_id=1, source_target_pairs={{0,2},{1,3},{2,0},{3,1},{4,6},{5,7},{6,4},{7,5},{8,10},{9,11},{10,... | collective-permute-start | bytes 700424 | tf_op jit(solution)/shard_map/ppermute | solution.py:24
  16.6 7.5 %collective-permute-start.4 = (bf16[16,7296]{1,0:T(8,128)(2,1)S(1)}, bf16[16,7296]{1,0:T(8,128)(2,1)S(1)}, u32[]{:S(2)}, u32[]{:S(2)}) collective-permute-start(bf16[16,7296]{1,0:T(8,128)(2,1)S(1)} %pack_rows.1.refs_1_.own_ref), channel_id=1, source_target_pairs={{0,16},{16,0},{1,17},{17,1},{2,18},{18,2},{3,19},{19,3},{4,20},{20... | collective-permute-start | bytes 700424 | tf_op jit(solution)/shard_map/ppermute | solution.py:22
  18.1 8.4 %collective-permute-start.5 = (bf16[16,7296]{1,0:T(8,128)(2,1)S(1)}, bf16[16,7296]{1,0:T(8,128)(2,1)S(1)}, u32[]{:S(2)}, u32[]{:S(2)}) collective-permute-start(bf16[16,7296]{1,0:T(8,128)(2,1)S(1)} %pack_rows.1.refs_1_.own_ref), channel_id=1, source_target_pairs={{0,18},{1,19},{2,16},{3,17},{4,22},{5,23},{6,20},{7,21},{8,26},{9,... | collective-permute-start | bytes 700424 | tf_op jit(solution)/shard_map/ppermute | solution.py:30
  18.5 8.0 %collective-permute-start.6 = (bf16[16,7296]{1,0:T(8,128)(2,1)S(1)}, bf16[16,7296]{1,0:T(8,128)(2,1)S(1)}, u32[]{:S(2)}, u32[]{:S(2)}) collective-permute-start(bf16[16,7296]{1,0:T(8,128)(2,1)S(1)} %pack_rows.1.refs_1_.own_ref), channel_id=1, source_target_pairs={{0,1},{1,0},{2,3},{3,2},{4,5},{5,4},{6,7},{7,6},{8,9},{9,8},{10,11... | collective-permute-start | bytes 700424 | tf_op jit(solution)/shard_map/ppermute | solution.py:24
  23.6 3.0 %collective-permute-start.7 = (bf16[16,7296]{1,0:T(8,128)(2,1)S(1)}, bf16[16,7296]{1,0:T(8,128)(2,1)S(1)}, u32[]{:S(2)}, u32[]{:S(2)}) collective-permute-start(bf16[16,7296]{1,0:T(8,128)(2,1)S(1)} %collective-permute-done.3.refs_2_.low_ref), channel_id=1, source_target_pairs={{0,1},{1,0},{2,3},{3,2},{4,5},{5,4},{6,7},{7,6},{8,9},{9,8},{10,11... | collective-permute-start | bytes 700424 | tf_op jit(solution)/shard_map/ppermute | solution.py:24
  24.0 2.6 %collective-permute-start.8 = (bf16[16,7296]{1,0:T(8,128)(2,1)S(1)}, bf16[16,7296]{1,0:T(8,128)(2,1)S(1)}, u32[]{:S(2)}, u32[]{:S(2)}) collective-permute-start(bf16[16,7296]{1,0:T(8,128)(2,1)S(1)} %collective-permute-done.4.refs_3_), channel_id=1, source_target_pairs={{0,1},{1,0},{2,3},{3,2},{4,5},{5,4},{6,7},{7,6},{8,9},{9,8},{10,11... | collective-permute-start | bytes 700424 | tf_op jit(solution)/shard_map/ppermute | solution.py:24
  26.5 1.5 %collective-permute-start.9 = (bf16[16,7296]{1,0:T(8,128)(2,1)S(1)}, bf16[16,7296]{1,0:T(8,128)(2,1)S(1)}, u32[]{:S(2)}, u32[]{:S(2)}) collective-permute-start(bf16[16,7296]{1,0:T(8,128)(2,1)S(1)} %collective-permute-done.5.refs_4_), channel_id=1, source_target_pairs={{0,1},{1,0},{2,3},{3,2},{4,5},{5,4},{6,7},{7,6},{8,9},{9,8},{10,11... | collective-permute-start | bytes 700424 | tf_op jit(solution)/shard_map/ppermute | solution.py:24
  26.6 12.5 %copy-start.3 = (bf16[448,576]{1,0:T(8,128)(2,1)S(1)}, bf16[448,576]{1,0:T(8,128)(2,1)}, u32[]{:S(2)}) copy-start(bf16[448,576]{1,0:T(8,128)(2,1)} %refs_3_.1) | copy-start | bytes 1548292
  26.6 12.5 %copy-start.1 = (bf16[4,64,576]{2,1,0:T(8,128)(2,1)S(1)}, bf16[4,64,576]{2,1,0:T(8,128)(2,1)}, u32[]{:S(2)}) copy-start(bf16[4,64,576]{2,1,0:T(8,128)(2,1)} %q_ref.3) | copy-start | bytes 884740
  26.6 12.5 %copy-start.2 = (bf16[4,256,576]{1,2,0:T(8,128)(2,1)S(1)}, bf16[4,256,576]{1,2,0:T(8,128)(2,1)}, u32[]{:S(2)}) copy-start(bf16[4,256,576]{1,2,0:T(8,128)(2,1)} %param.20) | copy-start | bytes 3538948
  26.6 12.5 %copy-start.5 = (s32[4]{0:T(128)S(1)}, s32[4]{0:T(128)}, u32[]{:S(2)}) copy-start(s32[4]{0:T(128)} %lengths_ref.1) | copy-start | bytes 52
  33.3 22.9 %copy-start.4 = (f32[7168]{0:T(1024)S(1)}, f32[7168]{0:T(1024)}, u32[]{:S(2)}) copy-start(f32[7168]{0:T(1024)} %param.17) | copy-start | bytes 86020
  33.4 1.9 %collective-permute-start.11 = (bf16[64,3584]{1,0:T(8,128)(2,1)S(1)}, bf16[64,3584]{1,0:T(8,128)(2,1)S(1)}, u32[]{:S(2)}, u32[]{:S(2)}) collective-permute-start(bf16[64,3584]{1,0:T(8,128)(2,1)S(1)} %get-tuple-element.35), channel_id=1, source_target_pairs={{0,1},{1,0},{2,3},{3,2},{4,5},{5,4},{6,7},{7,6},{8,9},{9,8},{10,11... | collective-permute-start | bytes 1376264 | tf_op jit(solution)/shard_map/ppermute | solution.py:24
  33.5 3.3 %collective-permute-start.12 = (bf16[64,3584]{1,0:T(8,128)(2,1)S(1)}, bf16[64,3584]{1,0:T(8,128)(2,1)S(1)}, u32[]{:S(2)}, u32[]{:S(2)}) collective-permute-start(bf16[64,3584]{1,0:T(8,128)(2,1)S(1)} %get-tuple-element.37), channel_id=1, source_target_pairs={{0,1},{1,0},{2,3},{3,2},{4,5},{5,4},{6,7},{7,6},{8,9},{9,8},{10,11... | collective-permute-start | bytes 1376264 | tf_op jit(solution)/shard_map/ppermute | solution.py:24
  35.3 8.5 %collective-permute-start.14 = (bf16[32,3584]{1,0:T(8,128)(2,1)S(1)}, bf16[32,3584]{1,0:T(8,128)(2,1)S(1)}, u32[]{:S(2)}, u32[]{:S(2)}) collective-permute-start(bf16[32,3584]{1,0:T(8,128)(2,1)S(1)} %add_convert_fusion.1), channel_id=1, source_target_pairs={{0,16},{16,0},{1,17},{17,1},{2,18},{18,2},{3,19},{19,3},{4,20},{20... | collective-permute-start | bytes 688136 | tf_op jit(solution)/shard_map/ppermute | solution.py:22
  37.0 12.4 %collective-permute-start.13 = (bf16[32,3584]{1,0:T(8,128)(2,1)S(1)}, bf16[32,3584]{1,0:T(8,128)(2,1)S(1)}, u32[]{:S(2)}, u32[]{:S(2)}) collective-permute-start(bf16[32,3584]{1,0:T(8,128)(2,1)S(1)} %get-tuple-element.57), channel_id=1, source_target_pairs={{0,2},{1,3},{2,0},{3,1},{4,6},{5,7},{6,4},{7,5},{8,10},{9,11},{10,... | collective-permute-start | bytes 688136 | tf_op jit(solution)/shard_map/ppermute | solution.py:24
  38.6 10.8 %collective-permute-start.15 = (bf16[32,3584]{1,0:T(8,128)(2,1)S(1)}, bf16[32,3584]{1,0:T(8,128)(2,1)S(1)}, u32[]{:S(2)}, u32[]{:S(2)}) collective-permute-start(bf16[32,3584]{1,0:T(8,128)(2,1)S(1)} %get-tuple-element.56), channel_id=1, source_target_pairs={{0,18},{1,19},{2,16},{3,17},{4,22},{5,23},{6,20},{7,21},{8,26},{9,... | collective-permute-start | bytes 688136 | tf_op jit(solution)/shard_map/ppermute | solution.py:30
  39.0 14.0 %collective-permute-start.19 = (bf16[448,576]{1,0:T(8,128)(2,1)S(1)}, bf16[448,576]{1,0:T(8,128)(2,1)S(1)}, u32[]{:S(2)}, u32[]{:S(2)}) collective-permute-start(bf16[448,576]{1,0:T(8,128)(2,1)S(1)} %copy-done.3), channel_id=1, source_target_pairs={{0,1},{1,0},{2,3},{3,2},{4,5},{5,4},{6,7},{7,6},{8,9},{9,8},{10,11... | collective-permute-start | bytes 1548296 | tf_op jit(solution)/shard_map/ppermute | solution.py:24
  41.4 11.7 %collective-permute-start.20 = (bf16[448,576]{1,0:T(8,128)(2,1)S(1)}, bf16[448,576]{1,0:T(8,128)(2,1)S(1)}, u32[]{:S(2)}, u32[]{:S(2)}) collective-permute-start(bf16[448,576]{1,0:T(8,128)(2,1)S(1)} %collective-permute-done.10.refs_5_), channel_id=1, source_target_pairs={{0,1},{1,0},{2,3},{3,2},{4,5},{5,4},{6,7},{7,6},{8,9},{9,8},{10,11... | collective-permute-start | bytes 1548296 | tf_op jit(solution)/shard_map/ppermute | solution.py:24
  49.4 5.5 %collective-permute-start.16 = (bf16[16,1792]{1,0:T(8,128)(2,1)S(1)}, bf16[16,1792]{1,0:T(8,128)(2,1)S(1)}, u32[]{:S(2)}, u32[]{:S(2)}) collective-permute-start(bf16[16,1792]{1,0:T(8,128)(2,1)S(1)} %get-tuple-element.55), channel_id=1, source_target_pairs={{0,8},{1,9},{2,10},{3,11},{4,12},{5,13},{6,14},{7,15},{8,0},{9,1},... | collective-permute-start | bytes 172040 | tf_op jit(solution)/shard_map/ppermute | solution.py:24
  50.1 6.1 %collective-permute-start.17 = (bf16[16,1792]{1,0:T(8,128)(2,1)S(1)}, bf16[16,1792]{1,0:T(8,128)(2,1)S(1)}, u32[]{:S(2)}, u32[]{:S(2)}) collective-permute-start(bf16[16,1792]{1,0:T(8,128)(2,1)S(1)} %get-tuple-element.54), channel_id=1, source_target_pairs={{0,12},{1,13},{2,14},{3,15},{4,8},{5,9},{6,10},{7,11},{8,4},{9,5},... | collective-permute-start | bytes 172040 | tf_op jit(solution)/shard_map/ppermute | solution.py:24
  51.4 4.8 %collective-permute-start.18 = (bf16[16,1792]{1,0:T(8,128)(2,1)S(1)}, bf16[16,1792]{1,0:T(8,128)(2,1)S(1)}, u32[]{:S(2)}, u32[]{:S(2)}) collective-permute-start(bf16[16,1792]{1,0:T(8,128)(2,1)S(1)} %get-tuple-element.53), channel_id=1, source_target_pairs={{0,4},{1,5},{2,6},{3,7},{4,0},{5,1},{6,2},{7,3},{8,12},{9,13},{10,... | collective-permute-start | bytes 172040 | tf_op jit(solution)/shard_map/ppermute | solution.py:24
  57.3 4.5 %collective-permute-start.21 = (bf16[4,3072]{1,0:T(4,128)(2,1)S(1)}, bf16[4,3072]{1,0:T(4,128)(2,1)S(1)}, u32[]{:S(2)}, u32[]{:S(2)}) collective-permute-start(bf16[4,3072]{1,0:T(4,128)(2,1)S(1)} %get-tuple-element.50), channel_id=1, source_target_pairs={{0,2},{1,3},{2,0},{3,1},{4,6},{5,7},{6,4},{7,5},{8,10},{9,11},{10,... | collective-permute-start | bytes 73736 | tf_op jit(solution)/shard_map/ppermute | solution.py:24
  59.0 4.7 %collective-permute-start.22 = (bf16[4,3072]{1,0:T(4,128)(2,1)S(1)}, bf16[4,3072]{1,0:T(4,128)(2,1)S(1)}, u32[]{:S(2)}, u32[]{:S(2)}) collective-permute-start(bf16[4,3072]{1,0:T(4,128)(2,1)S(1)} %get-tuple-element.51), channel_id=1, source_target_pairs={{0,8},{1,9},{2,10},{3,11},{4,12},{5,13},{6,14},{7,15},{8,0},{9,1},... | collective-permute-start | bytes 73736 | tf_op jit(solution)/shard_map/ppermute | solution.py:24
  60.0 5.6 %collective-permute-start.23 = (bf16[4,3072]{1,0:T(4,128)(2,1)S(1)}, bf16[4,3072]{1,0:T(4,128)(2,1)S(1)}, u32[]{:S(2)}, u32[]{:S(2)}) collective-permute-start(bf16[4,3072]{1,0:T(4,128)(2,1)S(1)} %get-tuple-element.52), channel_id=1, source_target_pairs={{0,10},{1,11},{2,8},{3,9},{4,14},{5,15},{6,12},{7,13},{8,2},{9,3},... | collective-permute-start | bytes 73736 | tf_op jit(solution)/shard_map/ppermute | solution.py:24

commit v7 on v6

--- a/solution.py
+++ b/solution.py
@@ -412,8 +412,8 @@
     blocks, w_mid = gather_rows(hidden_in, expert_ids, gate_scores, w_kv)
     partial = experts(place, blocks, picks, w_gate, w_up, w_down)
     partial, w_mid = lax.optimization_barrier((partial, w_mid))
-    kept, received, late = scatter_rows(*partial, (cache,))
-    (cache,) = late
+    kept, received, late = scatter_rows(*partial, ())
+    del late
     stats, combined = cache
     residual = residual_rows(place, blocks[0], blocks[1])
     gain = norm_gain.reshape(1, -1)

time: 67.6 us -> 67.7 us (level)
    ppermute x2, waiting for transfers between devices: 2.29 us -> 4.01 us  [swap(): lax.ppermute(x, 'sec', [(i, i ^ 1) for i in range(lax.axis_size('sec'))])]
    ppermute x20, waiting for transfers between devices: 25.4 us -> 23.7 us  [swap(): lax.ppermute(x, 'dev', [(i, i ^ flips) for i in range(lax.axis_size('dev'...]
where the time goes in v7:
time: 67.7 us; the launch traced here: 67.5 us
  waiting for transfers between devices  30.1 us (44%)
  starting transfers between devices  23.7 us (35%)
  Pallas kernels  10.6 us (16%)
  other arithmetic  1.26 us (2%)
  matrix products  1.05 us (2%)
  between operations  0.78 us (1%)
    ppermute x20, waiting for transfers between devices, swap(): lax.ppermute(x, 'dev', [(i, i ^ flips) for i in range(lax.axis_size('dev'...  23.7 us
    ppermute x20, starting transfers between devices, swap(): lax.ppermute(x, 'dev', [(i, i ^ flips) for i in range(lax.axis_size('dev'...  19.7 us
    pallas_call x5, Pallas kernels, kernel_call(): pl.pallas_call(body, out_shape=out_shape, in_specs=specs, out_specs=jax.t...  8.86 us
    ppermute x2, waiting for transfers between devices, swap(): lax.ppermute(x, 'sec', [(i, i ^ 1) for i in range(lax.axis_size('sec'))])  4.01 us
    ppermute x2, starting transfers between devices, swap(): lax.ppermute(x, 'sec', [(i, i ^ 1) for i in range(lax.axis_size('sec'))])  3.04 us
    ppermute x2, waiting for transfers between devices, swap_both(): return lax.ppermute(x, ('sec', 'dev'), pairs)  2.34 us
    pallas_call x1, Pallas kernels, cache_part(): pl.pallas_call(cache_kernel, out_shape=(jax.ShapeDtypeStruct((rows, heads...  1.7 us
  transfers between devices with their start and end apart: 24, of which 13 were waited for; matrix products, arithmetic and copies ran while one was open for 1% of the time, Pallas kernels for 11%

profile of v7, /device:TPU:0, one launch (start us, length us, event | category | flops | bytes accessed | tf_op | source)
XLA Modules:
  0.0 67.5 jit_solution(13832475398576025716)
XLA Ops:
  0.6 0.0 copy-start
  0.7 0.9 %fusion.3 = f32[128,4]{0,1:T(4,128)S(1)} fusion(s32[4,2]{0,1:T(2,128)} %param.12), kind=kOutput, calls=%fused_computation.12 | convolution fusion | flops 2312 | bytes 2080 | tf_op jit(solution)/shard_map/dot_general | solution.py:100
  1.5 0.2 fusion.1
  1.7 0.9 %pad_maximum_fusion.refs_0_ = bf16[4,7296]{1,0:T(4,128)(2,1)S(1)} fusion(bf16[4,128]{1,0:T(4,128)(2,1)S(1)} %fusion.1, bf16[4,7168]{1,0:T(4,128)(2,1)} %param.11), kind=kLoop, calls=%fused_computation.10 | loop fusion | flops 116736 | bytes 116736 | tf_op jit(solution)/shard_map/concatenate | solution.py:103
  2.6 3.1 %collective-permute-start.1 = (bf16[4,7296]{1,0:T(4,128)(2,1)S(1)}, bf16[4,7296]{1,0:T(4,128)(2,1)S(1)}, u32[]{:S(2)}, u32[]{:S(2)}) collective-permute-start(bf16[4,7296]{1,0:T(4,128)(2,1)S(1)} %pad_maximum_fusion.refs_0_), channel_id=1, source_target_pairs={{0,4},{1,5},{2,6},{3,7},{4,0},{5,1},{6,2},{7,3},{8,12},{9,13},{10,... | collective-permute-start | bytes 175112 | tf_op jit(solution)/shard_map/ppermute | solution.py:24
  5.7 2.6 %collective-permute-start = (bf16[4,7296]{1,0:T(4,128)(2,1)S(1)}, bf16[4,7296]{1,0:T(4,128)(2,1)S(1)}, u32[]{:S(2)}, u32[]{:S(2)}) collective-permute-start(bf16[4,7296]{1,0:T(4,128)(2,1)S(1)} %pad_maximum_fusion.refs_0_), channel_id=1, source_target_pairs={{0,8},{1,9},{2,10},{3,11},{4,12},{5,13},{6,14},{7,15},{8,0},{9,1},... | collective-permute-start | bytes 175112 | tf_op jit(solution)/shard_map/ppermute | solution.py:24
  8.3 0.0 collective-permute-start.2
  8.3 0.0 collective-permute-done.1.refs_2_
  8.3 1.6 %collective-permute-start.10 = (bf16[448,576]{1,0:T(8,128)(2,1)}, bf16[448,576]{1,0:T(8,128)(2,1)S(1)}, u32[]{:S(2)}, u32[]{:S(2)}) collective-permute-start(bf16[448,576]{1,0:T(8,128)(2,1)} %refs_3_.1), channel_id=1, source_target_pairs={{0,4},{1,5},{2,6},{3,7},{4,0},{5,1},{6,2},{7,3},{8,12},{9,13},{10,... | collective-permute-start | bytes 1548296 | tf_op jit(solution)/shard_map/ppermute | solution.py:24
  9.9 2.1 %collective-permute-done.refs_1_ = bf16[4,7296]{1,0:T(4,128)(2,1)S(1)} collective-permute-done((bf16[4,7296]{1,0:T(4,128)(2,1)S(1)}, bf16[4,7296]{1,0:T(4,128)(2,1)S(1)}, u32[]{:S(2)}, u32[]{:S(2)}) %collective-permute-start) | collective-permute-done | bytes 58400 | tf_op jit(solution)/shard_map/ppermute | solution.py:24
  12.0 3.0 %collective-permute-done.2.refs_3_ = bf16[4,7296]{1,0:T(4,128)(2,1)S(1)} collective-permute-done((bf16[4,7296]{1,0:T(4,128)(2,1)S(1)}, bf16[4,7296]{1,0:T(4,128)(2,1)S(1)}, u32[]{:S(2)}, u32[]{:S(2)}) %collective-permute-start.2) | collective-permute-done | bytes 58400 | tf_op jit(solution)/shard_map/ppermute | solution.py:24
  14.9 0.1 pack_rows.1.refs_1_.own_ref
  15.0 1.6 %collective-permute-start.3 = (bf16[16,7296]{1,0:T(8,128)(2,1)S(1)}, bf16[16,7296]{1,0:T(8,128)(2,1)S(1)}, u32[]{:S(2)}, u32[]{:S(2)}) collective-permute-start(bf16[16,7296]{1,0:T(8,128)(2,1)S(1)} %pack_rows.1.refs_1_.own_ref), channel_id=1, source_target_pairs={{0,2},{1,3},{2,0},{3,1},{4,6},{5,7},{6,4},{7,5},{8,10},{9,11},{10,... | collective-permute-start | bytes 700424 | tf_op jit(solution)/shard_map/ppermute | solution.py:24
  16.6 1.5 %collective-permute-start.4 = (bf16[16,7296]{1,0:T(8,128)(2,1)S(1)}, bf16[16,7296]{1,0:T(8,128)(2,1)S(1)}, u32[]{:S(2)}, u32[]{:S(2)}) collective-permute-start(bf16[16,7296]{1,0:T(8,128)(2,1)S(1)} %pack_rows.1.refs_1_.own_ref), channel_id=1, source_target_pairs={{0,16},{16,0},{1,17},{17,1},{2,18},{18,2},{3,19},{19,3},{4,20},{20... | collective-permute-start | bytes 700424 | tf_op jit(solution)/shard_map/ppermute | solution.py:22
  18.1 0.5 collective-permute-start.5
  18.5 0.0 collective-permute-start.6
  18.6 5.1 %collective-permute-done.3.refs_2_.low_ref = bf16[16,7296]{1,0:T(8,128)(2,1)S(1)} collective-permute-done((bf16[16,7296]{1,0:T(8,128)(2,1)S(1)}, bf16[16,7296]{1,0:T(8,128)(2,1)S(1)}, u32[]{:S(2)}, u32[]{:S(2)}) %collective-permute-start.3) | collective-permute-done | bytes 233504 | tf_op jit(solution)/shard_map/ppermute | solution.py:24
  23.6 0.0 collective-permute-start.7
  23.6 0.4 collective-permute-done.4.refs_3_
  24.0 0.1 collective-permute-start.8
  24.1 2.3 %collective-permute-done.5.refs_4_ = bf16[16,7296]{1,0:T(8,128)(2,1)S(1)} collective-permute-done((bf16[16,7296]{1,0:T(8,128)(2,1)S(1)}, bf16[16,7296]{1,0:T(8,128)(2,1)S(1)}, u32[]{:S(2)}, u32[]{:S(2)}) %collective-permute-start.5) | collective-permute-done | bytes 233504 | tf_op jit(solution)/shard_map/ppermute | solution.py:30
  26.5 0.0 collective-permute-start.9
  26.5 0.1 pad_add_fusion.refs_0_.place_ref
  26.6 0.0 collective-permute-done.6.refs_5_
  26.6 0.0 collective-permute-done.7.refs_6_
  26.6 0.0 collective-permute-done.8.refs_7_
  26.6 1.4 %collective-permute-done.9.refs_8_ = bf16[16,7296]{1,0:T(8,128)(2,1)S(1)} collective-permute-done((bf16[16,7296]{1,0:T(8,128)(2,1)S(1)}, bf16[16,7296]{1,0:T(8,128)(2,1)S(1)}, u32[]{:S(2)}, u32[]{:S(2)}) %collective-permute-start.9) | collective-permute-done | bytes 233504 | tf_op jit(solution)/shard_map/ppermute | solution.py:24
  28.0 5.3 %experts.1 = (bf16[64,3584]{1,0:T(8,128)(2,1)S(1)}, bf16[64,3584]{1,0:T(8,128)(2,1)S(1)}, bf16[64,3584]{1,0:T(8,128)(2,1)S(1)}, bf16[64,3584]{1,0:T(8,128)(2,1)S(1)}) custom-call(s32[4]{0:T(128)S(1)} %pad_add_fusion.refs_0_.place_ref, bf16[16,7296]{1,0:T(8,128)(2,1)S(1)} %pack_rows.1.refs_1_.own_ref, ...), custom_call_target="tpu_custom_call" | custom-call | tf_op jit(solution)/shard_map/experts/pallas_call | solution.py:85
  33.3 0.0 copy-start.4
  33.3 0.0 copy-start.1
  33.4 0.0 copy-start.2
  33.4 0.0 copy-start.5
  33.4 0.0 collective-permute-done.10.refs_5_
  33.4 0.2 collective-permute-start.11
  33.6 0.4 collective-permute-start.12
  34.0 1.3 %collective-permute-done.11 = bf16[64,3584]{1,0:T(8,128)(2,1)S(1)} collective-permute-done((bf16[64,3584]{1,0:T(8,128)(2,1)S(1)}, bf16[64,3584]{1,0:T(8,128)(2,1)S(1)}, u32[]{:S(2)}, u32[]{:S(2)}) %collective-permute-start.11) | collective-permute-done | bytes 458784 | tf_op jit(solution)/shard_map/ppermute | solution.py:24
  35.3 0.1 add_convert_fusion.1
  35.3 1.5 %collective-permute-start.14 = (bf16[32,3584]{1,0:T(8,128)(2,1)S(1)}, bf16[32,3584]{1,0:T(8,128)(2,1)S(1)}, u32[]{:S(2)}, u32[]{:S(2)}) collective-permute-start(bf16[32,3584]{1,0:T(8,128)(2,1)S(1)} %add_convert_fusion.1), channel_id=1, source_target_pairs={{0,16},{16,0},{1,17},{17,1},{2,18},{18,2},{3,19},{19,3},{4,20},{20... | collective-permute-start | bytes 688136 | tf_op jit(solution)/shard_map/ppermute | solution.py:22
  36.9 0.1 add_convert_fusion
  37.0 1.6 %collective-permute-start.13 = (bf16[32,3584]{1,0:T(8,128)(2,1)S(1)}, bf16[32,3584]{1,0:T(8,128)(2,1)S(1)}, u32[]{:S(2)}, u32[]{:S(2)}) collective-permute-start(bf16[32,3584]{1,0:T(8,128)(2,1)S(1)} %get-tuple-element.53), channel_id=1, source_target_pairs={{0,2},{1,3},{2,0},{3,1},{4,6},{5,7},{6,4},{7,5},{8,10},{9,11},{10,... | collective-permute-start | bytes 688136 | tf_op jit(solution)/shard_map/ppermute | solution.py:24
  38.6 0.5 collective-permute-start.15
  39.1 0.0 collective-permute-start.19
  39.1 0.6 residual_rows.1.residual_ref
  39.7 0.6 collective-permute-start.20
  40.3 3.6 %collective-permute-done.14 = bf16[32,3584]{1,0:T(8,128)(2,1)S(1)} collective-permute-done((bf16[32,3584]{1,0:T(8,128)(2,1)S(1)}, bf16[32,3584]{1,0:T(8,128)(2,1)S(1)}, u32[]{:S(2)}, u32[]{:S(2)}) %collective-permute-start.14) | collective-permute-done | bytes 229408 | tf_op jit(solution)/shard_map/ppermute | solution.py:22
  43.8 5.5 %collective-permute-done.13 = bf16[32,3584]{1,0:T(8,128)(2,1)S(1)} collective-permute-done((bf16[32,3584]{1,0:T(8,128)(2,1)S(1)}, bf16[32,3584]{1,0:T(8,128)(2,1)S(1)}, u32[]{:S(2)}, u32[]{:S(2)}) %collective-permute-start.13) | collective-permute-done | bytes 229408 | tf_op jit(solution)/shard_map/ppermute | solution.py:24
  49.4 0.0 collective-permute-done.15
  49.4 0.1 add_convert_fusion.3
  49.5 0.6 collective-permute-start.16
  50.1 1.4 %collective-permute-start.17 = (bf16[16,1792]{1,0:T(8,128)(2,1)S(1)}, bf16[16,1792]{1,0:T(8,128)(2,1)S(1)}, u32[]{:S(2)}, u32[]{:S(2)}) collective-permute-start(bf16[16,1792]{1,0:T(8,128)(2,1)S(1)} %get-tuple-element.50), channel_id=1, source_target_pairs={{0,12},{1,13},{2,14},{3,15},{4,8},{5,9},{6,10},{7,11},{8,4},{9,5},... | collective-permute-start | bytes 172040 | tf_op jit(solution)/shard_map/ppermute | solution.py:24
  51.5 1.6 %collective-permute-start.18 = (bf16[16,1792]{1,0:T(8,128)(2,1)S(1)}, bf16[16,1792]{1,0:T(8,128)(2,1)S(1)}, u32[]{:S(2)}, u32[]{:S(2)}) collective-permute-start(bf16[16,1792]{1,0:T(8,128)(2,1)S(1)} %get-tuple-element.49), channel_id=1, source_target_pairs={{0,4},{1,5},{2,6},{3,7},{4,0},{5,1},{6,2},{7,3},{8,12},{9,13},{10,... | collective-permute-start | bytes 172040 | tf_op jit(solution)/shard_map/ppermute | solution.py:24
  53.1 0.0 collective-permute-done.20.refs_6_
  53.1 1.9 %collective-permute-done.16.refs_0_ = bf16[16,1792]{1,0:T(8,128)(2,1)S(1)} collective-permute-done((bf16[16,1792]{1,0:T(8,128)(2,1)S(1)}, bf16[16,1792]{1,0:T(8,128)(2,1)S(1)}, u32[]{:S(2)}, u32[]{:S(2)}) %collective-permute-start.16) | collective-permute-done | bytes 57376 | tf_op jit(solution)/shard_map/ppermute | solution.py:24
  55.0 1.2 %collective-permute-done.17.refs_1_ = bf16[16,1792]{1,0:T(8,128)(2,1)S(1)} collective-permute-done((bf16[16,1792]{1,0:T(8,128)(2,1)S(1)}, bf16[16,1792]{1,0:T(8,128)(2,1)S(1)}, u32[]{:S(2)}, u32[]{:S(2)}) %collective-permute-start.17) | collective-permute-done | bytes 57376 | tf_op jit(solution)/shard_map/ppermute | solution.py:24
  56.2 0.0 collective-permute-done.18.refs_2_
  56.3 1.1 %latent_parts.1 = (f32[4,640]{1,0:T(4,128)S(1)}, bf16[4,1792]{1,0:T(4,128)(2,1)S(1)}, bf16[4,3072]{1,0:T(4,128)(2,1)S(1)}, bf16[4,3072]{1,0:T(4,128)(2,1)S(1)}, bf16[4,3072]{1,0:T(4,128)(2,1)S(1)}) custom-call(s32[4]{0:T(128)S(1)} %pad_add_fusion.refs_0_.place_ref, f32[16,1792]{1,0:T(8,128)S(1)} %convert_add_fusion.sum_ref, ...), custom_call_target="tpu_custom_call" | custom-call | tf_op jit(solution)/shard_map/latent_parts/pallas_call | solution.py:85
  57.4 1.7 %collective-permute-start.21 = (bf16[4,3072]{1,0:T(4,128)(2,1)S(1)}, bf16[4,3072]{1,0:T(4,128)(2,1)S(1)}, u32[]{:S(2)}, u32[]{:S(2)}) collective-permute-start(bf16[4,3072]{1,0:T(4,128)(2,1)S(1)} %get-tuple-element.46), channel_id=1, source_target_pairs={{0,2},{1,3},{2,0},{3,1},{4,6},{5,7},{6,4},{7,5},{8,10},{9,11},{10,... | collective-permute-start | bytes 73736 | tf_op jit(solution)/shard_map/ppermute | solution.py:24
  59.0 1.0 %collective-permute-start.22 = (bf16[4,3072]{1,0:T(4,128)(2,1)S(1)}, bf16[4,3072]{1,0:T(4,128)(2,1)S(1)}, u32[]{:S(2)}, u32[]{:S(2)}) collective-permute-start(bf16[4,3072]{1,0:T(4,128)(2,1)S(1)} %get-tuple-element.47), channel_id=1, source_target_pairs={{0,8},{1,9},{2,10},{3,11},{4,12},{5,13},{6,14},{7,15},{8,0},{9,1},... | collective-permute-start | bytes 73736 | tf_op jit(solution)/shard_map/ppermute | solution.py:24
  60.1 1.7 %collective-permute-start.23 = (bf16[4,3072]{1,0:T(4,128)(2,1)S(1)}, bf16[4,3072]{1,0:T(4,128)(2,1)S(1)}, u32[]{:S(2)}, u32[]{:S(2)}) collective-permute-start(bf16[4,3072]{1,0:T(4,128)(2,1)S(1)} %get-tuple-element.48), channel_id=1, source_target_pairs={{0,10},{1,11},{2,8},{3,9},{4,14},{5,15},{6,12},{7,13},{8,2},{9,3},... | collective-permute-start | bytes 73736 | tf_op jit(solution)/shard_map/ppermute | solution.py:24
  61.8 1.7 %cache_part.1 = (f32[4,64,128]{2,1,0:T(8,128)S(1)}, f32[4,64,512]{2,1,0:T(8,128)S(1)}) custom-call(s32[4]{0:T(128)S(1)} %copy-done.5, bf16[4,64,576]{2,1,0:T(8,128)(2,1)S(1)} %copy-done.1, bf16[4,576,256]{2,1,0:T(8,128)(2,1)S(1)} %bitcast.9), custom_call_target="tpu_custom_call" | custom-call | flops 150994944 | bytes 1179648 | tf_op jit(solution)/shard_map/cache_part/pallas_call | solution.py:63
  63.5 0.0 collective-permute-done.21.refs_0_
  63.5 0.2 collective-permute-done.22.refs_1_
  63.8 1.9 %collective-permute-done.23.refs_2_ = bf16[4,3072]{1,0:T(4,128)(2,1)S(1)} collective-permute-done((bf16[4,3072]{1,0:T(4,128)(2,1)S(1)}, bf16[4,3072]{1,0:T(4,128)(2,1)S(1)}, u32[]{:S(2)}, u32[]{:S(2)}) %collective-permute-start.23) | collective-permute-done | bytes 24608 | tf_op jit(solution)/shard_map/ppermute | solution.py:24
  65.7 1.8 %finish.1 = (bf16[4,7168]{1,0:T(4,128)(2,1)}, bf16[4,576]{1,0:T(4,128)(2,1)}, bf16[4,64,512]{2,1,0:T(8,128)(2,1)}) custom-call(s32[4]{0:T(128)S(1)} %pad_add_fusion.refs_0_.place_ref, f32[4,640]{1,0:T(4,128)S(1)} %get-tuple-element.42.sums_ref, bf16[4,1792]{1,0:T(4,128)(2,1)S(1)} %get-tuple-element.43.moe_ref, bf16[4,64,576]{2,1,0:T(8,128)(2,1)S(1)} %copy-done.1, ...), custom_call_target="tpu_custom_call" | custom-call | tf_op jit(solution)/shard_map/finish/pallas_call | solution.py:85
  (11 shorter events, 0.1 us)
Async XLA Ops:
  0.6 0.9 %copy-start = (bf16[4,2]{0,1:T(2,128)(2,1)S(1)}, bf16[4,2]{0,1:T(2,128)(2,1)}, u32[]{:S(2)}) copy-start(bf16[4,2]{0,1:T(2,128)(2,1)} %param.13) | copy-start | bytes 52
  2.6 5.7 %collective-permute-start.1 = (bf16[4,7296]{1,0:T(4,128)(2,1)S(1)}, bf16[4,7296]{1,0:T(4,128)(2,1)S(1)}, u32[]{:S(2)}, u32[]{:S(2)}) collective-permute-start(bf16[4,7296]{1,0:T(4,128)(2,1)S(1)} %pad_maximum_fusion.refs_0_), channel_id=1, source_target_pairs={{0,4},{1,5},{2,6},{3,7},{4,0},{5,1},{6,2},{7,3},{8,12},{9,13},{10,... | collective-permute-start | bytes 175112 | tf_op jit(solution)/shard_map/ppermute | solution.py:24
  5.7 6.3 %collective-permute-start = (bf16[4,7296]{1,0:T(4,128)(2,1)S(1)}, bf16[4,7296]{1,0:T(4,128)(2,1)S(1)}, u32[]{:S(2)}, u32[]{:S(2)}) collective-permute-start(bf16[4,7296]{1,0:T(4,128)(2,1)S(1)} %pad_maximum_fusion.refs_0_), channel_id=1, source_target_pairs={{0,8},{1,9},{2,10},{3,11},{4,12},{5,13},{6,14},{7,15},{8,0},{9,1},... | collective-permute-start | bytes 175112 | tf_op jit(solution)/shard_map/ppermute | solution.py:24
  8.3 6.7 %collective-permute-start.2 = (bf16[4,7296]{1,0:T(4,128)(2,1)S(1)}, bf16[4,7296]{1,0:T(4,128)(2,1)S(1)}, u32[]{:S(2)}, u32[]{:S(2)}) collective-permute-start(bf16[4,7296]{1,0:T(4,128)(2,1)S(1)} %pad_maximum_fusion.refs_0_), channel_id=1, source_target_pairs={{0,12},{1,13},{2,14},{3,15},{4,8},{5,9},{6,10},{7,11},{8,4},{9,5},... | collective-permute-start | bytes 175112 | tf_op jit(solution)/shard_map/ppermute | solution.py:24
  8.3 25.1 %collective-permute-start.10 = (bf16[448,576]{1,0:T(8,128)(2,1)}, bf16[448,576]{1,0:T(8,128)(2,1)S(1)}, u32[]{:S(2)}, u32[]{:S(2)}) collective-permute-start(bf16[448,576]{1,0:T(8,128)(2,1)} %refs_3_.1), channel_id=1, source_target_pairs={{0,4},{1,5},{2,6},{3,7},{4,0},{5,1},{6,2},{7,3},{8,12},{9,13},{10,... | collective-permute-start | bytes 1548296 | tf_op jit(solution)/shard_map/ppermute | solution.py:24
  15.0 8.6 %collective-permute-start.3 = (bf16[16,7296]{1,0:T(8,128)(2,1)S(1)}, bf16[16,7296]{1,0:T(8,128)(2,1)S(1)}, u32[]{:S(2)}, u32[]{:S(2)}) collective-permute-start(bf16[16,7296]{1,0:T(8,128)(2,1)S(1)} %pack_rows.1.refs_1_.own_ref), channel_id=1, source_target_pairs={{0,2},{1,3},{2,0},{3,1},{4,6},{5,7},{6,4},{7,5},{8,10},{9,11},{10,... | collective-permute-start | bytes 700424 | tf_op jit(solution)/shard_map/ppermute | solution.py:24
  16.6 7.5 %collective-permute-start.4 = (bf16[16,7296]{1,0:T(8,128)(2,1)S(1)}, bf16[16,7296]{1,0:T(8,128)(2,1)S(1)}, u32[]{:S(2)}, u32[]{:S(2)}) collective-permute-start(bf16[16,7296]{1,0:T(8,128)(2,1)S(1)} %pack_rows.1.refs_1_.own_ref), channel_id=1, source_target_pairs={{0,16},{16,0},{1,17},{17,1},{2,18},{18,2},{3,19},{19,3},{4,20},{20... | collective-permute-start | bytes 700424 | tf_op jit(solution)/shard_map/ppermute | solution.py:22
  18.1 8.4 %collective-permute-start.5 = (bf16[16,7296]{1,0:T(8,128)(2,1)S(1)}, bf16[16,7296]{1,0:T(8,128)(2,1)S(1)}, u32[]{:S(2)}, u32[]{:S(2)}) collective-permute-start(bf16[16,7296]{1,0:T(8,128)(2,1)S(1)} %pack_rows.1.refs_1_.own_ref), channel_id=1, source_target_pairs={{0,18},{1,19},{2,16},{3,17},{4,22},{5,23},{6,20},{7,21},{8,26},{9,... | collective-permute-start | bytes 700424 | tf_op jit(solution)/shard_map/ppermute | solution.py:30
  18.5 8.0 %collective-permute-start.6 = (bf16[16,7296]{1,0:T(8,128)(2,1)S(1)}, bf16[16,7296]{1,0:T(8,128)(2,1)S(1)}, u32[]{:S(2)}, u32[]{:S(2)}) collective-permute-start(bf16[16,7296]{1,0:T(8,128)(2,1)S(1)} %pack_rows.1.refs_1_.own_ref), channel_id=1, source_target_pairs={{0,1},{1,0},{2,3},{3,2},{4,5},{5,4},{6,7},{7,6},{8,9},{9,8},{10,11... | collective-permute-start | bytes 700424 | tf_op jit(solution)/shard_map/ppermute | solution.py:24
  23.6 2.9 %collective-permute-start.7 = (bf16[16,7296]{1,0:T(8,128)(2,1)S(1)}, bf16[16,7296]{1,0:T(8,128)(2,1)S(1)}, u32[]{:S(2)}, u32[]{:S(2)}) collective-permute-start(bf16[16,7296]{1,0:T(8,128)(2,1)S(1)} %collective-permute-done.3.refs_2_.low_ref), channel_id=1, source_target_pairs={{0,1},{1,0},{2,3},{3,2},{4,5},{5,4},{6,7},{7,6},{8,9},{9,8},{10,11... | collective-permute-start | bytes 700424 | tf_op jit(solution)/shard_map/ppermute | solution.py:24
  24.0 2.5 %collective-permute-start.8 = (bf16[16,7296]{1,0:T(8,128)(2,1)S(1)}, bf16[16,7296]{1,0:T(8,128)(2,1)S(1)}, u32[]{:S(2)}, u32[]{:S(2)}) collective-permute-start(bf16[16,7296]{1,0:T(8,128)(2,1)S(1)} %collective-permute-done.4.refs_3_), channel_id=1, source_target_pairs={{0,1},{1,0},{2,3},{3,2},{4,5},{5,4},{6,7},{7,6},{8,9},{9,8},{10,11... | collective-permute-start | bytes 700424 | tf_op jit(solution)/shard_map/ppermute | solution.py:24
  26.5 1.5 %collective-permute-start.9 = (bf16[16,7296]{1,0:T(8,128)(2,1)S(1)}, bf16[16,7296]{1,0:T(8,128)(2,1)S(1)}, u32[]{:S(2)}, u32[]{:S(2)}) collective-permute-start(bf16[16,7296]{1,0:T(8,128)(2,1)S(1)} %collective-permute-done.5.refs_4_), channel_id=1, source_target_pairs={{0,1},{1,0},{2,3},{3,2},{4,5},{5,4},{6,7},{7,6},{8,9},{9,8},{10,11... | collective-permute-start | bytes 700424 | tf_op jit(solution)/shard_map/ppermute | solution.py:24
  26.6 12.5 %copy-start.3 = (bf16[448,576]{1,0:T(8,128)(2,1)S(1)}, bf16[448,576]{1,0:T(8,128)(2,1)}, u32[]{:S(2)}) copy-start(bf16[448,576]{1,0:T(8,128)(2,1)} %refs_3_.1) | copy-start | bytes 1548292
  33.3 22.9 %copy-start.4 = (f32[7168]{0:T(1024)S(1)}, f32[7168]{0:T(1024)}, u32[]{:S(2)}) copy-start(f32[7168]{0:T(1024)} %param.17) | copy-start | bytes 86020
  33.3 28.5 %copy-start.1 = (bf16[4,64,576]{2,1,0:T(8,128)(2,1)S(1)}, bf16[4,64,576]{2,1,0:T(8,128)(2,1)}, u32[]{:S(2)}) copy-start(bf16[4,64,576]{2,1,0:T(8,128)(2,1)} %q_ref.3) | copy-start | bytes 884740
  33.4 28.5 %copy-start.2 = (bf16[4,256,576]{1,2,0:T(8,128)(2,1)S(1)}, bf16[4,256,576]{1,2,0:T(8,128)(2,1)}, u32[]{:S(2)}) copy-start(bf16[4,256,576]{1,2,0:T(8,128)(2,1)} %param.20) | copy-start | bytes 3538948
  33.4 28.5 %copy-start.5 = (s32[4]{0:T(128)S(1)}, s32[4]{0:T(128)}, u32[]{:S(2)}) copy-start(s32[4]{0:T(128)} %lengths_ref.1) | copy-start | bytes 52
  33.4 1.9 %collective-permute-start.11 = (bf16[64,3584]{1,0:T(8,128)(2,1)S(1)}, bf16[64,3584]{1,0:T(8,128)(2,1)S(1)}, u32[]{:S(2)}, u32[]{:S(2)}) collective-permute-start(bf16[64,3584]{1,0:T(8,128)(2,1)S(1)} %get-tuple-element.33), channel_id=1, source_target_pairs={{0,1},{1,0},{2,3},{3,2},{4,5},{5,4},{6,7},{7,6},{8,9},{9,8},{10,11... | collective-permute-start | bytes 1376264 | tf_op jit(solution)/shard_map/ppermute | solution.py:24
  33.6 3.3 %collective-permute-start.12 = (bf16[64,3584]{1,0:T(8,128)(2,1)S(1)}, bf16[64,3584]{1,0:T(8,128)(2,1)S(1)}, u32[]{:S(2)}, u32[]{:S(2)}) collective-permute-start(bf16[64,3584]{1,0:T(8,128)(2,1)S(1)} %get-tuple-element.35), channel_id=1, source_target_pairs={{0,1},{1,0},{2,3},{3,2},{4,5},{5,4},{6,7},{7,6},{8,9},{9,8},{10,11... | collective-permute-start | bytes 1376264 | tf_op jit(solution)/shard_map/ppermute | solution.py:24
  35.3 8.5 %collective-permute-start.14 = (bf16[32,3584]{1,0:T(8,128)(2,1)S(1)}, bf16[32,3584]{1,0:T(8,128)(2,1)S(1)}, u32[]{:S(2)}, u32[]{:S(2)}) collective-permute-start(bf16[32,3584]{1,0:T(8,128)(2,1)S(1)} %add_convert_fusion.1), channel_id=1, source_target_pairs={{0,16},{16,0},{1,17},{17,1},{2,18},{18,2},{3,19},{19,3},{4,20},{20... | collective-permute-start | bytes 688136 | tf_op jit(solution)/shard_map/ppermute | solution.py:22
  37.0 12.4 %collective-permute-start.13 = (bf16[32,3584]{1,0:T(8,128)(2,1)S(1)}, bf16[32,3584]{1,0:T(8,128)(2,1)S(1)}, u32[]{:S(2)}, u32[]{:S(2)}) collective-permute-start(bf16[32,3584]{1,0:T(8,128)(2,1)S(1)} %get-tuple-element.53), channel_id=1, source_target_pairs={{0,2},{1,3},{2,0},{3,1},{4,6},{5,7},{6,4},{7,5},{8,10},{9,11},{10,... | collective-permute-start | bytes 688136 | tf_op jit(solution)/shard_map/ppermute | solution.py:24
  38.6 10.8 %collective-permute-start.15 = (bf16[32,3584]{1,0:T(8,128)(2,1)S(1)}, bf16[32,3584]{1,0:T(8,128)(2,1)S(1)}, u32[]{:S(2)}, u32[]{:S(2)}) collective-permute-start(bf16[32,3584]{1,0:T(8,128)(2,1)S(1)} %get-tuple-element.52), channel_id=1, source_target_pairs={{0,18},{1,19},{2,16},{3,17},{4,22},{5,23},{6,20},{7,21},{8,26},{9,... | collective-permute-start | bytes 688136 | tf_op jit(solution)/shard_map/ppermute | solution.py:30
  39.1 14.0 %collective-permute-start.19 = (bf16[448,576]{1,0:T(8,128)(2,1)S(1)}, bf16[448,576]{1,0:T(8,128)(2,1)S(1)}, u32[]{:S(2)}, u32[]{:S(2)}) collective-permute-start(bf16[448,576]{1,0:T(8,128)(2,1)S(1)} %copy-done.3), channel_id=1, source_target_pairs={{0,1},{1,0},{2,3},{3,2},{4,5},{5,4},{6,7},{7,6},{8,9},{9,8},{10,11... | collective-permute-start | bytes 1548296 | tf_op jit(solution)/shard_map/ppermute | solution.py:24
  39.7 13.4 %collective-permute-start.20 = (bf16[448,576]{1,0:T(8,128)(2,1)S(1)}, bf16[448,576]{1,0:T(8,128)(2,1)S(1)}, u32[]{:S(2)}, u32[]{:S(2)}) collective-permute-start(bf16[448,576]{1,0:T(8,128)(2,1)S(1)} %collective-permute-done.10.refs_5_), channel_id=1, source_target_pairs={{0,1},{1,0},{2,3},{3,2},{4,5},{5,4},{6,7},{7,6},{8,9},{9,8},{10,11... | collective-permute-start | bytes 1548296 | tf_op jit(solution)/shard_map/ppermute | solution.py:24
  49.5 5.5 %collective-permute-start.16 = (bf16[16,1792]{1,0:T(8,128)(2,1)S(1)}, bf16[16,1792]{1,0:T(8,128)(2,1)S(1)}, u32[]{:S(2)}, u32[]{:S(2)}) collective-permute-start(bf16[16,1792]{1,0:T(8,128)(2,1)S(1)} %get-tuple-element.51), channel_id=1, source_target_pairs={{0,8},{1,9},{2,10},{3,11},{4,12},{5,13},{6,14},{7,15},{8,0},{9,1},... | collective-permute-start | bytes 172040 | tf_op jit(solution)/shard_map/ppermute | solution.py:24
  50.1 6.1 %collective-permute-start.17 = (bf16[16,1792]{1,0:T(8,128)(2,1)S(1)}, bf16[16,1792]{1,0:T(8,128)(2,1)S(1)}, u32[]{:S(2)}, u32[]{:S(2)}) collective-permute-start(bf16[16,1792]{1,0:T(8,128)(2,1)S(1)} %get-tuple-element.50), channel_id=1, source_target_pairs={{0,12},{1,13},{2,14},{3,15},{4,8},{5,9},{6,10},{7,11},{8,4},{9,5},... | collective-permute-start | bytes 172040 | tf_op jit(solution)/shard_map/ppermute | solution.py:24
  51.5 4.8 %collective-permute-start.18 = (bf16[16,1792]{1,0:T(8,128)(2,1)S(1)}, bf16[16,1792]{1,0:T(8,128)(2,1)S(1)}, u32[]{:S(2)}, u32[]{:S(2)}) collective-permute-start(bf16[16,1792]{1,0:T(8,128)(2,1)S(1)} %get-tuple-element.49), channel_id=1, source_target_pairs={{0,4},{1,5},{2,6},{3,7},{4,0},{5,1},{6,2},{7,3},{8,12},{9,13},{10,... | collective-permute-start | bytes 172040 | tf_op jit(solution)/shard_map/ppermute | solution.py:24
  57.4 6.2 %collective-permute-start.21 = (bf16[4,3072]{1,0:T(4,128)(2,1)S(1)}, bf16[4,3072]{1,0:T(4,128)(2,1)S(1)}, u32[]{:S(2)}, u32[]{:S(2)}) collective-permute-start(bf16[4,3072]{1,0:T(4,128)(2,1)S(1)} %get-tuple-element.46), channel_id=1, source_target_pairs={{0,2},{1,3},{2,0},{3,1},{4,6},{5,7},{6,4},{7,5},{8,10},{9,11},{10,... | collective-permute-start | bytes 73736 | tf_op jit(solution)/shard_map/ppermute | solution.py:24
  59.0 4.7 %collective-permute-start.22 = (bf16[4,3072]{1,0:T(4,128)(2,1)S(1)}, bf16[4,3072]{1,0:T(4,128)(2,1)S(1)}, u32[]{:S(2)}, u32[]{:S(2)}) collective-permute-start(bf16[4,3072]{1,0:T(4,128)(2,1)S(1)} %get-tuple-element.47), channel_id=1, source_target_pairs={{0,8},{1,9},{2,10},{3,11},{4,12},{5,13},{6,14},{7,15},{8,0},{9,1},... | collective-permute-start | bytes 73736 | tf_op jit(solution)/shard_map/ppermute | solution.py:24
  60.1 5.6 %collective-permute-start.23 = (bf16[4,3072]{1,0:T(4,128)(2,1)S(1)}, bf16[4,3072]{1,0:T(4,128)(2,1)S(1)}, u32[]{:S(2)}, u32[]{:S(2)}) collective-permute-start(bf16[4,3072]{1,0:T(4,128)(2,1)S(1)} %get-tuple-element.48), channel_id=1, source_target_pairs={{0,10},{1,11},{2,8},{3,9},{4,14},{5,15},{6,12},{7,13},{8,2},{9,3},... | collective-permute-start | bytes 73736 | tf_op jit(solution)/shard_map/ppermute | solution.py:24
